TPU v7x, 32 devices: a whole 2x2x4 slice. The times are simulated.
32 devices in a mesh: dp: 8 (over y, x, core), mp: 4 (over z).
Axes of the slice: x: 2, y: 2, z: 4, core: 2. Of those that a mesh axis runs over, the one named last changes fastest.
Arguments:
- hidden_in: bfloat16 [8192, 2048], P(('dp', 'mp')), may hold values from -48 to 48
- output_grad: bfloat16 [8192, 2048], P(('dp', 'mp')), may hold values from -6 to 6
- first_gain: bfloat16 [2048], P('dp'), may hold values from 0.25 to 1.75
- first_shift: bfloat16 [2048], P('dp'), may hold values from -1.75 to 1.75
- query_weight: bfloat16 [2048, 2048], P('dp', 'mp'), may hold values from -0.1875 to 0.1875
- query_bias: bfloat16 [2048], P('dp'), may hold values from -3 to 3
- key_weight: bfloat16 [2048, 2048], P('dp', 'mp'), may hold values from -0.1875 to 0.1875
- value_weight: bfloat16 [2048, 2048], P('dp', 'mp'), may hold values from -0.125 to 0.125
- value_bias: bfloat16 [2048], P('dp'), may hold values from -3 to 3
- out_weight: bfloat16 [2048, 2048], P('dp', 'mp'), may hold values from -0.5 to 0.5
- out_bias: bfloat16 [2048], P('dp'), may hold values from -3 to 3
- second_gain: bfloat16 [2048], P('dp'), may hold values from 0.25 to 1.75
- second_shift: bfloat16 [2048], P('dp'), may hold values from -1.75 to 1.75
- up_weight: bfloat16 [2048, 8192], P('dp', 'mp'), may hold values from -0.125 to 0.125
- up_bias: bfloat16 [8192], P('dp'), may hold values from -3 to 3
- down_weight: bfloat16 [2048, 8192], P('dp', 'mp'), may hold values from -0.0625 to 0.0625
- down_bias: bfloat16 [2048], P('dp'), may hold values from -3 to 3
- seq_lengths: int32 [8], replicated, may hold values from 1 to 4096, as said below
- block_order: int32 [64], replicated, may hold values from 0 to 63, as said below
- block_slot: int32 [64], replicated, may hold values from 0 to 63, as said below
Outputs:
- output: bfloat16 [8192, 2048], P(('dp', 'mp'))
- input_grad: float32 [8192, 2048], P(('dp', 'mp'))
- first_gain_grad: float32 [2048], P('dp')
- first_shift_grad: float32 [2048], P('dp')
- query_weight_grad: float32 [2048, 2048], P('dp', 'mp')
- query_bias_grad: float32 [2048], P('dp')
- key_weight_grad: float32 [2048, 2048], P('dp', 'mp')
- value_weight_grad: float32 [2048, 2048], P('dp', 'mp')
- value_bias_grad: float32 [2048], P('dp')
- out_weight_grad: float32 [2048, 2048], P('dp', 'mp')
- out_bias_grad: float32 [2048], P('dp')
- second_gain_grad: float32 [2048], P('dp')
- second_shift_grad: float32 [2048], P('dp')
- up_weight_grad: float32 [2048, 8192], P('dp', 'mp')
- up_bias_grad: float32 [8192], P('dp')
- down_weight_grad: float32 [2048, 8192], P('dp', 'mp')
- down_bias_grad: float32 [2048], P('dp')
Inputs may be any that keep to these rules, and one draw needn't show every extreme that they name: Sequence s covers ceil(seq_lengths[s] / 128) whole blocks, and these block counts add up to 64. `block_order`: a permutation of the blocks; dealt blocks 8 * g to 8 * g + 7 are those of index g of dp. The inverse of block_order: block_slot[block_order[j]] = j.
All inputs are finite; a program needn't handle non-finite values.
Results may differ from a plain program's by a relative error of at most 0.025.
Values may be sent and summed in bfloat16 or wider, within the bound.
A program may use at most 576 MiB of HBM per device.

v0:
```python
import math

import jax
import jax.numpy as jnp
from jax import lax
from jax.sharding import PartitionSpec as P

HEAD_DIM = 128
BLOCK = 128


big_negative = -1e30
norm_epsilon = 1e-05


def layer_norm(values, gain_row, offset):
    average = jnp.mean(values, axis=-1, keepdims=True)
    centred = values - average
    variance = jnp.mean(centred * centred, axis=-1, keepdims=True)
    inverse = lax.rsqrt(variance + norm_epsilon)
    normed = centred * inverse
    return (normed * gain_row + offset, normed, inverse)


def norm_back(upstream, normed, inverse, gain_row):
    scaled = upstream * gain_row
    mean_grad = jnp.mean(scaled, axis=-1, keepdims=True)
    second = jnp.mean(scaled * normed, axis=-1, keepdims=True)
    return inverse * (scaled - mean_grad - normed * second)


def gelu_exact(values):
    return jax.nn.gelu(values, approximate=False)


def contract_last(left, right):
    return lax.dot_general(
        left, right, (((1,), (1,)), ((), ())), preferred_element_type=jnp.float32
    )


def contract_first(left, right):
    return lax.dot_general(
        left, right, (((0,), (0,)), ((), ())), preferred_element_type=jnp.float32
    )


def row_meta(seq_lengths, block_order, first_row, row_count):
    block_count = block_order.shape[0]
    seq_count = seq_lengths.shape[0]
    row_ids = first_row + jnp.arange(row_count, dtype=jnp.int32)
    slot_ids = row_ids // BLOCK
    within = row_ids % BLOCK
    slot_hit = slot_ids[:, None] == jnp.arange(block_count, dtype=jnp.int32)[None, :]
    initial = jnp.sum(jnp.where(slot_hit, block_order[None, :], 0), axis=1)
    block_counts = (seq_lengths + BLOCK - 1) // BLOCK
    starts = jnp.cumsum(block_counts) - block_counts
    seq_ids = jnp.sum((initial[:, None] >= starts[None, :]).astype(jnp.int32), axis=1) - 1
    seq_hit = seq_ids[:, None] == jnp.arange(seq_count, dtype=jnp.int32)[None, :]
    seq_start = jnp.sum(jnp.where(seq_hit, starts[None, :], 0), axis=1)
    seq_length = jnp.sum(jnp.where(seq_hit, seq_lengths[None, :], 0), axis=1)
    position = (initial - seq_start) * BLOCK + within
    return (seq_ids, position, position < seq_length)


def gather_attention(
    query_weight,
    key_weight,
    value_weight,
    out_weight,
    first_gain,
    first_shift,
    query_bias,
    value_bias,
    out_bias,
):
    return (
        lax.all_gather(query_weight, "dp", axis=0, tiled=True),
        lax.all_gather(key_weight, "dp", axis=0, tiled=True),
        lax.all_gather(value_weight, "dp", axis=0, tiled=True),
        lax.all_gather(out_weight, "dp", axis=0, tiled=True),
        lax.all_gather(first_gain, "dp", axis=0, tiled=True),
        lax.all_gather(first_shift, "dp", axis=0, tiled=True),
        lax.all_gather(query_bias, "dp", axis=0, tiled=True),
        lax.all_gather(value_bias, "dp", axis=0, tiled=True),
        lax.all_gather(out_bias, "dp", axis=0, tiled=True),
    )


def gather_feed(up_weight, down_weight, second_gain, second_shift, up_bias, down_bias):
    return (
        lax.all_gather(up_weight, "dp", axis=0, tiled=True),
        lax.all_gather(down_weight, "dp", axis=0, tiled=True),
        lax.all_gather(second_gain, "dp", axis=0, tiled=True),
        lax.all_gather(second_shift, "dp", axis=0, tiled=True),
        lax.all_gather(up_bias, "dp", axis=0, tiled=True),
        lax.all_gather(down_bias, "dp", axis=0, tiled=True),
    )


def whole_rows(local_part):
    return lax.all_gather(local_part, "mp", axis=0, tiled=True)


def row_share(term, local_rows):
    return lax.psum_scatter(
        term(jnp.int32(0), local_rows * lax.axis_size("mp")).astype(jnp.bfloat16),
        "mp",
        scatter_dimension=0,
        tiled=True,
    ).astype(jnp.float32)


def per_device(
    hidden_in,
    output_grad,
    first_gain,
    first_shift,
    query_weight,
    query_bias,
    key_weight,
    value_weight,
    value_bias,
    out_weight,
    out_bias,
    second_gain,
    second_shift,
    up_weight,
    up_bias,
    down_weight,
    down_bias,
    seq_lengths,
    block_order,
    block_slot,
):
    local_rows = hidden_in.shape[0]
    model_width = hidden_in.shape[1]
    mp_count = lax.axis_size("mp")
    mp_index = lax.axis_index("mp")
    dp_index = lax.axis_index("dp")
    group_rows = local_rows * mp_count
    head_width = query_weight.shape[1]
    heads_local = head_width // HEAD_DIM
    hidden_width = up_weight.shape[1]
    score_scale = 1.0 / math.sqrt(HEAD_DIM)
    query_seq, query_pos, query_valid = row_meta(
        seq_lengths, block_order, dp_index * group_rows, group_rows
    )
    own_valid = lax.dynamic_slice_in_dim(query_valid, mp_index * local_rows, local_rows, 0)

    def project(normed_rows, gathered):
        all_rows = whole_rows(normed_rows.astype(jnp.bfloat16))
        bias_query = lax.dynamic_slice_in_dim(
            gathered[6], mp_index * head_width, head_width, 0
        ).astype(jnp.float32)
        bias_value = lax.dynamic_slice_in_dim(
            gathered[7], mp_index * head_width, head_width, 0
        ).astype(jnp.float32)
        queries = (
            jnp.dot(all_rows, gathered[0], preferred_element_type=jnp.float32) + bias_query
        ).astype(jnp.bfloat16)
        key_rows = jnp.dot(all_rows, gathered[1], preferred_element_type=jnp.float32).astype(
            jnp.bfloat16
        )
        value_rows = (
            jnp.dot(all_rows, gathered[2], preferred_element_type=jnp.float32) + bias_value
        ).astype(jnp.bfloat16)
        return (all_rows, queries, key_rows, value_rows)

    def expand(normed_rows, gathered):
        all_rows = whole_rows(normed_rows.astype(jnp.bfloat16))
        bias_up = lax.dynamic_slice_in_dim(
            gathered[4], mp_index * hidden_width, hidden_width, 0
        ).astype(jnp.float32)
        pre_act = jnp.dot(all_rows, gathered[0], preferred_element_type=jnp.float32) + bias_up
        return (all_rows, pre_act, gelu_exact(pre_act).astype(jnp.bfloat16))

    def visible(first_row, row_count):
        key_meta = row_meta(seq_lengths, block_order, first_row, row_count)
        return (
            (query_seq[:, None] == key_meta[0][None, :])
            & (key_meta[1][None, :] <= query_pos[:, None])
            & query_valid[:, None]
        )[None]

    input_rows = hidden_in.astype(jnp.float32)
    attn_params = gather_attention(
        query_weight,
        key_weight,
        value_weight,
        out_weight,
        first_gain,
        first_shift,
        query_bias,
        value_bias,
        out_bias,
    )
    normed_one, unit_one, inverse_one = layer_norm(
        input_rows, attn_params[4].astype(jnp.float32), attn_params[5].astype(jnp.float32)
    )
    rows_one, queries, key_rows, value_rows = project(normed_one, attn_params)
    query_heads = queries.reshape(group_rows, heads_local, HEAD_DIM)
    shard_piece = (
        lax.all_gather(key_rows, "dp", axis=0, tiled=True),
        lax.all_gather(value_rows, "dp", axis=0, tiled=True),
    )
    key_piece = shard_piece[0].reshape(shard_piece[0].shape[0], heads_local, HEAD_DIM)
    value_piece = shard_piece[1].reshape(shard_piece[1].shape[0], heads_local, HEAD_DIM)
    allowed = visible(jnp.int32(0), key_piece.shape[0])
    largest = jnp.full((heads_local, group_rows), big_negative, jnp.float32)
    scores = (
        jnp.einsum("qhd,khd->hqk", query_heads, key_piece, preferred_element_type=jnp.float32)
        * score_scale
    )
    masked = jnp.where(allowed, scores, big_negative)
    new_largest = jnp.maximum(largest, jnp.max(masked, axis=2))
    weights = jnp.where(allowed, jnp.exp(masked - new_largest[:, :, None]), 0.0)
    value_mix = jnp.einsum(
        "hqk,khd->qhd",
        weights.astype(jnp.bfloat16),
        value_piece,
        preferred_element_type=jnp.float32,
    )
    running_total = jnp.sum(weights, axis=2)
    safe_total = jnp.where(query_valid[None, :], running_total, 1.0)
    attended = jnp.where(
        query_valid[:, None, None], value_mix / jnp.transpose(safe_total)[:, :, None], 0.0
    )
    log_total = jnp.where(query_valid[None, :], new_largest + jnp.log(safe_total), 0.0)
    attended_low = attended.reshape(group_rows, head_width).astype(jnp.bfloat16)

    def attention_term(first_row, row_count):
        return contract_last(attended_low, attn_params[3])

    residual = (
        input_rows + row_share(attention_term, local_rows) + attn_params[8].astype(jnp.float32)
    )
    feed_params = gather_feed(up_weight, down_weight, second_gain, second_shift, up_bias, down_bias)
    normed_two, unit_two, inverse_two = layer_norm(
        residual, feed_params[2].astype(jnp.float32), feed_params[3].astype(jnp.float32)
    )
    rows_two, pre_act, hidden_low = expand(normed_two, feed_params)

    def feed_term(first_row, row_count):
        return contract_last(hidden_low, feed_params[1])

    result = residual + row_share(feed_term, local_rows) + feed_params[5].astype(jnp.float32)
    output = jnp.where(own_valid[:, None], result, 0.0).astype(jnp.bfloat16)
    result_grad = jnp.where(own_valid[:, None], output_grad.astype(jnp.float32), 0.0)
    branch_two = result_grad.astype(jnp.bfloat16)
    down_bias_part = jnp.sum(branch_two.astype(jnp.float32), axis=0)
    barrier_out = lax.optimization_barrier(
        (
            up_weight,
            down_weight,
            second_gain,
            second_shift,
            up_bias,
            down_bias,
            normed_two,
            branch_two,
        )
    )
    feed_now = gather_feed(
        barrier_out[0],
        barrier_out[1],
        barrier_out[2],
        barrier_out[3],
        barrier_out[4],
        barrier_out[5],
    )
    rows_two_now, pre_now, hidden_now = expand(barrier_out[6], feed_now)
    branch_rows_two = whole_rows(branch_two)
    down_weight_part = contract_first(branch_rows_two, hidden_now)
    hidden_grad = jnp.dot(branch_rows_two, feed_now[1], preferred_element_type=jnp.float32)
    act_grad = jax.vjp(gelu_exact, pre_now)[1](hidden_grad)[0]
    pre_grad = act_grad.astype(jnp.bfloat16)
    up_bias_local = jnp.sum(pre_grad.astype(jnp.float32), axis=0)
    up_weight_part = contract_first(rows_two_now, pre_grad)

    def feed_back_term(first_row, row_count):
        return contract_last(pre_grad, feed_now[0])

    normed_two_grad = row_share(feed_back_term, local_rows)
    second_gain_part = jnp.sum(normed_two_grad * unit_two, axis=0)
    second_shift_part = jnp.sum(normed_two_grad, axis=0)
    residual_grad = result_grad + norm_back(
        normed_two_grad, unit_two, inverse_two, feed_now[2].astype(jnp.float32)
    )
    branch_one = residual_grad.astype(jnp.bfloat16)
    out_bias_part = jnp.sum(branch_one.astype(jnp.float32), axis=0)
    barrier_out = lax.optimization_barrier(
        (
            query_weight,
            key_weight,
            value_weight,
            out_weight,
            first_gain,
            first_shift,
            query_bias,
            value_bias,
            out_bias,
            normed_one,
            branch_one,
        )
    )
    attn_now = gather_attention(
        barrier_out[0],
        barrier_out[1],
        barrier_out[2],
        barrier_out[3],
        barrier_out[4],
        barrier_out[5],
        barrier_out[6],
        barrier_out[7],
        barrier_out[8],
    )
    rows_one_now, queries_now, key_rows_now, value_rows_now = project(barrier_out[9], attn_now)
    branch_rows_one = whole_rows(branch_one)
    out_weight_part = contract_first(branch_rows_one, attended_low)
    attended_grad = jnp.dot(
        branch_rows_one, attn_now[3], preferred_element_type=jnp.float32
    ).astype(jnp.bfloat16)
    grad_heads = attended_grad.reshape(group_rows, heads_local, HEAD_DIM)
    row_delta = jnp.einsum("qhd,qhd->hq", grad_heads.astype(jnp.float32), attended)
    heads_now = queries_now.reshape(group_rows, heads_local, HEAD_DIM)
    shard_piece = (
        lax.all_gather(key_rows_now, "dp", axis=0, tiled=True),
        lax.all_gather(value_rows_now, "dp", axis=0, tiled=True),
    )
    key_piece = shard_piece[0].reshape(shard_piece[0].shape[0], heads_local, HEAD_DIM)
    value_piece = shard_piece[1].reshape(shard_piece[1].shape[0], heads_local, HEAD_DIM)
    allowed = visible(jnp.int32(0), key_piece.shape[0])
    scores = (
        jnp.einsum("qhd,khd->hqk", heads_now, key_piece, preferred_element_type=jnp.float32)
        * score_scale
    )
    probability = jnp.where(
        allowed, jnp.exp(jnp.where(allowed, scores, big_negative) - log_total[:, :, None]), 0.0
    )
    value_piece_grad = jnp.einsum(
        "hqk,qhd->khd",
        probability.astype(jnp.bfloat16),
        grad_heads,
        preferred_element_type=jnp.float32,
    )
    prob_grad = jnp.einsum(
        "qhd,khd->hqk", grad_heads, value_piece, preferred_element_type=jnp.float32
    )
    score_grad = (probability * (prob_grad - row_delta[:, :, None])).astype(jnp.bfloat16)
    query_more = (
        jnp.einsum("hqk,khd->qhd", score_grad, key_piece, preferred_element_type=jnp.float32)
        * score_scale
    )
    key_piece_grad = (
        jnp.einsum("hqk,qhd->khd", score_grad, heads_now, preferred_element_type=jnp.float32)
        * score_scale
    )
    query_more, key_piece_grad, value_piece_grad = (query_more, key_piece_grad, value_piece_grad)
    key_grad, value_grad = (
        lax.psum_scatter(
            key_piece_grad.astype(jnp.bfloat16), "dp", scatter_dimension=0, tiled=True
        ).astype(jnp.float32),
        lax.psum_scatter(
            value_piece_grad.astype(jnp.bfloat16), "dp", scatter_dimension=0, tiled=True
        ).astype(jnp.float32),
    )
    query_low = query_more.reshape(group_rows, head_width).astype(jnp.bfloat16)
    key_low = key_grad.reshape(group_rows, head_width).astype(jnp.bfloat16)
    value_low = value_grad.reshape(group_rows, head_width).astype(jnp.bfloat16)
    query_weight_part = contract_first(rows_one_now, query_low)
    key_weight_part = contract_first(rows_one_now, key_low)
    value_weight_part = contract_first(rows_one_now, value_low)
    query_bias_local = jnp.sum(query_low.astype(jnp.float32), axis=0)
    value_bias_local = jnp.sum(value_low.astype(jnp.float32), axis=0)

    def attention_back_term(first_row, row_count):
        total_term = contract_last(query_low, attn_now[0])
        total_term = total_term + contract_last(key_low, attn_now[1])
        return total_term + contract_last(value_low, attn_now[2])

    normed_one_grad = row_share(attention_back_term, local_rows)
    first_gain_part = jnp.sum(normed_one_grad * unit_one, axis=0)
    first_shift_part = jnp.sum(normed_one_grad, axis=0)
    input_grad = residual_grad + norm_back(
        normed_one_grad, unit_one, inverse_one, attn_now[4].astype(jnp.float32)
    )
    query_bias_full = lax.dynamic_update_slice_in_dim(
        jnp.zeros((model_width,), jnp.float32), query_bias_local, mp_index * head_width, 0
    )
    value_bias_full = lax.dynamic_update_slice_in_dim(
        jnp.zeros((model_width,), jnp.float32), value_bias_local, mp_index * head_width, 0
    )
    up_bias_full = lax.dynamic_update_slice_in_dim(
        jnp.zeros((hidden_width * mp_count,), jnp.float32),
        up_bias_local,
        mp_index * hidden_width,
        0,
    )
    vector_sums = (
        lax.psum(first_gain_part.astype(jnp.bfloat16), "mp").astype(jnp.float32),
        lax.psum(first_shift_part.astype(jnp.bfloat16), "mp").astype(jnp.float32),
        lax.psum(query_bias_full.astype(jnp.bfloat16), "mp").astype(jnp.float32),
        lax.psum(value_bias_full.astype(jnp.bfloat16), "mp").astype(jnp.float32),
        lax.psum(out_bias_part.astype(jnp.bfloat16), "mp").astype(jnp.float32),
        lax.psum(second_gain_part.astype(jnp.bfloat16), "mp").astype(jnp.float32),
        lax.psum(second_shift_part.astype(jnp.bfloat16), "mp").astype(jnp.float32),
        lax.psum(up_bias_full.astype(jnp.bfloat16), "mp").astype(jnp.float32),
        lax.psum(down_bias_part.astype(jnp.bfloat16), "mp").astype(jnp.float32),
    )
    owned_grads = (
        lax.psum_scatter(
            vector_sums[0].astype(jnp.bfloat16), "dp", scatter_dimension=0, tiled=True
        ).astype(jnp.float32),
        lax.psum_scatter(
            vector_sums[1].astype(jnp.bfloat16), "dp", scatter_dimension=0, tiled=True
        ).astype(jnp.float32),
        lax.psum_scatter(
            query_weight_part.astype(jnp.bfloat16), "dp", scatter_dimension=0, tiled=True
        ).astype(jnp.float32),
        lax.psum_scatter(
            vector_sums[2].astype(jnp.bfloat16), "dp", scatter_dimension=0, tiled=True
        ).astype(jnp.float32),
        lax.psum_scatter(
            key_weight_part.astype(jnp.bfloat16), "dp", scatter_dimension=0, tiled=True
        ).astype(jnp.float32),
        lax.psum_scatter(
            value_weight_part.astype(jnp.bfloat16), "dp", scatter_dimension=0, tiled=True
        ).astype(jnp.float32),
        lax.psum_scatter(
            vector_sums[3].astype(jnp.bfloat16), "dp", scatter_dimension=0, tiled=True
        ).astype(jnp.float32),
        lax.psum_scatter(
            out_weight_part.astype(jnp.bfloat16), "dp", scatter_dimension=0, tiled=True
        ).astype(jnp.float32),
        lax.psum_scatter(
            vector_sums[4].astype(jnp.bfloat16), "dp", scatter_dimension=0, tiled=True
        ).astype(jnp.float32),
        lax.psum_scatter(
            vector_sums[5].astype(jnp.bfloat16), "dp", scatter_dimension=0, tiled=True
        ).astype(jnp.float32),
        lax.psum_scatter(
            vector_sums[6].astype(jnp.bfloat16), "dp", scatter_dimension=0, tiled=True
        ).astype(jnp.float32),
        lax.psum_scatter(
            up_weight_part.astype(jnp.bfloat16), "dp", scatter_dimension=0, tiled=True
        ).astype(jnp.float32),
        lax.psum_scatter(
            vector_sums[7].astype(jnp.bfloat16), "dp", scatter_dimension=0, tiled=True
        ).astype(jnp.float32),
        lax.psum_scatter(
            down_weight_part.astype(jnp.bfloat16), "dp", scatter_dimension=0, tiled=True
        ).astype(jnp.float32),
        lax.psum_scatter(
            vector_sums[8].astype(jnp.bfloat16), "dp", scatter_dimension=0, tiled=True
        ).astype(jnp.float32),
    )
    return (
        output,
        input_grad,
        owned_grads[0],
        owned_grads[1],
        owned_grads[2],
        owned_grads[3],
        owned_grads[4],
        owned_grads[5],
        owned_grads[6],
        owned_grads[7],
        owned_grads[8],
        owned_grads[9],
        owned_grads[10],
        owned_grads[11],
        owned_grads[12],
        owned_grads[13],
        owned_grads[14],
    )


def solution(mesh):
    return jax.shard_map(
        per_device,
        mesh=mesh,
        in_specs=(
            P(("dp", "mp"), None),
            P(("dp", "mp"), None),
            P("dp"),
            P("dp"),
            P("dp", "mp"),
            P("dp"),
            P("dp", "mp"),
            P("dp", "mp"),
            P("dp"),
            P("dp", "mp"),
            P("dp"),
            P("dp"),
            P("dp"),
            P("dp", "mp"),
            P("dp"),
            P("dp", "mp"),
            P("dp"),
            P(),
            P(),
            P(),
        ),
        out_specs=(
            P(("dp", "mp"), None),
            P(("dp", "mp"), None),
            P("dp"),
            P("dp"),
            P("dp", "mp"),
            P("dp"),
            P("dp", "mp"),
            P("dp", "mp"),
            P("dp"),
            P("dp", "mp"),
            P("dp"),
            P("dp"),
            P("dp"),
            P("dp", "mp"),
            P("dp"),
            P("dp", "mp"),
            P("dp"),
        ),
        check_vma=False,
    )
```

profile of v0, /device:TPU:0, one launch (start us, length us, event | category | flops | bytes accessed | tf_op | source)
XLA Modules:
  0.0 2229.8 jit_solution(2618317081438978636)
XLA Ops:
  9.3 10.3 all-gather.1
  40.6 82.9 %all-gather.35.cloned.1.call-done = bf16[1024,2048]{1,0:T(8,128)(2,1)} async-done(((bf16[256,2048]{1,0:T(8,128)(2,1)}), bf16[1024,2048]{1,0:T(8,128)(2,1)}) %all-gather.35.cloned.1.call-update) | async-done | bytes 4194320 | tf_op jit(solution)/shard_map/all_gather | solution.py:102
  138.8 13.1 all-gather.37.cloned.1.call-done
  159.3 9.0 all-gather.3
  169.3 9.6 and_and_fusion
  186.8 51.5 %all-gather.45.cloned.1.call-done = bf16[8192,512]{1,0:T(8,128)(2,1)} async-done(((bf16[1024,512]{1,0:T(8,128)(2,1)}), bf16[8192,512]{1,0:T(8,128)(2,1)}) %all-gather.45.cloned.1.call-update) | async-done | bytes 8388624 | tf_op jit(solution)/shard_map/all_gather | solution.py:204
  238.3 56.5 %fusion = (f32[4,1024]{1,0:T(4,128)S(1)}, f32[4,1024,8192]{2,1,0:T(8,128)}) fusion(pred[1024,8192]{1,0:T(8,128)(4,1)} %and_and_fusion, bf16[1024,4,128]{0,2,1:T(8,128)(2,1)S(1)} %bitcast.168, bf16[8192,512]{1,0:T(8,128)(2,1)} %all-gather.45.cloned.1.call-done), kind=kOutput, calls=%fused_computation.4 | convolution fusion | flops 8690593792 | bytes 152059904 | tf_op jit(solution)/shard_map/qhd,khd->hqk/dot_general | solution.py:212
  294.8 44.0 %fusion.1 = f32[4,1024]{1,0:T(4,128)S(1)} fusion(f32[4,1024,8192]{2,1,0:T(8,128)} %get-tuple-element.85, f32[4,1024]{1,0:T(4,128)S(1)} %broadcast_maximum_fusion, pred[1024,8192]{1,0:T(8,128)(4,1)} %and_and_fusion), kind=kLoop, calls=%fused_computation.5 | loop fusion | flops 167768064 | bytes 142639104 | tf_op jit(solution)/shard_map/reduce_sum | solution.py:224
  339.5 12.0 copy.77
  351.4 54.6 %fusion.166 = (bf16[1024,4,128]{0,2,1:T(8,128)(2,1)S(1)}, f32[1024,4,128]{0,2,1:T(8,128)}) fusion(f32[1024,4]{0,1:T(4,128)S(1)} %get-tuple-element.83, bf16[8192,4,128]{0,2,1:T(8,128)(2,1)} %bitcast.135, f32[4,1024,8192]{2,1,0:T(8,128)} %get-tuple-element.85, f32[4,1024]{1,0:T(4,128)S(1)} %broadcast_maximum_fusion, pred[1024,8192]{1,0:T(8,128)(4,1)} %and_and_fusion, ...), kind=kOutput, calls=%fused_computation.258 | convolution fusion | flops 8759279616 | bytes 154174464 | tf_op jit(solution)/shard_map/hqk,khd->qhd/dot_general | solution.py:218
  440.2 49.8 %reduce-scatter.13.cloned.1.call-done = bf16[256,2048]{1,0:T(8,128)(2,1)} async-done(((bf16[1024,2048]{1,0:T(8,128)(2,1)}), bf16[256,2048]{1,0:T(8,128)(2,1)}) %reduce-scatter.13.cloned.1.call-update) | async-done | bytes 1048592 | tf_op jit(solution)/shard_map/reduce_scatter | solution.py:106
  518.7 28.4 %all-gather.51.cloned.1.call-done = bf16[2048,2048]{1,0:T(8,128)(2,1)} async-done(((bf16[256,2048]{1,0:T(8,128)(2,1)}), bf16[2048,2048]{1,0:T(8,128)(2,1)}) %all-gather.51.cloned.1.call-update) | async-done | bytes 8388624 | tf_op jit(solution)/shard_map/all_gather | solution.py:92
  547.1 56.3 %all-gather.53.cloned.1.call-done = bf16[2048,2048]{1,0:T(8,128)(2,1)} async-done(((bf16[256,2048]{1,0:T(8,128)(2,1)}), bf16[2048,2048]{1,0:T(8,128)(2,1)}) %all-gather.53.cloned.1.call-update) | async-done | bytes 8388624 | tf_op jit(solution)/shard_map/all_gather | solution.py:93
  603.4 83.0 %all-gather.49.cloned.1.call-done = bf16[1024,2048]{1,0:T(8,128)(2,1)} async-done(((bf16[256,2048]{1,0:T(8,128)(2,1)}), bf16[1024,2048]{1,0:T(8,128)(2,1)}) %all-gather.49.cloned.1.call-update) | async-done | bytes 4194320 | tf_op jit(solution)/shard_map/all_gather | solution.py:102
  686.4 39.1 %fusion.75 = bf16[1024,2048]{1,0:T(8,128)(2,1)} fusion(bf16[2048,2048]{1,0:T(8,128)(2,1)} %all-gather.53.cloned.1.call-done, bf16[1024,2048]{1,0:T(8,128)(2,1)} %all-gather.49.cloned.1.call-done, bf16[2048,2048]{1,0:T(8,128)(2,1)} %all-gather.51.cloned.1.call-done, f32[2048]{0:T(1024)S(1)} %dynamic-slice_convert_fusion.1), kind=kOutput, calls=%fused_computation.97 | convolution fusion | flops 17320378368 | bytes 25174016 | tf_op jit(solution)/shard_map/dot_general | solution.py:37
  725.6 42.2 %all-gather.55.cloned.1.call-done = bf16[1024,2048]{1,0:T(8,128)(2,1)} async-done(((bf16[256,2048]{1,0:T(8,128)(2,1)}), bf16[1024,2048]{1,0:T(8,128)(2,1)}) %all-gather.55.cloned.1.call-update) | async-done | bytes 4194320 | tf_op jit(solution)/shard_map/all_gather | solution.py:102
  767.8 55.0 %all-gather.57.cloned.1.call-done = bf16[2048,2048]{1,0:T(8,128)(2,1)} async-done(((bf16[256,2048]{1,0:T(8,128)(2,1)}), bf16[2048,2048]{1,0:T(8,128)(2,1)}) %all-gather.57.cloned.1.call-update) | async-done | bytes 8388624 | tf_op jit(solution)/shard_map/all_gather | solution.py:92
  822.8 14.5 fusion.167
  837.3 68.4 %all-gather.59.cloned.1.call-done = bf16[1024,2048]{1,0:T(8,128)(2,1)} async-done(((bf16[256,2048]{1,0:T(8,128)(2,1)}), bf16[1024,2048]{1,0:T(8,128)(2,1)}) %all-gather.59.cloned.1.call-update) | async-done | bytes 4194320 | tf_op jit(solution)/shard_map/all_gather | solution.py:102
  905.7 54.8 %all-gather.61.cloned.1.call-done = bf16[2048,2048]{1,0:T(8,128)(2,1)} async-done(((bf16[256,2048]{1,0:T(8,128)(2,1)}), bf16[2048,2048]{1,0:T(8,128)(2,1)}) %all-gather.61.cloned.1.call-update) | async-done | bytes 8388624 | tf_op jit(solution)/shard_map/all_gather | solution.py:93
  960.6 33.6 %convert_reduce_fusion = (bf16[2048]{0:T(1024)(128)(2,1)}, bf16[1024,2048]{1,0:T(8,128)(2,1)S(1)}, f32[1024,2048]{1,0:T(8,128)}) fusion(f32[1024,2048]{1,0:T(8,128)} %fusion.167, f32[2048]{0:T(1024)S(1)} %dynamic-slice_convert_fusion, bf16[1024,2048]{1,0:T(8,128)(2,1)} %all-gather.59.cloned.1.call-done, bf16[2048,2048]{1,0:T(8,128)(2,1)} %all-gather.61.cloned.1.call-done), kind=kOutput, calls=%fused_computation.29 | convolution fusion | flops 8747218944 | bytes 33566720 | tf_op jit(solution)/shard_map/dot_general | solution.py:275
  996.1 10.7 convolution_convert_fusion.2
  1006.9 9.0 all-gather.7
  1023.9 15.7 reduce-scatter.15.cloned.1.call-done
  1039.6 79.4 %reduce-scatter.17.cloned.1.call-done = bf16[256,2048]{1,0:T(8,128)(2,1)} async-done(((bf16[1024,2048]{1,0:T(8,128)(2,1)}), bf16[256,2048]{1,0:T(8,128)(2,1)}) %reduce-scatter.17.cloned.1.call-update) | async-done | bytes 1048592 | tf_op jit(solution)/shard_map/reduce_scatter | solution.py:106
  1132.7 24.9 %all-gather.65.cloned.1.call-done = bf16[2048,512]{1,0:T(8,128)(2,1)} async-done(((bf16[256,512]{1,0:T(8,128)(2,1)}), bf16[2048,512]{1,0:T(8,128)(2,1)}) %all-gather.65.cloned.1.call-update) | async-done | bytes 2097168 | tf_op jit(solution)/shard_map/all_gather | solution.py:79
  1157.7 82.4 %all-gather.63.cloned.1.call-done = bf16[1024,2048]{1,0:T(8,128)(2,1)} async-done(((bf16[256,2048]{1,0:T(8,128)(2,1)}), bf16[1024,2048]{1,0:T(8,128)(2,1)}) %all-gather.63.cloned.1.call-update) | async-done | bytes 4194320 | tf_op jit(solution)/shard_map/all_gather | solution.py:102
  1275.1 23.3 %all-gather.69.cloned.1.call-done = bf16[2048,512]{1,0:T(8,128)(2,1)} async-done(((bf16[256,512]{1,0:T(8,128)(2,1)}), bf16[2048,512]{1,0:T(8,128)(2,1)}) %all-gather.69.cloned.1.call-update) | async-done | bytes 2097168 | tf_op jit(solution)/shard_map/all_gather | solution.py:78
  1303.7 24.7 %all-gather.73.cloned.1.call-done = bf16[2048,512]{1,0:T(8,128)(2,1)} async-done(((bf16[256,512]{1,0:T(8,128)(2,1)}), bf16[2048,512]{1,0:T(8,128)(2,1)}) %all-gather.73.cloned.1.call-update) | async-done | bytes 2097168 | tf_op jit(solution)/shard_map/all_gather | solution.py:81
  1328.4 83.0 %all-gather.71.cloned.1.call-done = bf16[1024,2048]{1,0:T(8,128)(2,1)} async-done(((bf16[256,2048]{1,0:T(8,128)(2,1)}), bf16[1024,2048]{1,0:T(8,128)(2,1)}) %all-gather.71.cloned.1.call-update) | async-done | bytes 4194320 | tf_op jit(solution)/shard_map/all_gather | solution.py:102
  1417.3 49.0 %all-gather.67.cloned.1.call-done = bf16[8192,512]{1,0:T(8,128)(2,1)} async-done(((bf16[1024,512]{1,0:T(8,128)(2,1)}), bf16[8192,512]{1,0:T(8,128)(2,1)}) %all-gather.67.cloned.1.call-update) | async-done | bytes 8388624 | tf_op jit(solution)/shard_map/all_gather | solution.py:328
  1466.3 11.7 copy.79
  1478.0 48.7 %fusion.168 = f32[4,1024,8192]{2,1,0:T(8,128)} fusion(bf16[1024,4,128]{0,2,1:T(8,128)(2,1)S(1)} %bitcast.131, bf16[8192,4,128]{0,2,1:T(8,128)(2,1)} %bitcast.129), kind=kOutput, calls=%fused_computation.260 | convolution fusion | flops 8589934592 | bytes 143654912 | tf_op jit(solution)/shard_map/qhd,khd->hqk/dot_general | solution.py:335
  1526.7 54.7 %fusion.13 = bf16[8192,4,128]{0,2,1:T(8,128)(2,1)} fusion(bf16[1024,4,128]{0,2,1:T(8,128)(2,1)S(1)} %bitcast.166, f32[4,1024,8192]{2,1,0:T(8,128)} %fusion.168, f32[4,1024]{1,0:T(4,128)S(1)} %copy-done.27, pred[1024,8192]{1,0:T(8,128)(4,1)} %and_and_fusion), kind=kOutput, calls=%fused_computation.17 | convolution fusion | flops 8761901056 | bytes 152059904 | tf_op jit(solution)/shard_map/hqk,qhd->khd/dot_general | solution.py:341
  1581.5 86.2 %multiply_convert_fusion = bf16[4,1024,8192]{2,1,0:T(8,128)(2,1)} fusion(f32[4,1024,8192]{2,1,0:T(8,128)} %fusion.168, bf16[1024,4,128]{0,2,1:T(8,128)(2,1)S(1)} %bitcast.167, f32[4,1024]{1,0:T(4,128)S(1)} %get-tuple-element.88, f32[4,1024]{1,0:T(4,128)S(1)} %copy-done.27, pred[1024,8192]{1,0:T(8,128)(4,1)} %and_and_fusion, ...), kind=kOutput, calls=%fused_computation | convolution fusion | flops 8824815616 | bytes 219185152 | tf_op jit(solution)/shard_map/qhd,khd->hqk/dot_general | solution.py:347
  1667.8 27.0 %fusion.20 = bf16[8192,4,128]{0,2,1:T(8,128)(2,1)} fusion(bf16[1024,4,128]{0,2,1:T(8,128)(2,1)S(1)} %bitcast.132, bf16[4,1024,8192]{2,1,0:T(8,128)(2,1)} %multiply_convert_fusion), kind=kOutput, calls=%fused_computation.22 | convolution fusion | flops 8598323200 | bytes 76546048 | tf_op jit(solution)/shard_map/hqk,qhd->khd/dot_general | solution.py:356
  1695.5 16.0 convolution_convert_fusion
  1711.5 14.5 convolution_convert_fusion.1
  1733.4 30.2 %convert_reduce_fusion.3 = (f32[4,128]{1,0:T(4,128)S(1)}, bf16[4,128,1024]{2,1,0:T(8,128)(2,1)S(1)}) fusion(bf16[8192,4,128]{0,2,1:T(8,128)(2,1)} %bitcast.130, bf16[4,1024,8192]{2,1,0:T(8,128)(2,1)} %multiply_convert_fusion), kind=kOutput, calls=%fused_computation.139 | convolution fusion | flops 8592031744 | bytes 76548096 | tf_op jit(solution)/shard_map/hqk,khd->qhd/dot_general | solution.py:352
  1807.6 34.1 %reduce-scatter.35.cloned.1.call-done = bf16[256,2048]{1,0:T(8,128)(2,1)} async-done(((bf16[2048,2048]{1,0:T(8,128)(2,1)}), bf16[256,2048]{1,0:T(8,128)(2,1)}) %reduce-scatter.35.cloned.1.call-update) | async-done | bytes 1048592 | tf_op jit(solution)/shard_map/reduce_scatter | solution.py:451
  1844.4 72.0 %reduce-scatter.33.cloned.1.call-done = bf16[256,2048]{1,0:T(8,128)(2,1)} async-done(((bf16[2048,2048]{1,0:T(8,128)(2,1)}), bf16[256,2048]{1,0:T(8,128)(2,1)}) %reduce-scatter.33.cloned.1.call-update) | async-done | bytes 1048592 | tf_op jit(solution)/shard_map/reduce_scatter | solution.py:445
  1919.2 41.9 %reduce-scatter.31.cloned.1.call-done = bf16[256,512]{1,0:T(8,128)(2,1)} async-done(((bf16[2048,512]{1,0:T(8,128)(2,1)}), bf16[256,512]{1,0:T(8,128)(2,1)}) %reduce-scatter.31.cloned.1.call-update) | async-done | bytes 262160 | tf_op jit(solution)/shard_map/reduce_scatter | solution.py:433
  1963.0 42.6 %reduce-scatter.25.cloned.1.call-done = bf16[256,512]{1,0:T(8,128)(2,1)} async-done(((bf16[2048,512]{1,0:T(8,128)(2,1)}), bf16[256,512]{1,0:T(8,128)(2,1)}) %reduce-scatter.25.cloned.1.call-update) | async-done | bytes 262160 | tf_op jit(solution)/shard_map/reduce_scatter | solution.py:418
  2009.0 41.5 %reduce-scatter.29.cloned.1.call-done = bf16[256,512]{1,0:T(8,128)(2,1)} async-done(((bf16[2048,512]{1,0:T(8,128)(2,1)}), bf16[256,512]{1,0:T(8,128)(2,1)}) %reduce-scatter.29.cloned.1.call-update) | async-done | bytes 262160 | tf_op jit(solution)/shard_map/reduce_scatter | solution.py:427
  2052.4 42.6 %reduce-scatter.27.cloned.1.call-done = bf16[256,512]{1,0:T(8,128)(2,1)} async-done(((bf16[2048,512]{1,0:T(8,128)(2,1)}), bf16[256,512]{1,0:T(8,128)(2,1)}) %reduce-scatter.27.cloned.1.call-update) | async-done | bytes 262160 | tf_op jit(solution)/shard_map/reduce_scatter | solution.py:424
  2096.7 77.4 %reduce-scatter.23.cloned.1.call-done = bf16[256,2048]{1,0:T(8,128)(2,1)} async-done(((bf16[1024,2048]{1,0:T(8,128)(2,1)}), bf16[256,2048]{1,0:T(8,128)(2,1)}) %reduce-scatter.23.cloned.1.call-update) | async-done | bytes 1048592 | tf_op jit(solution)/shard_map/reduce_scatter | solution.py:106
  2177.8 24.6 %all-reduce.9 = (bf16[2048]{0:T(1024)(128)(2,1)S(1)}, bf16[2048]{0:T(1024)(128)(2,1)S(1)}, bf16[2048]{0:T(1024)(128)(2,1)S(1)}, bf16[2048]{0:T(1024)(128)(2,1)S(...) all-reduce(bf16[2048]{0:T(1024)(128)(2,1)S(1)} %get-tuple-element.4, ...), channel_id=8, replica_groups=mesh['dp'=8,'mp'=4] {'dp'}, use_global_device_ids=true, to_apply=%region_26.27.clone | all-reduce | flops 24576 | bytes 98304
  2203.0 11.3 all-reduce.10
  (319 shorter events, 264.6 us)
Async XLA Ops:
  7.2 33.4 %all-gather.43.cloned.1.call-start = ((), (), s32[]{:S(2)}) async-start(), calls=%async_computation.16 | async-start | bytes 2359296 | tf_op jit(solution)/shard_map/all_gather | solution.py:79
  7.9 115.6 %all-gather.35.cloned.1.call-start = ((), (), s32[]{:S(2)}) async-start(), calls=%async_computation.12 | async-start | bytes 5242880 | tf_op jit(solution)/shard_map/all_gather | solution.py:102
  34.9 116.9 %all-gather.37.cloned.1.call-start = ((), (), s32[]{:S(2)}) async-start(), calls=%async_computation.13 | async-start | bytes 2359296 | tf_op jit(solution)/shard_map/all_gather | solution.py:80
  35.6 145.9 %all-gather.41.cloned.1.call-start = ((), (), s32[]{:S(2)}) async-start(), calls=%async_computation.15 | async-start | bytes 2359296 | tf_op jit(solution)/shard_map/all_gather | solution.py:78
  36.2 202.1 %all-gather.45.cloned.1.call-start = ((), (), s32[]{:S(2)}) async-start(), calls=%async_computation.17 | async-start | bytes 9437184 | tf_op jit(solution)/shard_map/all_gather | solution.py:204
  129.7 209.8 %all-gather.39.cloned.1.call-start = ((), (), s32[]{:S(2)}) async-start(), calls=%async_computation.14 | async-start | bytes 9437184 | tf_op jit(solution)/shard_map/all_gather | solution.py:205
  158.0 248.0 %all-gather.47.cloned.1.call-start = ((), (), s32[]{:S(2)}) async-start(), calls=%async_computation.18 | async-start | bytes 2359296 | tf_op jit(solution)/shard_map/all_gather | solution.py:81
  158.8 331.2 %reduce-scatter.13.cloned.1.call-start = ((), (), s32[]{:S(2)}) async-start(), calls=%async_computation.19 | async-start | bytes 5242880 | tf_op jit(solution)/shard_map/reduce_scatter | solution.py:106
  413.1 134.0 %all-gather.51.cloned.1.call-start = ((), (), s32[]{:S(2)}) async-start(), calls=%async_computation.21 | async-start | bytes 9437184 | tf_op jit(solution)/shard_map/all_gather | solution.py:92
  413.9 189.5 %all-gather.53.cloned.1.call-start = ((), (), s32[]{:S(2)}) async-start(), calls=%async_computation.22 | async-start | bytes 9437184 | tf_op jit(solution)/shard_map/all_gather | solution.py:93
  414.4 272.0 %all-gather.49.cloned.1.call-start = ((), (), s32[]{:S(2)}) async-start(), calls=%async_computation.20 | async-start | bytes 5242880 | tf_op jit(solution)/shard_map/all_gather | solution.py:102
  440.2 285.3 %copy-start.10 = (f32[8,1,256]{2,1,0:T(1,128)}, f32[8,1,256]{2,1,0:T(1,128)S(1)}, u32[]{:S(2)}) copy-start(f32[8,1,256]{2,1,0:T(1,128)S(1)} %convert_element_type.382) | copy-start | bytes 24580
  496.9 270.9 %all-gather.55.cloned.1.call-start = ((), (), s32[]{:S(2)}) async-start(), calls=%async_computation.24 | async-start | bytes 5242880 | tf_op jit(solution)/shard_map/all_gather | solution.py:102
  499.0 323.8 %all-gather.57.cloned.1.call-start = ((), (), s32[]{:S(2)}) async-start(), calls=%async_computation.25 | async-start | bytes 9437184 | tf_op jit(solution)/shard_map/all_gather | solution.py:92
  499.7 406.0 %all-gather.59.cloned.1.call-start = ((), (), s32[]{:S(2)}) async-start(), calls=%async_computation.26 | async-start | bytes 5242880 | tf_op jit(solution)/shard_map/all_gather | solution.py:102
  500.3 460.2 %all-gather.61.cloned.1.call-start = ((), (), s32[]{:S(2)}) async-start(), calls=%async_computation.27 | async-start | bytes 9437184 | tf_op jit(solution)/shard_map/all_gather | solution.py:93
  500.9 538.7 %reduce-scatter.15.cloned.1.call-start = ((), (), s32[]{:S(2)}) async-start(), calls=%async_computation.23 | async-start | bytes 5242880 | tf_op jit(solution)/shard_map/reduce_scatter | solution.py:106
  518.7 441.9 %copy-start.32 = (f32[2048]{0:T(1024)}, f32[2048]{0:T(1024)S(1)}, u32[]{:S(2)}) copy-start(f32[2048]{0:T(1024)S(1)} %dynamic-slice_convert_fusion) | copy-start | bytes 24580
  725.5 393.5 %reduce-scatter.17.cloned.1.call-start = ((), (), s32[]{:S(2)}) async-start(), calls=%async_computation.28 | async-start | bytes 5242880 | tf_op jit(solution)/shard_map/reduce_scatter | solution.py:106
  996.1 123.0 %copy-start.1 = (bf16[256,2048]{1,0:T(8,128)(2,1)S(1)}, bf16[256,2048]{1,0:T(8,128)(2,1)}, u32[]{:S(2)}) copy-start(bf16[256,2048]{1,0:T(8,128)(2,1)} %param.20) | copy-start | bytes 3145732
  996.1 123.0 %copy-start.5 = (bf16[256,2048]{1,0:T(8,128)(2,1)S(1)}, bf16[256,2048]{1,0:T(8,128)(2,1)}, u32[]{:S(2)}) copy-start(bf16[256,2048]{1,0:T(8,128)(2,1)} %reduce-scatter.13.cloned.1.call-done) | copy-start | bytes 3145732
  996.1 122.9 %copy-start.11 = (f32[8,1,256]{2,1,0:T(1,128)S(1)}, f32[8,1,256]{2,1,0:T(1,128)}, u32[]{:S(2)}) copy-start(f32[8,1,256]{2,1,0:T(1,128)} %copy-done.10) | copy-start | bytes 24580
  1006.9 150.8 %all-gather.65.cloned.1.call-start = ((), (), s32[]{:S(2)}) async-start(), calls=%async_computation.30 | async-start | bytes 2359296 | tf_op jit(solution)/shard_map/all_gather | solution.py:79
  1129.1 111.0 %all-gather.63.cloned.1.call-start = ((), (), s32[]{:S(2)}) async-start(), calls=%async_computation.29 | async-start | bytes 5242880 | tf_op jit(solution)/shard_map/all_gather | solution.py:102
  1129.8 138.6 %all-gather.75.cloned.1.call-start = ((), (), s32[]{:S(2)}) async-start(), calls=%async_computation.35 | async-start | bytes 2359296 | tf_op jit(solution)/shard_map/all_gather | solution.py:80
  1130.4 168.0 %all-gather.69.cloned.1.call-start = ((), (), s32[]{:S(2)}) async-start(), calls=%async_computation.32 | async-start | bytes 2359296 | tf_op jit(solution)/shard_map/all_gather | solution.py:78
  1131.2 197.3 %all-gather.73.cloned.1.call-start = ((), (), s32[]{:S(2)}) async-start(), calls=%async_computation.34 | async-start | bytes 2359296 | tf_op jit(solution)/shard_map/all_gather | solution.py:81
  1131.9 279.5 %all-gather.71.cloned.1.call-start = ((), (), s32[]{:S(2)}) async-start(), calls=%async_computation.33 | async-start | bytes 5242880 | tf_op jit(solution)/shard_map/all_gather | solution.py:102
  1132.7 333.6 %all-gather.67.cloned.1.call-start = ((), (), s32[]{:S(2)}) async-start(), calls=%async_computation.31 | async-start | bytes 9437184 | tf_op jit(solution)/shard_map/all_gather | solution.py:328
  1246.3 335.2 %all-gather.77.cloned.1.call-start = ((), (), s32[]{:S(2)}) async-start(), calls=%async_computation.36 | async-start | bytes 9437184 | tf_op jit(solution)/shard_map/all_gather | solution.py:329
  1274.6 495.1 %reduce-scatter.21.cloned.1.call-start = ((), (), s32[]{:S(2)}) async-start(), calls=%async_computation.38 | async-start | bytes 9437184 | tf_op jit(solution)/shard_map/reduce_scatter | solution.py:364
  1303.7 174.3 %copy-start.3 = (bf16[1024,512]{0,1:T(8,128)(2,1)}, bf16[1024,512]{0,1:T(8,128)(2,1)S(1)}, u32[]{:S(2)}) copy-start(bf16[1024,512]{0,1:T(8,128)(2,1)S(1)} %add_convert_fusion.3) | copy-start | bytes 3145732
  1581.5 194.7 %reduce-scatter.19.cloned.1.call-start = ((), (), s32[]{:S(2)}) async-start(), calls=%async_computation.37 | async-start | bytes 9437184 | tf_op jit(solution)/shard_map/reduce_scatter | solution.py:361
  1694.8 146.8 %reduce-scatter.35.cloned.1.call-start = ((), (), s32[]{:S(2)}) async-start(), calls=%async_computation.45 | async-start | bytes 9437184 | tf_op jit(solution)/shard_map/reduce_scatter | solution.py:451
  1711.5 205.0 %reduce-scatter.33.cloned.1.call-start = ((), (), s32[]{:S(2)}) async-start(), calls=%async_computation.44 | async-start | bytes 9437184 | tf_op jit(solution)/shard_map/reduce_scatter | solution.py:445
  1726.0 235.1 %reduce-scatter.31.cloned.1.call-start = ((), (), s32[]{:S(2)}) async-start(), calls=%async_computation.43 | async-start | bytes 2359296 | tf_op jit(solution)/shard_map/reduce_scatter | solution.py:433
  1733.3 272.3 %reduce-scatter.25.cloned.1.call-start = ((), (), s32[]{:S(2)}) async-start(), calls=%async_computation.40 | async-start | bytes 2359296 | tf_op jit(solution)/shard_map/reduce_scatter | solution.py:418
  1769.6 281.0 %reduce-scatter.29.cloned.1.call-start = ((), (), s32[]{:S(2)}) async-start(), calls=%async_computation.42 | async-start | bytes 2359296 | tf_op jit(solution)/shard_map/reduce_scatter | solution.py:427
  1776.1 318.8 %reduce-scatter.27.cloned.1.call-start = ((), (), s32[]{:S(2)}) async-start(), calls=%async_computation.41 | async-start | bytes 2359296 | tf_op jit(solution)/shard_map/reduce_scatter | solution.py:424
  1783.2 391.0 %reduce-scatter.23.cloned.1.call-start = ((), (), s32[]{:S(2)}) async-start(), calls=%async_computation.39 | async-start | bytes 5242880 | tf_op jit(solution)/shard_map/reduce_scatter | solution.py:106
  1796.0 379.5 %copy-start.2 = (bf16[256,2048]{1,0:T(8,128)(2,1)S(1)}, bf16[256,2048]{1,0:T(8,128)(2,1)}, u32[]{:S(2)}) copy-start(bf16[256,2048]{1,0:T(8,128)(2,1)} %param.20) | copy-start | bytes 3145732
  1796.0 379.5 %copy-start.18 = (f32[256]{0:T(256)S(1)}, f32[256]{0:T(256)}, u32[]{:S(2)}) copy-start(f32[256]{0:T(256)} %copy-done.16) | copy-start | bytes 3076
  1796.0 379.5 %copy-start.21 = (f32[256]{0:T(256)S(1)}, f32[256]{0:T(256)}, u32[]{:S(2)}) copy-start(f32[256]{0:T(256)} %copy-done.19) | copy-start | bytes 3076
  1796.0 381.7 %copy-start.24 = (bf16[2048]{0:T(1024)(128)(2,1)S(1)}, bf16[2048]{0:T(1024)(128)(2,1)}, u32[]{:S(2)}) copy-start(bf16[2048]{0:T(1024)(128)(2,1)} %get-tuple-element.69) | copy-start | bytes 12292
  1796.0 381.7 %copy-start.25 = (bf16[2048]{0:T(1024)(128)(2,1)S(1)}, bf16[2048]{0:T(1024)(128)(2,1)}, u32[]{:S(2)}) copy-start(bf16[2048]{0:T(1024)(128)(2,1)} %get-tuple-element.74) | copy-start | bytes 12292
  1796.0 381.7 %copy-start.26 = (bf16[2048]{0:T(1024)(128)(2,1)S(1)}, bf16[2048]{0:T(1024)(128)(2,1)}, u32[]{:S(2)}) copy-start(bf16[2048]{0:T(1024)(128)(2,1)} %get-tuple-element.80) | copy-start | bytes 12292
  1796.1 381.7 %copy-start.28 = (bf16[2048]{0:T(1024)(128)(2,1)S(1)}, bf16[2048]{0:T(1024)(128)(2,1)}, u32[]{:S(2)}) copy-start(bf16[2048]{0:T(1024)(128)(2,1)} %get-tuple-element.43) | copy-start | bytes 12292
  1796.1 423.4 %copy-start.6 = (f32[256,2048]{1,0:T(8,128)S(1)}, f32[256,2048]{1,0:T(8,128)}, u32[]{:S(2)}) copy-start(f32[256,2048]{1,0:T(8,128)} %get-tuple-element.76) | copy-start | bytes 6291460
  (42 other events, 1878.8 us)
Sparse Core Ops, SparseCore 0:
  9.9 30.6 all-gather.42
  42.7 80.7 all-gather.34
  125.4 26.4 all-gather.36
  153.6 27.9 all-gather.40
  183.9 54.3 all-gather.44
  240.6 54.3 all-gather.38
  296.9 27.8 all-gather.46
  413.2 76.7 reduce-scatter.12
  492.1 54.9 all-gather.50
  549.0 54.3 all-gather.52
  605.6 80.7 all-gather.48
  688.5 79.2 all-gather.54
  769.9 52.9 all-gather.56
  824.9 80.7 all-gather.58
  907.6 52.9 all-gather.60
  962.8 76.7 reduce-scatter.14
  1041.7 77.2 reduce-scatter.16
  1129.2 28.4 all-gather.64
  1159.3 80.7 all-gather.62
  1242.0 26.4 all-gather.74
  1270.5 27.8 all-gather.68
  1300.5 27.8 all-gather.72
  1330.6 80.7 all-gather.70
  1413.3 52.9 all-gather.66
  1468.3 54.3 all-gather.76
  1581.6 71.4 reduce-scatter.20
  1694.9 71.4 reduce-scatter.18
  1770.3 71.2 reduce-scatter.34
  1845.1 71.2 reduce-scatter.32
  1919.9 41.1 reduce-scatter.30
  1964.4 41.1 reduce-scatter.24
  2009.3 41.2 reduce-scatter.28
  2053.7 41.1 reduce-scatter.26
  2097.3 76.7 reduce-scatter.22
where the time goes:
time: 2240 us; the launch traced here: 2230 us
  waiting for transfers between devices  1340 us (60%)
  matrix products  571 us (25%)
  blocking collectives  160 us (7%)
  other arithmetic  106 us (5%)
  local copies, waits for them, and re-layouts  33 us (1%)
    all_gather x6, waiting for transfers between devices, whole_rows(): return lax.all_gather(local_part, 'mp', axis=0, tiled=True)  442 us
    reduce_scatter x4, waiting for transfers between devices, row_share(): lax.psum_scatter(term(jnp.int32(0), local_rows * lax.axis_size('mp')).ast...  222 us
    all_gather x2, waiting for transfers between devices, gather_feed(): lax.all_gather(down_weight, 'dp', axis=0, tiled=True)  111 us
    dot_general x1, matrix products, per_device(): jnp.einsum('qhd,khd->hqk', grad_heads, value_piece, preferred_element_typ...  86.2 us
    all_gather x2, waiting for transfers between devices, gather_feed(): lax.all_gather(up_weight, 'dp', axis=0, tiled=True)  83.4 us
    reduce_scatter x1, waiting for transfers between devices, per_device(): lax.psum_scatter(up_weight_part.astype(jnp.bfloat16), 'dp', scatter_dimen...  72 us
    dot_general x6, matrix products, contract_last(): lax.dot_general(left, right, (((1,), (1,)), ((), ())), preferred_element_...  68.5 us
    dot_general x1, matrix products, per_device(): jnp.einsum('qhd,khd->hqk', query_heads, key_piece, preferred_element_type...  56.5 us
  transfers between devices with their start and end apart: 34, of which 29 were waited for; matrix products, arithmetic and copies ran while one was open for 30% of the time, Pallas kernels for 0%

commit v1 on v0

--- a/solution.py
+++ b/solution.py
@@ -3,10 +3,18 @@
 import jax
 import jax.numpy as jnp
 from jax import lax
+from jax.experimental import pallas as pl
+from jax.experimental.pallas import tpu as pltpu
 from jax.sharding import PartitionSpec as P
 
 HEAD_DIM = 128
 BLOCK = 128
+KEY_BLOCKS = 4
+MESH = pl.DeviceIdType.MESH
+ANY = pl.BlockSpec(memory_space=pl.ANY)
+VMEM = pl.BlockSpec(memory_space=pltpu.VMEM)
+SMEM = pl.BlockSpec(memory_space=pltpu.SMEM)
+MIB = 1 << 20
 
 
 big_negative = -1e30
@@ -61,6 +69,353 @@
     seq_length = jnp.sum(jnp.where(seq_hit, seq_lengths[None, :], 0), axis=1)
     position = (initial - seq_start) * BLOCK + within
     return (seq_ids, position, position < seq_length)
+
+
+def greet(peers):
+    barrier = pltpu.get_barrier_semaphore()
+    for peer in peers:
+        pl.semaphore_signal(barrier, inc=1, device_id=peer, device_id_type=MESH)
+    pl.semaphore_wait(barrier, len(peers))
+
+
+def remote(src, dst, send_sem, recv_sem, peer):
+    return pltpu.make_async_remote_copy(
+        src_ref=src, dst_ref=dst, send_sem=send_sem, recv_sem=recv_sem,
+        device_id=peer, device_id_type=MESH,
+    )
+
+
+def head_place(heads, members):
+    me = lax.axis_index("dp")
+    return me, me // members, me % members, lax.axis_index("mp")
+
+
+def lanes(head):
+    return pl.ds(pl.multiple_of(head * HEAD_DIM, HEAD_DIM), HEAD_DIM)
+
+
+def to_heads(owned, shared, heads, members, collective_id):
+    rows = (owned + shared)[0].shape[0]
+    n_owned, n_shared = len(owned), len(shared)
+    count = n_owned + n_shared
+
+    def kernel(*refs):
+        ins, outs = refs[:count], refs[count : 2 * count]
+        local_sem, send_sem, recv_sem, fwd_send, fwd_recv = refs[2 * count :]
+        me, group, member, mp = head_place(heads, members)
+
+        def dest(array, source):
+            place = (source // members) if array < n_owned else source
+            return outs[array].at[pl.ds(pl.multiple_of(place * rows, rows), rows)]
+
+        head_peers = [((group ^ o) * members + member, mp) for o in range(1, heads)]
+        pair_peers = [(group * members + (member ^ o), mp) for o in range(1, members)]
+        greet(head_peers + pair_peers)
+        order = list(range(n_owned, count)) + list(range(n_owned))
+        sends, locals_, forwards = {}, [], []
+        for a in order:
+            for o in range(1, heads):
+                copy = remote(ins[a].at[:, lanes(group ^ o)], dest(a, me), send_sem.at[a, o],
+                              recv_sem.at[a, o], head_peers[o - 1])
+                copy.start()
+                sends[a, o] = copy
+        for a in range(count):
+            copy = pltpu.make_async_copy(ins[a].at[:, lanes(group)], dest(a, me), local_sem.at[a])
+            copy.start()
+            locals_.append(copy)
+        for a in range(n_owned, count):
+            for o in range(heads):
+                source = (group ^ o) * members + member
+                if o:
+                    sends[a, o].wait_recv()
+                for p in range(1, members):
+                    piece = ins[a].at[:, lanes(group)] if o == 0 else dest(a, source)
+                    copy = remote(piece, dest(a, source), fwd_send.at[a - n_owned, o, p],
+                                  fwd_recv.at[a - n_owned, o, p], pair_peers[p - 1])
+                    copy.start()
+                    forwards.append(copy)
+        for copy in locals_:
+            copy.wait()
+        for (a, o), copy in sends.items():
+            copy.wait_send()
+            if a < n_owned:
+                copy.wait_recv()
+        for copy in forwards:
+            copy.wait()
+
+    total = rows * lax.axis_size("dp")
+    shapes = [jax.ShapeDtypeStruct((heads * rows, HEAD_DIM), a.dtype) for a in owned]
+    shapes += [jax.ShapeDtypeStruct((total, HEAD_DIM), a.dtype) for a in shared]
+    dma = pltpu.SemaphoreType.DMA
+    return pl.pallas_call(
+        kernel,
+        out_shape=shapes,
+        in_specs=[ANY] * count,
+        out_specs=[ANY] * count,
+        scratch_shapes=[
+            dma((count,)), dma((count, heads)), dma((count, heads)),
+            dma((max(n_shared, 1), heads, members)), dma((max(n_shared, 1), heads, members)),
+        ],
+        compiler_params=pltpu.CompilerParams(collective_id=collective_id, has_side_effects=True),
+        cost_estimate=pl.CostEstimate(flops=0, bytes_accessed=100 * MIB, transcendentals=0),
+    )(*owned, *shared)
+
+
+def to_rows(owned, shared, heads, members, collective_id):
+    rows = owned[0].shape[0] // heads
+    n_owned, n_shared = len(owned), len(shared)
+    count = n_owned + n_shared
+
+    def kernel(*refs):
+        ins, outs = refs[:count], refs[count : 2 * count]
+        local_sem, send_sem, recv_sem, own_sem, part_send, part_recv = refs[2 * count : 2 * count + 6]
+        me, group, member, mp = head_place(heads, members)
+        head_peers = [((group ^ o) * members + member, mp) for o in range(1, heads)]
+        pair_peers = [(group * members + (member ^ o), mp) for o in range(1, members)]
+        greet(head_peers + pair_peers)
+        if n_shared:
+            own, parts, total = refs[2 * count + 6 :]
+        copies, pending = [], {}
+
+        def part(array, o, who):
+            first = pl.multiple_of(((group ^ o) * members + who) * rows, rows)
+            return ins[array].at[pl.ds(first, rows)]
+
+        for s in range(n_shared):
+            for o in range(heads):
+                copy = pltpu.make_async_copy(part(n_owned + s, o, member), own.at[s, o], own_sem.at[s, o])
+                copy.start()
+                pending[s, o, 0] = copy
+                for p in range(1, members):
+                    copy = remote(part(n_owned + s, o, member ^ p), parts.at[s, o, p - 1],
+                                  part_send.at[s, o, p], part_recv.at[s, o, p], pair_peers[p - 1])
+                    copy.start()
+                    pending[s, o, p] = copy
+        for a in range(n_owned):
+            for o in range(heads):
+                piece = ins[a].at[pl.ds(pl.multiple_of((group ^ o) * rows, rows), rows)]
+                place = outs[a].at[:, lanes(group)]
+                if o:
+                    copy = remote(piece, place, send_sem.at[a, o], recv_sem.at[a, o], head_peers[o - 1])
+                else:
+                    copy = pltpu.make_async_copy(piece, place, local_sem.at[a])
+                copy.start()
+                copies.append(copy)
+        for o in list(range(1, heads)) + [0]:
+            for s in range(n_shared):
+                for p in range(members):
+                    if p:
+                        pending[s, o, p].wait_recv()
+                    else:
+                        pending[s, o, p].wait()
+                value = own[s, o].astype(jnp.float32)
+                for p in range(1, members):
+                    value = value + parts[s, o, p - 1].astype(jnp.float32)
+                total[s, o] = value.astype(total.dtype)
+                a = n_owned + s
+                place = outs[a].at[:, lanes(group)]
+                if o:
+                    copy = remote(total.at[s, o], place, send_sem.at[a, o], recv_sem.at[a, o], head_peers[o - 1])
+                else:
+                    copy = pltpu.make_async_copy(total.at[s, o], place, local_sem.at[a])
+                copy.start()
+                copies.append(copy)
+        for s in range(n_shared):
+            for o in range(heads):
+                for p in range(1, members):
+                    pending[s, o, p].wait_send()
+        for copy in copies:
+            copy.wait()
+
+    dma = pltpu.SemaphoreType.DMA
+    slots = max(n_shared, 1)
+    scratch = [
+        dma((count,)), dma((count, heads)), dma((count, heads)),
+        dma((slots, heads)), dma((slots, heads, members)), dma((slots, heads, members)),
+    ]
+    if n_shared:
+        kind = shared[0].dtype
+        scratch += [
+            pltpu.VMEM((n_shared, heads, rows, HEAD_DIM), kind),
+            pltpu.VMEM((n_shared, heads, members - 1, rows, HEAD_DIM), kind),
+            pltpu.VMEM((n_shared, heads, rows, HEAD_DIM), kind),
+        ]
+    return pl.pallas_call(
+        kernel,
+        out_shape=[jax.ShapeDtypeStruct((rows, heads * HEAD_DIM), a.dtype) for a in owned + shared],
+        in_specs=[ANY] * count,
+        out_specs=[ANY] * count,
+        scratch_shapes=scratch,
+        compiler_params=pltpu.CompilerParams(
+            collective_id=collective_id, has_side_effects=True, vmem_limit_bytes=48 * MIB
+        ),
+        cost_estimate=pl.CostEstimate(flops=0, bytes_accessed=100 * MIB, transcendentals=0),
+    )(*owned, *shared)
+
+
+def query_block(index, lengths, order, members, blocks_each):
+    member = lax.axis_index("dp") % members
+    dealt = ((index // blocks_each) * members + member) * blocks_each + index % blocks_each
+    place = order[dealt]
+    first, length, running = jnp.int32(0), jnp.int32(0), jnp.int32(0)
+    for s in range(lengths.shape[0]):
+        inside = place >= running
+        first = jnp.where(inside, running, first)
+        length = jnp.where(inside, lengths[s], length)
+        running = running + (lengths[s] + (BLOCK - 1)) // BLOCK
+    behind = place - first
+    return first, behind, length - behind * BLOCK
+
+
+def key_blocks(block_count, slot, visit):
+    @pl.loop(0, block_count)
+    def _(block):
+        visit(pl.multiple_of(block * BLOCK, BLOCK), pl.multiple_of(slot[block] * BLOCK, BLOCK))
+
+
+def allowed_keys(tile, behind):
+    width = KEY_BLOCKS * BLOCK
+    key_pos = lax.broadcasted_iota(jnp.int32, (width, BLOCK), 0) + tile * width
+    query_pos = lax.broadcasted_iota(jnp.int32, (width, BLOCK), 1) + behind * BLOCK
+    return key_pos <= query_pos
+
+
+def attend(queries, key_rows, value_rows, lengths, order, slot, members, blocks_each):
+    query_count, key_count = queries.shape[0] // BLOCK, key_rows.shape[0] // BLOCK
+    width = KEY_BLOCKS * BLOCK
+    padded = (key_count + KEY_BLOCKS - 1) * BLOCK
+    scale = math.log2(math.e) / math.sqrt(HEAD_DIM)
+
+    def kernel(lengths_ref, order_ref, slot_ref, q_ref, k_ref, v_ref, out_ref, exact_ref, log_ref, keys, values_t):
+        def visit(to, source):
+            keys[pl.ds(to, BLOCK)] = k_ref[pl.ds(source, BLOCK)]
+            values_t[:, pl.ds(to, BLOCK)] = v_ref[pl.ds(source, BLOCK)].T
+
+        key_blocks(key_count, slot_ref, visit)
+        keys[pl.ds(key_count * BLOCK, padded - key_count * BLOCK)] = jnp.zeros(
+            (padded - key_count * BLOCK, HEAD_DIM), keys.dtype)
+        values_t[:, pl.ds(key_count * BLOCK, padded - key_count * BLOCK)] = jnp.zeros(
+            (HEAD_DIM, padded - key_count * BLOCK), keys.dtype)
+
+        @pl.loop(0, query_count)
+        def _(index):
+            first, behind, valid = query_block(index, lengths_ref, order_ref, members, blocks_each)
+            query_t = q_ref[pl.ds(pl.multiple_of(index * BLOCK, BLOCK), BLOCK)].T
+
+            def step(tile, carry):
+                top, total, mix = carry
+                row = pl.multiple_of((first + tile * KEY_BLOCKS) * BLOCK, BLOCK)
+                scores = jnp.dot(keys[pl.ds(row, width)], query_t, preferred_element_type=jnp.float32) * scale
+                scores = jnp.where(allowed_keys(tile, behind), scores, big_negative)
+                new_top = jnp.maximum(top, jnp.max(scores, axis=0, keepdims=True))
+                weights = jnp.exp2(scores - new_top)
+                fade = jnp.exp2(top - new_top)
+                total = total * fade + jnp.sum(weights, axis=0, keepdims=True)
+                mix = mix * fade + jnp.dot(
+                    values_t[:, pl.ds(row, width)], weights.astype(jnp.bfloat16), preferred_element_type=jnp.float32)
+                return new_top, total, mix
+
+            top, total, mix = lax.fori_loop(
+                0, behind // KEY_BLOCKS + 1, step,
+                (jnp.full((1, BLOCK), big_negative, jnp.float32), jnp.zeros((1, BLOCK), jnp.float32),
+                 jnp.zeros((HEAD_DIM, BLOCK), jnp.float32)))
+            live = lax.broadcasted_iota(jnp.int32, (1, BLOCK), 1) < valid
+            mix = jnp.where(live, mix / total, 0.0)
+            exact_ref[index] = mix
+            out_ref[pl.ds(pl.multiple_of(index * BLOCK, BLOCK), BLOCK)] = mix.T.astype(out_ref.dtype)
+            log_ref[index] = jnp.where(live, top + jnp.log2(total), -big_negative)
+
+    return pl.pallas_call(
+        kernel,
+        out_shape=[
+            jax.ShapeDtypeStruct(queries.shape, jnp.bfloat16),
+            jax.ShapeDtypeStruct((query_count, HEAD_DIM, BLOCK), jnp.float32),
+            jax.ShapeDtypeStruct((query_count, 1, BLOCK), jnp.float32),
+        ],
+        in_specs=[SMEM] * 3 + [VMEM] * 3,
+        out_specs=[VMEM] * 3,
+        scratch_shapes=[pltpu.VMEM((padded, HEAD_DIM), jnp.bfloat16), pltpu.VMEM((HEAD_DIM, padded), jnp.bfloat16)],
+        compiler_params=pltpu.CompilerParams(vmem_limit_bytes=56 * MIB),
+        cost_estimate=pl.CostEstimate(flops=8 << 30, bytes_accessed=50 * MIB, transcendentals=8 << 20),
+    )(lengths, order, slot, queries, key_rows, value_rows)
+
+
+def attend_back(queries, key_rows, value_rows, upstream, exact, logs, lengths, order, slot, members, blocks_each):
+    query_count, key_count = queries.shape[0] // BLOCK, key_rows.shape[0] // BLOCK
+    width = KEY_BLOCKS * BLOCK
+    padded = (key_count + KEY_BLOCKS - 1) * BLOCK
+    scale = math.log2(math.e) / math.sqrt(HEAD_DIM)
+    plain_scale = 1.0 / math.sqrt(HEAD_DIM)
+
+    def kernel(lengths_ref, order_ref, slot_ref, q_ref, k_ref, v_ref, g_ref, exact_ref, log_ref,
+               dq_ref, dk_ref, dv_ref, keys, keys_t, values, key_sum, value_sum):
+        def visit(to, source):
+            block = k_ref[pl.ds(source, BLOCK)]
+            keys[pl.ds(to, BLOCK)] = block
+            keys_t[:, pl.ds(to, BLOCK)] = block.T
+            values[pl.ds(to, BLOCK)] = v_ref[pl.ds(source, BLOCK)]
+            key_sum[pl.ds(to, BLOCK)] = jnp.zeros((BLOCK, HEAD_DIM), jnp.float32)
+            value_sum[pl.ds(to, BLOCK)] = jnp.zeros((BLOCK, HEAD_DIM), jnp.float32)
+
+        key_blocks(key_count, slot_ref, visit)
+        tail = pl.ds(key_count * BLOCK, padded - key_count * BLOCK)
+        keys[tail] = jnp.zeros((padded - key_count * BLOCK, HEAD_DIM), keys.dtype)
+        values[tail] = jnp.zeros((padded - key_count * BLOCK, HEAD_DIM), keys.dtype)
+        keys_t[:, tail] = jnp.zeros((HEAD_DIM, padded - key_count * BLOCK), keys.dtype)
+        key_sum[tail] = jnp.zeros((padded - key_count * BLOCK, HEAD_DIM), jnp.float32)
+        value_sum[tail] = jnp.zeros((padded - key_count * BLOCK, HEAD_DIM), jnp.float32)
+
+        @pl.loop(0, query_count)
+        def _(index):
+            first, behind, _ = query_block(index, lengths_ref, order_ref, members, blocks_each)
+            mine = pl.ds(pl.multiple_of(index * BLOCK, BLOCK), BLOCK)
+            query = q_ref[mine]
+            grad = g_ref[mine]
+            query_t, grad_t = query.T, grad.T
+            delta = jnp.sum(grad_t.astype(jnp.float32) * exact_ref[index], axis=0, keepdims=True)
+            log_total = log_ref[index]
+
+            def step(tile, query_grad):
+                row = pl.multiple_of((first + tile * KEY_BLOCKS) * BLOCK, BLOCK)
+                span = pl.ds(row, width)
+                scores = jnp.dot(keys[span], query_t, preferred_element_type=jnp.float32) * scale
+                probability = jnp.where(allowed_keys(tile, behind), jnp.exp2(scores - log_total), 0.0)
+                prob_grad = jnp.dot(values[span], grad_t, preferred_element_type=jnp.float32)
+                score_grad = (probability * (prob_grad - delta)).astype(jnp.bfloat16)
+                value_sum[span] += jnp.dot(
+                    probability.astype(jnp.bfloat16), grad, preferred_element_type=jnp.float32)
+                key_sum[span] += jnp.dot(score_grad, query, preferred_element_type=jnp.float32)
+                return query_grad + jnp.dot(keys_t[:, span], score_grad, preferred_element_type=jnp.float32)
+
+            query_grad = lax.fori_loop(
+                0, behind // KEY_BLOCKS + 1, step, jnp.zeros((HEAD_DIM, BLOCK), jnp.float32))
+            dq_ref[mine] = (query_grad * plain_scale).T.astype(dq_ref.dtype)
+
+        def leave(at, dealt):
+            dk_ref[pl.ds(dealt, BLOCK)] = (key_sum[pl.ds(at, BLOCK)] * plain_scale).astype(dk_ref.dtype)
+            dv_ref[pl.ds(dealt, BLOCK)] = value_sum[pl.ds(at, BLOCK)].astype(dv_ref.dtype)
+
+        key_blocks(key_count, slot_ref, leave)
+
+    return pl.pallas_call(
+        kernel,
+        out_shape=[
+            jax.ShapeDtypeStruct(queries.shape, jnp.bfloat16),
+            jax.ShapeDtypeStruct(key_rows.shape, jnp.bfloat16),
+            jax.ShapeDtypeStruct(key_rows.shape, jnp.bfloat16),
+        ],
+        in_specs=[SMEM] * 3 + [VMEM] * 6,
+        out_specs=[VMEM] * 3,
+        scratch_shapes=[
+            pltpu.VMEM((padded, HEAD_DIM), jnp.bfloat16),
+            pltpu.VMEM((HEAD_DIM, padded), jnp.bfloat16),
+            pltpu.VMEM((padded, HEAD_DIM), jnp.bfloat16),
+            pltpu.VMEM((padded, HEAD_DIM), jnp.float32),
+            pltpu.VMEM((padded, HEAD_DIM), jnp.float32),
+        ],
+        compiler_params=pltpu.CompilerParams(vmem_limit_bytes=60 * MIB),
+        cost_estimate=pl.CostEstimate(flops=20 << 30, bytes_accessed=100 * MIB, transcendentals=8 << 20),
+    )(lengths, order, slot, queries, key_rows, value_rows, upstream, exact, logs)
 
 
 def gather_attention(
@@ -142,11 +497,9 @@
     head_width = query_weight.shape[1]
     heads_local = head_width // HEAD_DIM
     hidden_width = up_weight.shape[1]
-    score_scale = 1.0 / math.sqrt(HEAD_DIM)
-    query_seq, query_pos, query_valid = row_meta(
-        seq_lengths, block_order, dp_index * group_rows, group_rows
-    )
-    own_valid = lax.dynamic_slice_in_dim(query_valid, mp_index * local_rows, local_rows, 0)
+    _, _, own_valid = row_meta(
+        seq_lengths, block_order, dp_index * group_rows + mp_index * local_rows, local_rows
+    )
 
     def project(normed_rows, gathered):
         all_rows = whole_rows(normed_rows.astype(jnp.bfloat16))
@@ -175,14 +528,6 @@
         pre_act = jnp.dot(all_rows, gathered[0], preferred_element_type=jnp.float32) + bias_up
         return (all_rows, pre_act, gelu_exact(pre_act).astype(jnp.bfloat16))
 
-    def visible(first_row, row_count):
-        key_meta = row_meta(seq_lengths, block_order, first_row, row_count)
-        return (
-            (query_seq[:, None] == key_meta[0][None, :])
-            & (key_meta[1][None, :] <= query_pos[:, None])
-            & query_valid[:, None]
-        )[None]
-
     input_rows = hidden_in.astype(jnp.float32)
     attn_params = gather_attention(
         query_weight,
@@ -199,35 +544,15 @@
         input_rows, attn_params[4].astype(jnp.float32), attn_params[5].astype(jnp.float32)
     )
     rows_one, queries, key_rows, value_rows = project(normed_one, attn_params)
-    query_heads = queries.reshape(group_rows, heads_local, HEAD_DIM)
-    shard_piece = (
-        lax.all_gather(key_rows, "dp", axis=0, tiled=True),
-        lax.all_gather(value_rows, "dp", axis=0, tiled=True),
-    )
-    key_piece = shard_piece[0].reshape(shard_piece[0].shape[0], heads_local, HEAD_DIM)
-    value_piece = shard_piece[1].reshape(shard_piece[1].shape[0], heads_local, HEAD_DIM)
-    allowed = visible(jnp.int32(0), key_piece.shape[0])
-    largest = jnp.full((heads_local, group_rows), big_negative, jnp.float32)
-    scores = (
-        jnp.einsum("qhd,khd->hqk", query_heads, key_piece, preferred_element_type=jnp.float32)
-        * score_scale
-    )
-    masked = jnp.where(allowed, scores, big_negative)
-    new_largest = jnp.maximum(largest, jnp.max(masked, axis=2))
-    weights = jnp.where(allowed, jnp.exp(masked - new_largest[:, :, None]), 0.0)
-    value_mix = jnp.einsum(
-        "hqk,khd->qhd",
-        weights.astype(jnp.bfloat16),
-        value_piece,
-        preferred_element_type=jnp.float32,
-    )
-    running_total = jnp.sum(weights, axis=2)
-    safe_total = jnp.where(query_valid[None, :], running_total, 1.0)
-    attended = jnp.where(
-        query_valid[:, None, None], value_mix / jnp.transpose(safe_total)[:, :, None], 0.0
-    )
-    log_total = jnp.where(query_valid[None, :], new_largest + jnp.log(safe_total), 0.0)
-    attended_low = attended.reshape(group_rows, head_width).astype(jnp.bfloat16)
+    members = lax.axis_size("dp") // heads_local
+    blocks_each = group_rows // BLOCK
+    head_queries, head_keys, head_values = to_heads(
+        [queries], [key_rows, value_rows], heads_local, members, 0
+    )
+    head_mix, exact_mix, log_total = attend(
+        head_queries, head_keys, head_values, seq_lengths, block_order, block_slot, members, blocks_each
+    )
+    (attended_low,) = to_rows([head_mix], [], heads_local, members, 1)
 
     def attention_term(first_row, row_count):
         return contract_last(attended_low, attn_params[3])
@@ -249,27 +574,7 @@
     result_grad = jnp.where(own_valid[:, None], output_grad.astype(jnp.float32), 0.0)
     branch_two = result_grad.astype(jnp.bfloat16)
     down_bias_part = jnp.sum(branch_two.astype(jnp.float32), axis=0)
-    barrier_out = lax.optimization_barrier(
-        (
-            up_weight,
-            down_weight,
-            second_gain,
-            second_shift,
-            up_bias,
-            down_bias,
-            normed_two,
-            branch_two,
-        )
-    )
-    feed_now = gather_feed(
-        barrier_out[0],
-        barrier_out[1],
-        barrier_out[2],
-        barrier_out[3],
-        barrier_out[4],
-        barrier_out[5],
-    )
-    rows_two_now, pre_now, hidden_now = expand(barrier_out[6], feed_now)
+    feed_now, rows_two_now, pre_now, hidden_now = feed_params, rows_two, pre_act, hidden_low
     branch_rows_two = whole_rows(branch_two)
     down_weight_part = contract_first(branch_rows_two, hidden_now)
     hidden_grad = jnp.dot(branch_rows_two, feed_now[1], preferred_element_type=jnp.float32)
@@ -289,85 +594,20 @@
     )
     branch_one = residual_grad.astype(jnp.bfloat16)
     out_bias_part = jnp.sum(branch_one.astype(jnp.float32), axis=0)
-    barrier_out = lax.optimization_barrier(
-        (
-            query_weight,
-            key_weight,
-            value_weight,
-            out_weight,
-            first_gain,
-            first_shift,
-            query_bias,
-            value_bias,
-            out_bias,
-            normed_one,
-            branch_one,
-        )
-    )
-    attn_now = gather_attention(
-        barrier_out[0],
-        barrier_out[1],
-        barrier_out[2],
-        barrier_out[3],
-        barrier_out[4],
-        barrier_out[5],
-        barrier_out[6],
-        barrier_out[7],
-        barrier_out[8],
-    )
-    rows_one_now, queries_now, key_rows_now, value_rows_now = project(barrier_out[9], attn_now)
+    attn_now, rows_one_now = attn_params, rows_one
     branch_rows_one = whole_rows(branch_one)
     out_weight_part = contract_first(branch_rows_one, attended_low)
     attended_grad = jnp.dot(
         branch_rows_one, attn_now[3], preferred_element_type=jnp.float32
     ).astype(jnp.bfloat16)
-    grad_heads = attended_grad.reshape(group_rows, heads_local, HEAD_DIM)
-    row_delta = jnp.einsum("qhd,qhd->hq", grad_heads.astype(jnp.float32), attended)
-    heads_now = queries_now.reshape(group_rows, heads_local, HEAD_DIM)
-    shard_piece = (
-        lax.all_gather(key_rows_now, "dp", axis=0, tiled=True),
-        lax.all_gather(value_rows_now, "dp", axis=0, tiled=True),
-    )
-    key_piece = shard_piece[0].reshape(shard_piece[0].shape[0], heads_local, HEAD_DIM)
-    value_piece = shard_piece[1].reshape(shard_piece[1].shape[0], heads_local, HEAD_DIM)
-    allowed = visible(jnp.int32(0), key_piece.shape[0])
-    scores = (
-        jnp.einsum("qhd,khd->hqk", heads_now, key_piece, preferred_element_type=jnp.float32)
-        * score_scale
-    )
-    probability = jnp.where(
-        allowed, jnp.exp(jnp.where(allowed, scores, big_negative) - log_total[:, :, None]), 0.0
-    )
-    value_piece_grad = jnp.einsum(
-        "hqk,qhd->khd",
-        probability.astype(jnp.bfloat16),
-        grad_heads,
-        preferred_element_type=jnp.float32,
-    )
-    prob_grad = jnp.einsum(
-        "qhd,khd->hqk", grad_heads, value_piece, preferred_element_type=jnp.float32
-    )
-    score_grad = (probability * (prob_grad - row_delta[:, :, None])).astype(jnp.bfloat16)
-    query_more = (
-        jnp.einsum("hqk,khd->qhd", score_grad, key_piece, preferred_element_type=jnp.float32)
-        * score_scale
-    )
-    key_piece_grad = (
-        jnp.einsum("hqk,qhd->khd", score_grad, heads_now, preferred_element_type=jnp.float32)
-        * score_scale
-    )
-    query_more, key_piece_grad, value_piece_grad = (query_more, key_piece_grad, value_piece_grad)
-    key_grad, value_grad = (
-        lax.psum_scatter(
-            key_piece_grad.astype(jnp.bfloat16), "dp", scatter_dimension=0, tiled=True
-        ).astype(jnp.float32),
-        lax.psum_scatter(
-            value_piece_grad.astype(jnp.bfloat16), "dp", scatter_dimension=0, tiled=True
-        ).astype(jnp.float32),
-    )
-    query_low = query_more.reshape(group_rows, head_width).astype(jnp.bfloat16)
-    key_low = key_grad.reshape(group_rows, head_width).astype(jnp.bfloat16)
-    value_low = value_grad.reshape(group_rows, head_width).astype(jnp.bfloat16)
+    (head_grad,) = to_heads([attended_grad], [], heads_local, members, 2)
+    head_query_grad, head_key_grad, head_value_grad = attend_back(
+        head_queries, head_keys, head_values, head_grad, exact_mix, log_total,
+        seq_lengths, block_order, block_slot, members, blocks_each,
+    )
+    query_low, key_low, value_low = to_rows(
+        [head_query_grad], [head_key_grad, head_value_grad], heads_local, members, 3
+    )
     query_weight_part = contract_first(rows_one_now, query_low)
     key_weight_part = contract_first(rows_one_now, key_low)
     value_weight_part = contract_first(rows_one_now, value_low)

time: 2240 us -> 1470 us (0.66)
  waiting for transfers between devices: 1340 us -> 819 us
  matrix products: 571 us -> 175 us
  Pallas kernels: 0 us -> 273 us
  other arithmetic: 106 us -> 56.5 us
  blocking collectives: 160 us -> 115 us
  local copies, waits for them, and re-layouts: 33 us -> 7.68 us
    dot_general x7 -> x0, matrix products: 358 us -> none  [the longest x1 86.2 us: per_device(): jnp.einsum('qhd,khd->hqk', grad_heads, value_piece, preferred_element_typ...]
    pallas_call x0 -> x6, Pallas kernels: none -> 273 us  [the longest x2 74.7 us: to_rows(): pl.pallas_call(kernel, out_shape=[jax.ShapeDtypeStruct((rows, heads * HEA...]
    all_gather x6 -> x4, waiting for transfers between devices: 442 us -> 273 us  [whole_rows(): return lax.all_gather(local_part, 'mp', axis=0, tiled=True)]
    all_gather x4 -> x0, waiting for transfers between devices: 101 us -> none  [the longest x1 51.5 us: per_device(): lax.all_gather(key_rows, 'dp', axis=0, tiled=True)]
    reduce_scatter x1, waiting for transfers between devices: 72 us -> 0.01 us  [per_device(): lax.psum_scatter(up_weight_part.astype(jnp.bfloat16), 'dp', scatter_dimen...]
    all_gather x2 -> x1, waiting for transfers between devices: 111 us -> 54.8 us  [gather_feed(): lax.all_gather(down_weight, 'dp', axis=0, tiled=True)]
    reduce_sum x2 -> x1, other arithmetic: 44.1 us -> 0.21 us  [per_device(): query_bias_local = jnp.sum(query_low.astype(jnp.float32), axis=0)]
    all_gather x2 -> x1, waiting for transfers between devices: 83.4 us -> 39.7 us  [gather_feed(): lax.all_gather(up_weight, 'dp', axis=0, tiled=True)]
  transfers between devices with their start and end apart: 34 -> 20, of which waited for: 29 -> 16; matrix products, arithmetic and copies ran while one was open for 30% -> 10% of each run, Pallas kernels for 0% -> 19%
where the time goes in v1:
time: 1470 us; the launch traced here: 1460 us
  waiting for transfers between devices  819 us (56%)
  Pallas kernels  273 us (19%)
  matrix products  175 us (12%)
  blocking collectives  115 us (8%)
  other arithmetic  56.5 us (4%)
  between operations  16.6 us (1%)
    all_gather x4, waiting for transfers between devices, whole_rows(): return lax.all_gather(local_part, 'mp', axis=0, tiled=True)  273 us
    reduce_scatter x4, waiting for transfers between devices, row_share(): lax.psum_scatter(term(jnp.int32(0), local_rows * lax.axis_size('mp')).ast...  260 us
    pallas_call x2, Pallas kernels, to_rows(): pl.pallas_call(kernel, out_shape=[jax.ShapeDtypeStruct((rows, heads * HEA...  74.7 us
    pallas_call x1, Pallas kernels, attend_back(): pl.pallas_call(kernel, out_shape=[jax.ShapeDtypeStruct(queries.shape, jnp...  68.6 us
    pallas_call x1, Pallas kernels, attend(): pl.pallas_call(kernel, out_shape=[jax.ShapeDtypeStruct(queries.shape, jnp...  67.3 us
    pallas_call x2, Pallas kernels, to_heads(): pl.pallas_call(kernel, out_shape=shapes, in_specs=[ANY] * count, out_spec...  62.1 us
    all_gather x1, waiting for transfers between devices, gather_feed(): lax.all_gather(down_weight, 'dp', axis=0, tiled=True)  54.8 us
    dot_general x6, matrix products, contract_last(): lax.dot_general(left, right, (((1,), (1,)), ((), ())), preferred_element_...  52.8 us
  transfers between devices with their start and end apart: 20, of which 16 were waited for; matrix products, arithmetic and copies ran while one was open for 10% of the time, Pallas kernels for 19%

profile of v1, /device:TPU:0, one launch (start us, length us, event | category | flops | bytes accessed | tf_op | source)
XLA Modules:
  0.0 1464.6 jit_solution(2614499993766681791)
XLA Ops:
  8.7 10.3 all-gather
  19.7 8.9 all-gather.1
  36.9 7.9 all-gather.2
  44.9 8.9 all-gather.3
  53.9 69.6 %all-gather.19.cloned.1.call-done = bf16[1024,2048]{1,0:T(8,128)(2,1)} async-done(((bf16[256,2048]{1,0:T(8,128)(2,1)}), bf16[1024,2048]{1,0:T(8,128)(2,1)}) %all-gather.19.cloned.1.call-update) | async-done | bytes 4194320 | tf_op jit(solution)/shard_map/all_gather | solution.py:457
  123.5 6.2 convolution_convert_fusion.10.refs_1_
  129.7 22.2 %all-gather.25.cloned.1.call-done = bf16[2048,512]{1,0:T(8,128)(2,1)} async-done(((bf16[256,512]{1,0:T(8,128)(2,1)}), bf16[2048,512]{1,0:T(8,128)(2,1)}) %all-gather.25.cloned.1.call-update) | async-done | bytes 2097168 | tf_op jit(solution)/shard_map/all_gather | solution.py:435
  151.9 6.2 add_convert_fusion.3.refs_2_
  158.0 23.5 %all-gather.21.cloned.1.call-done = bf16[2048,512]{1,0:T(8,128)(2,1)} async-done(((bf16[256,512]{1,0:T(8,128)(2,1)}), bf16[2048,512]{1,0:T(8,128)(2,1)}) %all-gather.21.cloned.1.call-update) | async-done | bytes 2097168 | tf_op jit(solution)/shard_map/all_gather | solution.py:433
  181.5 6.2 add_convert_fusion.4.refs_0_
  187.7 46.8 %shard_map.323 = (bf16[4096,128]{1,0:T(8,128)(2,1)}, bf16[8192,128]{1,0:T(8,128)(2,1)}, bf16[8192,128]{1,0:T(8,128)(2,1)}) custom-call(bf16[1024,512]{1,0:T(8,128)(2,1)} %add_convert_fusion.4.refs_0_, bf16[1024,512]{1,0:T(8,128)(2,1)} %convolution_convert_fusion.10.refs_1_, bf16[1024,512]{1,0:T(8,128)(2,1)} %add_convert_fusion.3.refs_2_), custom_call_target="tpu_custom_call" | custom-call | bytes 104857600 | tf_op jit(solution)/shard_map/pallas_call | solution.py:150
  234.5 67.3 %shard_map.324 = (bf16[4096,128]{1,0:T(8,128)(2,1)}, f32[32,128,128]{2,1,0:T(8,128)}, f32[32,1,128]{2,1,0:T(1,128)}) custom-call(s32[8]{0:T(128)} %lengths_ref.3, s32[64]{0:T(128)} %order_ref.3, s32[64]{0:T(128)} %slot_ref.3, bf16[4096,128]{1,0:T(8,128)(2,1)} %get-tuple-element.29.q_ref, bf16[8192,128]{1,0:T(8,128)(2,1)} %get-tuple-element.30.k_ref, ...), custom_call_target="tpu_custom_call" | custom-call | flops 8589934592 | bytes 52428800 | tf_op jit(solution)/shard_map/pallas_call | solution.py:328
  303.0 14.4 shard_map.325
  317.4 6.3 convolution_convert_fusion.4
  324.6 8.8 all-gather.4
  333.5 7.9 all-gather.5
  341.5 9.1 all-gather.6
  350.5 50.2 %reduce-scatter.11.cloned.1.call-done = bf16[256,2048]{1,0:T(8,128)(2,1)} async-done(((bf16[1024,2048]{1,0:T(8,128)(2,1)}), bf16[256,2048]{1,0:T(8,128)(2,1)}) %reduce-scatter.11.cloned.1.call-update) | async-done | bytes 1048592 | tf_op jit(solution)/shard_map/reduce_scatter | solution.py:461
  409.1 8.9 all_gather.71
  418.0 39.7 %all-gather.31.cloned.1.call-done = bf16[2048,2048]{1,0:T(8,128)(2,1)} async-done(((bf16[256,2048]{1,0:T(8,128)(2,1)}), bf16[2048,2048]{1,0:T(8,128)(2,1)}) %all-gather.31.cloned.1.call-update) | async-done | bytes 8388624 | tf_op jit(solution)/shard_map/all_gather | solution.py:447
  457.7 83.0 %all-gather.29.cloned.1.call-done = bf16[1024,2048]{1,0:T(8,128)(2,1)} async-done(((bf16[256,2048]{1,0:T(8,128)(2,1)}), bf16[1024,2048]{1,0:T(8,128)(2,1)}) %all-gather.29.cloned.1.call-update) | async-done | bytes 4194320 | tf_op jit(solution)/shard_map/all_gather | solution.py:457
  540.7 14.4 fusion.40
  555.1 67.2 %all-gather.35.cloned.1.call-done = bf16[1024,2048]{1,0:T(8,128)(2,1)} async-done(((bf16[256,2048]{1,0:T(8,128)(2,1)}), bf16[1024,2048]{1,0:T(8,128)(2,1)}) %all-gather.35.cloned.1.call-update) | async-done | bytes 4194320 | tf_op jit(solution)/shard_map/all_gather | solution.py:457
  622.3 54.8 %all-gather.33.cloned.1.call-done = bf16[2048,2048]{1,0:T(8,128)(2,1)} async-done(((bf16[256,2048]{1,0:T(8,128)(2,1)}), bf16[2048,2048]{1,0:T(8,128)(2,1)}) %all-gather.33.cloned.1.call-update) | async-done | bytes 8388624 | tf_op jit(solution)/shard_map/all_gather | solution.py:448
  677.1 33.7 %convert_reduce_fusion = (bf16[2048]{0:T(1024)(128)(2,1)}, bf16[1024,2048]{1,0:T(8,128)(2,1)}, f32[1024,2048]{1,0:T(8,128)}) fusion(f32[1024,2048]{1,0:T(8,128)} %fusion.40, f32[2048]{0:T(1024)S(1)} %dynamic-slice_convert_fusion, bf16[1024,2048]{1,0:T(8,128)(2,1)} %all-gather.35.cloned.1.call-done, bf16[2048,2048]{1,0:T(8,128)(2,1)} %all-gather.33.cloned.1.call-done), kind=kOutput, calls=%fused_computation.2 | convolution fusion | flops 8747218944 | bytes 33566720 | tf_op jit(solution)/shard_map/dot_general | solution.py:580
  710.9 9.9 multiply_convert_fusion
  720.8 14.3 convolution_convert_fusion.3
  735.2 13.9 convolution_convert_fusion.2
  749.8 8.8 all-gather.7
  758.6 53.5 %reduce-scatter.13.cloned.1.call-done = bf16[256,2048]{1,0:T(8,128)(2,1)} async-done(((bf16[1024,2048]{1,0:T(8,128)(2,1)}), bf16[256,2048]{1,0:T(8,128)(2,1)}) %reduce-scatter.13.cloned.1.call-update) | async-done | bytes 1048592 | tf_op jit(solution)/shard_map/reduce_scatter | solution.py:461
  812.1 79.5 %reduce-scatter.15.cloned.1.call-done = bf16[256,2048]{1,0:T(8,128)(2,1)} async-done(((bf16[1024,2048]{1,0:T(8,128)(2,1)}), bf16[256,2048]{1,0:T(8,128)(2,1)}) %reduce-scatter.15.cloned.1.call-update) | async-done | bytes 1048592 | tf_op jit(solution)/shard_map/reduce_scatter | solution.py:461
  898.6 14.2 convolution_convert_fusion.1
  912.9 14.1 convolution_convert_fusion
  927.1 52.9 %all-gather.37.cloned.1.call-done = bf16[1024,2048]{1,0:T(8,128)(2,1)} async-done(((bf16[256,2048]{1,0:T(8,128)(2,1)}), bf16[1024,2048]{1,0:T(8,128)(2,1)}) %all-gather.37.cloned.1.call-update) | async-done | bytes 4194320 | tf_op jit(solution)/shard_map/all_gather | solution.py:457
  980.0 5.9 convolution_convert_fusion.5
  986.2 6.2 convolution_convert_fusion.9.refs_0_
  992.4 15.3 %shard_map.326.g_ref = bf16[4096,128]{1,0:T(8,128)(2,1)} custom-call(bf16[1024,512]{1,0:T(8,128)(2,1)} %convolution_convert_fusion.9.refs_0_), custom_call_target="tpu_custom_call" | custom-call | bytes 104857600 | tf_op jit(solution)/shard_map/pallas_call | solution.py:150
  1007.7 68.6 %shard_map.327 = (bf16[4096,128]{1,0:T(8,128)(2,1)}, bf16[8192,128]{1,0:T(8,128)(2,1)}, bf16[8192,128]{1,0:T(8,128)(2,1)}) custom-call(s32[8]{0:T(128)} %lengths_ref.3, s32[64]{0:T(128)} %order_ref.3, s32[64]{0:T(128)} %slot_ref.3, bf16[4096,128]{1,0:T(8,128)(2,1)} %get-tuple-element.29.q_ref, bf16[8192,128]{1,0:T(8,128)(2,1)} %get-tuple-element.30.k_ref, ...), custom_call_target="tpu_custom_call" | custom-call | flops 21474836480 | bytes 104857600 | tf_op jit(solution)/shard_map/pallas_call | solution.py:400
  1077.5 60.4 %shard_map.328 = (bf16[1024,512]{1,0:T(8,128)(2,1)S(1)}, bf16[1024,512]{1,0:T(8,128)(2,1)S(1)}, bf16[1024,512]{1,0:T(8,128)(2,1)S(1)}) custom-call(bf16[4096,128]{1,0:T(8,128)(2,1)S(1)} %copy-done, bf16[8192,128]{1,0:T(8,128)(2,1)} %get-tuple-element.36.refs_1_, bf16[8192,128]{1,0:T(8,128)(2,1)} %get-tuple-element.37.refs_2_), custom_call_target="tpu_custom_call" | custom-call | bytes 104857600 | tf_op jit(solution)/shard_map/pallas_call | solution.py:243
  1141.7 5.9 convolution_convert_fusion.7
  1163.7 8.5 add_convert_fusion
  1181.8 13.6 reduce-scatter.25.cloned.1.call-done
  1197.2 42.6 %reduce-scatter.19.cloned.1.call-done = bf16[256,512]{1,0:T(8,128)(2,1)} async-done(((bf16[2048,512]{1,0:T(8,128)(2,1)}), bf16[256,512]{1,0:T(8,128)(2,1)}) %reduce-scatter.19.cloned.1.call-update) | async-done | bytes 262160 | tf_op jit(solution)/shard_map/reduce_scatter | solution.py:658
  1241.6 42.9 %reduce-scatter.21.cloned.1.call-done = bf16[256,512]{1,0:T(8,128)(2,1)} async-done(((bf16[2048,512]{1,0:T(8,128)(2,1)}), bf16[256,512]{1,0:T(8,128)(2,1)}) %reduce-scatter.21.cloned.1.call-update) | async-done | bytes 262160 | tf_op jit(solution)/shard_map/reduce_scatter | solution.py:664
  1286.3 42.7 %reduce-scatter.23.cloned.1.call-done = bf16[256,512]{1,0:T(8,128)(2,1)} async-done(((bf16[2048,512]{1,0:T(8,128)(2,1)}), bf16[256,512]{1,0:T(8,128)(2,1)}) %reduce-scatter.23.cloned.1.call-update) | async-done | bytes 262160 | tf_op jit(solution)/shard_map/reduce_scatter | solution.py:667
  1330.8 77.2 %reduce-scatter.17.cloned.1.call-done = bf16[256,2048]{1,0:T(8,128)(2,1)} async-done(((bf16[1024,2048]{1,0:T(8,128)(2,1)}), bf16[256,2048]{1,0:T(8,128)(2,1)}) %reduce-scatter.17.cloned.1.call-update) | async-done | bytes 1048592 | tf_op jit(solution)/shard_map/reduce_scatter | solution.py:461
  1411.7 24.6 %all-reduce.9 = (bf16[2048]{0:T(1024)(128)(2,1)S(1)}, bf16[2048]{0:T(1024)(128)(2,1)S(1)}, bf16[2048]{0:T(1024)(128)(2,1)S(1)}, bf16[2048]{0:T(1024)(128)(2,1)S(...) all-reduce(bf16[2048]{0:T(1024)(128)(2,1)S(1)} %get-tuple-element.4, ...), channel_id=6, replica_groups=mesh['dp'=8,'mp'=4] {'dp'}, use_global_device_ids=true, to_apply=%region_19.20.clone | all-reduce | flops 24576 | bytes 98304
  1436.9 11.3 all-reduce.10
  (192 shorter events, 78.8 us)
Async XLA Ops:
  7.2 29.7 %copy-start.24 = (bf16[256]{0:T(256)(128)(2,1)S(1)}, bf16[256]{0:T(256)(128)(2,1)}, u32[]{:S(2)}) copy-start(bf16[256]{0:T(256)(128)(2,1)} %param.25) | copy-start | bytes 1540
  7.2 37.7 %copy-start.25 = (bf16[256]{0:T(256)(128)(2,1)S(1)}, bf16[256]{0:T(256)(128)(2,1)}, u32[]{:S(2)}) copy-start(bf16[256]{0:T(256)(128)(2,1)} %param.28) | copy-start | bytes 1540
  7.2 46.7 %all-gather.23.cloned.1.call-start = ((), (), s32[]{:S(2)}) async-start(), calls=%async_computation.12 | async-start | bytes 2359296 | tf_op jit(solution)/shard_map/all_gather | solution.py:434
  7.9 115.6 %all-gather.19.cloned.1.call-start = ((), (), s32[]{:S(2)}) async-start(), calls=%async_computation.10 | async-start | bytes 5242880 | tf_op jit(solution)/shard_map/all_gather | solution.py:457
  19.0 12.7 copy-start.10
  30.0 1.7 copy-start.12
  34.9 117.0 %all-gather.25.cloned.1.call-start = ((), (), s32[]{:S(2)}) async-start(), calls=%async_computation.13 | async-start | bytes 2359296 | tf_op jit(solution)/shard_map/all_gather | solution.py:435
  35.6 145.9 %all-gather.21.cloned.1.call-start = ((), (), s32[]{:S(2)}) async-start(), calls=%async_computation.11 | async-start | bytes 2359296 | tf_op jit(solution)/shard_map/all_gather | solution.py:433
  36.2 281.2 %all-gather.27.cloned.1.call-start = ((), (), s32[]{:S(2)}) async-start(), calls=%async_computation.14 | async-start | bytes 2359296 | tf_op jit(solution)/shard_map/all_gather | solution.py:436
  36.8 363.9 %reduce-scatter.11.cloned.1.call-start = ((), (), s32[]{:S(2)}) async-start(), calls=%async_computation.15 | async-start | bytes 5242880 | tf_op jit(solution)/shard_map/reduce_scatter | solution.py:461
  301.8 1.2 copy-start.3
  317.4 6.3 copy-start.1
  323.7 0.8 copy-start.26
  323.7 9.7 copy-start.27
  323.7 17.7 %copy-start.28 = (bf16[256]{0:T(256)(128)(2,1)S(1)}, bf16[256]{0:T(256)(128)(2,1)}, u32[]{:S(2)}) copy-start(bf16[256]{0:T(256)(128)(2,1)} %param.32) | copy-start | bytes 1540
  323.7 77.0 %copy-start.4 = (bf16[256,2048]{1,0:T(8,128)(2,1)S(1)}, bf16[256,2048]{1,0:T(8,128)(2,1)}, u32[]{:S(2)}) copy-start(bf16[256,2048]{1,0:T(8,128)(2,1)} %param.20) | copy-start | bytes 3145732
  323.8 133.9 %all-gather.31.cloned.1.call-start = ((), (), s32[]{:S(2)}) async-start(), calls=%async_computation.17 | async-start | bytes 9437184 | tf_op jit(solution)/shard_map/all_gather | solution.py:447
  324.5 216.2 %all-gather.29.cloned.1.call-start = ((), (), s32[]{:S(2)}) async-start(), calls=%async_computation.16 | async-start | bytes 5242880 | tf_op jit(solution)/shard_map/all_gather | solution.py:457
  400.7 3.6 copy-start.6
  400.7 5.4 copy-start.20
  400.7 5.6 copy-start.19
  400.7 5.9 copy-start.7
  404.3 4.8 copy-start.18
  406.0 216.3 %all-gather.35.cloned.1.call-start = ((), (), s32[]{:S(2)}) async-start(), calls=%async_computation.20 | async-start | bytes 5242880 | tf_op jit(solution)/shard_map/all_gather | solution.py:457
  408.5 268.6 %all-gather.33.cloned.1.call-start = ((), (), s32[]{:S(2)}) async-start(), calls=%async_computation.18 | async-start | bytes 9437184 | tf_op jit(solution)/shard_map/all_gather | solution.py:448
  409.1 403.0 %reduce-scatter.13.cloned.1.call-start = ((), (), s32[]{:S(2)}) async-start(), calls=%async_computation.19 | async-start | bytes 5242880 | tf_op jit(solution)/shard_map/reduce_scatter | solution.py:461
  735.1 156.4 %reduce-scatter.15.cloned.1.call-start = ((), (), s32[]{:S(2)}) async-start(), calls=%async_computation.21 | async-start | bytes 5242880 | tf_op jit(solution)/shard_map/reduce_scatter | solution.py:461
  749.1 230.9 %all-gather.37.cloned.1.call-start = ((), (), s32[]{:S(2)}) async-start(), calls=%async_computation.22 | async-start | bytes 5242880 | tf_op jit(solution)/shard_map/all_gather | solution.py:457
  891.5 4.0 copy-start.8
  898.6 276.5 %reduce-scatter.27.cloned.1.call-start = ((), (), s32[]{:S(2)}) async-start(), calls=%async_computation.28 | async-start | bytes 9437184 | tf_op jit(solution)/shard_map/reduce_scatter | solution.py:685
  912.9 265.1 %reduce-scatter.29.cloned.1.call-start = ((), (), s32[]{:S(2)}) async-start(), calls=%async_computation.29 | async-start | bytes 9437184 | tf_op jit(solution)/shard_map/reduce_scatter | solution.py:691
  927.0 53.0 %copy-start.2 = (bf16[1024,512]{1,0:T(8,128)(2,1)S(1)}, bf16[1024,512]{1,0:T(8,128)(2,1)}, u32[]{:S(2)}) copy-start(bf16[1024,512]{1,0:T(8,128)(2,1)} %copy-done.1) | copy-start | bytes 3145732
  927.0 59.2 %copy-start.23 = (bf16[2048,512]{1,0:T(8,128)(2,1)S(1)}, bf16[2048,512]{1,0:T(8,128)(2,1)}, u32[]{:S(2)}) copy-start(bf16[2048,512]{1,0:T(8,128)(2,1)} %all-gather.27.cloned.1.call-done) | copy-start | bytes 6291460
  927.0 268.4 %reduce-scatter.25.cloned.1.call-start = ((), (), s32[]{:S(2)}) async-start(), calls=%async_computation.27 | async-start | bytes 2359296 | tf_op jit(solution)/shard_map/reduce_scatter | solution.py:673
  985.9 253.8 %reduce-scatter.19.cloned.1.call-start = ((), (), s32[]{:S(2)}) async-start(), calls=%async_computation.24 | async-start | bytes 2359296 | tf_op jit(solution)/shard_map/reduce_scatter | solution.py:658
  1076.3 1.2 copy-start
  1077.5 60.4 %copy-start.21 = (bf16[1024,2048]{1,0:T(8,128)(2,1)S(1)}, bf16[1024,2048]{1,0:T(8,128)(2,1)}, u32[]{:S(2)}) copy-start(bf16[1024,2048]{1,0:T(8,128)(2,1)} %all-gather.19.cloned.1.call-done) | copy-start | bytes 12582916
  1141.6 142.9 %reduce-scatter.21.cloned.1.call-start = ((), (), s32[]{:S(2)}) async-start(), calls=%async_computation.25 | async-start | bytes 2359296 | tf_op jit(solution)/shard_map/reduce_scatter | solution.py:664
  1147.6 181.4 %reduce-scatter.23.cloned.1.call-start = ((), (), s32[]{:S(2)}) async-start(), calls=%async_computation.26 | async-start | bytes 2359296 | tf_op jit(solution)/shard_map/reduce_scatter | solution.py:667
  1153.6 254.5 %reduce-scatter.17.cloned.1.call-start = ((), (), s32[]{:S(2)}) async-start(), calls=%async_computation.23 | async-start | bytes 5242880 | tf_op jit(solution)/shard_map/reduce_scatter | solution.py:461
  1153.9 4.1 copy-start.22
  1158.0 5.7 copy-start.9
  1172.2 2.5 copy-start.17
  1177.9 230.1 %copy-start.5 = (bf16[256,2048]{1,0:T(8,128)(2,1)S(1)}, bf16[256,2048]{1,0:T(8,128)(2,1)}, u32[]{:S(2)}) copy-start(bf16[256,2048]{1,0:T(8,128)(2,1)} %param.20) | copy-start | bytes 3145732
  1177.9 230.1 %copy-start.11 = (f32[8,1,256]{2,1,0:T(1,128)S(1)}, f32[8,1,256]{2,1,0:T(1,128)}, u32[]{:S(2)}) copy-start(f32[8,1,256]{2,1,0:T(1,128)} %copy-done.10) | copy-start | bytes 24580
  1177.9 230.1 %copy-start.13 = (f32[256]{0:T(256)S(1)}, f32[256]{0:T(256)}, u32[]{:S(2)}) copy-start(f32[256]{0:T(256)} %copy-done.12) | copy-start | bytes 3076
  1177.9 230.1 %copy-start.16 = (f32[256]{0:T(256)S(1)}, f32[256]{0:T(256)}, u32[]{:S(2)}) copy-start(f32[256]{0:T(256)} %copy-done.15) | copy-start | bytes 3076
  1180.8 230.8 %copy-start.14 = (bf16[2048]{0:T(1024)(128)(2,1)S(1)}, bf16[2048]{0:T(1024)(128)(2,1)}, u32[]{:S(2)}) copy-start(bf16[2048]{0:T(1024)(128)(2,1)} %get-tuple-element.67) | copy-start | bytes 12292
  (3 other events, 1.9 us)
Sparse Core Ops, SparseCore 0:
  9.9 30.6 all-gather.22
  42.7 80.7 all-gather.18
  125.4 26.4 all-gather.24
  153.6 27.8 all-gather.20
  183.3 42.1 all-gather.26
  323.9 76.7 reduce-scatter.10
  402.7 54.9 all-gather.30
  459.9 80.7 all-gather.28
  543.0 79.2 all-gather.34
  624.2 52.9 all-gather.32
  735.3 76.7 reduce-scatter.12
  814.2 77.2 reduce-scatter.14
  898.7 81.2 all-gather.36
  983.7 69.8 reduce-scatter.26
  1056.9 93.7 reduce-scatter.28
  1154.2 41.1 reduce-scatter.24
  1198.5 41.1 reduce-scatter.18
  1243.2 41.2 reduce-scatter.20
  1287.8 41.1 reduce-scatter.22
  1331.3 76.7 reduce-scatter.16

commit v2 on v1

--- a/solution.py
+++ b/solution.py
@@ -21,15 +21,6 @@
 norm_epsilon = 1e-05
 
 
-def layer_norm(values, gain_row, offset):
-    average = jnp.mean(values, axis=-1, keepdims=True)
-    centred = values - average
-    variance = jnp.mean(centred * centred, axis=-1, keepdims=True)
-    inverse = lax.rsqrt(variance + norm_epsilon)
-    normed = centred * inverse
-    return (normed * gain_row + offset, normed, inverse)
-
-
 def norm_back(upstream, normed, inverse, gain_row):
     scaled = upstream * gain_row
     mean_grad = jnp.mean(scaled, axis=-1, keepdims=True)
@@ -53,22 +44,30 @@
     )
 
 
-def row_meta(seq_lengths, block_order, first_row, row_count):
-    block_count = block_order.shape[0]
-    seq_count = seq_lengths.shape[0]
+def valid_rows(seq_lengths, block_order, first_row, row_count):
     row_ids = first_row + jnp.arange(row_count, dtype=jnp.int32)
-    slot_ids = row_ids // BLOCK
-    within = row_ids % BLOCK
-    slot_hit = slot_ids[:, None] == jnp.arange(block_count, dtype=jnp.int32)[None, :]
+    slot_hit = (row_ids // BLOCK)[:, None] == jnp.arange(block_order.shape[0], dtype=jnp.int32)[None, :]
     initial = jnp.sum(jnp.where(slot_hit, block_order[None, :], 0), axis=1)
     block_counts = (seq_lengths + BLOCK - 1) // BLOCK
-    starts = jnp.cumsum(block_counts) - block_counts
-    seq_ids = jnp.sum((initial[:, None] >= starts[None, :]).astype(jnp.int32), axis=1) - 1
-    seq_hit = seq_ids[:, None] == jnp.arange(seq_count, dtype=jnp.int32)[None, :]
-    seq_start = jnp.sum(jnp.where(seq_hit, starts[None, :], 0), axis=1)
-    seq_length = jnp.sum(jnp.where(seq_hit, seq_lengths[None, :], 0), axis=1)
-    position = (initial - seq_start) * BLOCK + within
-    return (seq_ids, position, position < seq_length)
+    ends = jnp.cumsum(block_counts)
+    starts = ends - block_counts
+    inside = (initial[:, None] >= starts[None, :]) & (initial[:, None] < ends[None, :])
+    left = seq_lengths[None, :] - (initial[:, None] - starts[None, :]) * BLOCK
+    return (row_ids % BLOCK) < jnp.sum(jnp.where(inside, left, 0), axis=1)
+
+
+def whole_rows(local_part):
+    return lax.all_gather(local_part, "mp", axis=0, tiled=True)
+
+
+def row_share(term):
+    term = term.astype(jnp.bfloat16)
+    return lax.psum_scatter(term, "mp", scatter_dimension=0, tiled=True).astype(jnp.float32)
+
+
+def owner_share(term):
+    term = term.astype(jnp.bfloat16)
+    return lax.psum_scatter(term, "dp", scatter_dimension=0, tiled=True).astype(jnp.float32)
 
 
 def greet(peers):
@@ -418,52 +417,506 @@
     )(lengths, order, slot, queries, key_rows, value_rows, upstream, exact, logs)
 
 
-def gather_attention(
-    query_weight,
-    key_weight,
-    value_weight,
-    out_weight,
-    first_gain,
-    first_shift,
-    query_bias,
-    value_bias,
-    out_bias,
-):
-    return (
-        lax.all_gather(query_weight, "dp", axis=0, tiled=True),
-        lax.all_gather(key_weight, "dp", axis=0, tiled=True),
-        lax.all_gather(value_weight, "dp", axis=0, tiled=True),
-        lax.all_gather(out_weight, "dp", axis=0, tiled=True),
-        lax.all_gather(first_gain, "dp", axis=0, tiled=True),
-        lax.all_gather(first_shift, "dp", axis=0, tiled=True),
-        lax.all_gather(query_bias, "dp", axis=0, tiled=True),
-        lax.all_gather(value_bias, "dp", axis=0, tiled=True),
-        lax.all_gather(out_bias, "dp", axis=0, tiled=True),
-    )
-
-
-def gather_feed(up_weight, down_weight, second_gain, second_shift, up_bias, down_bias):
-    return (
-        lax.all_gather(up_weight, "dp", axis=0, tiled=True),
-        lax.all_gather(down_weight, "dp", axis=0, tiled=True),
-        lax.all_gather(second_gain, "dp", axis=0, tiled=True),
-        lax.all_gather(second_shift, "dp", axis=0, tiled=True),
-        lax.all_gather(up_bias, "dp", axis=0, tiled=True),
-        lax.all_gather(down_bias, "dp", axis=0, tiled=True),
-    )
-
-
-def whole_rows(local_part):
-    return lax.all_gather(local_part, "mp", axis=0, tiled=True)
-
-
-def row_share(term, local_rows):
-    return lax.psum_scatter(
-        term(jnp.int32(0), local_rows * lax.axis_size("mp")).astype(jnp.bfloat16),
-        "mp",
-        scatter_dimension=0,
-        tiled=True,
-    ).astype(jnp.float32)
+def line_neighbours(mp, count):
+    return ((1, mp + 1 < count, jnp.minimum(mp + 1, count - 1)), (-1, mp >= 1, jnp.maximum(mp - 1, 0)))
+
+
+def greet_all(fixed, dp, mp, count):
+    barrier = pltpu.get_barrier_semaphore()
+    for peer in fixed:
+        pl.semaphore_signal(barrier, inc=1, device_id=peer, device_id_type=MESH)
+    expected = jnp.int32(len(fixed))
+    for _, there, place in line_neighbours(mp, count):
+
+        @pl.when(there)
+        def _():
+            pl.semaphore_signal(barrier, inc=1, device_id=(dp, place), device_id_type=MESH)
+
+        expected = expected + there.astype(jnp.int32)
+    pl.semaphore_wait(barrier, expected)
+
+
+class LineGather:
+    def __init__(self, own, full, rows, pieces, send_sem, recv_sem, dp, mp, count):
+        self.own, self.full, self.rows, self.pieces = own, full, rows, pieces
+        self.send_sem, self.recv_sem, self.dp, self.mp, self.count = send_sem, recv_sem, dp, mp, count
+        self.size = rows // pieces
+
+    def place(self, block, piece):
+        return self.full.at[pl.ds(pl.multiple_of(block * self.rows + piece * self.size, self.size), self.size)]
+
+    def hop(self, way, step, piece):
+        sign, there, neighbour = line_neighbours(self.mp, self.count)[way]
+        origin = self.mp - sign * step
+        exists = (origin >= 0) & (origin < self.count)
+        origin = jnp.clip(origin, 0, self.count - 1)
+        if step == 0:
+            source = self.own.at[pl.ds(pl.multiple_of(piece * self.size, self.size), self.size)]
+        else:
+            source = self.place(origin, piece)
+        def copy():
+            return remote(source, self.place(origin, piece), self.send_sem.at[way, step, piece],
+                          self.recv_sem.at[way, step, piece], (self.dp, neighbour))
+
+        return exists, exists & there, copy
+
+    def advance(self, step, piece, also=True):
+        for way in range(2):
+            if step:
+                exists, _, _ = self.hop(way, step, piece)
+                _, _, earlier = self.hop(way, step - 1, piece)
+
+                @pl.when(exists & also)
+                def _():
+                    earlier().wait_recv()
+
+            if step < self.count - 1:
+                _, sends, copy = self.hop(way, step, piece)
+
+                @pl.when(sends & also)
+                def _():
+                    copy().start()
+
+    def finish(self):
+        @pl.loop(0, self.pieces)
+        def _(piece):
+            for way in range(2):
+                for step in range(self.count - 1):
+                    _, sends, copy = self.hop(way, step, piece)
+
+                    @pl.when(sends)
+                    def _():
+                        copy().wait_send()
+
+    @staticmethod
+    def semaphores(count, pieces):
+        return [pltpu.SemaphoreType.DMA((2, count, pieces)), pltpu.SemaphoreType.DMA((2, count, pieces))]
+
+
+class LineReduce:
+    def __init__(self, part, flows, rows, pieces, send_sem, recv_sem, dp, mp, count):
+        self.part, self.flows, self.rows, self.pieces = part, flows, rows, pieces
+        self.send_sem, self.recv_sem, self.dp, self.mp, self.count = send_sem, recv_sem, dp, mp, count
+        self.size = rows // pieces
+
+    def span(self, block, piece):
+        return pl.ds(pl.multiple_of(block * self.rows + piece * self.size, self.size), self.size)
+
+    def hop(self, way, block, piece, first=False):
+        neighbour = line_neighbours(self.mp, self.count)[way][2]
+        span = self.span(block, piece)
+        source = self.part.at[span] if first else self.flows.at[way, span]
+        return remote(source, self.flows.at[way, span], self.send_sem.at[way, block, piece],
+                      self.recv_sem.at[way, block, piece], (self.dp, neighbour))
+
+    def roles(self, way, block):
+        if way == 0:
+            behind, ahead = self.mp >= 1, self.mp < block
+            ends = self.mp <= block
+        else:
+            behind, ahead = self.mp < self.count - 1, self.mp > block
+            ends = self.mp >= block
+        return ahead & jnp.logical_not(behind), ahead & behind, ends & behind
+
+    def targets(self):
+        for index in range(self.count - 1):
+            yield 0, self.count - 1 - index
+            yield 1, index
+
+    def begin(self):
+        @pl.loop(0, self.pieces)
+        def _(piece):
+            for way, block in self.targets():
+                begins, _, _ = self.roles(way, block)
+
+                @pl.when(begins)
+                def _():
+                    self.hop(way, block, piece, True).start()
+
+    def advance(self, piece):
+        for way, block in self.targets():
+            _, hands_on, receives = self.roles(way, block)
+
+            @pl.when(receives)
+            def _():
+                self.hop(way, block, piece).wait_recv()
+
+            @pl.when(hands_on)
+            def _():
+                span = self.span(block, piece)
+                value = self.flows[way, span].astype(jnp.float32) + self.part[span].astype(jnp.float32)
+                self.flows[way, span] = value.astype(self.flows.dtype)
+                self.hop(way, block, piece).start()
+
+    def total(self, piece, result):
+        span = self.span(self.mp, piece)
+        result[...] = self.part[span].astype(jnp.float32)
+        for way in range(2):
+
+            @pl.when(self.mp >= 1 if way == 0 else self.mp < self.count - 1)
+            def _():
+                result[...] += self.flows[way, span].astype(jnp.float32)
+
+    def finish(self):
+        @pl.loop(0, self.pieces)
+        def _(piece):
+            for way, block in self.targets():
+                begins, hands_on, _ = self.roles(way, block)
+
+                @pl.when(begins)
+                def _():
+                    self.hop(way, block, piece, True).wait_send()
+
+                @pl.when(hands_on)
+                def _():
+                    self.hop(way, block, piece).wait_send()
+
+    @staticmethod
+    def scratch(count, rows, width, pieces):
+        return [pltpu.VMEM((2, count * rows, width), jnp.bfloat16),
+                pltpu.SemaphoreType.DMA((2, count, pieces)), pltpu.SemaphoreType.DMA((2, count, pieces))]
+
+
+PIECES = 8
+
+
+def gather_first(hidden, vectors, weights, collective_id):
+    rows, width = hidden.shape
+    dp_count, mp_count = lax.axis_size("dp"), lax.axis_size("mp")
+    chips = dp_count // 2
+    arrays = [vectors] + list(weights)
+    count = len(arrays)
+    depth = [a.shape[0] for a in arrays]
+
+    def kernel(*refs):
+        own_rows, ins = refs[0], refs[1 : 1 + count]
+        full_rows, outs = refs[1 + count], refs[2 + count : 2 + 2 * count]
+        row_sem, local_sem, line_send, line_recv, send_sem, recv_sem, fwd_send, fwd_recv = refs[2 + 2 * count :]
+        dp, mp = lax.axis_index("dp"), lax.axis_index("mp")
+        peers = [(dp ^ (2 * o), mp) for o in range(1, chips)]
+        partner = (dp ^ 1, mp)
+        greet_all(peers + [partner], dp, mp, mp_count)
+        line = LineGather(own_rows, full_rows, rows, PIECES, line_send, line_recv, dp, mp, mp_count)
+
+        def place(array, owner):
+            return outs[array].at[pl.ds(pl.multiple_of(owner * depth[array], depth[array]), depth[array])]
+
+        def cross(array, o):
+            return remote(ins[array], place(array, dp), send_sem.at[array, o], recv_sem.at[array, o], peers[o - 1])
+
+        def forward(array, o):
+            owner = dp ^ (2 * o)
+            source = place(array, owner) if o else ins[array]
+            return remote(source, place(array, owner), fwd_send.at[array, o], fwd_recv.at[array, o], partner)
+
+        @pl.loop(0, PIECES)
+        def _(piece):
+            line.advance(0, piece)
+
+        for a in range(count):
+            for o in range(1, chips):
+                cross(a, o).start()
+            forward(a, 0).start()
+        own_copy = pltpu.make_async_copy(own_rows, full_rows.at[pl.ds(pl.multiple_of(mp * rows, rows), rows)], row_sem)
+        own_copy.start()
+        locals_ = [pltpu.make_async_copy(ins[a], place(a, dp), local_sem.at[a]) for a in range(count)]
+        for copy in locals_:
+            copy.start()
+        for step in range(1, mp_count - 1):
+
+            @pl.loop(0, PIECES)
+            def _(piece):
+                line.advance(step, piece)
+
+        for a in range(count):
+            for o in range(1, chips):
+                cross(a, o).wait_recv()
+                forward(a, o).start()
+
+        @pl.loop(0, PIECES)
+        def _(piece):
+            line.advance(mp_count - 1, piece)
+
+        line.finish()
+        own_copy.wait()
+        for a in range(count):
+            locals_[a].wait()
+            for o in range(chips):
+                if o:
+                    cross(a, o).wait_send()
+                forward(a, o).wait()
+
+    dma = pltpu.SemaphoreType.DMA
+    return pl.pallas_call(
+        kernel,
+        out_shape=[jax.ShapeDtypeStruct((mp_count * rows, width), hidden.dtype)]
+        + [jax.ShapeDtypeStruct((dp_count * a.shape[0], a.shape[1]), a.dtype) for a in arrays],
+        in_specs=[ANY] * (1 + count),
+        out_specs=[ANY] * (1 + count),
+        scratch_shapes=[dma(()), dma((count,))] + LineGather.semaphores(mp_count, PIECES)
+        + [dma((count, chips)) for _ in range(4)],
+        compiler_params=pltpu.CompilerParams(collective_id=collective_id, has_side_effects=True),
+        cost_estimate=pl.CostEstimate(flops=0, bytes_accessed=200 * MIB, transcendentals=0),
+    )(hidden, *arrays)
+
+
+def unit_rows(values):
+    average = jnp.mean(values, axis=-1, keepdims=True)
+    centred = values - average
+    inverse = lax.rsqrt(jnp.mean(centred * centred, axis=-1, keepdims=True) + norm_epsilon)
+    return centred * inverse, inverse
+
+
+def reduce_norm_gather(part, hidden, out_bias, gain, shift, collective_id):
+    mp_count = lax.axis_size("mp")
+    rows, width = hidden.shape
+    size = rows // PIECES
+
+    def kernel(part_ref, hidden_ref, bias_ref, gain_ref, shift_ref, residual_ref, full_ref,
+               total, normed, flows, red_send, red_recv, line_send, line_recv, own_sem):
+        dp, mp = lax.axis_index("dp"), lax.axis_index("mp")
+        greet_all([], dp, mp, mp_count)
+        reduce = LineReduce(part_ref, flows, rows, PIECES, red_send, red_recv, dp, mp, mp_count)
+        gather = LineGather(normed, full_ref, rows, PIECES, line_send, line_recv, dp, mp, mp_count)
+        reduce.begin()
+
+        @pl.loop(0, PIECES + mp_count - 1)
+        def _(turn):
+            @pl.when(turn < PIECES)
+            def _():
+                reduce.advance(turn)
+                reduce.total(turn, total)
+                span = pl.ds(pl.multiple_of(turn * size, size), size)
+                residual = hidden_ref[span].astype(jnp.float32) + total[...] + bias_ref[...]
+                residual_ref[span] = residual
+                unit, _ = unit_rows(residual)
+                normed[span] = (unit * gain_ref[...] + shift_ref[...]).astype(normed.dtype)
+                gather.advance(0, turn)
+
+            for step in range(1, mp_count):
+                piece = jnp.clip(turn - step, 0, PIECES - 1)
+                gather.advance(step, piece, (turn >= step) & (turn - step < PIECES))
+
+        own = pltpu.make_async_copy(normed, full_ref.at[pl.ds(pl.multiple_of(mp * rows, rows), rows)], own_sem)
+        own.start()
+        reduce.finish()
+        gather.finish()
+        own.wait()
+
+    return pl.pallas_call(
+        kernel,
+        out_shape=[
+            jax.ShapeDtypeStruct((rows, width), jnp.float32),
+            jax.ShapeDtypeStruct((mp_count * rows, width), jnp.bfloat16),
+        ],
+        in_specs=[VMEM] * 5,
+        out_specs=[VMEM, ANY],
+        scratch_shapes=[pltpu.VMEM((size, width), jnp.float32), pltpu.VMEM((rows, width), jnp.bfloat16)]
+        + LineReduce.scratch(mp_count, rows, width, PIECES) + LineGather.semaphores(mp_count, PIECES)
+        + [pltpu.SemaphoreType.DMA(())],
+        compiler_params=pltpu.CompilerParams(
+            collective_id=collective_id, has_side_effects=True, vmem_limit_bytes=48 * MIB),
+        cost_estimate=pl.CostEstimate(flops=0, bytes_accessed=300 * MIB, transcendentals=0),
+    )(part, hidden, out_bias, gain, shift)
+
+
+def reduce_back_gather(part, residual, branch_two, gain, collective_id):
+    mp_count = lax.axis_size("mp")
+    rows, width = residual.shape
+    size = rows // PIECES
+
+    def kernel(part_ref, residual_ref, branch_ref, gain_ref, grad_ref, sums_ref, full_ref,
+               total, low, flows, red_send, red_recv, line_send, line_recv, own_sem):
+        dp, mp = lax.axis_index("dp"), lax.axis_index("mp")
+        greet_all([], dp, mp, mp_count)
+        reduce = LineReduce(part_ref, flows, rows, PIECES, red_send, red_recv, dp, mp, mp_count)
+        gather = LineGather(low, full_ref, rows, PIECES, line_send, line_recv, dp, mp, mp_count)
+        reduce.begin()
+        sums_ref[...] = jnp.zeros_like(sums_ref)
+
+        @pl.loop(0, PIECES + mp_count - 1)
+        def _(turn):
+            @pl.when(turn < PIECES)
+            def _():
+                reduce.advance(turn)
+                reduce.total(turn, total)
+                span = pl.ds(pl.multiple_of(turn * size, size), size)
+                unit, inverse = unit_rows(residual_ref[span])
+                upstream = total[...]
+                sums_ref[0:1] += jnp.sum(upstream * unit, axis=0, keepdims=True)
+                sums_ref[1:2] += jnp.sum(upstream, axis=0, keepdims=True)
+                grad = branch_ref[span].astype(jnp.float32) + norm_back(upstream, unit, inverse, gain_ref[...])
+                grad_ref[span] = grad
+                rounded = grad.astype(low.dtype)
+                low[span] = rounded
+                sums_ref[2:3] += jnp.sum(rounded.astype(jnp.float32), axis=0, keepdims=True)
+                gather.advance(0, turn)
+
+            for step in range(1, mp_count):
+                piece = jnp.clip(turn - step, 0, PIECES - 1)
+                gather.advance(step, piece, (turn >= step) & (turn - step < PIECES))
+
+        own = pltpu.make_async_copy(low, full_ref.at[pl.ds(pl.multiple_of(mp * rows, rows), rows)], own_sem)
+        own.start()
+        reduce.finish()
+        gather.finish()
+        own.wait()
+
+    return pl.pallas_call(
+        kernel,
+        out_shape=[
+            jax.ShapeDtypeStruct((rows, width), jnp.float32),
+            jax.ShapeDtypeStruct((8, width), jnp.float32),
+            jax.ShapeDtypeStruct((mp_count * rows, width), jnp.bfloat16),
+        ],
+        in_specs=[VMEM] * 4,
+        out_specs=[VMEM, VMEM, ANY],
+        scratch_shapes=[pltpu.VMEM((size, width), jnp.float32), pltpu.VMEM((rows, width), jnp.bfloat16)]
+        + LineReduce.scratch(mp_count, rows, width, PIECES) + LineGather.semaphores(mp_count, PIECES)
+        + [pltpu.SemaphoreType.DMA(())],
+        compiler_params=pltpu.CompilerParams(
+            collective_id=collective_id, has_side_effects=True, vmem_limit_bytes=48 * MIB),
+        cost_estimate=pl.CostEstimate(flops=0, bytes_accessed=300 * MIB, transcendentals=0),
+    )(part, residual, branch_two, gain)
+
+
+def reduce_last(part, residual_grad, hidden, gain, weight_parts, collective_id):
+    dp_count, mp_count = lax.axis_size("dp"), lax.axis_size("mp")
+    chips = dp_count // 2
+    rows, width = hidden.shape
+    size = rows // PIECES
+    count = len(weight_parts)
+    depth, columns = weight_parts[0].shape[0] // dp_count, weight_parts[0].shape[1]
+
+    def kernel(*refs):
+        part_ref, residual_ref, hidden_ref, gain_ref = refs[:4]
+        weights = refs[4 : 4 + count]
+        grad_ref, sums_ref = refs[4 + count : 6 + count]
+        outs = refs[6 + count : 6 + 2 * count]
+        (total, flows, red_send, red_recv, from_partner, chip_sum, from_chips,
+         pair_send, pair_recv, send_sem, recv_sem) = refs[6 + 2 * count :]
+        dp, mp = lax.axis_index("dp"), lax.axis_index("mp")
+        peers = [(dp ^ (2 * o), mp) for o in range(1, chips)]
+        partner = (dp ^ 1, mp)
+        greet_all(peers + [partner], dp, mp, mp_count)
+        reduce = LineReduce(part_ref, flows, rows, PIECES, red_send, red_recv, dp, mp, mp_count)
+        reduce.begin()
+
+        def piece_of(weight, owner):
+            return weights[weight].at[pl.ds(pl.multiple_of(owner * depth, depth), depth)]
+
+        def pair(weight, o):
+            return remote(piece_of(weight, dp ^ (2 * o) ^ 1), from_partner.at[weight, o],
+                          pair_send.at[weight, o], pair_recv.at[weight, o], partner)
+
+        def cross(weight, o):
+            return remote(chip_sum.at[weight, o], from_chips.at[weight, o - 1],
+                          send_sem.at[weight, o], recv_sem.at[weight, o], peers[o - 1])
+
+        order = list(range(1, chips)) + [0]
+        for w in range(count):
+            for o in order:
+                pair(w, o).start()
+        for w in range(count):
+            for o in order:
+                pair(w, o).wait_recv()
+                value = piece_of(w, dp ^ (2 * o))[...].astype(jnp.float32)
+                value = value + from_partner[w, o].astype(jnp.float32)
+                if o:
+                    chip_sum[w, o] = value.astype(chip_sum.dtype)
+                    cross(w, o).start()
+                else:
+                    outs[w][...] = value
+        sums_ref[...] = jnp.zeros_like(sums_ref)
+
+        @pl.loop(0, PIECES)
+        def _(turn):
+            reduce.advance(turn)
+            reduce.total(turn, total)
+            span = pl.ds(pl.multiple_of(turn * size, size), size)
+            unit, inverse = unit_rows(hidden_ref[span].astype(jnp.float32))
+            upstream = total[...]
+            sums_ref[0:1] += jnp.sum(upstream * unit, axis=0, keepdims=True)
+            sums_ref[1:2] += jnp.sum(upstream, axis=0, keepdims=True)
+            grad_ref[span] = residual_ref[span] + norm_back(upstream, unit, inverse, gain_ref[...])
+
+        reduce.finish()
+        for w in range(count):
+            for o in range(1, chips):
+                cross(w, o).wait()
+                outs[w][...] += from_chips[w, o - 1].astype(jnp.float32)
+            for o in range(chips):
+                pair(w, o).wait_send()
+
+    dma = pltpu.SemaphoreType.DMA
+    kind = weight_parts[0].dtype
+    return pl.pallas_call(
+        kernel,
+        out_shape=[jax.ShapeDtypeStruct((rows, width), jnp.float32), jax.ShapeDtypeStruct((8, width), jnp.float32)]
+        + [jax.ShapeDtypeStruct((depth, columns), jnp.float32)] * count,
+        in_specs=[VMEM] * (4 + count),
+        out_specs=[VMEM] * (2 + count),
+        scratch_shapes=[pltpu.VMEM((size, width), jnp.float32)]
+        + LineReduce.scratch(mp_count, rows, width, PIECES)
+        + [pltpu.VMEM((count, chips, depth, columns), kind), pltpu.VMEM((count, chips, depth, columns), kind),
+           pltpu.VMEM((count, chips - 1, depth, columns), kind)]
+        + [dma((count, chips)) for _ in range(4)],
+        compiler_params=pltpu.CompilerParams(
+            collective_id=collective_id, has_side_effects=True, vmem_limit_bytes=60 * MIB),
+        cost_estimate=pl.CostEstimate(flops=0, bytes_accessed=300 * MIB, transcendentals=0),
+    )(part, residual_grad, hidden, gain, *weight_parts)
+
+
+def sum_vectors(packed, collective_id):
+    dp_count, mp_count = lax.axis_size("dp"), lax.axis_size("mp")
+    depth, width = packed.shape[1:]
+
+    def kernel(in_ref, out_ref, landed, mine, others, send_sem, recv_sem, line_send, line_recv):
+        dp, mp = lax.axis_index("dp"), lax.axis_index("mp")
+        peers = [(dp ^ o, mp) for o in range(1, dp_count)]
+        along = [(dp, mp ^ o) for o in range(1, mp_count)]
+        greet(peers + along)
+        copies = []
+        for o in range(1, dp_count):
+            copies.append(remote(in_ref.at[dp ^ o], landed.at[o - 1], send_sem.at[o], recv_sem.at[o], peers[o - 1]))
+            copies[-1].start()
+        value = in_ref[dp]
+        for o in range(1, dp_count):
+            copies[o - 1].wait()
+            value = value + landed[o - 1]
+        mine[...] = value
+        others[mp] = value
+        copies = []
+        for o in range(1, mp_count):
+            copies.append(remote(mine, others.at[mp], line_send.at[o], line_recv.at[o], along[o - 1]))
+            copies[-1].start()
+        for copy in copies:
+            copy.wait()
+        value = others[0]
+        for index in range(1, mp_count):
+            value = value + others[index]
+        out_ref[...] = value
+
+    dma = pltpu.SemaphoreType.DMA
+    return pl.pallas_call(
+        kernel,
+        out_shape=jax.ShapeDtypeStruct((depth, width), jnp.float32),
+        in_specs=[VMEM],
+        out_specs=VMEM,
+        scratch_shapes=[
+            pltpu.VMEM((dp_count - 1, depth, width), jnp.float32), pltpu.VMEM((depth, width), jnp.float32),
+            pltpu.VMEM((mp_count, depth, width), jnp.float32),
+            dma((dp_count,)), dma((dp_count,)), dma((mp_count,)), dma((mp_count,)),
+        ],
+        compiler_params=pltpu.CompilerParams(collective_id=collective_id, has_side_effects=True),
+        cost_estimate=pl.CostEstimate(flops=0, bytes_accessed=20 * MIB, transcendentals=0),
+    )(packed)
+
+
+def packed_rows(vectors):
+    flat = jnp.concatenate([v.astype(jnp.float32) for v in vectors])
+    rows = flat.shape[0] // 128
+    return jnp.pad(flat.reshape(rows, 128), ((0, -rows % 8), (0, 0)))
 
 
 def per_device(
@@ -488,231 +941,123 @@
     block_order,
     block_slot,
 ):
-    local_rows = hidden_in.shape[0]
-    model_width = hidden_in.shape[1]
-    mp_count = lax.axis_size("mp")
-    mp_index = lax.axis_index("mp")
-    dp_index = lax.axis_index("dp")
+    local_rows, model_width = hidden_in.shape
+    mp_count, dp_count = lax.axis_size("mp"), lax.axis_size("dp")
+    mp_index, dp_index = lax.axis_index("mp"), lax.axis_index("dp")
     group_rows = local_rows * mp_count
     head_width = query_weight.shape[1]
     heads_local = head_width // HEAD_DIM
     hidden_width = up_weight.shape[1]
-    _, _, own_valid = row_meta(
-        seq_lengths, block_order, dp_index * group_rows + mp_index * local_rows, local_rows
+    members = dp_count // heads_local
+    blocks_each = group_rows // BLOCK
+    plan = (seq_lengths, block_order, block_slot)
+
+    own_valid = valid_rows(seq_lengths, block_order, dp_index * group_rows + mp_index * local_rows, local_rows)
+
+    vectors = (first_gain, first_shift, query_bias, value_bias, out_bias, second_gain, second_shift, down_bias, up_bias)
+    rows_in, vector_rows, query_all, key_all, value_all, out_all = gather_first(
+        hidden_in, packed_rows(vectors), (query_weight, key_weight, value_weight, out_weight), 0
     )
-
-    def project(normed_rows, gathered):
-        all_rows = whole_rows(normed_rows.astype(jnp.bfloat16))
-        bias_query = lax.dynamic_slice_in_dim(
-            gathered[6], mp_index * head_width, head_width, 0
-        ).astype(jnp.float32)
-        bias_value = lax.dynamic_slice_in_dim(
-            gathered[7], mp_index * head_width, head_width, 0
-        ).astype(jnp.float32)
-        queries = (
-            jnp.dot(all_rows, gathered[0], preferred_element_type=jnp.float32) + bias_query
-        ).astype(jnp.bfloat16)
-        key_rows = jnp.dot(all_rows, gathered[1], preferred_element_type=jnp.float32).astype(
-            jnp.bfloat16
-        )
-        value_rows = (
-            jnp.dot(all_rows, gathered[2], preferred_element_type=jnp.float32) + bias_value
-        ).astype(jnp.bfloat16)
-        return (all_rows, queries, key_rows, value_rows)
-
-    def expand(normed_rows, gathered):
-        all_rows = whole_rows(normed_rows.astype(jnp.bfloat16))
-        bias_up = lax.dynamic_slice_in_dim(
-            gathered[4], mp_index * hidden_width, hidden_width, 0
-        ).astype(jnp.float32)
-        pre_act = jnp.dot(all_rows, gathered[0], preferred_element_type=jnp.float32) + bias_up
-        return (all_rows, pre_act, gelu_exact(pre_act).astype(jnp.bfloat16))
-
-    input_rows = hidden_in.astype(jnp.float32)
-    attn_params = gather_attention(
-        query_weight,
-        key_weight,
-        value_weight,
-        out_weight,
-        first_gain,
-        first_shift,
-        query_bias,
-        value_bias,
-        out_bias,
+    vector_rows = vector_rows.reshape(dp_count, -1, 128)
+    each = model_width // dp_count // 128
+    (gain_one, shift_one, bias_query, bias_value, bias_out, gain_two, shift_two, bias_down) = (
+        vector_rows[:, k * each : (k + 1) * each].reshape(1, model_width) for k in range(8)
     )
-    normed_one, unit_one, inverse_one = layer_norm(
-        input_rows, attn_params[4].astype(jnp.float32), attn_params[5].astype(jnp.float32)
-    )
-    rows_one, queries, key_rows, value_rows = project(normed_one, attn_params)
-    members = lax.axis_size("dp") // heads_local
-    blocks_each = group_rows // BLOCK
-    head_queries, head_keys, head_values = to_heads(
-        [queries], [key_rows, value_rows], heads_local, members, 0
-    )
-    head_mix, exact_mix, log_total = attend(
-        head_queries, head_keys, head_values, seq_lengths, block_order, block_slot, members, blocks_each
-    )
-    (attended_low,) = to_rows([head_mix], [], heads_local, members, 1)
-
-    def attention_term(first_row, row_count):
-        return contract_last(attended_low, attn_params[3])
-
-    residual = (
-        input_rows + row_share(attention_term, local_rows) + attn_params[8].astype(jnp.float32)
-    )
-    feed_params = gather_feed(up_weight, down_weight, second_gain, second_shift, up_bias, down_bias)
-    normed_two, unit_two, inverse_two = layer_norm(
-        residual, feed_params[2].astype(jnp.float32), feed_params[3].astype(jnp.float32)
-    )
-    rows_two, pre_act, hidden_low = expand(normed_two, feed_params)
-
-    def feed_term(first_row, row_count):
-        return contract_last(hidden_low, feed_params[1])
-
-    result = residual + row_share(feed_term, local_rows) + feed_params[5].astype(jnp.float32)
+    up_each = up_bias.shape[0] // 128
+    bias_up = vector_rows[:, 8 * each : 8 * each + up_each].reshape(1, up_bias.shape[0] * dp_count)
+
+    def heads_of(vector):
+        return lax.dynamic_slice_in_dim(vector, mp_index * head_width, head_width, 1)
+
+    unit_one, _ = unit_rows(rows_in.astype(jnp.float32))
+    rows_one = (unit_one * gain_one + shift_one).astype(jnp.bfloat16)
+
+    def project(weight, bias):
+        return (jnp.dot(rows_one, weight, preferred_element_type=jnp.float32) + bias).astype(jnp.bfloat16)
+
+    key_rows = project(key_all, 0.0)
+    value_rows = project(value_all, heads_of(bias_value))
+    queries = project(query_all, heads_of(bias_query))
+    head_queries, head_keys, head_values = to_heads([queries], [key_rows, value_rows], heads_local, members, 1)
+    head_mix, exact_mix, log_total = attend(head_queries, head_keys, head_values, *plan, members, blocks_each)
+    (attended_low,) = to_rows([head_mix], [], heads_local, members, 2)
+    out_part = contract_last(attended_low, out_all).astype(jnp.bfloat16)
+    residual, rows_two = reduce_norm_gather(out_part, hidden_in, bias_out, gain_two, shift_two, 3)
+
+    up_all = lax.all_gather(up_weight, "dp", axis=0, tiled=True)
+    down_all = lax.all_gather(down_weight, "dp", axis=0, tiled=True)
+    branch_two = jnp.where(own_valid[:, None], output_grad, 0).astype(jnp.bfloat16)
+    branch_rows_two = whole_rows(branch_two)
+
+    bias_hidden = lax.dynamic_slice_in_dim(bias_up, mp_index * hidden_width, hidden_width, 1)
+    pre_act = jnp.dot(rows_two, up_all, preferred_element_type=jnp.float32) + bias_hidden
+    hidden_low = gelu_exact(pre_act).astype(jnp.bfloat16)
+    hidden_grad = jnp.dot(branch_rows_two, down_all, preferred_element_type=jnp.float32)
+    pre_grad = jax.vjp(gelu_exact, pre_act)[1](hidden_grad)[0].astype(jnp.bfloat16)
+    up_part = contract_last(pre_grad, up_all).astype(jnp.bfloat16)
+    residual_grad, sums_two, branch_rows_one = reduce_back_gather(up_part, residual, branch_two, gain_two, 4)
+
+    feed = row_share(contract_last(hidden_low, down_all))
+    result = residual + feed + bias_down
     output = jnp.where(own_valid[:, None], result, 0.0).astype(jnp.bfloat16)
-    result_grad = jnp.where(own_valid[:, None], output_grad.astype(jnp.float32), 0.0)
-    branch_two = result_grad.astype(jnp.bfloat16)
-    down_bias_part = jnp.sum(branch_two.astype(jnp.float32), axis=0)
-    feed_now, rows_two_now, pre_now, hidden_now = feed_params, rows_two, pre_act, hidden_low
-    branch_rows_two = whole_rows(branch_two)
-    down_weight_part = contract_first(branch_rows_two, hidden_now)
-    hidden_grad = jnp.dot(branch_rows_two, feed_now[1], preferred_element_type=jnp.float32)
-    act_grad = jax.vjp(gelu_exact, pre_now)[1](hidden_grad)[0]
-    pre_grad = act_grad.astype(jnp.bfloat16)
-    up_bias_local = jnp.sum(pre_grad.astype(jnp.float32), axis=0)
-    up_weight_part = contract_first(rows_two_now, pre_grad)
-
-    def feed_back_term(first_row, row_count):
-        return contract_last(pre_grad, feed_now[0])
-
-    normed_two_grad = row_share(feed_back_term, local_rows)
-    second_gain_part = jnp.sum(normed_two_grad * unit_two, axis=0)
-    second_shift_part = jnp.sum(normed_two_grad, axis=0)
-    residual_grad = result_grad + norm_back(
-        normed_two_grad, unit_two, inverse_two, feed_now[2].astype(jnp.float32)
-    )
-    branch_one = residual_grad.astype(jnp.bfloat16)
-    out_bias_part = jnp.sum(branch_one.astype(jnp.float32), axis=0)
-    attn_now, rows_one_now = attn_params, rows_one
-    branch_rows_one = whole_rows(branch_one)
-    out_weight_part = contract_first(branch_rows_one, attended_low)
-    attended_grad = jnp.dot(
-        branch_rows_one, attn_now[3], preferred_element_type=jnp.float32
-    ).astype(jnp.bfloat16)
-    (head_grad,) = to_heads([attended_grad], [], heads_local, members, 2)
+    down_weight_grad = owner_share(contract_first(branch_rows_two, hidden_low))
+    up_weight_grad = owner_share(contract_first(rows_two, pre_grad))
+
+    attended_grad = jnp.dot(branch_rows_one, out_all, preferred_element_type=jnp.float32).astype(jnp.bfloat16)
+    (head_grad,) = to_heads([attended_grad], [], heads_local, members, 5)
     head_query_grad, head_key_grad, head_value_grad = attend_back(
-        head_queries, head_keys, head_values, head_grad, exact_mix, log_total,
-        seq_lengths, block_order, block_slot, members, blocks_each,
+        head_queries, head_keys, head_values, head_grad, exact_mix, log_total, *plan, members, blocks_each
     )
     query_low, key_low, value_low = to_rows(
-        [head_query_grad], [head_key_grad, head_value_grad], heads_local, members, 3
+        [head_query_grad], [head_key_grad, head_value_grad], heads_local, members, 6
     )
-    query_weight_part = contract_first(rows_one_now, query_low)
-    key_weight_part = contract_first(rows_one_now, key_low)
-    value_weight_part = contract_first(rows_one_now, value_low)
-    query_bias_local = jnp.sum(query_low.astype(jnp.float32), axis=0)
-    value_bias_local = jnp.sum(value_low.astype(jnp.float32), axis=0)
-
-    def attention_back_term(first_row, row_count):
-        total_term = contract_last(query_low, attn_now[0])
-        total_term = total_term + contract_last(key_low, attn_now[1])
-        return total_term + contract_last(value_low, attn_now[2])
-
-    normed_one_grad = row_share(attention_back_term, local_rows)
-    first_gain_part = jnp.sum(normed_one_grad * unit_one, axis=0)
-    first_shift_part = jnp.sum(normed_one_grad, axis=0)
-    input_grad = residual_grad + norm_back(
-        normed_one_grad, unit_one, inverse_one, attn_now[4].astype(jnp.float32)
+    last_part = contract_last(query_low, query_all)
+    last_part = last_part + contract_last(key_low, key_all)
+    last_part = (last_part + contract_last(value_low, value_all)).astype(jnp.bfloat16)
+    weight_parts = [
+        contract_first(left, right).astype(jnp.bfloat16)
+        for left, right in (
+            (rows_one, query_low), (rows_one, key_low), (rows_one, value_low), (branch_rows_one, attended_low)
+        )
+    ]
+    input_grad, sums_one, query_weight_grad, key_weight_grad, value_weight_grad, out_weight_grad = reduce_last(
+        last_part, residual_grad, hidden_in, gain_one, weight_parts, 7
     )
-    query_bias_full = lax.dynamic_update_slice_in_dim(
-        jnp.zeros((model_width,), jnp.float32), query_bias_local, mp_index * head_width, 0
+
+    def column_sums(values):
+        return jnp.sum(values.astype(jnp.float32), axis=0)
+
+    def placed(values):
+        whole = jnp.zeros((values.shape[0] * mp_count,), jnp.float32)
+        return lax.dynamic_update_slice_in_dim(whole, values, mp_index * values.shape[0], 0)
+
+    sums = (
+        sums_one[0], sums_one[1], placed(column_sums(query_low)), placed(column_sums(value_low)), sums_two[2],
+        sums_two[0], sums_two[1], column_sums(branch_two), placed(column_sums(pre_grad)),
     )
-    value_bias_full = lax.dynamic_update_slice_in_dim(
-        jnp.zeros((model_width,), jnp.float32), value_bias_local, mp_index * head_width, 0
-    )
-    up_bias_full = lax.dynamic_update_slice_in_dim(
-        jnp.zeros((hidden_width * mp_count,), jnp.float32),
-        up_bias_local,
-        mp_index * hidden_width,
-        0,
-    )
-    vector_sums = (
-        lax.psum(first_gain_part.astype(jnp.bfloat16), "mp").astype(jnp.float32),
-        lax.psum(first_shift_part.astype(jnp.bfloat16), "mp").astype(jnp.float32),
-        lax.psum(query_bias_full.astype(jnp.bfloat16), "mp").astype(jnp.float32),
-        lax.psum(value_bias_full.astype(jnp.bfloat16), "mp").astype(jnp.float32),
-        lax.psum(out_bias_part.astype(jnp.bfloat16), "mp").astype(jnp.float32),
-        lax.psum(second_gain_part.astype(jnp.bfloat16), "mp").astype(jnp.float32),
-        lax.psum(second_shift_part.astype(jnp.bfloat16), "mp").astype(jnp.float32),
-        lax.psum(up_bias_full.astype(jnp.bfloat16), "mp").astype(jnp.float32),
-        lax.psum(down_bias_part.astype(jnp.bfloat16), "mp").astype(jnp.float32),
-    )
-    owned_grads = (
-        lax.psum_scatter(
-            vector_sums[0].astype(jnp.bfloat16), "dp", scatter_dimension=0, tiled=True
-        ).astype(jnp.float32),
-        lax.psum_scatter(
-            vector_sums[1].astype(jnp.bfloat16), "dp", scatter_dimension=0, tiled=True
-        ).astype(jnp.float32),
-        lax.psum_scatter(
-            query_weight_part.astype(jnp.bfloat16), "dp", scatter_dimension=0, tiled=True
-        ).astype(jnp.float32),
-        lax.psum_scatter(
-            vector_sums[2].astype(jnp.bfloat16), "dp", scatter_dimension=0, tiled=True
-        ).astype(jnp.float32),
-        lax.psum_scatter(
-            key_weight_part.astype(jnp.bfloat16), "dp", scatter_dimension=0, tiled=True
-        ).astype(jnp.float32),
-        lax.psum_scatter(
-            value_weight_part.astype(jnp.bfloat16), "dp", scatter_dimension=0, tiled=True
-        ).astype(jnp.float32),
-        lax.psum_scatter(
-            vector_sums[3].astype(jnp.bfloat16), "dp", scatter_dimension=0, tiled=True
-        ).astype(jnp.float32),
-        lax.psum_scatter(
-            out_weight_part.astype(jnp.bfloat16), "dp", scatter_dimension=0, tiled=True
-        ).astype(jnp.float32),
-        lax.psum_scatter(
-            vector_sums[4].astype(jnp.bfloat16), "dp", scatter_dimension=0, tiled=True
-        ).astype(jnp.float32),
-        lax.psum_scatter(
-            vector_sums[5].astype(jnp.bfloat16), "dp", scatter_dimension=0, tiled=True
-        ).astype(jnp.float32),
-        lax.psum_scatter(
-            vector_sums[6].astype(jnp.bfloat16), "dp", scatter_dimension=0, tiled=True
-        ).astype(jnp.float32),
-        lax.psum_scatter(
-            up_weight_part.astype(jnp.bfloat16), "dp", scatter_dimension=0, tiled=True
-        ).astype(jnp.float32),
-        lax.psum_scatter(
-            vector_sums[7].astype(jnp.bfloat16), "dp", scatter_dimension=0, tiled=True
-        ).astype(jnp.float32),
-        lax.psum_scatter(
-            down_weight_part.astype(jnp.bfloat16), "dp", scatter_dimension=0, tiled=True
-        ).astype(jnp.float32),
-        lax.psum_scatter(
-            vector_sums[8].astype(jnp.bfloat16), "dp", scatter_dimension=0, tiled=True
-        ).astype(jnp.float32),
-    )
+    packed = jnp.concatenate([v.reshape(dp_count, -1, 128) for v in sums], axis=1)
+    packed = jnp.pad(packed, ((0, 0), (0, -packed.shape[1] % 8), (0, 0)))
+    summed = sum_vectors(packed, 8)
+    vector_grads = [summed[k * each : (k + 1) * each].reshape(-1) for k in range(8)]
+    up_bias_grad = summed[8 * each : 8 * each + up_each].reshape(-1)
     return (
         output,
         input_grad,
-        owned_grads[0],
-        owned_grads[1],
-        owned_grads[2],
-        owned_grads[3],
-        owned_grads[4],
-        owned_grads[5],
-        owned_grads[6],
-        owned_grads[7],
-        owned_grads[8],
-        owned_grads[9],
-        owned_grads[10],
-        owned_grads[11],
-        owned_grads[12],
-        owned_grads[13],
-        owned_grads[14],
+        vector_grads[0],
+        vector_grads[1],
+        query_weight_grad,
+        vector_grads[2],
+        key_weight_grad,
+        value_weight_grad,
+        vector_grads[3],
+        out_weight_grad,
+        vector_grads[4],
+        vector_grads[5],
+        vector_grads[6],
+        up_weight_grad,
+        up_bias_grad,
+        down_weight_grad,
+        vector_grads[7],
     )
 
 

time: 1470 us -> 1200 us (0.82)
  waiting for transfers between devices: 819 us -> 1.47 us
  Pallas kernels: 273 us -> 959 us
  blocking collectives: 115 us -> 0 us
  other arithmetic: 56.5 us -> 35.3 us
  local copies, waits for them, and re-layouts: 7.68 us -> 28 us
  matrix products: 175 us -> 160 us
    pallas_call x0 -> x5, Pallas kernels: none -> 718 us  [the longest x1 242 us: reduce_back_gather(): pl.pallas_call(kernel, out_shape=[jax.ShapeDtypeStruct((rows, width), jnp...]
    reduce_scatter x10 -> x3, waiting for transfers between devices: 402 us -> 0.02 us  [the longest x1 0.01 us: row_share(): lax.psum_scatter(term, 'mp', scatter_dimension=0, tiled=True)]
    all_gather x4 -> x1, waiting for transfers between devices: 273 us -> 0.01 us  [whole_rows(): return lax.all_gather(local_part, 'mp', axis=0, tiled=True)]
    all_gather x6 -> x2, waiting for transfers between devices: 140 us -> 0.02 us  [the longest x1 0.02 us: per_device(): up_all = lax.all_gather(up_weight, 'dp', axis=0, tiled=True)]
    all_gather x9 -> x0, blocking collectives: 79.5 us -> none  [the longest x1 10.3 us: gather_attention(): lax.all_gather(first_gain, 'dp', axis=0, tiled=True)]
    unnamed x1 -> x0, blocking collectives: 24.6 us -> none
    convert_element_type x26 -> x5, other arithmetic: 32.4 us -> 20.2 us  [the longest x1 10 us: per_device(): hidden_low = gelu_exact(pre_act).astype(jnp.bfloat16)]
  transfers between devices with their start and end apart: 20 -> 6, of which waited for: 16 -> 0; matrix products, arithmetic and copies ran while one was open for 10% -> 13% of each run, Pallas kernels for 19% -> 80%
where the time goes in v2:
time: 1200 us
  Pallas kernels  959 us (80%)
  matrix products  160 us (13%)
  other arithmetic  35.3 us (3%)
  local copies, waits for them, and re-layouts  28 us (2%)
  between operations  14.7 us (1%)
    pallas_call x1, Pallas kernels, reduce_back_gather(): pl.pallas_call(kernel, out_shape=[jax.ShapeDtypeStruct((rows, width), jnp...  242 us
    pallas_call x1, Pallas kernels, reduce_norm_gather(): pl.pallas_call(kernel, out_shape=[jax.ShapeDtypeStruct((rows, width), jnp...  223 us
    pallas_call x1, Pallas kernels, reduce_last(): pl.pallas_call(kernel, out_shape=[jax.ShapeDtypeStruct((rows, width), jnp...  153 us
    pallas_call x1, Pallas kernels, gather_first(): pl.pallas_call(kernel, out_shape=[jax.ShapeDtypeStruct((mp_count * rows,...  83.5 us
    pallas_call x1, Pallas kernels, attend_back(): pl.pallas_call(kernel, out_shape=[jax.ShapeDtypeStruct(queries.shape, jnp...  63.4 us
    pallas_call x1, Pallas kernels, attend(): pl.pallas_call(kernel, out_shape=[jax.ShapeDtypeStruct(queries.shape, jnp...  61.5 us
    pallas_call x2, Pallas kernels, to_rows(): pl.pallas_call(kernel, out_shape=[jax.ShapeDtypeStruct((rows, heads * HEA...  60.5 us
    pallas_call x2, Pallas kernels, to_heads(): pl.pallas_call(kernel, out_shape=shapes, in_specs=[ANY] * count, out_spec...  54.9 us
  transfers between devices with their start and end apart: 6, of which 0 were waited for; matrix products, arithmetic and copies ran while one was open for 13% of the time, Pallas kernels for 80%

profile of v2, /device:TPU:0, one launch (start us, length us, event | category | flops | bytes accessed | tf_op | source)
XLA Modules:
  0.0 1198.7 jit_solution(3844108247972964893)
XLA Ops:
  11.5 3.1 convert_reduce_fusion.2
  23.4 83.5 %shard_map.323 = (bf16[1024,2048]{1,0:T(8,128)(2,1)}, f32[192,128]{1,0:T(8,128)}, bf16[2048,512]{1,0:T(8,128)(2,1)}, bf16[2048,512]{1,0:T(8,128)(2,1)}, bf16[204...) custom-call(bf16[256,2048]{1,0:T(8,128)(2,1)} %refs_2_.3, f32[24,128]{1,0:T(8,128)} %bitcast_convert_fusion.refs_1_, ...), custom_call_target="tpu_custom_call" | custom-call | bytes 209715200 | tf_op jit(solution)/shard_map/pallas_call | solution.py:650
  107.7 1.6 fusion.15
  109.3 3.0 convert_reduce_fusion
  112.3 3.7 fusion.2
  116.1 1.9 fusion.5
  118.0 3.3 convolution_convert_fusion.10.refs_1_
  121.3 3.3 add_convert_fusion.3.refs_0_
  124.6 3.3 add_convert_fusion.2.refs_2_
  127.9 38.5 %shard_map.324 = (bf16[4096,128]{1,0:T(8,128)(2,1)}, bf16[8192,128]{1,0:T(8,128)(2,1)}, bf16[8192,128]{1,0:T(8,128)(2,1)}) custom-call(bf16[1024,512]{1,0:T(8,128)(2,1)} %add_convert_fusion.3.refs_0_, bf16[1024,512]{1,0:T(8,128)(2,1)} %convolution_convert_fusion.10.refs_1_, bf16[1024,512]{1,0:T(8,128)(2,1)} %add_convert_fusion.2.refs_2_), custom_call_target="tpu_custom_call" | custom-call | bytes 104857600 | tf_op jit(solution)/shard_map/pallas_call | solution.py:149
  166.5 61.5 %shard_map.325 = (bf16[4096,128]{1,0:T(8,128)(2,1)}, f32[32,128,128]{2,1,0:T(8,128)}, f32[32,1,128]{2,1,0:T(1,128)}) custom-call(s32[8]{0:T(128)} %lengths_ref.3, s32[64]{0:T(128)} %order_ref.3, s32[64]{0:T(128)} %slot_ref.3, bf16[4096,128]{1,0:T(8,128)(2,1)} %get-tuple-element.51.q_ref, bf16[8192,128]{1,0:T(8,128)(2,1)} %get-tuple-element.52.k_ref, ...), custom_call_target="tpu_custom_call" | custom-call | flops 8589934592 | bytes 52428800 | tf_op jit(solution)/shard_map/pallas_call | solution.py:327
  227.9 1.2 copy-done.7
  229.2 24.1 %shard_map.326 = bf16[1024,512]{1,0:T(8,128)(2,1)S(1)} custom-call(bf16[4096,128]{1,0:T(8,128)(2,1)S(1)} %copy-done.7), custom_call_target="tpu_custom_call" | custom-call | bytes 104857600 | tf_op jit(solution)/shard_map/pallas_call | solution.py:242
  253.2 6.3 convolution_convert_fusion.4.part_ref
  259.5 222.8 %shard_map.327 = (f32[256,2048]{1,0:T(8,128)S(1)}, bf16[1024,2048]{1,0:T(8,128)(2,1)}) custom-call(bf16[1024,2048]{1,0:T(8,128)(2,1)} %convolution_convert_fusion.4.part_ref, bf16[256,2048]{1,0:T(8,128)(2,1)S(1)} %copy-done, f32[1,2048]{1,0:T(1,128)S(1)} %bitcast.87, f32[1,2048]{1,0:T(1,128)S(1)} %bitcast.84, f32[1,2048]{1,0:T(1,128)S(1)} %bitcast.86), custom_call_target="tpu_custom_call" | custom-call | bytes 314572800 | tf_op jit(solution)/shard_map/pallas_call | solution.py:706
  482.4 14.5 %fusion.18 = f32[1024,2048]{1,0:T(8,128)} fusion(bf16[1024,2048]{1,0:T(8,128)(2,1)} %get-tuple-element.57, bf16[2048,2048]{1,0:T(8,128)(2,1)} %all-gather.4.cloned.1.call-done), kind=kOutput, calls=%fused_computation.81 | convolution fusion | flops 8589934592 | bytes 20971520 | tf_op jit(solution)/shard_map/dot_general | solution.py:993
  496.9 34.1 %convert_reduce_fusion.1 = (f32[2048]{0:T(1024)}, bf16[1024,2048]{1,0:T(8,128)(2,1)}, f32[1024,2048]{1,0:T(8,128)}) fusion(f32[1024,2048]{1,0:T(8,128)} %fusion.18, f32[2048]{0:T(1024)S(1)} %bitcast.97, bf16[1024,2048]{1,0:T(8,128)(2,1)} %all-gather.8.cloned.1.call-done, bf16[2048,2048]{1,0:T(8,128)(2,1)} %all-gather.6.cloned.1.call-done), kind=kOutput, calls=%fused_computation.10 | convolution fusion | flops 8747218944 | bytes 33570816 | tf_op jit(solution)/shard_map/dot_general | solution.py:995
  531.0 10.0 multiply_convert_fusion
  541.1 13.9 %convolution_convert_fusion.3 = bf16[1024,2048]{1,0:T(8,128)(2,1)} fusion(bf16[1024,2048]{1,0:T(8,128)(2,1)} %multiply_convert_fusion, bf16[2048,2048]{1,0:T(8,128)(2,1)} %all-gather.6.cloned.1.call-done), kind=kOutput, calls=%fused_computation.30 | convolution fusion | flops 8592031744 | bytes 16777216 | tf_op jit(solution)/shard_map/dot_general | solution.py:36
  555.1 14.3 %convolution_convert_fusion.1 = bf16[2048,2048]{1,0:T(8,128)(2,1)} fusion(bf16[1024,2048]{1,0:T(8,128)(2,1)} %get-tuple-element.57, bf16[1024,2048]{1,0:T(8,128)(2,1)} %get-tuple-element.76), kind=kOutput, calls=%fused_computation.28 | convolution fusion | flops 8594128896 | bytes 16777216 | tf_op jit(solution)/shard_map/dot_general | solution.py:42
  569.5 14.2 %convolution_convert_fusion = bf16[2048,2048]{1,0:T(8,128)(2,1)} fusion(bf16[1024,2048]{1,0:T(8,128)(2,1)} %all-gather.8.cloned.1.call-done, bf16[1024,2048]{1,0:T(8,128)(2,1)} %multiply_convert_fusion), kind=kOutput, calls=%fused_computation.27 | convolution fusion | flops 8594128896 | bytes 16777216 | tf_op jit(solution)/shard_map/dot_general | solution.py:42
  583.7 14.1 %convolution_convert_fusion.2.part_ref = bf16[1024,2048]{1,0:T(8,128)(2,1)} fusion(bf16[1024,2048]{1,0:T(8,128)(2,1)} %get-tuple-element.76, bf16[2048,2048]{1,0:T(8,128)(2,1)} %all-gather.4.cloned.1.call-done), kind=kOutput, calls=%fused_computation.29 | convolution fusion | flops 8592031744 | bytes 16777216 | tf_op jit(solution)/shard_map/dot_general | solution.py:36
  597.8 242.3 %shard_map.328 = (f32[256,2048]{1,0:T(8,128)S(1)}, f32[8,2048]{1,0:T(8,128)S(1)}, bf16[1024,2048]{1,0:T(8,128)(2,1)}) custom-call(bf16[1024,2048]{1,0:T(8,128)(2,1)} %convolution_convert_fusion.2.part_ref, f32[256,2048]{1,0:T(8,128)S(1)} %get-tuple-element.56.residual_ref, bf16[256,2048]{1,0:T(8,128)(2,1)S(1)} %copy-done.1, f32[1,2048]{1,0:T(1,128)S(1)} %bitcast.85), custom_call_target="tpu_custom_call" | custom-call | bytes 314572800 | tf_op jit(solution)/shard_map/pallas_call | solution.py:765
  840.1 1.3 copy-done.2
  841.4 5.5 convolution_convert_fusion.9.refs_0_
  846.9 16.4 %shard_map.329.g_ref = bf16[4096,128]{1,0:T(8,128)(2,1)} custom-call(bf16[1024,512]{1,0:T(8,128)(2,1)} %convolution_convert_fusion.9.refs_0_), custom_call_target="tpu_custom_call" | custom-call | bytes 104857600 | tf_op jit(solution)/shard_map/pallas_call | solution.py:149
  863.3 63.4 %shard_map.330 = (bf16[4096,128]{1,0:T(8,128)(2,1)}, bf16[8192,128]{1,0:T(8,128)(2,1)}, bf16[8192,128]{1,0:T(8,128)(2,1)}) custom-call(s32[8]{0:T(128)} %lengths_ref.3, s32[64]{0:T(128)} %order_ref.3, s32[64]{0:T(128)} %slot_ref.3, bf16[4096,128]{1,0:T(8,128)(2,1)} %get-tuple-element.51.q_ref, bf16[8192,128]{1,0:T(8,128)(2,1)} %get-tuple-element.52.k_ref, ...), custom_call_target="tpu_custom_call" | custom-call | flops 21474836480 | bytes 104857600 | tf_op jit(solution)/shard_map/pallas_call | solution.py:399
  926.6 1.2 copy-done.3
  927.9 36.4 %shard_map.331 = (bf16[1024,512]{1,0:T(8,128)(2,1)S(1)}, bf16[1024,512]{1,0:T(8,128)(2,1)S(1)}, bf16[1024,512]{1,0:T(8,128)(2,1)S(1)}) custom-call(bf16[4096,128]{1,0:T(8,128)(2,1)S(1)} %copy-done.3, bf16[8192,128]{1,0:T(8,128)(2,1)} %get-tuple-element.62.refs_1_, bf16[8192,128]{1,0:T(8,128)(2,1)} %get-tuple-element.63.refs_2_), custom_call_target="tpu_custom_call" | custom-call | bytes 104857600 | tf_op jit(solution)/shard_map/pallas_call | solution.py:242
  964.3 4.4 fusion.19
  968.7 5.6 fusion.20
  974.3 3.8 convolution_convert_fusion.8.refs_4_
  978.1 3.8 convolution_convert_fusion.7.refs_5_
  981.9 3.8 convolution_convert_fusion.5.refs_7_
  985.7 4.0 convolution_convert_fusion.6.refs_6_
  989.7 8.1 add_convert_fusion.refs_0_
  997.9 152.6 %shard_map.332 = (f32[256,2048]{1,0:T(8,128)}, f32[8,2048]{1,0:T(8,128)}, f32[256,512]{1,0:T(8,128)}, f32[256,512]{1,0:T(8,128)}, f32[256,512]{1,0:T(8,128)}, /*index=5*/f32[256,512]{1,0:T(8,128)}) custom-call(bf16[1024,2048]{1,0:T(8,128)(2,1)} %add_convert_fusion.refs_0_, f32[256,2048]{1,0:T(8,128)} %copy-done.2, bf16[256,2048]{1,0:T(8,128)(2,1)} %refs_2_.3, ...), custom_call_target="tpu_custom_call" | custom-call | bytes 314572800 | tf_op jit(solution)/shard_map/pallas_call | solution.py:853
  1150.5 1.4 convert_reduce_fusion.4
  1153.1 0.9 fusion.17
  1154.0 1.9 concatenate.8.in_ref
  1155.9 17.2 %shard_map.333 = f32[24,128]{1,0:T(8,128)} custom-call(f32[8,24,128]{2,1,0:T(8,128)} %concatenate.8.in_ref), custom_call_target="tpu_custom_call" | custom-call | bytes 20971520 | tf_op jit(solution)/shard_map/pallas_call | solution.py:901
  1173.1 1.3 slice_bitcast_fusion
  1174.4 1.4 slice_bitcast_fusion.1
  1175.9 2.6 select_convert_fusion
  1178.5 2.8 convert_element_type.112
  1181.4 2.8 convert_element_type.114
  1184.2 3.1 copy.54
  1188.1 1.9 copy.56
  (103 shorter events, 17.6 us)
Async XLA Ops:
  7.2 475.2 %all-gather.4.cloned.1.call-start = ((), (), s32[]{:S(2)}) async-start(), calls=%async_computation.3 | async-start | bytes 9437184 | tf_op jit(solution)/shard_map/all_gather | solution.py:987
  7.9 489.0 %all-gather.8.cloned.1.call-start = ((), (), s32[]{:S(2)}) async-start(), calls=%async_computation.6 | async-start | bytes 5242880 | tf_op jit(solution)/shard_map/all_gather | solution.py:60
  11.0 0.5 copy-start.20
  14.6 482.3 %all-gather.6.cloned.1.call-start = ((), (), s32[]{:S(2)}) async-start(), calls=%async_computation.4 | async-start | bytes 9437184 | tf_op jit(solution)/shard_map/all_gather | solution.py:988
  15.4 1160.5 %reduce-scatter.4.cloned.1.call-start = ((), (), s32[]{:S(2)}) async-start(), calls=%async_computation.5 | async-start | bytes 5242880 | tf_op jit(solution)/shard_map/reduce_scatter | solution.py:65
  107.7 8.4 copy-start.8
  109.3 8.6 copy-start.16
  109.3 8.7 copy-start.23
  118.0 6.7 copy-start.9
  118.0 3.3 copy-start.25
  121.3 3.3 copy-start.11
  227.9 1.2 copy-start.7
  229.2 30.4 %copy-start = (bf16[256,2048]{1,0:T(8,128)(2,1)S(1)}, bf16[256,2048]{1,0:T(8,128)(2,1)}, u32[]{:S(2)}) copy-start(bf16[256,2048]{1,0:T(8,128)(2,1)} %refs_2_.3) | copy-start | bytes 3145732
  253.2 6.3 copy-start.4
  555.0 623.5 %reduce-scatter.6.cloned.1.call-start = ((), (), s32[]{:S(2)}) async-start(), calls=%async_computation.7 | async-start | bytes 9437184 | tf_op jit(solution)/shard_map/reduce_scatter | solution.py:70
  569.4 611.9 %reduce-scatter.8.cloned.1.call-start = ((), (), s32[]{:S(2)}) async-start(), calls=%async_computation.8 | async-start | bytes 9437184 | tf_op jit(solution)/shard_map/reduce_scatter | solution.py:70
  583.7 14.1 %copy-start.1 = (bf16[256,2048]{1,0:T(8,128)(2,1)S(1)}, bf16[256,2048]{1,0:T(8,128)(2,1)}, u32[]{:S(2)}) copy-start(bf16[256,2048]{1,0:T(8,128)(2,1)} %get-tuple-element.79.branch_ref) | copy-start | bytes 3145732
  583.7 257.7 %copy-start.26 = (bf16[2048,512]{1,0:T(8,128)(2,1)S(1)}, bf16[2048,512]{1,0:T(8,128)(2,1)}, u32[]{:S(2)}) copy-start(bf16[2048,512]{1,0:T(8,128)(2,1)} %get-tuple-element.55) | copy-start | bytes 6291460
  840.1 1.3 copy-start.2
  926.6 1.2 copy-start.3
  964.3 10.0 copy-start.6
  964.3 4.4 copy-start.24
  968.7 5.6 copy-start.10
  978.1 3.8 copy-start.5
  978.1 3.8 copy-start.22
  985.7 4.0 copy-start.12
  997.9 154.9 %copy-start.19 = (f32[2048]{0:T(1024)S(1)}, f32[2048]{0:T(1024)}, u32[]{:S(2)}) copy-start(f32[2048]{0:T(1024)} %get-tuple-element.75) | copy-start | bytes 24580
  997.9 156.2 %copy-start.17 = (f32[2048]{0:T(1024)S(1)}, f32[2048]{0:T(1024)}, u32[]{:S(2)}) copy-start(f32[2048]{0:T(1024)} %get-tuple-element.78) | copy-start | bytes 24580
  997.9 178.0 %copy-start.18 = (f32[8,2,128]{2,1,0:T(2,128)S(1)}, f32[8,2,128]{2,1,0:T(2,128)}, u32[]{:S(2)}) copy-start(f32[8,2,128]{2,1,0:T(2,128)} %get-tuple-element.80) | copy-start | bytes 24580
  997.9 178.0 %copy-start.21 = (pred[256]{0:T(512)(128)(4,1)S(1)}, pred[256]{0:T(512)(128)(4,1)}, u32[]{:S(2)}) copy-start(pred[256]{0:T(512)(128)(4,1)} %copy-done.20) | copy-start | bytes 772
  1175.9 14.1 %copy-start.14 = (f32[256,512]{1,0:T(8,128)S(1)}, f32[256,512]{1,0:T(8,128)}, u32[]{:S(2)}) copy-start(f32[256,512]{1,0:T(8,128)} %get-tuple-element.127) | copy-start | bytes 1572868
  1175.9 14.9 %copy-start.13 = (f32[256,512]{1,0:T(8,128)S(1)}, f32[256,512]{1,0:T(8,128)}, u32[]{:S(2)}) copy-start(f32[256,512]{1,0:T(8,128)} %get-tuple-element.129) | copy-start | bytes 1572868
  1178.5 8.8 copy-start.15
Sparse Core Ops, SparseCore 0:
  9.9 92.2 all-gather.3
  104.3 83.5 all-gather.7
  189.8 62.1 all-gather.5
  555.2 112.6 reduce-scatter.3
  671.6 75.9 reduce-scatter.5
  750.9 71.2 reduce-scatter.7

commit v3 on v2

--- a/solution.py
+++ b/solution.py
@@ -512,42 +512,44 @@
     def roles(self, way, block):
         if way == 0:
             behind, ahead = self.mp >= 1, self.mp < block
-            ends = self.mp <= block
         else:
             behind, ahead = self.mp < self.count - 1, self.mp > block
-            ends = self.mp >= block
-        return ahead & jnp.logical_not(behind), ahead & behind, ends & behind
+        return ahead & jnp.logical_not(behind), ahead & behind
 
     def targets(self):
         for index in range(self.count - 1):
             yield 0, self.count - 1 - index
             yield 1, index
 
-    def begin(self):
-        @pl.loop(0, self.pieces)
-        def _(piece):
-            for way, block in self.targets():
-                begins, _, _ = self.roles(way, block)
-
-                @pl.when(begins)
-                def _():
-                    self.hop(way, block, piece, True).start()
-
-    def advance(self, piece):
+    def begin(self, piece, also=True):
         for way, block in self.targets():
-            _, hands_on, receives = self.roles(way, block)
-
-            @pl.when(receives)
+            begins, _ = self.roles(way, block)
+
+            @pl.when(begins & also)
+            def _():
+                self.hop(way, block, piece, True).start()
+
+    def advance(self, turn):
+        for way, block in self.targets():
+            _, hands_on = self.roles(way, block)
+            passed = SKEW * (self.mp - 1 if way == 0 else self.count - 2 - self.mp)
+            piece = jnp.clip(turn - passed, 0, self.pieces - 1)
+
+            @pl.when(hands_on & (turn >= passed) & (turn - passed < self.pieces))
             def _():
                 self.hop(way, block, piece).wait_recv()
-
-            @pl.when(hands_on)
-            def _():
                 span = self.span(block, piece)
                 value = self.flows[way, span].astype(jnp.float32) + self.part[span].astype(jnp.float32)
                 self.flows[way, span] = value.astype(self.flows.dtype)
                 self.hop(way, block, piece).start()
 
+    def arrive(self, piece):
+        for way in range(2):
+
+            @pl.when(self.mp >= 1 if way == 0 else self.mp < self.count - 1)
+            def _():
+                self.hop(way, self.mp, piece).wait_recv()
+
     def total(self, piece, result):
         span = self.span(self.mp, piece)
         result[...] = self.part[span].astype(jnp.float32)
@@ -561,7 +563,7 @@
         @pl.loop(0, self.pieces)
         def _(piece):
             for way, block in self.targets():
-                begins, hands_on, _ = self.roles(way, block)
+                begins, hands_on = self.roles(way, block)
 
                 @pl.when(begins)
                 def _():
@@ -577,11 +579,18 @@
                 pltpu.SemaphoreType.DMA((2, count, pieces)), pltpu.SemaphoreType.DMA((2, count, pieces))]
 
 
-PIECES = 8
+AHEAD = 1
+MAX_PIECES = 16
+SKEW = 1
+
+
+def pieces_of(rows):
+    return min(MAX_PIECES, rows // 16)
 
 
 def gather_first(hidden, vectors, weights, collective_id):
     rows, width = hidden.shape
+    pieces = pieces_of(rows)
     dp_count, mp_count = lax.axis_size("dp"), lax.axis_size("mp")
     chips = dp_count // 2
     arrays = [vectors] + list(weights)
@@ -596,7 +605,7 @@
         peers = [(dp ^ (2 * o), mp) for o in range(1, chips)]
         partner = (dp ^ 1, mp)
         greet_all(peers + [partner], dp, mp, mp_count)
-        line = LineGather(own_rows, full_rows, rows, PIECES, line_send, line_recv, dp, mp, mp_count)
+        line = LineGather(own_rows, full_rows, rows, pieces, line_send, line_recv, dp, mp, mp_count)
 
         def place(array, owner):
             return outs[array].at[pl.ds(pl.multiple_of(owner * depth[array], depth[array]), depth[array])]
@@ -609,7 +618,7 @@
             source = place(array, owner) if o else ins[array]
             return remote(source, place(array, owner), fwd_send.at[array, o], fwd_recv.at[array, o], partner)
 
-        @pl.loop(0, PIECES)
+        @pl.loop(0, pieces)
         def _(piece):
             line.advance(0, piece)
 
@@ -624,7 +633,7 @@
             copy.start()
         for step in range(1, mp_count - 1):
 
-            @pl.loop(0, PIECES)
+            @pl.loop(0, pieces)
             def _(piece):
                 line.advance(step, piece)
 
@@ -633,7 +642,7 @@
                 cross(a, o).wait_recv()
                 forward(a, o).start()
 
-        @pl.loop(0, PIECES)
+        @pl.loop(0, pieces)
         def _(piece):
             line.advance(mp_count - 1, piece)
 
@@ -653,7 +662,7 @@
         + [jax.ShapeDtypeStruct((dp_count * a.shape[0], a.shape[1]), a.dtype) for a in arrays],
         in_specs=[ANY] * (1 + count),
         out_specs=[ANY] * (1 + count),
-        scratch_shapes=[dma(()), dma((count,))] + LineGather.semaphores(mp_count, PIECES)
+        scratch_shapes=[dma(()), dma((count,))] + LineGather.semaphores(mp_count, pieces)
         + [dma((count, chips)) for _ in range(4)],
         compiler_params=pltpu.CompilerParams(collective_id=collective_id, has_side_effects=True),
         cost_estimate=pl.CostEstimate(flops=0, bytes_accessed=200 * MIB, transcendentals=0),
@@ -670,32 +679,38 @@
 def reduce_norm_gather(part, hidden, out_bias, gain, shift, collective_id):
     mp_count = lax.axis_size("mp")
     rows, width = hidden.shape
-    size = rows // PIECES
+    pieces = pieces_of(rows)
+    size = rows // pieces
 
     def kernel(part_ref, hidden_ref, bias_ref, gain_ref, shift_ref, residual_ref, full_ref,
                total, normed, flows, red_send, red_recv, line_send, line_recv, own_sem):
         dp, mp = lax.axis_index("dp"), lax.axis_index("mp")
         greet_all([], dp, mp, mp_count)
-        reduce = LineReduce(part_ref, flows, rows, PIECES, red_send, red_recv, dp, mp, mp_count)
-        gather = LineGather(normed, full_ref, rows, PIECES, line_send, line_recv, dp, mp, mp_count)
-        reduce.begin()
-
-        @pl.loop(0, PIECES + mp_count - 1)
+        reduce = LineReduce(part_ref, flows, rows, pieces, red_send, red_recv, dp, mp, mp_count)
+        gather = LineGather(normed, full_ref, rows, pieces, line_send, line_recv, dp, mp, mp_count)
+        for piece in range(AHEAD):
+            reduce.begin(piece)
+
+        @pl.loop(0, pieces + 2 * SKEW * (mp_count - 1))
         def _(turn):
-            @pl.when(turn < PIECES)
+            reduce.begin(jnp.minimum(turn + AHEAD, pieces - 1), turn + AHEAD < pieces)
+            reduce.advance(turn)
+            done = turn - SKEW * (mp_count - 1)
+
+            @pl.when((done >= 0) & (done < pieces))
             def _():
-                reduce.advance(turn)
-                reduce.total(turn, total)
-                span = pl.ds(pl.multiple_of(turn * size, size), size)
+                reduce.arrive(done)
+                reduce.total(done, total)
+                span = pl.ds(pl.multiple_of(done * size, size), size)
                 residual = hidden_ref[span].astype(jnp.float32) + total[...] + bias_ref[...]
                 residual_ref[span] = residual
                 unit, _ = unit_rows(residual)
                 normed[span] = (unit * gain_ref[...] + shift_ref[...]).astype(normed.dtype)
-                gather.advance(0, turn)
+                gather.advance(0, done)
 
             for step in range(1, mp_count):
-                piece = jnp.clip(turn - step, 0, PIECES - 1)
-                gather.advance(step, piece, (turn >= step) & (turn - step < PIECES))
+                late = done - SKEW * step
+                gather.advance(step, jnp.clip(late, 0, pieces - 1), (late >= 0) & (late < pieces))
 
         own = pltpu.make_async_copy(normed, full_ref.at[pl.ds(pl.multiple_of(mp * rows, rows), rows)], own_sem)
         own.start()
@@ -712,7 +727,7 @@
         in_specs=[VMEM] * 5,
         out_specs=[VMEM, ANY],
         scratch_shapes=[pltpu.VMEM((size, width), jnp.float32), pltpu.VMEM((rows, width), jnp.bfloat16)]
-        + LineReduce.scratch(mp_count, rows, width, PIECES) + LineGather.semaphores(mp_count, PIECES)
+        + LineReduce.scratch(mp_count, rows, width, pieces) + LineGather.semaphores(mp_count, pieces)
         + [pltpu.SemaphoreType.DMA(())],
         compiler_params=pltpu.CompilerParams(
             collective_id=collective_id, has_side_effects=True, vmem_limit_bytes=48 * MIB),
@@ -723,24 +738,30 @@
 def reduce_back_gather(part, residual, branch_two, gain, collective_id):
     mp_count = lax.axis_size("mp")
     rows, width = residual.shape
-    size = rows // PIECES
+    pieces = pieces_of(rows)
+    size = rows // pieces
 
     def kernel(part_ref, residual_ref, branch_ref, gain_ref, grad_ref, sums_ref, full_ref,
                total, low, flows, red_send, red_recv, line_send, line_recv, own_sem):
         dp, mp = lax.axis_index("dp"), lax.axis_index("mp")
         greet_all([], dp, mp, mp_count)
-        reduce = LineReduce(part_ref, flows, rows, PIECES, red_send, red_recv, dp, mp, mp_count)
-        gather = LineGather(low, full_ref, rows, PIECES, line_send, line_recv, dp, mp, mp_count)
-        reduce.begin()
+        reduce = LineReduce(part_ref, flows, rows, pieces, red_send, red_recv, dp, mp, mp_count)
+        gather = LineGather(low, full_ref, rows, pieces, line_send, line_recv, dp, mp, mp_count)
+        for piece in range(AHEAD):
+            reduce.begin(piece)
         sums_ref[...] = jnp.zeros_like(sums_ref)
 
-        @pl.loop(0, PIECES + mp_count - 1)
+        @pl.loop(0, pieces + 2 * SKEW * (mp_count - 1))
         def _(turn):
-            @pl.when(turn < PIECES)
+            reduce.begin(jnp.minimum(turn + AHEAD, pieces - 1), turn + AHEAD < pieces)
+            reduce.advance(turn)
+            done = turn - SKEW * (mp_count - 1)
+
+            @pl.when((done >= 0) & (done < pieces))
             def _():
-                reduce.advance(turn)
-                reduce.total(turn, total)
-                span = pl.ds(pl.multiple_of(turn * size, size), size)
+                reduce.arrive(done)
+                reduce.total(done, total)
+                span = pl.ds(pl.multiple_of(done * size, size), size)
                 unit, inverse = unit_rows(residual_ref[span])
                 upstream = total[...]
                 sums_ref[0:1] += jnp.sum(upstream * unit, axis=0, keepdims=True)
@@ -750,11 +771,11 @@
                 rounded = grad.astype(low.dtype)
                 low[span] = rounded
                 sums_ref[2:3] += jnp.sum(rounded.astype(jnp.float32), axis=0, keepdims=True)
-                gather.advance(0, turn)
+                gather.advance(0, done)
 
             for step in range(1, mp_count):
-                piece = jnp.clip(turn - step, 0, PIECES - 1)
-                gather.advance(step, piece, (turn >= step) & (turn - step < PIECES))
+                late = done - SKEW * step
+                gather.advance(step, jnp.clip(late, 0, pieces - 1), (late >= 0) & (late < pieces))
 
         own = pltpu.make_async_copy(low, full_ref.at[pl.ds(pl.multiple_of(mp * rows, rows), rows)], own_sem)
         own.start()
@@ -772,7 +793,7 @@
         in_specs=[VMEM] * 4,
         out_specs=[VMEM, VMEM, ANY],
         scratch_shapes=[pltpu.VMEM((size, width), jnp.float32), pltpu.VMEM((rows, width), jnp.bfloat16)]
-        + LineReduce.scratch(mp_count, rows, width, PIECES) + LineGather.semaphores(mp_count, PIECES)
+        + LineReduce.scratch(mp_count, rows, width, pieces) + LineGather.semaphores(mp_count, pieces)
         + [pltpu.SemaphoreType.DMA(())],
         compiler_params=pltpu.CompilerParams(
             collective_id=collective_id, has_side_effects=True, vmem_limit_bytes=48 * MIB),
@@ -784,7 +805,8 @@
     dp_count, mp_count = lax.axis_size("dp"), lax.axis_size("mp")
     chips = dp_count // 2
     rows, width = hidden.shape
-    size = rows // PIECES
+    pieces = pieces_of(rows)
+    size = rows // pieces
     count = len(weight_parts)
     depth, columns = weight_parts[0].shape[0] // dp_count, weight_parts[0].shape[1]
 
@@ -799,8 +821,9 @@
         peers = [(dp ^ (2 * o), mp) for o in range(1, chips)]
         partner = (dp ^ 1, mp)
         greet_all(peers + [partner], dp, mp, mp_count)
-        reduce = LineReduce(part_ref, flows, rows, PIECES, red_send, red_recv, dp, mp, mp_count)
-        reduce.begin()
+        reduce = LineReduce(part_ref, flows, rows, pieces, red_send, red_recv, dp, mp, mp_count)
+        for piece in range(AHEAD):
+            reduce.begin(piece)
 
         def piece_of(weight, owner):
             return weights[weight].at[pl.ds(pl.multiple_of(owner * depth, depth), depth)]
@@ -829,16 +852,22 @@
                     outs[w][...] = value
         sums_ref[...] = jnp.zeros_like(sums_ref)
 
-        @pl.loop(0, PIECES)
+        @pl.loop(0, pieces + SKEW * (mp_count - 1))
         def _(turn):
+            reduce.begin(jnp.minimum(turn + AHEAD, pieces - 1), turn + AHEAD < pieces)
             reduce.advance(turn)
-            reduce.total(turn, total)
-            span = pl.ds(pl.multiple_of(turn * size, size), size)
-            unit, inverse = unit_rows(hidden_ref[span].astype(jnp.float32))
-            upstream = total[...]
-            sums_ref[0:1] += jnp.sum(upstream * unit, axis=0, keepdims=True)
-            sums_ref[1:2] += jnp.sum(upstream, axis=0, keepdims=True)
-            grad_ref[span] = residual_ref[span] + norm_back(upstream, unit, inverse, gain_ref[...])
+            done = turn - SKEW * (mp_count - 1)
+
+            @pl.when(done >= 0)
+            def _():
+                reduce.arrive(done)
+                reduce.total(done, total)
+                span = pl.ds(pl.multiple_of(done * size, size), size)
+                unit, inverse = unit_rows(hidden_ref[span].astype(jnp.float32))
+                upstream = total[...]
+                sums_ref[0:1] += jnp.sum(upstream * unit, axis=0, keepdims=True)
+                sums_ref[1:2] += jnp.sum(upstream, axis=0, keepdims=True)
+                grad_ref[span] = residual_ref[span] + norm_back(upstream, unit, inverse, gain_ref[...])
 
         reduce.finish()
         for w in range(count):
@@ -857,7 +886,7 @@
         in_specs=[VMEM] * (4 + count),
         out_specs=[VMEM] * (2 + count),
         scratch_shapes=[pltpu.VMEM((size, width), jnp.float32)]
-        + LineReduce.scratch(mp_count, rows, width, PIECES)
+        + LineReduce.scratch(mp_count, rows, width, pieces)
         + [pltpu.VMEM((count, chips, depth, columns), kind), pltpu.VMEM((count, chips, depth, columns), kind),
            pltpu.VMEM((count, chips - 1, depth, columns), kind)]
         + [dma((count, chips)) for _ in range(4)],

time: 1200 us -> 931 us (0.78)
  Pallas kernels: 959 us -> 683 us
    pallas_call x1, Pallas kernels: 223 us -> 119 us  [reduce_norm_gather(): pl.pallas_call(kernel, out_shape=[jax.ShapeDtypeStruct((rows, width), jnp...]
    pallas_call x1, Pallas kernels: 242 us -> 144 us  [reduce_back_gather(): pl.pallas_call(kernel, out_shape=[jax.ShapeDtypeStruct((rows, width), jnp...]
    pallas_call x1, Pallas kernels: 153 us -> 90.1 us  [reduce_last(): pl.pallas_call(kernel, out_shape=[jax.ShapeDtypeStruct((rows, width), jnp...]
  transfers between devices with their start and end apart: 6 -> 6, of which waited for: 0 -> 0; matrix products, arithmetic and copies ran while one was open for 13% -> 16% of each run, Pallas kernels for 80% -> 74%
where the time goes in v3:
time: 931 us; the launch traced here: 923 us
  Pallas kernels  683 us (73%)
  matrix products  160 us (17%)
  other arithmetic  35.4 us (4%)
  local copies, waits for them, and re-layouts  28 us (3%)
  between operations  14.8 us (2%)
    pallas_call x1, Pallas kernels, reduce_back_gather(): pl.pallas_call(kernel, out_shape=[jax.ShapeDtypeStruct((rows, width), jnp...  144 us
    pallas_call x1, Pallas kernels, reduce_norm_gather(): pl.pallas_call(kernel, out_shape=[jax.ShapeDtypeStruct((rows, width), jnp...  119 us
    pallas_call x1, Pallas kernels, reduce_last(): pl.pallas_call(kernel, out_shape=[jax.ShapeDtypeStruct((rows, width), jnp...  90.1 us
    pallas_call x1, Pallas kernels, gather_first(): pl.pallas_call(kernel, out_shape=[jax.ShapeDtypeStruct((mp_count * rows,...  84.6 us
    pallas_call x2, Pallas kernels, to_rows(): pl.pallas_call(kernel, out_shape=[jax.ShapeDtypeStruct((rows, heads * HEA...  65.1 us
    pallas_call x1, Pallas kernels, attend_back(): pl.pallas_call(kernel, out_shape=[jax.ShapeDtypeStruct(queries.shape, jnp...  58.7 us
    pallas_call x1, Pallas kernels, attend(): pl.pallas_call(kernel, out_shape=[jax.ShapeDtypeStruct(queries.shape, jnp...  56.1 us
    pallas_call x2, Pallas kernels, to_heads(): pl.pallas_call(kernel, out_shape=shapes, in_specs=[ANY] * count, out_spec...  54.2 us
  transfers between devices with their start and end apart: 6, of which 0 were waited for; matrix products, arithmetic and copies ran while one was open for 16% of the time, Pallas kernels for 74%

profile of v3, /device:TPU:0, one launch (start us, length us, event | category | flops | bytes accessed | tf_op | source)
XLA Modules:
  0.0 923.1 jit_solution(6654585243511039114)
XLA Ops:
  11.5 3.1 convert_reduce_fusion.2
  23.4 84.6 %shard_map.323 = (bf16[1024,2048]{1,0:T(8,128)(2,1)}, f32[192,128]{1,0:T(8,128)}, bf16[2048,512]{1,0:T(8,128)(2,1)}, bf16[2048,512]{1,0:T(8,128)(2,1)}, bf16[204...) custom-call(bf16[256,2048]{1,0:T(8,128)(2,1)} %refs_2_.3, f32[24,128]{1,0:T(8,128)} %bitcast_convert_fusion.refs_1_, ...), custom_call_target="tpu_custom_call" | custom-call | bytes 209715200 | tf_op jit(solution)/shard_map/pallas_call | solution.py:659
  108.8 1.6 fusion.15
  110.5 3.0 convert_reduce_fusion
  113.4 3.8 fusion.2
  117.3 1.9 fusion.5
  119.2 3.3 convolution_convert_fusion.10.refs_1_
  122.5 3.3 add_convert_fusion.3.refs_0_
  125.8 3.3 add_convert_fusion.2.refs_2_
  129.2 38.5 %shard_map.324 = (bf16[4096,128]{1,0:T(8,128)(2,1)}, bf16[8192,128]{1,0:T(8,128)(2,1)}, bf16[8192,128]{1,0:T(8,128)(2,1)}) custom-call(bf16[1024,512]{1,0:T(8,128)(2,1)} %add_convert_fusion.3.refs_0_, bf16[1024,512]{1,0:T(8,128)(2,1)} %convolution_convert_fusion.10.refs_1_, bf16[1024,512]{1,0:T(8,128)(2,1)} %add_convert_fusion.2.refs_2_), custom_call_target="tpu_custom_call" | custom-call | bytes 104857600 | tf_op jit(solution)/shard_map/pallas_call | solution.py:149
  167.7 56.1 %shard_map.325 = (bf16[4096,128]{1,0:T(8,128)(2,1)}, f32[32,128,128]{2,1,0:T(8,128)}, f32[32,1,128]{2,1,0:T(1,128)}) custom-call(s32[8]{0:T(128)} %lengths_ref.3, s32[64]{0:T(128)} %order_ref.3, s32[64]{0:T(128)} %slot_ref.3, bf16[4096,128]{1,0:T(8,128)(2,1)} %get-tuple-element.51.q_ref, bf16[8192,128]{1,0:T(8,128)(2,1)} %get-tuple-element.52.k_ref, ...), custom_call_target="tpu_custom_call" | custom-call | flops 8589934592 | bytes 52428800 | tf_op jit(solution)/shard_map/pallas_call | solution.py:327
  223.8 1.2 copy-done.7
  225.0 26.9 %shard_map.326 = bf16[1024,512]{1,0:T(8,128)(2,1)S(1)} custom-call(bf16[4096,128]{1,0:T(8,128)(2,1)S(1)} %copy-done.7), custom_call_target="tpu_custom_call" | custom-call | bytes 104857600 | tf_op jit(solution)/shard_map/pallas_call | solution.py:242
  252.0 6.3 convolution_convert_fusion.4.part_ref
  258.3 119.0 %shard_map.327 = (f32[256,2048]{1,0:T(8,128)S(1)}, bf16[1024,2048]{1,0:T(8,128)(2,1)}) custom-call(bf16[1024,2048]{1,0:T(8,128)(2,1)} %convolution_convert_fusion.4.part_ref, bf16[256,2048]{1,0:T(8,128)(2,1)S(1)} %copy-done, f32[1,2048]{1,0:T(1,128)S(1)} %bitcast.87, f32[1,2048]{1,0:T(1,128)S(1)} %bitcast.84, f32[1,2048]{1,0:T(1,128)S(1)} %bitcast.86), custom_call_target="tpu_custom_call" | custom-call | bytes 314572800 | tf_op jit(solution)/shard_map/pallas_call | solution.py:721
  377.4 14.5 %fusion.18 = f32[1024,2048]{1,0:T(8,128)} fusion(bf16[1024,2048]{1,0:T(8,128)(2,1)} %get-tuple-element.57, bf16[2048,2048]{1,0:T(8,128)(2,1)} %all-gather.4.cloned.1.call-done), kind=kOutput, calls=%fused_computation.81 | convolution fusion | flops 8589934592 | bytes 20971520 | tf_op jit(solution)/shard_map/dot_general | solution.py:1022
  391.9 34.1 %convert_reduce_fusion.1 = (f32[2048]{0:T(1024)}, bf16[1024,2048]{1,0:T(8,128)(2,1)}, f32[1024,2048]{1,0:T(8,128)}) fusion(f32[1024,2048]{1,0:T(8,128)} %fusion.18, f32[2048]{0:T(1024)S(1)} %bitcast.97, bf16[1024,2048]{1,0:T(8,128)(2,1)} %all-gather.8.cloned.1.call-done, bf16[2048,2048]{1,0:T(8,128)(2,1)} %all-gather.6.cloned.1.call-done), kind=kOutput, calls=%fused_computation.10 | convolution fusion | flops 8747218944 | bytes 33570816 | tf_op jit(solution)/shard_map/dot_general | solution.py:1024
  426.0 10.0 %multiply_convert_fusion = bf16[1024,2048]{1,0:T(8,128)(2,1)} fusion(f32[1024,2048]{1,0:T(8,128)} %get-tuple-element.77, f32[1024,2048]{1,0:T(8,128)} %fusion.18, f32[2048]{0:T(1024)S(1)} %bitcast.98), kind=kLoop, calls=%fused_computation.13 | loop fusion | flops 8388608 | bytes 20979712 | tf_op jit(solution)/shard_map/convert_element_type | solution.py:1023
  436.1 13.9 %convolution_convert_fusion.3 = bf16[1024,2048]{1,0:T(8,128)(2,1)} fusion(bf16[1024,2048]{1,0:T(8,128)(2,1)} %multiply_convert_fusion, bf16[2048,2048]{1,0:T(8,128)(2,1)} %all-gather.6.cloned.1.call-done), kind=kOutput, calls=%fused_computation.30 | convolution fusion | flops 8592031744 | bytes 16777216 | tf_op jit(solution)/shard_map/dot_general | solution.py:36
  450.1 14.1 %convolution_convert_fusion.1 = bf16[2048,2048]{1,0:T(8,128)(2,1)} fusion(bf16[1024,2048]{1,0:T(8,128)(2,1)} %get-tuple-element.57, bf16[1024,2048]{1,0:T(8,128)(2,1)} %get-tuple-element.76), kind=kOutput, calls=%fused_computation.28 | convolution fusion | flops 8594128896 | bytes 16777216 | tf_op jit(solution)/shard_map/dot_general | solution.py:42
  464.2 14.2 %convolution_convert_fusion = bf16[2048,2048]{1,0:T(8,128)(2,1)} fusion(bf16[1024,2048]{1,0:T(8,128)(2,1)} %all-gather.8.cloned.1.call-done, bf16[1024,2048]{1,0:T(8,128)(2,1)} %multiply_convert_fusion), kind=kOutput, calls=%fused_computation.27 | convolution fusion | flops 8594128896 | bytes 16777216 | tf_op jit(solution)/shard_map/dot_general | solution.py:42
  478.5 14.1 %convolution_convert_fusion.2.part_ref = bf16[1024,2048]{1,0:T(8,128)(2,1)} fusion(bf16[1024,2048]{1,0:T(8,128)(2,1)} %get-tuple-element.76, bf16[2048,2048]{1,0:T(8,128)(2,1)} %all-gather.4.cloned.1.call-done), kind=kOutput, calls=%fused_computation.29 | convolution fusion | flops 8592031744 | bytes 16777216 | tf_op jit(solution)/shard_map/dot_general | solution.py:36
  492.6 143.9 %shard_map.328 = (f32[256,2048]{1,0:T(8,128)S(1)}, f32[8,2048]{1,0:T(8,128)S(1)}, bf16[1024,2048]{1,0:T(8,128)(2,1)}) custom-call(bf16[1024,2048]{1,0:T(8,128)(2,1)} %convolution_convert_fusion.2.part_ref, f32[256,2048]{1,0:T(8,128)S(1)} %get-tuple-element.56.residual_ref, bf16[256,2048]{1,0:T(8,128)(2,1)S(1)} %copy-done.1, f32[1,2048]{1,0:T(1,128)S(1)} %bitcast.85), custom_call_target="tpu_custom_call" | custom-call | bytes 314572800 | tf_op jit(solution)/shard_map/pallas_call | solution.py:786
  636.5 1.3 copy-done.2
  637.8 5.6 convolution_convert_fusion.9.refs_0_
  643.4 15.6 %shard_map.329.g_ref = bf16[4096,128]{1,0:T(8,128)(2,1)} custom-call(bf16[1024,512]{1,0:T(8,128)(2,1)} %convolution_convert_fusion.9.refs_0_), custom_call_target="tpu_custom_call" | custom-call | bytes 104857600 | tf_op jit(solution)/shard_map/pallas_call | solution.py:149
  659.0 58.7 %shard_map.330 = (bf16[4096,128]{1,0:T(8,128)(2,1)}, bf16[8192,128]{1,0:T(8,128)(2,1)}, bf16[8192,128]{1,0:T(8,128)(2,1)}) custom-call(s32[8]{0:T(128)} %lengths_ref.3, s32[64]{0:T(128)} %order_ref.3, s32[64]{0:T(128)} %slot_ref.3, bf16[4096,128]{1,0:T(8,128)(2,1)} %get-tuple-element.51.q_ref, bf16[8192,128]{1,0:T(8,128)(2,1)} %get-tuple-element.52.k_ref, ...), custom_call_target="tpu_custom_call" | custom-call | flops 21474836480 | bytes 104857600 | tf_op jit(solution)/shard_map/pallas_call | solution.py:399
  717.8 1.2 copy-done.3
  719.0 38.2 %shard_map.331 = (bf16[1024,512]{1,0:T(8,128)(2,1)S(1)}, bf16[1024,512]{1,0:T(8,128)(2,1)S(1)}, bf16[1024,512]{1,0:T(8,128)(2,1)S(1)}) custom-call(bf16[4096,128]{1,0:T(8,128)(2,1)S(1)} %copy-done.3, bf16[8192,128]{1,0:T(8,128)(2,1)} %get-tuple-element.62.refs_1_, bf16[8192,128]{1,0:T(8,128)(2,1)} %get-tuple-element.63.refs_2_), custom_call_target="tpu_custom_call" | custom-call | bytes 104857600 | tf_op jit(solution)/shard_map/pallas_call | solution.py:242
  757.2 4.4 fusion.19
  761.6 5.6 fusion.20
  767.2 3.8 convolution_convert_fusion.8.refs_4_
  771.0 3.8 convolution_convert_fusion.7.refs_5_
  774.8 3.8 convolution_convert_fusion.5.refs_7_
  778.6 4.0 convolution_convert_fusion.6.refs_6_
  782.6 8.1 add_convert_fusion.refs_0_
  790.8 90.1 %shard_map.332 = (f32[256,2048]{1,0:T(8,128)}, f32[8,2048]{1,0:T(8,128)}, f32[256,512]{1,0:T(8,128)}, f32[256,512]{1,0:T(8,128)}, f32[256,512]{1,0:T(8,128)}, /*index=5*/f32[256,512]{1,0:T(8,128)}) custom-call(bf16[1024,2048]{1,0:T(8,128)(2,1)} %add_convert_fusion.refs_0_, f32[256,2048]{1,0:T(8,128)} %copy-done.2, bf16[256,2048]{1,0:T(8,128)(2,1)} %refs_2_.3, ...), custom_call_target="tpu_custom_call" | custom-call | bytes 314572800 | tf_op jit(solution)/shard_map/pallas_call | solution.py:882
  880.9 1.4 convert_reduce_fusion.4
  883.5 0.9 fusion.17
  884.4 1.9 concatenate.8.in_ref
  886.3 11.2 %shard_map.333 = f32[24,128]{1,0:T(8,128)} custom-call(f32[8,24,128]{2,1,0:T(8,128)} %concatenate.8.in_ref), custom_call_target="tpu_custom_call" | custom-call | bytes 20971520 | tf_op jit(solution)/shard_map/pallas_call | solution.py:930
  897.6 1.3 slice_bitcast_fusion
  898.8 1.4 slice_bitcast_fusion.1
  900.3 2.6 select_convert_fusion
  902.9 2.8 convert_element_type.112
  905.8 2.8 convert_element_type.114
  908.6 3.1 copy.54
  912.5 1.9 copy.56
  (103 shorter events, 17.6 us)
Async XLA Ops:
  7.2 370.2 %all-gather.4.cloned.1.call-start = ((), (), s32[]{:S(2)}) async-start(), calls=%async_computation.3 | async-start | bytes 9437184 | tf_op jit(solution)/shard_map/all_gather | solution.py:1016
  7.9 384.0 %all-gather.8.cloned.1.call-start = ((), (), s32[]{:S(2)}) async-start(), calls=%async_computation.6 | async-start | bytes 5242880 | tf_op jit(solution)/shard_map/all_gather | solution.py:60
  11.0 0.5 copy-start.20
  14.6 377.3 %all-gather.6.cloned.1.call-start = ((), (), s32[]{:S(2)}) async-start(), calls=%async_computation.4 | async-start | bytes 9437184 | tf_op jit(solution)/shard_map/all_gather | solution.py:1017
  15.4 884.9 %reduce-scatter.4.cloned.1.call-start = ((), (), s32[]{:S(2)}) async-start(), calls=%async_computation.5 | async-start | bytes 5242880 | tf_op jit(solution)/shard_map/reduce_scatter | solution.py:65
  108.8 8.5 copy-start.8
  110.5 8.7 copy-start.16
  110.5 8.8 copy-start.23
  119.2 6.6 copy-start.9
  119.2 3.3 copy-start.25
  122.5 3.3 copy-start.11
  223.8 1.2 copy-start.7
  225.0 33.3 %copy-start = (bf16[256,2048]{1,0:T(8,128)(2,1)S(1)}, bf16[256,2048]{1,0:T(8,128)(2,1)}, u32[]{:S(2)}) copy-start(bf16[256,2048]{1,0:T(8,128)(2,1)} %refs_2_.3) | copy-start | bytes 3145732
  252.0 6.3 copy-start.4
  450.0 452.9 %reduce-scatter.6.cloned.1.call-start = ((), (), s32[]{:S(2)}) async-start(), calls=%async_computation.7 | async-start | bytes 9437184 | tf_op jit(solution)/shard_map/reduce_scatter | solution.py:70
  464.2 441.6 %reduce-scatter.8.cloned.1.call-start = ((), (), s32[]{:S(2)}) async-start(), calls=%async_computation.8 | async-start | bytes 9437184 | tf_op jit(solution)/shard_map/reduce_scatter | solution.py:70
  478.5 14.1 %copy-start.1 = (bf16[256,2048]{1,0:T(8,128)(2,1)S(1)}, bf16[256,2048]{1,0:T(8,128)(2,1)}, u32[]{:S(2)}) copy-start(bf16[256,2048]{1,0:T(8,128)(2,1)} %get-tuple-element.79.branch_ref) | copy-start | bytes 3145732
  478.5 159.3 %copy-start.26 = (bf16[2048,512]{1,0:T(8,128)(2,1)S(1)}, bf16[2048,512]{1,0:T(8,128)(2,1)}, u32[]{:S(2)}) copy-start(bf16[2048,512]{1,0:T(8,128)(2,1)} %get-tuple-element.55) | copy-start | bytes 6291460
  636.5 1.3 copy-start.2
  717.8 1.2 copy-start.3
  757.2 10.0 %copy-start.6 = (bf16[1024,512]{1,0:T(8,128)(2,1)}, bf16[1024,512]{1,0:T(8,128)(2,1)S(1)}, u32[]{:S(2)}) copy-start(bf16[1024,512]{1,0:T(8,128)(2,1)S(1)} %get-tuple-element.64) | copy-start | bytes 3145732
  757.2 4.4 copy-start.24
  761.6 5.6 copy-start.10
  771.0 3.8 copy-start.5
  771.0 3.8 copy-start.22
  778.6 4.0 copy-start.12
  790.8 92.4 %copy-start.19 = (f32[2048]{0:T(1024)S(1)}, f32[2048]{0:T(1024)}, u32[]{:S(2)}) copy-start(f32[2048]{0:T(1024)} %get-tuple-element.75) | copy-start | bytes 24580
  790.8 93.6 %copy-start.17 = (f32[2048]{0:T(1024)S(1)}, f32[2048]{0:T(1024)}, u32[]{:S(2)}) copy-start(f32[2048]{0:T(1024)} %get-tuple-element.78) | copy-start | bytes 24580
  790.8 109.5 %copy-start.18 = (f32[8,2,128]{2,1,0:T(2,128)S(1)}, f32[8,2,128]{2,1,0:T(2,128)}, u32[]{:S(2)}) copy-start(f32[8,2,128]{2,1,0:T(2,128)} %get-tuple-element.80) | copy-start | bytes 24580
  790.8 109.5 %copy-start.21 = (pred[256]{0:T(512)(128)(4,1)S(1)}, pred[256]{0:T(512)(128)(4,1)}, u32[]{:S(2)}) copy-start(pred[256]{0:T(512)(128)(4,1)} %copy-done.20) | copy-start | bytes 772
  900.3 14.1 %copy-start.14 = (f32[256,512]{1,0:T(8,128)S(1)}, f32[256,512]{1,0:T(8,128)}, u32[]{:S(2)}) copy-start(f32[256,512]{1,0:T(8,128)} %get-tuple-element.127) | copy-start | bytes 1572868
  900.3 14.9 %copy-start.13 = (f32[256,512]{1,0:T(8,128)S(1)}, f32[256,512]{1,0:T(8,128)}, u32[]{:S(2)}) copy-start(f32[256,512]{1,0:T(8,128)} %get-tuple-element.129) | copy-start | bytes 1572868
  902.9 8.8 copy-start.15
Sparse Core Ops, SparseCore 0:
  9.9 92.1 all-gather.3
  104.3 83.5 all-gather.7
  189.8 64.0 all-gather.5
  450.2 101.4 reduce-scatter.3
  555.3 75.7 reduce-scatter.5
  634.5 71.2 reduce-scatter.7

commit v4 on v3

--- a/solution.py
+++ b/solution.py
@@ -9,7 +9,7 @@
 
 HEAD_DIM = 128
 BLOCK = 128
-KEY_BLOCKS = 4
+KEY_BLOCKS = 8
 MESH = pl.DeviceIdType.MESH
 ANY = pl.BlockSpec(memory_space=pl.ANY)
 VMEM = pl.BlockSpec(memory_space=pltpu.VMEM)
@@ -42,18 +42,6 @@
     return lax.dot_general(
         left, right, (((0,), (0,)), ((), ())), preferred_element_type=jnp.float32
     )
-
-
-def valid_rows(seq_lengths, block_order, first_row, row_count):
-    row_ids = first_row + jnp.arange(row_count, dtype=jnp.int32)
-    slot_hit = (row_ids // BLOCK)[:, None] == jnp.arange(block_order.shape[0], dtype=jnp.int32)[None, :]
-    initial = jnp.sum(jnp.where(slot_hit, block_order[None, :], 0), axis=1)
-    block_counts = (seq_lengths + BLOCK - 1) // BLOCK
-    ends = jnp.cumsum(block_counts)
-    starts = ends - block_counts
-    inside = (initial[:, None] >= starts[None, :]) & (initial[:, None] < ends[None, :])
-    left = seq_lengths[None, :] - (initial[:, None] - starts[None, :]) * BLOCK
-    return (row_ids % BLOCK) < jnp.sum(jnp.where(inside, left, 0), axis=1)
 
 
 def whole_rows(local_part):
@@ -252,111 +240,163 @@
     )(*owned, *shared)
 
 
-def query_block(index, lengths, order, members, blocks_each):
-    member = lax.axis_index("dp") % members
-    dealt = ((index // blocks_each) * members + member) * blocks_each + index % blocks_each
-    place = order[dealt]
+def sequence_of(place, lengths):
     first, length, running = jnp.int32(0), jnp.int32(0), jnp.int32(0)
     for s in range(lengths.shape[0]):
         inside = place >= running
         first = jnp.where(inside, running, first)
         length = jnp.where(inside, lengths[s], length)
         running = running + (lengths[s] + (BLOCK - 1)) // BLOCK
-    behind = place - first
-    return first, behind, length - behind * BLOCK
-
-
-def key_blocks(block_count, slot, visit):
-    @pl.loop(0, block_count)
-    def _(block):
-        visit(pl.multiple_of(block * BLOCK, BLOCK), pl.multiple_of(slot[block] * BLOCK, BLOCK))
-
-
-def allowed_keys(tile, behind):
-    width = KEY_BLOCKS * BLOCK
-    key_pos = lax.broadcasted_iota(jnp.int32, (width, BLOCK), 0) + tile * width
-    query_pos = lax.broadcasted_iota(jnp.int32, (width, BLOCK), 1) + behind * BLOCK
-    return key_pos <= query_pos
-
-
-def attend(queries, key_rows, value_rows, lengths, order, slot, members, blocks_each):
-    query_count, key_count = queries.shape[0] // BLOCK, key_rows.shape[0] // BLOCK
+    return first, length - (place - first) * BLOCK
+
+
+def list_queries(slot, index_list, place_list, members, blocks_each):
+    member = lax.axis_index("dp") % members
+
+    def visit(block, count):
+        dealt = slot[block]
+        owner = dealt // blocks_each
+
+        @pl.when(owner % members == member)
+        def _():
+            index_list[count] = (owner // members) * blocks_each + dealt % blocks_each
+            place_list[count] = block
+
+        return count + (owner % members == member).astype(jnp.int32)
+
+    lax.fori_loop(0, slot.shape[0], visit, jnp.int32(0))
+
+
+def block_rows(block):
+    return pl.ds(pl.multiple_of(block * BLOCK, BLOCK), BLOCK)
+
+
+class QueryPair:
+    def __init__(self, pair, lengths, index_list, place_list):
+        self.index = [index_list[2 * pair + i] for i in range(2)]
+        self.place = [place_list[2 * pair + i] for i in range(2)]
+        found = [sequence_of(place, lengths) for place in self.place]
+        self.start = found[0][0]
+        lane = lax.broadcasted_iota(jnp.int32, (1, 2 * BLOCK), 1)
+        right = lane >= BLOCK
+
+        def lanes_of(left_value, right_value):
+            return jnp.where(right, right_value, left_value)
+
+        within = lane - lanes_of(0, BLOCK)
+        base = self.start * BLOCK
+        self.position = lanes_of(self.place[0], self.place[1]) * BLOCK + within - base
+        self.lowest = lanes_of(found[0][0], found[1][0]) * BLOCK - base
+        self.live = within < lanes_of(found[0][1], found[1][1])
+        self.tiles = (self.place[1] - self.start) // KEY_BLOCKS + 1
+        self.open_tiles = jnp.where(found[0][0] == found[1][0], (self.place[0] - self.start) // KEY_BLOCKS, 0)
+
+    def row(self, tile):
+        return pl.multiple_of((self.start + tile * KEY_BLOCKS) * BLOCK, BLOCK)
+
+    def allowed(self, tile):
+        width = KEY_BLOCKS * BLOCK
+        key = lax.broadcasted_iota(jnp.int32, (width, 2 * BLOCK), 0)
+        return (key <= self.position - tile * width) & (key >= self.lowest - tile * width)
+
+    def load_t(self, ref):
+        return jnp.concatenate([ref[block_rows(index)].T for index in self.index], axis=1)
+
+    def load(self, ref):
+        return jnp.concatenate([ref[block_rows(index)] for index in self.index], axis=0)
+
+    def store_t(self, ref, value_t):
+        for i, index in enumerate(self.index):
+            ref[block_rows(index)] = value_t[:, i * BLOCK : (i + 1) * BLOCK].T.astype(ref.dtype)
+
+
+def attend(queries, shared, lengths, order, slot, members, blocks_each):
+    pairs, key_count = queries.shape[0] // (2 * BLOCK), shared.shape[1] // BLOCK
     width = KEY_BLOCKS * BLOCK
     padded = (key_count + KEY_BLOCKS - 1) * BLOCK
     scale = math.log2(math.e) / math.sqrt(HEAD_DIM)
 
-    def kernel(lengths_ref, order_ref, slot_ref, q_ref, k_ref, v_ref, out_ref, exact_ref, log_ref, keys, values_t):
-        def visit(to, source):
-            keys[pl.ds(to, BLOCK)] = k_ref[pl.ds(source, BLOCK)]
-            values_t[:, pl.ds(to, BLOCK)] = v_ref[pl.ds(source, BLOCK)].T
-
-        key_blocks(key_count, slot_ref, visit)
-        keys[pl.ds(key_count * BLOCK, padded - key_count * BLOCK)] = jnp.zeros(
-            (padded - key_count * BLOCK, HEAD_DIM), keys.dtype)
-        values_t[:, pl.ds(key_count * BLOCK, padded - key_count * BLOCK)] = jnp.zeros(
-            (HEAD_DIM, padded - key_count * BLOCK), keys.dtype)
-
-        @pl.loop(0, query_count)
+    def kernel(lengths_ref, slot_ref, q_ref, shared_ref, out_ref, exact_ref, log_ref,
+               index_list, place_list, keys, values_t):
+        list_queries(slot_ref, index_list, place_list, members, blocks_each)
+
+        @pl.loop(0, key_count)
+        def _(block):
+            source = block_rows(slot_ref[block])
+            keys[block_rows(block)] = shared_ref[0, source]
+            values_t[:, block_rows(block)] = shared_ref[1, source].T
+
+        tail = pl.ds(key_count * BLOCK, padded - key_count * BLOCK)
+        keys[tail] = jnp.zeros((padded - key_count * BLOCK, HEAD_DIM), keys.dtype)
+        values_t[:, tail] = jnp.zeros((HEAD_DIM, padded - key_count * BLOCK), keys.dtype)
+
+        @pl.loop(0, pairs)
         def _(index):
-            first, behind, valid = query_block(index, lengths_ref, order_ref, members, blocks_each)
-            query_t = q_ref[pl.ds(pl.multiple_of(index * BLOCK, BLOCK), BLOCK)].T
-
-            def step(tile, carry):
+            pair = QueryPair(index, lengths_ref, index_list, place_list)
+            query_t = pair.load_t(q_ref)
+
+            def step(tile, carry, masked):
                 top, total, mix = carry
-                row = pl.multiple_of((first + tile * KEY_BLOCKS) * BLOCK, BLOCK)
-                scores = jnp.dot(keys[pl.ds(row, width)], query_t, preferred_element_type=jnp.float32) * scale
-                scores = jnp.where(allowed_keys(tile, behind), scores, big_negative)
+                span = pl.ds(pair.row(tile), width)
+                scores = jnp.dot(keys[span], query_t, preferred_element_type=jnp.float32)
+                if masked:
+                    scores = jnp.where(pair.allowed(tile), scores, big_negative)
                 new_top = jnp.maximum(top, jnp.max(scores, axis=0, keepdims=True))
-                weights = jnp.exp2(scores - new_top)
-                fade = jnp.exp2(top - new_top)
+                weights = jnp.exp2((scores - new_top) * scale)
+                fade = jnp.exp2((top - new_top) * scale)
                 total = total * fade + jnp.sum(weights, axis=0, keepdims=True)
                 mix = mix * fade + jnp.dot(
-                    values_t[:, pl.ds(row, width)], weights.astype(jnp.bfloat16), preferred_element_type=jnp.float32)
+                    values_t[:, span], weights.astype(jnp.bfloat16), preferred_element_type=jnp.float32)
                 return new_top, total, mix
 
-            top, total, mix = lax.fori_loop(
-                0, behind // KEY_BLOCKS + 1, step,
-                (jnp.full((1, BLOCK), big_negative, jnp.float32), jnp.zeros((1, BLOCK), jnp.float32),
-                 jnp.zeros((HEAD_DIM, BLOCK), jnp.float32)))
-            live = lax.broadcasted_iota(jnp.int32, (1, BLOCK), 1) < valid
-            mix = jnp.where(live, mix / total, 0.0)
+            carry = (jnp.full((1, 2 * BLOCK), big_negative, jnp.float32), jnp.zeros((1, 2 * BLOCK), jnp.float32),
+                     jnp.zeros((HEAD_DIM, 2 * BLOCK), jnp.float32))
+            carry = lax.fori_loop(0, pair.open_tiles, lambda tile, c: step(tile, c, False), carry)
+            top, total, mix = lax.fori_loop(pair.open_tiles, pair.tiles, lambda tile, c: step(tile, c, True), carry)
+            mix = jnp.where(pair.live, mix / total, 0.0)
             exact_ref[index] = mix
-            out_ref[pl.ds(pl.multiple_of(index * BLOCK, BLOCK), BLOCK)] = mix.T.astype(out_ref.dtype)
-            log_ref[index] = jnp.where(live, top + jnp.log2(total), -big_negative)
+            pair.store_t(out_ref, mix)
+            log_ref[index] = jnp.where(pair.live, top * scale + jnp.log2(total), -big_negative)
 
     return pl.pallas_call(
         kernel,
         out_shape=[
             jax.ShapeDtypeStruct(queries.shape, jnp.bfloat16),
-            jax.ShapeDtypeStruct((query_count, HEAD_DIM, BLOCK), jnp.float32),
-            jax.ShapeDtypeStruct((query_count, 1, BLOCK), jnp.float32),
+            jax.ShapeDtypeStruct((pairs, HEAD_DIM, 2 * BLOCK), jnp.float32),
+            jax.ShapeDtypeStruct((pairs, 1, 2 * BLOCK), jnp.float32),
         ],
-        in_specs=[SMEM] * 3 + [VMEM] * 3,
+        in_specs=[SMEM] * 2 + [VMEM] * 2,
         out_specs=[VMEM] * 3,
-        scratch_shapes=[pltpu.VMEM((padded, HEAD_DIM), jnp.bfloat16), pltpu.VMEM((HEAD_DIM, padded), jnp.bfloat16)],
+        scratch_shapes=[
+            pltpu.SMEM((2 * pairs,), jnp.int32), pltpu.SMEM((2 * pairs,), jnp.int32),
+            pltpu.VMEM((padded, HEAD_DIM), jnp.bfloat16), pltpu.VMEM((HEAD_DIM, padded), jnp.bfloat16),
+        ],
         compiler_params=pltpu.CompilerParams(vmem_limit_bytes=56 * MIB),
         cost_estimate=pl.CostEstimate(flops=8 << 30, bytes_accessed=50 * MIB, transcendentals=8 << 20),
-    )(lengths, order, slot, queries, key_rows, value_rows)
-
-
-def attend_back(queries, key_rows, value_rows, upstream, exact, logs, lengths, order, slot, members, blocks_each):
-    query_count, key_count = queries.shape[0] // BLOCK, key_rows.shape[0] // BLOCK
+    )(lengths, slot, queries, shared)
+
+
+def attend_back(queries, shared, upstream, exact, logs, lengths, order, slot, members, blocks_each):
+    pairs, key_count = queries.shape[0] // (2 * BLOCK), shared.shape[1] // BLOCK
     width = KEY_BLOCKS * BLOCK
     padded = (key_count + KEY_BLOCKS - 1) * BLOCK
     scale = math.log2(math.e) / math.sqrt(HEAD_DIM)
     plain_scale = 1.0 / math.sqrt(HEAD_DIM)
 
-    def kernel(lengths_ref, order_ref, slot_ref, q_ref, k_ref, v_ref, g_ref, exact_ref, log_ref,
-               dq_ref, dk_ref, dv_ref, keys, keys_t, values, key_sum, value_sum):
-        def visit(to, source):
-            block = k_ref[pl.ds(source, BLOCK)]
-            keys[pl.ds(to, BLOCK)] = block
-            keys_t[:, pl.ds(to, BLOCK)] = block.T
-            values[pl.ds(to, BLOCK)] = v_ref[pl.ds(source, BLOCK)]
-            key_sum[pl.ds(to, BLOCK)] = jnp.zeros((BLOCK, HEAD_DIM), jnp.float32)
-            value_sum[pl.ds(to, BLOCK)] = jnp.zeros((BLOCK, HEAD_DIM), jnp.float32)
-
-        key_blocks(key_count, slot_ref, visit)
+    def kernel(lengths_ref, slot_ref, q_ref, shared_ref, g_ref, exact_ref, log_ref, dq_ref, dk_ref, dv_ref,
+               index_list, place_list, keys, keys_t, values, key_sum, value_sum):
+        list_queries(slot_ref, index_list, place_list, members, blocks_each)
+
+        @pl.loop(0, key_count)
+        def _(block):
+            source, to = block_rows(slot_ref[block]), block_rows(block)
+            rows = shared_ref[0, source]
+            keys[to] = rows
+            keys_t[:, to] = rows.T
+            values[to] = shared_ref[1, source]
+            key_sum[to] = jnp.zeros((BLOCK, HEAD_DIM), jnp.float32)
+            value_sum[to] = jnp.zeros((BLOCK, HEAD_DIM), jnp.float32)
+
         tail = pl.ds(key_count * BLOCK, padded - key_count * BLOCK)
         keys[tail] = jnp.zeros((padded - key_count * BLOCK, HEAD_DIM), keys.dtype)
         values[tail] = jnp.zeros((padded - key_count * BLOCK, HEAD_DIM), keys.dtype)
@@ -364,21 +404,20 @@
         key_sum[tail] = jnp.zeros((padded - key_count * BLOCK, HEAD_DIM), jnp.float32)
         value_sum[tail] = jnp.zeros((padded - key_count * BLOCK, HEAD_DIM), jnp.float32)
 
-        @pl.loop(0, query_count)
+        @pl.loop(0, pairs)
         def _(index):
-            first, behind, _ = query_block(index, lengths_ref, order_ref, members, blocks_each)
-            mine = pl.ds(pl.multiple_of(index * BLOCK, BLOCK), BLOCK)
-            query = q_ref[mine]
-            grad = g_ref[mine]
-            query_t, grad_t = query.T, grad.T
+            pair = QueryPair(index, lengths_ref, index_list, place_list)
+            query, grad = pair.load(q_ref), pair.load(g_ref)
+            query_t, grad_t = pair.load_t(q_ref), pair.load_t(g_ref)
             delta = jnp.sum(grad_t.astype(jnp.float32) * exact_ref[index], axis=0, keepdims=True)
             log_total = log_ref[index]
 
-            def step(tile, query_grad):
-                row = pl.multiple_of((first + tile * KEY_BLOCKS) * BLOCK, BLOCK)
-                span = pl.ds(row, width)
-                scores = jnp.dot(keys[span], query_t, preferred_element_type=jnp.float32) * scale
-                probability = jnp.where(allowed_keys(tile, behind), jnp.exp2(scores - log_total), 0.0)
+            def step(tile, query_grad, masked):
+                span = pl.ds(pair.row(tile), width)
+                scores = jnp.dot(keys[span], query_t, preferred_element_type=jnp.float32)
+                probability = jnp.exp2(scores * scale - log_total)
+                if masked:
+                    probability = jnp.where(pair.allowed(tile), probability, 0.0)
                 prob_grad = jnp.dot(values[span], grad_t, preferred_element_type=jnp.float32)
                 score_grad = (probability * (prob_grad - delta)).astype(jnp.bfloat16)
                 value_sum[span] += jnp.dot(
@@ -386,26 +425,28 @@
                 key_sum[span] += jnp.dot(score_grad, query, preferred_element_type=jnp.float32)
                 return query_grad + jnp.dot(keys_t[:, span], score_grad, preferred_element_type=jnp.float32)
 
-            query_grad = lax.fori_loop(
-                0, behind // KEY_BLOCKS + 1, step, jnp.zeros((HEAD_DIM, BLOCK), jnp.float32))
-            dq_ref[mine] = (query_grad * plain_scale).T.astype(dq_ref.dtype)
-
-        def leave(at, dealt):
-            dk_ref[pl.ds(dealt, BLOCK)] = (key_sum[pl.ds(at, BLOCK)] * plain_scale).astype(dk_ref.dtype)
-            dv_ref[pl.ds(dealt, BLOCK)] = value_sum[pl.ds(at, BLOCK)].astype(dv_ref.dtype)
-
-        key_blocks(key_count, slot_ref, leave)
+            query_grad = jnp.zeros((HEAD_DIM, 2 * BLOCK), jnp.float32)
+            query_grad = lax.fori_loop(0, pair.open_tiles, lambda tile, c: step(tile, c, False), query_grad)
+            query_grad = lax.fori_loop(pair.open_tiles, pair.tiles, lambda tile, c: step(tile, c, True), query_grad)
+            pair.store_t(dq_ref, query_grad * plain_scale)
+
+        @pl.loop(0, key_count)
+        def _(block):
+            at, dealt = block_rows(block), block_rows(slot_ref[block])
+            dk_ref[dealt] = (key_sum[at] * plain_scale).astype(dk_ref.dtype)
+            dv_ref[dealt] = value_sum[at].astype(dv_ref.dtype)
 
     return pl.pallas_call(
         kernel,
         out_shape=[
             jax.ShapeDtypeStruct(queries.shape, jnp.bfloat16),
-            jax.ShapeDtypeStruct(key_rows.shape, jnp.bfloat16),
-            jax.ShapeDtypeStruct(key_rows.shape, jnp.bfloat16),
+            jax.ShapeDtypeStruct(shared.shape[1:], jnp.bfloat16),
+            jax.ShapeDtypeStruct(shared.shape[1:], jnp.bfloat16),
         ],
-        in_specs=[SMEM] * 3 + [VMEM] * 6,
+        in_specs=[SMEM] * 2 + [VMEM] * 5,
         out_specs=[VMEM] * 3,
         scratch_shapes=[
+            pltpu.SMEM((2 * pairs,), jnp.int32), pltpu.SMEM((2 * pairs,), jnp.int32),
             pltpu.VMEM((padded, HEAD_DIM), jnp.bfloat16),
             pltpu.VMEM((HEAD_DIM, padded), jnp.bfloat16),
             pltpu.VMEM((padded, HEAD_DIM), jnp.bfloat16),
@@ -414,7 +455,7 @@
         ],
         compiler_params=pltpu.CompilerParams(vmem_limit_bytes=60 * MIB),
         cost_estimate=pl.CostEstimate(flops=20 << 30, bytes_accessed=100 * MIB, transcendentals=8 << 20),
-    )(lengths, order, slot, queries, key_rows, value_rows, upstream, exact, logs)
+    )(lengths, slot, queries, shared, upstream, exact, logs)
 
 
 def line_neighbours(mp, count):
@@ -493,6 +534,54 @@
         return [pltpu.SemaphoreType.DMA((2, count, pieces)), pltpu.SemaphoreType.DMA((2, count, pieces))]
 
 
+class ShardGather:
+    def __init__(self, shards, wholes, depth, cross_send, cross_recv, core_send, core_recv, own_sem, dp, mp, chips):
+        self.shards, self.wholes, self.depth, self.own_sem = shards, wholes, depth, own_sem
+        self.cross_send, self.cross_recv, self.core_send, self.core_recv = cross_send, cross_recv, core_send, core_recv
+        self.dp, self.mp, self.chips = dp, mp, chips
+
+    def place(self, array, owner):
+        return self.wholes[array].at[pl.ds(pl.multiple_of(owner * self.depth, self.depth), self.depth)]
+
+    def cross(self, array, o):
+        return remote(self.shards[array], self.place(array, self.dp), self.cross_send.at[array, o],
+                      self.cross_recv.at[array, o], (self.dp ^ (2 * o), self.mp))
+
+    def core(self, array, o):
+        owner = self.dp ^ (2 * o)
+        source = self.place(array, owner) if o else self.shards[array]
+        return remote(source, self.place(array, owner), self.core_send.at[array, o], self.core_recv.at[array, o],
+                      (self.dp ^ 1, self.mp))
+
+    def own(self, array):
+        return pltpu.make_async_copy(self.shards[array], self.place(array, self.dp), self.own_sem.at[array])
+
+    def begin(self):
+        for array in range(len(self.shards)):
+            for o in range(1, self.chips):
+                self.cross(array, o).start()
+        for array in range(len(self.shards)):
+            self.own(array).start()
+            self.core(array, 0).start()
+
+    def spread(self, array):
+        for o in range(1, self.chips):
+            self.cross(array, o).wait_recv()
+            self.core(array, o).start()
+
+    def finish(self):
+        for array in range(len(self.shards)):
+            self.own(array).wait()
+            for o in range(self.chips):
+                self.core(array, o).wait()
+                if o:
+                    self.cross(array, o).wait_send()
+
+    @staticmethod
+    def semaphores(count, chips):
+        return [pltpu.SemaphoreType.DMA((count, chips)) for _ in range(4)] + [pltpu.SemaphoreType.DMA((count,))]
+
+
 class LineReduce:
     def __init__(self, part, flows, rows, pieces, send_sem, recv_sem, dp, mp, count):
         self.part, self.flows, self.rows, self.pieces = part, flows, rows, pieces
@@ -588,87 +677,6 @@
     return min(MAX_PIECES, rows // 16)
 
 
-def gather_first(hidden, vectors, weights, collective_id):
-    rows, width = hidden.shape
-    pieces = pieces_of(rows)
-    dp_count, mp_count = lax.axis_size("dp"), lax.axis_size("mp")
-    chips = dp_count // 2
-    arrays = [vectors] + list(weights)
-    count = len(arrays)
-    depth = [a.shape[0] for a in arrays]
-
-    def kernel(*refs):
-        own_rows, ins = refs[0], refs[1 : 1 + count]
-        full_rows, outs = refs[1 + count], refs[2 + count : 2 + 2 * count]
-        row_sem, local_sem, line_send, line_recv, send_sem, recv_sem, fwd_send, fwd_recv = refs[2 + 2 * count :]
-        dp, mp = lax.axis_index("dp"), lax.axis_index("mp")
-        peers = [(dp ^ (2 * o), mp) for o in range(1, chips)]
-        partner = (dp ^ 1, mp)
-        greet_all(peers + [partner], dp, mp, mp_count)
-        line = LineGather(own_rows, full_rows, rows, pieces, line_send, line_recv, dp, mp, mp_count)
-
-        def place(array, owner):
-            return outs[array].at[pl.ds(pl.multiple_of(owner * depth[array], depth[array]), depth[array])]
-
-        def cross(array, o):
-            return remote(ins[array], place(array, dp), send_sem.at[array, o], recv_sem.at[array, o], peers[o - 1])
-
-        def forward(array, o):
-            owner = dp ^ (2 * o)
-            source = place(array, owner) if o else ins[array]
-            return remote(source, place(array, owner), fwd_send.at[array, o], fwd_recv.at[array, o], partner)
-
-        @pl.loop(0, pieces)
-        def _(piece):
-            line.advance(0, piece)
-
-        for a in range(count):
-            for o in range(1, chips):
-                cross(a, o).start()
-            forward(a, 0).start()
-        own_copy = pltpu.make_async_copy(own_rows, full_rows.at[pl.ds(pl.multiple_of(mp * rows, rows), rows)], row_sem)
-        own_copy.start()
-        locals_ = [pltpu.make_async_copy(ins[a], place(a, dp), local_sem.at[a]) for a in range(count)]
-        for copy in locals_:
-            copy.start()
-        for step in range(1, mp_count - 1):
-
-            @pl.loop(0, pieces)
-            def _(piece):
-                line.advance(step, piece)
-
-        for a in range(count):
-            for o in range(1, chips):
-                cross(a, o).wait_recv()
-                forward(a, o).start()
-
-        @pl.loop(0, pieces)
-        def _(piece):
-            line.advance(mp_count - 1, piece)
-
-        line.finish()
-        own_copy.wait()
-        for a in range(count):
-            locals_[a].wait()
-            for o in range(chips):
-                if o:
-                    cross(a, o).wait_send()
-                forward(a, o).wait()
-
-    dma = pltpu.SemaphoreType.DMA
-    return pl.pallas_call(
-        kernel,
-        out_shape=[jax.ShapeDtypeStruct((mp_count * rows, width), hidden.dtype)]
-        + [jax.ShapeDtypeStruct((dp_count * a.shape[0], a.shape[1]), a.dtype) for a in arrays],
-        in_specs=[ANY] * (1 + count),
-        out_specs=[ANY] * (1 + count),
-        scratch_shapes=[dma(()), dma((count,))] + LineGather.semaphores(mp_count, pieces)
-        + [dma((count, chips)) for _ in range(4)],
-        compiler_params=pltpu.CompilerParams(collective_id=collective_id, has_side_effects=True),
-        cost_estimate=pl.CostEstimate(flops=0, bytes_accessed=200 * MIB, transcendentals=0),
-    )(hidden, *arrays)
-
-
 def unit_rows(values):
     average = jnp.mean(values, axis=-1, keepdims=True)
     centred = values - average
@@ -676,23 +684,300 @@
     return centred * inverse, inverse
 
 
-def reduce_norm_gather(part, hidden, out_bias, gain, shift, collective_id):
-    mp_count = lax.axis_size("mp")
+def project_first(
+    hidden, output_grad, lengths, order, vectors, projections, out_weight, heads, members, collective_id
+):
+    rows, width = hidden.shape
+    dp_count, mp_count = lax.axis_size("dp"), lax.axis_size("mp")
+    chips, pieces = dp_count // 2, pieces_of(rows)
+    group_rows, depth, columns = mp_count * rows, projections[0].shape[0], projections[0].shape[1]
+    each = width // dp_count // 128
+    tall = [v.shape[1] // 128 for v in vectors]
+    slab = sum(tall) + -sum(tall) % 8
+    halves, kinds = heads // 2, 3
+    arrays = kinds + 2
+    offsets = sorted({2 * o for o in range(1, chips)} | {o for o in range(1, members)} | {o * members for o in range(1, heads)})
+
+    def kernel(lengths_ref, order_ref, hidden_ref, upstream_ref, *refs):
+        parts, refs = refs[: len(vectors)], refs[len(vectors) :]
+        weight_refs, out_weight_ref = refs[:kinds], refs[kinds]
+        normed, all_vectors, weights, all_out, shared, queries, branch, live = refs[kinds + 1 : kinds + 9]
+        (vector_ref, raw, stage, gains, biases, line_send, line_recv, row_sem, own_sem, cross_send, cross_recv, core_send, core_recv,
+         head_local, head_send, head_recv, pair_send, pair_recv) = refs[kinds + 9 :]
+        dp, mp = lax.axis_index("dp"), lax.axis_index("mp")
+        vector_ref[...] = jnp.zeros_like(vector_ref)
+        first = 0
+        for part, count in zip(parts, tall):
+            for r in range(count):
+                vector_ref[first + r : first + r + 1] = part[:, r * 128 : (r + 1) * 128].astype(jnp.float32)
+            first += count
+        group, member = dp // members, dp % members
+        partner = (dp ^ 1, mp)
+        greet_all([(dp ^ o, mp) for o in offsets], dp, mp, mp_count)
+        line = LineGather(hidden_ref, raw, rows, pieces, line_send, line_recv, dp, mp, mp_count)
+
+        def source(array):
+            return (list(weight_refs) + [out_weight_ref, vector_ref])[array]
+
+        def place(array, owner):
+            if array < kinds:
+                return weights.at[array, pl.ds(pl.multiple_of(owner * depth, depth), depth)]
+            if array == kinds:
+                return all_out.at[pl.ds(pl.multiple_of(owner * depth, depth), depth)]
+            return all_vectors.at[pl.ds(pl.multiple_of(owner * slab, slab), slab)]
+
+        def cross(array, o):
+            return remote(source(array), place(array, dp), cross_send.at[array, o], cross_recv.at[array, o],
+                          (dp ^ (2 * o), mp))
+
+        def core(array, o):
+            owner = dp ^ (2 * o)
+            return remote(place(array, owner) if o else source(array), place(array, owner),
+                          core_send.at[array, o], core_recv.at[array, o], partner)
+
+        def own(array):
+            return pltpu.make_async_copy(source(array), place(array, dp), own_sem.at[array])
+
+        def block_span(block):
+            return pl.ds(pl.multiple_of(block * rows, rows), rows)
+
+        first_to_last = [kinds + 1] + list(range(kinds + 1))
+        for array in first_to_last:
+            for o in range(1, chips):
+                cross(array, o).start()
+            if array == first_to_last[0]:
+
+                @pl.loop(0, pieces)
+                def _(piece):
+                    line.advance(0, piece)
+
+        for block in range(rows // BLOCK):
+            found = order_ref[(dp * group_rows + mp * rows) // BLOCK + block]
+            valid = sequence_of(found, lengths_ref)[1]
+            span = slice(block * BLOCK, (block + 1) * BLOCK)
+            live[span] = (lax.broadcasted_iota(jnp.int32, (BLOCK, 128), 0) < valid).astype(jnp.float32)
+            keep = lax.broadcasted_iota(jnp.int32, (BLOCK, width), 0) < valid
+            branch[span] = jnp.where(keep, upstream_ref[span].astype(jnp.float32), 0.0).astype(branch.dtype)
+        own_rows = pltpu.make_async_copy(hidden_ref, raw.at[block_span(mp)], row_sem)
+        own_rows.start()
+        for array in first_to_last:
+            own(array).start()
+            core(array, 0).start()
+
+        def spread(array):
+            for o in range(1, chips):
+                cross(array, o).wait_recv()
+                core(array, o).start()
+
+        def settle(array):
+            own(array).wait()
+            for o in range(chips):
+                core(array, o).wait_recv()
+
+        def norm(block):
+            chunk = 64
+
+            @pl.loop(0, rows // chunk)
+            def _(part):
+                span = pl.ds(pl.multiple_of(block * rows + part * chunk, chunk), chunk)
+                unit, _ = unit_rows(raw[span].astype(jnp.float32))
+                normed[span] = (unit * gains[0:1] + gains[1:2]).astype(normed.dtype)
+
+        def each_block(low, high, visit):
+            @pl.loop(0, mp_count)
+            def _(block):
+                distance = jnp.abs(block - mp)
+
+                @pl.when((distance >= low) & (distance <= high))
+                def _():
+                    visit(block)
+
+        def rows_of(kind_ref, owner, block):
+            return kind_ref.at[pl.ds(pl.multiple_of(owner * group_rows + block * rows, rows), rows)]
+
+        def pass_on(kind, o, block, piece):
+            giver = (group ^ o) * members + member
+            return [remote(piece, rows_of(shared.at[kind], giver, block), pair_send.at[kind, o, block, p - 1],
+                           pair_recv.at[kind, o, block, p - 1], (group * members + (member ^ p), mp))
+                    for p in range(1, members)]
+
+        def head_copy(kind, o, block, to_shared):
+            target = group ^ o
+            piece = stage.at[kind, block, target]
+            landing = rows_of(shared.at[kind], dp, block) if to_shared else rows_of(queries, group, block)
+            return remote(piece, landing, head_send.at[kind, o, block], head_recv.at[kind, o, block],
+                          (target * members + member, mp))
+
+        def local_copy(kind, block, to_shared):
+            landing = rows_of(shared.at[kind], dp, block) if to_shared else rows_of(queries, group, block)
+            return pltpu.make_async_copy(stage.at[kind, block, group], landing, head_local.at[kind, block])
+
+        def project(tile, block):
+            kind, half = tile // halves, tile % halves
+            span = pl.ds(pl.multiple_of(half * 256, 256), 256)
+            value = jnp.dot(normed[block_span(block)], weights[kind, :, span], preferred_element_type=jnp.float32)
+            value = (value + biases[pl.ds(kind, 1), span]).astype(stage.dtype)
+            for h in range(2):
+                head = 2 * half + h
+                stage[kind, block, head] = value[:, h * HEAD_DIM : (h + 1) * HEAD_DIM]
+            for h in range(2):
+                o = (2 * half + h) ^ group
+                for to_shared in (True, False):
+                    chosen = (kind < 2) if to_shared else (kind == 2)
+
+                    @pl.when(chosen & (o != 0))
+                    def _():
+                        head_copy(kind, o, block, to_shared).start()
+
+                    @pl.when(chosen & (o == 0))
+                    def _():
+                        local_copy(kind, block, to_shared).start()
+                        if to_shared:
+                            for copy in pass_on(kind, 0, block, stage.at[kind, block, group]):
+                                copy.start()
+
+        def hand_on(block):
+            @pl.loop(0, 2)
+            def _(kind):
+                for o in range(1, heads):
+                    head_copy(kind, o, block, True).wait_recv()
+                    giver = (group ^ o) * members + member
+                    for copy in pass_on(kind, o, block, rows_of(shared.at[kind], giver, block)):
+                        copy.start()
+
+        last = mp_count - 1
+        for step in range(1, last):
+
+            @pl.loop(0, pieces)
+            def _(piece):
+                line.advance(step, piece)
+
+            if step == 1:
+                spread(kinds + 1)
+                settle(kinds + 1)
+                for owner in range(dp_count):
+                    for r in range(each):
+                        at = pl.ds((owner * each + r) * 128, 128)
+                        for k in range(2):
+                            gains[k : k + 1, at] = all_vectors[owner * slab + k * each + r : owner * slab + k * each + r + 1]
+                biases[...] = jnp.zeros_like(biases)
+                for head in range(heads):
+                    feature = mp * heads + head
+                    first = (feature // each) * slab + feature % each
+                    for kind, k in ((1, 3), (2, 2)):
+                        biases[kind : kind + 1, head * 128 : (head + 1) * 128] = all_vectors[pl.ds(first + k * each, 1)]
+                own_rows.wait()
+                each_block(0, 1, norm)
+            else:
+                each_block(step, step, norm)
+        for array in range(kinds + 1):
+            spread(array)
+        for array in range(kinds):
+            settle(array)
+        tiles = kinds * halves
+
+        @pl.loop(0, pieces)
+        def _(piece):
+            line.advance(last - 1 if last == 1 else last, piece)
+
+            @pl.when(piece < tiles)
+            def _():
+                each_block(0, last - 1, lambda block: project(piece, block))
+
+        each_block(last, last, norm)
+
+        @pl.loop(0, tiles)
+        def _(tile):
+            each_block(last, last, lambda block: project(tile, block))
+
+        each_block(0, last - 1, hand_on)
+        each_block(last, last, hand_on)
+        line.finish()
+        settle(kinds)
+        for array in first_to_last:
+            for o in range(chips):
+                core(array, o).wait_send()
+                if o:
+                    cross(array, o).wait_send()
+
+        @pl.loop(0, mp_count)
+        def _(block):
+            for kind in range(kinds):
+                to_shared = kind < 2
+                local_copy(kind, block, to_shared).wait()
+                for o in range(1, heads):
+                    head_copy(kind, o, block, to_shared).wait_send()
+                    if not to_shared:
+                        head_copy(kind, o, block, to_shared).wait_recv()
+                if to_shared:
+                    for o in range(heads):
+                        giver = (group ^ o) * members + member
+                        for copy in pass_on(kind, o, block, rows_of(shared.at[kind], giver, block)):
+                            copy.wait()
+
+    dma = pltpu.SemaphoreType.DMA
+    bf16, f32 = jnp.bfloat16, jnp.float32
+    return pl.pallas_call(
+        kernel,
+        out_shape=[
+            jax.ShapeDtypeStruct((group_rows, width), bf16),
+            jax.ShapeDtypeStruct((dp_count * slab, 128), f32),
+            jax.ShapeDtypeStruct((kinds, width, columns), bf16),
+            jax.ShapeDtypeStruct((width, columns), bf16),
+            jax.ShapeDtypeStruct((2, dp_count * group_rows, HEAD_DIM), bf16),
+            jax.ShapeDtypeStruct((heads * group_rows, HEAD_DIM), bf16),
+            jax.ShapeDtypeStruct((rows, width), bf16),
+            jax.ShapeDtypeStruct((rows, 128), f32),
+        ],
+        in_specs=[SMEM, SMEM, VMEM, VMEM] + [VMEM] * len(vectors) + [ANY] * (kinds + 1),
+        out_specs=[VMEM, VMEM, VMEM, ANY, ANY, ANY, VMEM, VMEM],
+        scratch_shapes=[
+            pltpu.VMEM((slab, 128), f32),
+            pltpu.VMEM((group_rows, width), bf16),
+            pltpu.VMEM((kinds, mp_count, heads, rows, HEAD_DIM), bf16),
+            pltpu.VMEM((8, width), f32),
+            pltpu.VMEM((8, columns), f32),
+        ]
+        + LineGather.semaphores(mp_count, pieces)
+        + [dma(()), dma((arrays,))]
+        + [dma((arrays, chips)) for _ in range(4)]
+        + [dma((kinds, mp_count)), dma((kinds, heads, mp_count)), dma((kinds, heads, mp_count))]
+        + [dma((2, heads, mp_count, members)) for _ in range(2)],
+        compiler_params=pltpu.CompilerParams(
+            collective_id=collective_id, has_side_effects=True, vmem_limit_bytes=48 * MIB),
+        cost_estimate=pl.CostEstimate(flops=8 << 30, bytes_accessed=250 * MIB, transcendentals=0),
+    )(lengths, order, hidden, output_grad, *vectors, *projections, out_weight)
+
+
+def reduce_norm_gather(part, hidden, out_bias, gain, shift, shards, collective_id):
+    dp_count, mp_count = lax.axis_size("dp"), lax.axis_size("mp")
+    chips, count = dp_count // 2, len(shards)
     rows, width = hidden.shape
     pieces = pieces_of(rows)
     size = rows // pieces
 
-    def kernel(part_ref, hidden_ref, bias_ref, gain_ref, shift_ref, residual_ref, full_ref,
-               total, normed, flows, red_send, red_recv, line_send, line_recv, own_sem):
+    turns = pieces + 2 * SKEW * (mp_count - 1)
+
+    def kernel(part_ref, hidden_ref, bias_ref, gain_ref, shift_ref, *refs):
+        shard_refs, (residual_ref, full_ref), whole_refs = refs[:count], refs[count : count + 2], refs[count + 2 : 2 * count + 2]
+        total, normed, flows, red_send, red_recv, line_send, line_recv, own_sem, *weight_sems = refs[2 * count + 2 :]
         dp, mp = lax.axis_index("dp"), lax.axis_index("mp")
-        greet_all([], dp, mp, mp_count)
+        greet_all([(dp ^ (2 * o), mp) for o in range(1, chips)] + [(dp ^ 1, mp)], dp, mp, mp_count)
+        weights = ShardGather(shard_refs, whole_refs, shards[0].shape[0], *weight_sems, dp, mp, chips)
+        weights.begin()
         reduce = LineReduce(part_ref, flows, rows, pieces, red_send, red_recv, dp, mp, mp_count)
         gather = LineGather(normed, full_ref, rows, pieces, line_send, line_recv, dp, mp, mp_count)
         for piece in range(AHEAD):
             reduce.begin(piece)
 
-        @pl.loop(0, pieces + 2 * SKEW * (mp_count - 1))
+        @pl.loop(0, turns)
         def _(turn):
+            for array in range(count):
+
+                @pl.when(turn == turns - 1 - 6 * (count - 1 - array))
+                def _():
+                    weights.spread(array)
+
             reduce.begin(jnp.minimum(turn + AHEAD, pieces - 1), turn + AHEAD < pieces)
             reduce.advance(turn)
             done = turn - SKEW * (mp_count - 1)
@@ -717,22 +1002,24 @@
         reduce.finish()
         gather.finish()
         own.wait()
+        weights.finish()
 
     return pl.pallas_call(
         kernel,
         out_shape=[
             jax.ShapeDtypeStruct((rows, width), jnp.float32),
             jax.ShapeDtypeStruct((mp_count * rows, width), jnp.bfloat16),
-        ],
-        in_specs=[VMEM] * 5,
-        out_specs=[VMEM, ANY],
+        ]
+        + [jax.ShapeDtypeStruct((dp_count * a.shape[0], a.shape[1]), a.dtype) for a in shards],
+        in_specs=[VMEM] * 5 + [ANY] * count,
+        out_specs=[VMEM, ANY] + [ANY] * count,
         scratch_shapes=[pltpu.VMEM((size, width), jnp.float32), pltpu.VMEM((rows, width), jnp.bfloat16)]
         + LineReduce.scratch(mp_count, rows, width, pieces) + LineGather.semaphores(mp_count, pieces)
-        + [pltpu.SemaphoreType.DMA(())],
+        + [pltpu.SemaphoreType.DMA(())] + ShardGather.semaphores(count, chips),
         compiler_params=pltpu.CompilerParams(
             collective_id=collective_id, has_side_effects=True, vmem_limit_bytes=48 * MIB),
         cost_estimate=pl.CostEstimate(flops=0, bytes_accessed=300 * MIB, transcendentals=0),
-    )(part, hidden, out_bias, gain, shift)
+    )(part, hidden, out_bias, gain, shift, *shards)
 
 
 def reduce_back_gather(part, residual, branch_two, gain, collective_id):
@@ -940,12 +1227,6 @@
         compiler_params=pltpu.CompilerParams(collective_id=collective_id, has_side_effects=True),
         cost_estimate=pl.CostEstimate(flops=0, bytes_accessed=20 * MIB, transcendentals=0),
     )(packed)
-
-
-def packed_rows(vectors):
-    flat = jnp.concatenate([v.astype(jnp.float32) for v in vectors])
-    rows = flat.shape[0] // 128
-    return jnp.pad(flat.reshape(rows, 128), ((0, -rows % 8), (0, 0)))
 
 
 def per_device(
@@ -981,42 +1262,28 @@
     blocks_each = group_rows // BLOCK
     plan = (seq_lengths, block_order, block_slot)
 
-    own_valid = valid_rows(seq_lengths, block_order, dp_index * group_rows + mp_index * local_rows, local_rows)
-
     vectors = (first_gain, first_shift, query_bias, value_bias, out_bias, second_gain, second_shift, down_bias, up_bias)
-    rows_in, vector_rows, query_all, key_all, value_all, out_all = gather_first(
-        hidden_in, packed_rows(vectors), (query_weight, key_weight, value_weight, out_weight), 0
+    rows_one, vector_rows, projections, out_all, head_shared, head_queries, branch_two, live = project_first(
+        hidden_in, output_grad, seq_lengths, block_order, [v.reshape(1, -1) for v in vectors],
+        (key_weight, value_weight, query_weight), out_weight, heads_local, members, 0,
     )
+    own_valid = live[:, :1] > 0
+    key_all, value_all, query_all = projections
     vector_rows = vector_rows.reshape(dp_count, -1, 128)
     each = model_width // dp_count // 128
-    (gain_one, shift_one, bias_query, bias_value, bias_out, gain_two, shift_two, bias_down) = (
+    gain_one, _, _, _, bias_out, gain_two, shift_two, bias_down = (
         vector_rows[:, k * each : (k + 1) * each].reshape(1, model_width) for k in range(8)
     )
     up_each = up_bias.shape[0] // 128
     bias_up = vector_rows[:, 8 * each : 8 * each + up_each].reshape(1, up_bias.shape[0] * dp_count)
 
-    def heads_of(vector):
-        return lax.dynamic_slice_in_dim(vector, mp_index * head_width, head_width, 1)
-
-    unit_one, _ = unit_rows(rows_in.astype(jnp.float32))
-    rows_one = (unit_one * gain_one + shift_one).astype(jnp.bfloat16)
-
-    def project(weight, bias):
-        return (jnp.dot(rows_one, weight, preferred_element_type=jnp.float32) + bias).astype(jnp.bfloat16)
-
-    key_rows = project(key_all, 0.0)
-    value_rows = project(value_all, heads_of(bias_value))
-    queries = project(query_all, heads_of(bias_query))
-    head_queries, head_keys, head_values = to_heads([queries], [key_rows, value_rows], heads_local, members, 1)
-    head_mix, exact_mix, log_total = attend(head_queries, head_keys, head_values, *plan, members, blocks_each)
+    branch_rows_two = whole_rows(branch_two)
+    head_mix, exact_mix, log_total = attend(head_queries, head_shared, *plan, members, blocks_each)
     (attended_low,) = to_rows([head_mix], [], heads_local, members, 2)
     out_part = contract_last(attended_low, out_all).astype(jnp.bfloat16)
-    residual, rows_two = reduce_norm_gather(out_part, hidden_in, bias_out, gain_two, shift_two, 3)
-
-    up_all = lax.all_gather(up_weight, "dp", axis=0, tiled=True)
-    down_all = lax.all_gather(down_weight, "dp", axis=0, tiled=True)
-    branch_two = jnp.where(own_valid[:, None], output_grad, 0).astype(jnp.bfloat16)
-    branch_rows_two = whole_rows(branch_two)
+    residual, rows_two, up_all, down_all = reduce_norm_gather(
+        out_part, hidden_in, bias_out, gain_two, shift_two, (up_weight, down_weight), 3
+    )
 
     bias_hidden = lax.dynamic_slice_in_dim(bias_up, mp_index * hidden_width, hidden_width, 1)
     pre_act = jnp.dot(rows_two, up_all, preferred_element_type=jnp.float32) + bias_hidden
@@ -1024,18 +1291,19 @@
     hidden_grad = jnp.dot(branch_rows_two, down_all, preferred_element_type=jnp.float32)
     pre_grad = jax.vjp(gelu_exact, pre_act)[1](hidden_grad)[0].astype(jnp.bfloat16)
     up_part = contract_last(pre_grad, up_all).astype(jnp.bfloat16)
+    down_weight_grad = owner_share(contract_first(branch_rows_two, hidden_low))
+    up_weight_grad = owner_share(contract_first(rows_two, pre_grad))
     residual_grad, sums_two, branch_rows_one = reduce_back_gather(up_part, residual, branch_two, gain_two, 4)
 
+    hidden_low, branch_rows_one = lax.optimization_barrier((hidden_low, branch_rows_one))
     feed = row_share(contract_last(hidden_low, down_all))
     result = residual + feed + bias_down
-    output = jnp.where(own_valid[:, None], result, 0.0).astype(jnp.bfloat16)
-    down_weight_grad = owner_share(contract_first(branch_rows_two, hidden_low))
-    up_weight_grad = owner_share(contract_first(rows_two, pre_grad))
+    output = jnp.where(own_valid, result, 0.0).astype(jnp.bfloat16)
 
     attended_grad = jnp.dot(branch_rows_one, out_all, preferred_element_type=jnp.float32).astype(jnp.bfloat16)
     (head_grad,) = to_heads([attended_grad], [], heads_local, members, 5)
     head_query_grad, head_key_grad, head_value_grad = attend_back(
-        head_queries, head_keys, head_values, head_grad, exact_mix, log_total, *plan, members, blocks_each
+        head_queries, head_shared, head_grad, exact_mix, log_total, *plan, members, blocks_each
     )
     query_low, key_low, value_low = to_rows(
         [head_query_grad], [head_key_grad, head_value_grad], heads_local, members, 6

time: 931 us -> 858 us (0.922)
  Pallas kernels: 683 us -> 630 us
  other arithmetic: 35.4 us -> 21.2 us
    pallas_call x2 -> x1, Pallas kernels: 54.2 us -> 15.8 us  [to_heads(): pl.pallas_call(kernel, out_shape=shapes, in_specs=[ANY] * count, out_spec...]
    pallas_call x1, Pallas kernels: 144 us -> 118 us  [reduce_back_gather(): pl.pallas_call(kernel, out_shape=[jax.ShapeDtypeStruct((rows, width), jnp...]
    pallas_call x1, Pallas kernels: 84.6 us -> 102 us  [project_first(): pl.pallas_call(kernel, out_shape=[jax.ShapeDtypeStruct((group_rows, width...]
    pallas_call x1, Pallas kernels: 56.1 us -> 42 us  [attend(): pl.pallas_call(kernel, out_shape=[jax.ShapeDtypeStruct(queries.shape, jnp...]
    pallas_call x2, Pallas kernels: 65.1 us -> 75.9 us  [to_rows(): pl.pallas_call(kernel, out_shape=[jax.ShapeDtypeStruct((rows, heads * HEA...]
    pallas_call x1, Pallas kernels: 58.7 us -> 48.8 us  [attend_back(): pl.pallas_call(kernel, out_shape=[jax.ShapeDtypeStruct(queries.shape, jnp...]
    dot_general x3 -> x0, matrix products: 9.91 us -> none  [project(): jnp.dot(rows_one, weight, preferred_element_type=jnp.float32) + bias]
    unnamed x67 -> x57, local copies, waits for them, and re-layouts: 18.4 us -> 23.2 us
  transfers between devices with their start and end apart: 6 -> 4, of which waited for: 0 -> 0; matrix products, arithmetic and copies ran while one was open for 16% -> 13% of each run, Pallas kernels for 74% -> 48%
where the time goes in v4:
time: 858 us; the launch traced here: 853 us
  Pallas kernels  630 us (73%)
  matrix products  151 us (18%)
  local copies, waits for them, and re-layouts  36.2 us (4%)
  other arithmetic  21.2 us (2%)
  between operations  14.5 us (2%)
    pallas_call x1, Pallas kernels, reduce_norm_gather(): pl.pallas_call(kernel, out_shape=[jax.ShapeDtypeStruct((rows, width), jnp...  127 us
    pallas_call x1, Pallas kernels, reduce_back_gather(): pl.pallas_call(kernel, out_shape=[jax.ShapeDtypeStruct((rows, width), jnp...  118 us
    pallas_call x1, Pallas kernels, project_first(): pl.pallas_call(kernel, out_shape=[jax.ShapeDtypeStruct((group_rows, width...  102 us
    pallas_call x1, Pallas kernels, reduce_last(): pl.pallas_call(kernel, out_shape=[jax.ShapeDtypeStruct((rows, width), jnp...  87.6 us
    pallas_call x2, Pallas kernels, to_rows(): pl.pallas_call(kernel, out_shape=[jax.ShapeDtypeStruct((rows, heads * HEA...  75.9 us
    dot_general x6, matrix products, contract_last(): lax.dot_general(left, right, (((1,), (1,)), ((), ())), preferred_element_...  52.8 us
    pallas_call x1, Pallas kernels, attend_back(): pl.pallas_call(kernel, out_shape=[jax.ShapeDtypeStruct(queries.shape, jnp...  48.8 us
    dot_general x6, matrix products, contract_first(): lax.dot_general(left, right, (((0,), (0,)), ((), ())), preferred_element_...  43.6 us
  transfers between devices with their start and end apart: 4, of which 0 were waited for; matrix products, arithmetic and copies ran while one was open for 13% of the time, Pallas kernels for 48%

profile of v4, /device:TPU:0, one launch (start us, length us, event | category | flops | bytes accessed | tf_op | source)
XLA Modules:
  0.0 852.9 jit_solution(4445421977888562481)
XLA Ops:
  13.2 1.2 copy-done
  14.4 1.2 copy-done.10
  15.6 0.9 copy-done.11
  16.6 0.9 copy-done.12
  17.5 0.9 copy-done.13
  18.5 0.9 copy-done.14
  20.8 102.2 %shard_map.323 = (bf16[1024,2048]{1,0:T(8,128)(2,1)}, f32[192,128]{1,0:T(8,128)S(1)}, bf16[3,2048,512]{2,1,0:T(8,128)(2,1)}, bf16[2048,512]{1,0:T(8,128)(2,1)}, ...) custom-call(s32[8]{0:T(128)S(1)} %copy-done.16, ...), custom_call_target="tpu_custom_call" | custom-call | flops 8589934592 | bytes 262144000 | tf_op jit(solution)/shard_map/pallas_call | solution.py:920
  123.9 42.0 %shard_map.324 = (bf16[4096,128]{1,0:T(8,128)(2,1)}, f32[16,128,256]{2,1,0:T(8,128)}, f32[16,1,256]{2,1,0:T(1,128)}) custom-call(s32[8]{0:T(128)} %lengths_ref.5, s32[64]{0:T(128)} %slot_ref.3, bf16[4096,128]{1,0:T(8,128)(2,1)} %copy-done.17, bf16[2,8192,128]{2,1,0:T(8,128)(2,1)} %get-tuple-element.51.shared_ref), custom_call_target="tpu_custom_call" | custom-call | flops 8589934592 | bytes 52428800 | tf_op jit(solution)/shard_map/pallas_call | solution.py:361
  165.9 1.2 copy-done.7
  167.1 16.6 %shard_map.325 = bf16[1024,512]{1,0:T(8,128)(2,1)S(1)} custom-call(bf16[4096,128]{1,0:T(8,128)(2,1)S(1)} %copy-done.7), custom_call_target="tpu_custom_call" | custom-call | bytes 104857600 | tf_op jit(solution)/shard_map/pallas_call | solution.py:230
  184.4 5.9 convolution_convert_fusion.4.part_ref
  190.3 1.2 copy-done.8
  191.5 1.2 copy-done.9
  192.8 127.3 %shard_map.326 = (f32[256,2048]{1,0:T(8,128)S(1)}, bf16[1024,2048]{1,0:T(8,128)(2,1)}, bf16[2048,2048]{1,0:T(8,128)(2,1)}, bf16[2048,2048]{1,0:T(8,128)(2,1)}) custom-call(bf16[1024,2048]{1,0:T(8,128)(2,1)} %convolution_convert_fusion.4.part_ref, bf16[256,2048]{1,0:T(8,128)(2,1)S(1)} %copy-done.1, f32[1,2048]{1,0:T(1,128)S(1)} %bitcast.76, ...), custom_call_target="tpu_custom_call" | custom-call | bytes 314572800 | tf_op jit(solution)/shard_map/pallas_call | solution.py:1007
  320.1 14.5 %fusion.19 = f32[1024,2048]{1,0:T(8,128)} fusion(bf16[1024,2048]{1,0:T(8,128)(2,1)} %get-tuple-element.56, bf16[2048,2048]{1,0:T(8,128)(2,1)} %get-tuple-element.57), kind=kOutput, calls=%fused_computation.56 | convolution fusion | flops 8589934592 | bytes 20971520 | tf_op jit(solution)/shard_map/dot_general | solution.py:1289
  334.6 33.5 %convert_reduce_fusion = (f32[2048]{0:T(1024)}, bf16[1024,2048]{1,0:T(8,128)(2,1)S(1)}, f32[1024,2048]{1,0:T(8,128)}) fusion(f32[1024,2048]{1,0:T(8,128)} %fusion.19, f32[2048]{0:T(1024)S(1)} %bitcast.82, bf16[1024,2048]{1,0:T(8,128)(2,1)} %all-gather.2.cloned.1.call-done, bf16[2048,2048]{1,0:T(8,128)(2,1)} %get-tuple-element.59), kind=kOutput, calls=%fused_computation.2 | convolution fusion | flops 8747218944 | bytes 33570816 | tf_op jit(solution)/shard_map/dot_general | solution.py:1291
  368.1 10.8 %convolution_convert_fusion.3.part_ref = bf16[1024,2048]{1,0:T(8,128)(2,1)} fusion(bf16[1024,2048]{1,0:T(8,128)(2,1)S(1)} %get-tuple-element.82, bf16[2048,2048]{1,0:T(8,128)(2,1)S(1)} %copy-done.22), kind=kOutput, calls=%fused_computation.22 | convolution fusion | flops 8592031744 | bytes 16777216 | tf_op jit(solution)/shard_map/dot_general | solution.py:36
  378.9 10.0 %multiply_convert_fusion = bf16[1024,2048]{1,0:T(8,128)(2,1)} fusion(f32[1024,2048]{1,0:T(8,128)} %get-tuple-element.83, f32[1024,2048]{1,0:T(8,128)} %fusion.19, f32[2048]{0:T(1024)S(1)} %bitcast.83), kind=kLoop, calls=%fused_computation.5 | loop fusion | flops 8388608 | bytes 20979712 | tf_op jit(solution)/shard_map/convert_element_type | solution.py:1290
  388.8 117.8 %shard_map.327 = (f32[256,2048]{1,0:T(8,128)S(1)}, f32[8,2048]{1,0:T(8,128)S(1)}, bf16[1024,2048]{1,0:T(8,128)(2,1)}) custom-call(bf16[1024,2048]{1,0:T(8,128)(2,1)} %convolution_convert_fusion.3.part_ref, f32[256,2048]{1,0:T(8,128)S(1)} %get-tuple-element.55.residual_ref, bf16[256,2048]{1,0:T(8,128)(2,1)} %get-tuple-element.58.branch_ref, ...), custom_call_target="tpu_custom_call" | custom-call | bytes 314572800 | tf_op jit(solution)/shard_map/pallas_call | solution.py:1073
  506.6 1.3 copy-done.2
  507.9 13.9 %convolution_convert_fusion.2 = bf16[1024,2048]{1,0:T(8,128)(2,1)} fusion(bf16[1024,2048]{1,0:T(8,128)(2,1)} %multiply_convert_fusion, bf16[2048,2048]{1,0:T(8,128)(2,1)} %get-tuple-element.59), kind=kOutput, calls=%fused_computation.21 | convolution fusion | flops 8592031744 | bytes 16777216 | tf_op jit(solution)/shard_map/dot_general | solution.py:36
  521.9 14.3 %convolution_convert_fusion = bf16[2048,2048]{1,0:T(8,128)(2,1)} fusion(bf16[1024,2048]{1,0:T(8,128)(2,1)} %all-gather.2.cloned.1.call-done, bf16[1024,2048]{1,0:T(8,128)(2,1)} %multiply_convert_fusion), kind=kOutput, calls=%fused_computation.19 | convolution fusion | flops 8594128896 | bytes 16777216 | tf_op jit(solution)/shard_map/dot_general | solution.py:42
  536.2 14.0 %convolution_convert_fusion.1 = bf16[2048,2048]{1,0:T(8,128)(2,1)} fusion(bf16[1024,2048]{1,0:T(8,128)(2,1)} %get-tuple-element.56, bf16[1024,2048]{1,0:T(8,128)(2,1)} %copy-done.25), kind=kOutput, calls=%fused_computation.20 | convolution fusion | flops 8594128896 | bytes 16777216 | tf_op jit(solution)/shard_map/dot_general | solution.py:42
  550.4 1.4 convert_reduce_fusion.1
  551.8 6.2 convolution_convert_fusion.9.refs_0_
  558.0 15.8 %shard_map.328.g_ref = bf16[4096,128]{1,0:T(8,128)(2,1)} custom-call(bf16[1024,512]{1,0:T(8,128)(2,1)} %convolution_convert_fusion.9.refs_0_), custom_call_target="tpu_custom_call" | custom-call | bytes 104857600 | tf_op jit(solution)/shard_map/pallas_call | solution.py:137
  573.7 48.8 %shard_map.329 = (bf16[4096,128]{1,0:T(8,128)(2,1)}, bf16[8192,128]{1,0:T(8,128)(2,1)}, bf16[8192,128]{1,0:T(8,128)(2,1)}) custom-call(s32[8]{0:T(128)} %lengths_ref.5, s32[64]{0:T(128)} %slot_ref.3, bf16[4096,128]{1,0:T(8,128)(2,1)} %copy-done.17, bf16[2,8192,128]{2,1,0:T(8,128)(2,1)} %get-tuple-element.51.shared_ref, bf16[4096,128]{1,0:T(8,128)(2,1)} %shard_map.328.g_ref, ...), custom_call_target="tpu_custom_call" | custom-call | flops 21474836480 | bytes 104857600 | tf_op jit(solution)/shard_map/pallas_call | solution.py:439
  622.5 1.2 copy-done.3
  623.8 59.4 %shard_map.330 = (bf16[1024,512]{1,0:T(8,128)(2,1)S(1)}, bf16[1024,512]{1,0:T(8,128)(2,1)S(1)}, bf16[1024,512]{1,0:T(8,128)(2,1)S(1)}) custom-call(bf16[4096,128]{1,0:T(8,128)(2,1)S(1)} %copy-done.3, bf16[8192,128]{1,0:T(8,128)(2,1)} %get-tuple-element.66.refs_1_, bf16[8192,128]{1,0:T(8,128)(2,1)} %get-tuple-element.67.refs_2_), custom_call_target="tpu_custom_call" | custom-call | bytes 104857600 | tf_op jit(solution)/shard_map/pallas_call | solution.py:230
  683.2 4.3 fusion.9
  687.5 7.4 fusion.7
  694.9 3.8 convolution_convert_fusion.5.refs_7_
  698.7 3.8 convolution_convert_fusion.7.refs_5_
  702.5 3.8 convolution_convert_fusion.8.refs_4_
  706.2 4.0 convolution_convert_fusion.6.refs_6_
  710.3 10.4 %add_convert_fusion.refs_0_ = bf16[1024,2048]{1,0:T(8,128)(2,1)} fusion(f32[1024,2048]{1,0:T(8,128)S(1)} %fusion.9, f32[1024,2048]{1,0:T(8,128)} %fusion.7, bf16[1024,512]{1,0:T(8,128)(2,1)S(1)} %get-tuple-element.71, bf16[3,2048,512]{2,1,0:T(8,128)(2,1)} %get-tuple-element.69), kind=kOutput, calls=%fused_computation.3 | convolution fusion | flops 2153775104 | bytes 24117248 | tf_op jit(solution)/shard_map/dot_general | solution.py:36
  720.7 87.6 %shard_map.331 = (f32[256,2048]{1,0:T(8,128)}, f32[8,2048]{1,0:T(8,128)}, f32[256,512]{1,0:T(8,128)}, f32[256,512]{1,0:T(8,128)}, f32[256,512]{1,0:T(8,128)}, /*index=5*/f32[256,512]{1,0:T(8,128)}) custom-call(bf16[1024,2048]{1,0:T(8,128)(2,1)} %add_convert_fusion.refs_0_, f32[256,2048]{1,0:T(8,128)} %copy-done.2, bf16[256,2048]{1,0:T(8,128)(2,1)} %refs_2_.1, ...), custom_call_target="tpu_custom_call" | custom-call | bytes 314572800 | tf_op jit(solution)/shard_map/pallas_call | solution.py:1169
  808.7 1.6 convert_reduce_fusion.2
  811.7 1.9 concatenate.3.in_ref
  813.6 12.9 %shard_map.332 = f32[24,128]{1,0:T(8,128)} custom-call(f32[8,24,128]{2,1,0:T(8,128)} %concatenate.3.in_ref), custom_call_target="tpu_custom_call" | custom-call | bytes 20971520 | tf_op jit(solution)/shard_map/pallas_call | solution.py:1217
  826.5 1.3 slice_bitcast_fusion
  827.8 1.4 slice_bitcast_fusion.1
  829.3 2.6 select_convert_fusion
  831.9 2.8 convert_element_type.83
  834.7 2.8 convert_element_type.81
  837.5 3.1 copy.45
  840.6 1.9 copy.46
  842.5 1.9 copy.47
  (76 shorter events, 12.6 us)
Async XLA Ops:
  7.2 327.4 %all-gather.2.cloned.1.call-start = ((), (), s32[]{:S(2)}) async-start(), calls=%async_computation.3 | async-start | bytes 5242880 | tf_op jit(solution)/shard_map/all_gather | solution.py:48
  13.2 1.2 copy-start
  14.4 1.2 copy-start.10
  15.6 0.9 copy-start.11
  16.6 0.9 copy-start.12
  17.5 0.9 copy-start.13
  18.5 0.9 copy-start.14
  19.4 0.7 copy-start.15
  20.1 0.7 copy-start.16
  123.0 1.0 copy-start.17
  123.0 706.3 %reduce-scatter.4.cloned.1.call-start = ((), (), s32[]{:S(2)}) async-start(), calls=%async_computation.4 | async-start | bytes 5242880 | tf_op jit(solution)/shard_map/reduce_scatter | solution.py:53
  165.9 1.2 copy-start.7
  167.1 23.2 %copy-start.1 = (bf16[256,2048]{1,0:T(8,128)(2,1)S(1)}, bf16[256,2048]{1,0:T(8,128)(2,1)}, u32[]{:S(2)}) copy-start(bf16[256,2048]{1,0:T(8,128)(2,1)} %refs_2_.1) | copy-start | bytes 3145732
  183.7 6.6 copy-start.4
  190.3 1.2 copy-start.8
  191.5 1.2 copy-start.9
  334.6 33.5 %copy-start.22 = (bf16[2048,2048]{1,0:T(8,128)(2,1)S(1)}, bf16[2048,2048]{1,0:T(8,128)(2,1)}, u32[]{:S(2)}) copy-start(bf16[2048,2048]{1,0:T(8,128)(2,1)} %get-tuple-element.57) | copy-start | bytes 25165828
  368.1 10.8 %copy-start.25 = (bf16[1024,2048]{1,0:T(8,128)(2,1)}, bf16[1024,2048]{1,0:T(8,128)(2,1)S(1)}, u32[]{:S(2)}) copy-start(bf16[1024,2048]{1,0:T(8,128)(2,1)S(1)} %get-tuple-element.82) | copy-start | bytes 12582916
  506.6 1.3 copy-start.2
  521.9 310.0 %reduce-scatter.8.cloned.1.call-start = ((), (), s32[]{:S(2)}) async-start(), calls=%async_computation.6 | async-start | bytes 9437184 | tf_op jit(solution)/shard_map/reduce_scatter | solution.py:58
  536.2 298.5 %reduce-scatter.6.cloned.1.call-start = ((), (), s32[]{:S(2)}) async-start(), calls=%async_computation.5 | async-start | bytes 9437184 | tf_op jit(solution)/shard_map/reduce_scatter | solution.py:58
  622.5 1.2 copy-start.3
  683.1 19.3 %copy-start.6 = (bf16[1024,512]{1,0:T(8,128)(2,1)}, bf16[1024,512]{1,0:T(8,128)(2,1)S(1)}, u32[]{:S(2)}) copy-start(bf16[1024,512]{1,0:T(8,128)(2,1)S(1)} %get-tuple-element.68) | copy-start | bytes 3145732
  687.5 7.4 copy-start.5
  687.5 7.4 copy-start.23
  694.9 3.8 copy-start.24
  720.7 87.6 %copy-start.21 = (f32[2048]{0:T(1024)S(1)}, f32[2048]{0:T(1024)}, u32[]{:S(2)}) copy-start(f32[2048]{0:T(1024)} %get-tuple-element.81) | copy-start | bytes 24580
  720.7 108.5 %copy-start.20 = (f32[8,2,128]{2,1,0:T(2,128)S(1)}, f32[8,2,128]{2,1,0:T(2,128)}, u32[]{:S(2)}) copy-start(f32[8,2,128]{2,1,0:T(2,128)} %get-tuple-element.85) | copy-start | bytes 24580
  829.3 15.1 %copy-start.19 = (f32[256,512]{1,0:T(8,128)S(1)}, f32[256,512]{1,0:T(8,128)}, u32[]{:S(2)}) copy-start(f32[256,512]{1,0:T(8,128)} %get-tuple-element.128) | copy-start | bytes 1572868
  829.3 15.9 %copy-start.18 = (f32[256,512]{1,0:T(8,128)S(1)}, f32[256,512]{1,0:T(8,128)}, u32[]{:S(2)}) copy-start(f32[256,512]{1,0:T(8,128)} %get-tuple-element.130) | copy-start | bytes 1572868
Sparse Core Ops, SparseCore 0:
  123.1 82.8 all-gather.1
  522.0 75.9 reduce-scatter.3
  601.8 94.3 reduce-scatter.7
  699.5 108.1 reduce-scatter.5

commit v5 on v4

--- a/solution.py
+++ b/solution.py
@@ -51,11 +51,6 @@
 def row_share(term):
     term = term.astype(jnp.bfloat16)
     return lax.psum_scatter(term, "mp", scatter_dimension=0, tiled=True).astype(jnp.float32)
-
-
-def owner_share(term):
-    term = term.astype(jnp.bfloat16)
-    return lax.psum_scatter(term, "dp", scatter_dimension=0, tiled=True).astype(jnp.float32)
 
 
 def greet(peers):
@@ -721,7 +716,7 @@
 
         def place(array, owner):
             if array < kinds:
-                return weights.at[array, pl.ds(pl.multiple_of(owner * depth, depth), depth)]
+                return weights.at[pl.ds(pl.multiple_of(owner * depth, depth), depth), pl.ds(array * columns, columns)]
             if array == kinds:
                 return all_out.at[pl.ds(pl.multiple_of(owner * depth, depth), depth)]
             return all_vectors.at[pl.ds(pl.multiple_of(owner * slab, slab), slab)]
@@ -815,7 +810,8 @@
         def project(tile, block):
             kind, half = tile // halves, tile % halves
             span = pl.ds(pl.multiple_of(half * 256, 256), 256)
-            value = jnp.dot(normed[block_span(block)], weights[kind, :, span], preferred_element_type=jnp.float32)
+            across = pl.ds(pl.multiple_of(kind * columns + half * 256, 256), 256)
+            value = jnp.dot(normed[block_span(block)], weights[:, across], preferred_element_type=jnp.float32)
             value = (value + biases[pl.ds(kind, 1), span]).astype(stage.dtype)
             for h in range(2):
                 head = 2 * half + h
@@ -922,7 +918,7 @@
         out_shape=[
             jax.ShapeDtypeStruct((group_rows, width), bf16),
             jax.ShapeDtypeStruct((dp_count * slab, 128), f32),
-            jax.ShapeDtypeStruct((kinds, width, columns), bf16),
+            jax.ShapeDtypeStruct((width, kinds * columns), bf16),
             jax.ShapeDtypeStruct((width, columns), bf16),
             jax.ShapeDtypeStruct((2, dp_count * group_rows, HEAD_DIM), bf16),
             jax.ShapeDtypeStruct((heads * group_rows, HEAD_DIM), bf16),
@@ -1022,23 +1018,73 @@
     )(part, hidden, out_bias, gain, shift, *shards)
 
 
-def reduce_back_gather(part, residual, branch_two, gain, collective_id):
-    mp_count = lax.axis_size("mp")
+def reduce_back_gather(part, residual, branch_two, gain, pairs, collective_id):
+    dp_count, mp_count = lax.axis_size("dp"), lax.axis_size("mp")
+    chips, count = dp_count // 2, len(pairs)
     rows, width = residual.shape
     pieces = pieces_of(rows)
-    size = rows // pieces
-
-    def kernel(part_ref, residual_ref, branch_ref, gain_ref, grad_ref, sums_ref, full_ref,
-               total, low, flows, red_send, red_recv, line_send, line_recv, own_sem):
+    size, depth = rows // pieces, width // dp_count
+    units = pairs[0][1].shape[1]
+    turns = pieces + 2 * SKEW * (mp_count - 1)
+    each = dp_count // 4
+    busy = count * dp_count // each
+    assert 1 + busy <= turns
+
+    def kernel(part_ref, residual_ref, branch_ref, gain_ref, *refs):
+        operands, refs = refs[: 2 * count], refs[2 * count :]
+        (grad_ref, sums_ref, full_ref), terms, refs = refs[:3], refs[3 : 3 + count], refs[3 + count :]
+        loaded, refs = refs[: 2 * count], refs[2 * count :]
+        (total, low, kept, slices, from_partner, chip_sum, load_sem, keep_sem, pair_send, pair_recv, cross_send, cross_recv,
+         flows, red_send, red_recv, line_send, line_recv, own_sem) = refs
         dp, mp = lax.axis_index("dp"), lax.axis_index("mp")
-        greet_all([], dp, mp, mp_count)
+        partner = (dp ^ 1, mp)
+        greet_all([(dp ^ (2 * o), mp) for o in range(1, chips)] + [partner], dp, mp, mp_count)
         reduce = LineReduce(part_ref, flows, rows, pieces, red_send, red_recv, dp, mp, mp_count)
         gather = LineGather(low, full_ref, rows, pieces, line_send, line_recv, dp, mp, mp_count)
         for piece in range(AHEAD):
             reduce.begin(piece)
+        loads = [pltpu.make_async_copy(operands[k], loaded[k], load_sem.at[k]) for k in range(2 * count)]
+        for copy in loads:
+            copy.start()
         sums_ref[...] = jnp.zeros_like(sums_ref)
 
-        @pl.loop(0, pieces + 2 * SKEW * (mp_count - 1))
+        def pair(mat, o):
+            return remote(slices.at[o], from_partner.at[mat, o], pair_send.at[mat, o], pair_recv.at[mat, o], partner)
+
+        def cross(mat, o, peer):
+            return remote(chip_sum.at[mat, o - 1], terms[mat].at[o], cross_send.at[mat, o], cross_recv.at[mat, o],
+                          (peer, mp))
+
+        def weight_slice(mat, index):
+            o = (index + 1) % chips
+            mine = index >= chips
+            owner = dp ^ (2 * o) ^ jnp.where(mine, 0, 1)
+            left = loaded[2 * mat][:, pl.ds(pl.multiple_of(owner * depth, depth), depth)]
+            value = contract_first(left, loaded[2 * mat + 1][...])
+
+            @pl.when(jnp.logical_not(mine))
+            def _():
+                if mat:
+                    pair(mat - 1, o).wait_send()
+                slices[o] = value.astype(slices.dtype)
+                pair(mat, o).start()
+
+            @pl.when(mine)
+            def _():
+                pair(mat, o).wait_recv()
+                both = (value + from_partner[mat, o].astype(jnp.float32)).astype(slices.dtype)
+
+                @pl.when(o == 0)
+                def _():
+                    kept[mat] = both
+                    pltpu.make_async_copy(kept.at[mat], terms[mat].at[0], keep_sem.at[mat]).start()
+
+                @pl.when(o != 0)
+                def _():
+                    chip_sum[mat, o - 1] = both
+                    cross(mat, o, owner).start()
+
+        @pl.loop(0, turns)
         def _(turn):
             reduce.begin(jnp.minimum(turn + AHEAD, pieces - 1), turn + AHEAD < pieces)
             reduce.advance(turn)
@@ -1063,85 +1109,227 @@
             for step in range(1, mp_count):
                 late = done - SKEW * step
                 gather.advance(step, jnp.clip(late, 0, pieces - 1), (late >= 0) & (late < pieces))
+            for mat in range(count):
+
+                @pl.when(turn == 1 + mat * busy // count)
+                def _():
+                    for copy in loads[2 * mat : 2 * mat + 2]:
+                        copy.wait()
+
+                first = turn - 1 - mat * busy // count
+
+                @pl.when((first >= 0) & (first < busy // count))
+                def _():
+                    for i in range(each):
+                        weight_slice(mat, first * each + i)
 
         own = pltpu.make_async_copy(low, full_ref.at[pl.ds(pl.multiple_of(mp * rows, rows), rows)], own_sem)
         own.start()
         reduce.finish()
         gather.finish()
         own.wait()
-
+        for mat in range(count):
+            pltpu.make_async_copy(kept.at[mat], terms[mat].at[0], keep_sem.at[mat]).wait()
+            for o in range(chips):
+                if mat == count - 1:
+                    pair(mat, o).wait_send()
+                if o:
+                    cross(mat, o, dp ^ (2 * o)).wait()
+
+    bf16, f32 = jnp.bfloat16, jnp.float32
+    dma = pltpu.SemaphoreType.DMA
+    flat = [array for two in pairs for array in two]
     return pl.pallas_call(
         kernel,
         out_shape=[
-            jax.ShapeDtypeStruct((rows, width), jnp.float32),
-            jax.ShapeDtypeStruct((8, width), jnp.float32),
-            jax.ShapeDtypeStruct((mp_count * rows, width), jnp.bfloat16),
-        ],
-        in_specs=[VMEM] * 4,
-        out_specs=[VMEM, VMEM, ANY],
-        scratch_shapes=[pltpu.VMEM((size, width), jnp.float32), pltpu.VMEM((rows, width), jnp.bfloat16)]
+            jax.ShapeDtypeStruct((rows, width), f32),
+            jax.ShapeDtypeStruct((8, width), f32),
+            jax.ShapeDtypeStruct((mp_count * rows, width), bf16),
+        ]
+        + [jax.ShapeDtypeStruct((chips, depth, units), bf16)] * count,
+        in_specs=[VMEM] * 4 + [ANY] * (2 * count),
+        out_specs=[VMEM, VMEM] + [ANY] * (1 + count),
+        scratch_shapes=[pltpu.VMEM(a.shape, a.dtype) for a in flat]
+        + [
+            pltpu.VMEM((size, width), f32),
+            pltpu.VMEM((rows, width), bf16),
+            pltpu.VMEM((count, depth, units), bf16),
+            pltpu.VMEM((chips, depth, units), bf16),
+            pltpu.VMEM((count, chips, depth, units), bf16),
+            pltpu.VMEM((count, chips - 1, depth, units), bf16),
+            dma((2 * count,)), dma((count,)),
+        ]
+        + [dma((count, chips)) for _ in range(4)]
         + LineReduce.scratch(mp_count, rows, width, pieces) + LineGather.semaphores(mp_count, pieces)
-        + [pltpu.SemaphoreType.DMA(())],
+        + [dma(())],
         compiler_params=pltpu.CompilerParams(
-            collective_id=collective_id, has_side_effects=True, vmem_limit_bytes=48 * MIB),
-        cost_estimate=pl.CostEstimate(flops=0, bytes_accessed=300 * MIB, transcendentals=0),
-    )(part, residual, branch_two, gain)
-
-
-def reduce_last(part, residual_grad, hidden, gain, weight_parts, collective_id):
+            collective_id=collective_id, has_side_effects=True, vmem_limit_bytes=63 * MIB),
+        cost_estimate=pl.CostEstimate(flops=40 << 30, bytes_accessed=300 * MIB, transcendentals=0),
+    )(part, residual, branch_two, gain, *flat)
+
+
+QUARTERS = 4
+
+
+def finish_back(query_grad, key_part, value_part, weights, normed, residual_grad, hidden, gain, out_part, heads, members,
+                collective_id):
+    rows, width = hidden.shape
     dp_count, mp_count = lax.axis_size("dp"), lax.axis_size("mp")
-    chips = dp_count // 2
-    rows, width = hidden.shape
-    pieces = pieces_of(rows)
-    size = rows // pieces
-    count = len(weight_parts)
-    depth, columns = weight_parts[0].shape[0] // dp_count, weight_parts[0].shape[1]
-
-    def kernel(*refs):
-        part_ref, residual_ref, hidden_ref, gain_ref = refs[:4]
-        weights = refs[4 : 4 + count]
-        grad_ref, sums_ref = refs[4 + count : 6 + count]
-        outs = refs[6 + count : 6 + 2 * count]
-        (total, flows, red_send, red_recv, from_partner, chip_sum, from_chips,
-         pair_send, pair_recv, send_sem, recv_sem) = refs[6 + 2 * count :]
+    chips, pieces = dp_count // 2, pieces_of(rows)
+    size, depth, columns = rows // pieces, width // dp_count, heads * HEAD_DIM
+    kinds, quarter = 3, rows // QUARTERS
+    per_quarter = pieces // QUARTERS
+    slice_rows = width // per_quarter
+    turns = pieces + SKEW * (mp_count - 1)
+    slices_each = max(dp_count // 8, 1)
+    slice_turn = turns // 3
+    group_rows = mp_count * rows
+    offsets = sorted({2 * o for o in range(1, chips)} | {o for o in range(1, members)} | {o * members for o in range(1, heads)})
+    query_grad = query_grad.reshape(heads, mp_count, rows, HEAD_DIM)
+    shared = [v.reshape(dp_count, mp_count, rows, HEAD_DIM) for v in (key_part, value_part)]
+
+    def kernel(query_ref, key_ref, value_ref, weights_hbm, normed_hbm, residual_ref, hidden_ref, gain_ref, out_ref,
+               grad_ref, sums_ref, weight_grad_ref, out_grad_ref, column_ref,
+               weights, normed, landed, own, parts, stage, part, total, flows, red_send, red_recv,
+               slices, from_partner, chip_sum, from_chips, out_partner, out_sum, out_chips,
+               load_sem, own_sem, part_send, part_recv, local_sem, head_send, head_recv,
+               pair_send, pair_recv, cross_send, cross_recv):
         dp, mp = lax.axis_index("dp"), lax.axis_index("mp")
-        peers = [(dp ^ (2 * o), mp) for o in range(1, chips)]
+        group, member = dp // members, dp % members
         partner = (dp ^ 1, mp)
-        greet_all(peers + [partner], dp, mp, mp_count)
-        reduce = LineReduce(part_ref, flows, rows, pieces, red_send, red_recv, dp, mp, mp_count)
-        for piece in range(AHEAD):
-            reduce.begin(piece)
-
-        def piece_of(weight, owner):
-            return weights[weight].at[pl.ds(pl.multiple_of(owner * depth, depth), depth)]
-
-        def pair(weight, o):
-            return remote(piece_of(weight, dp ^ (2 * o) ^ 1), from_partner.at[weight, o],
-                          pair_send.at[weight, o], pair_recv.at[weight, o], partner)
-
-        def cross(weight, o):
-            return remote(chip_sum.at[weight, o], from_chips.at[weight, o - 1],
-                          send_sem.at[weight, o], recv_sem.at[weight, o], peers[o - 1])
-
-        order = list(range(1, chips)) + [0]
-        for w in range(count):
-            for o in order:
-                pair(w, o).start()
-        for w in range(count):
-            for o in order:
-                pair(w, o).wait_recv()
-                value = piece_of(w, dp ^ (2 * o))[...].astype(jnp.float32)
-                value = value + from_partner[w, o].astype(jnp.float32)
-                if o:
-                    chip_sum[w, o] = value.astype(chip_sum.dtype)
-                    cross(w, o).start()
-                else:
-                    outs[w][...] = value
+        greet_all([(dp ^ o, mp) for o in offsets], dp, mp, mp_count)
+        reduce = LineReduce(part, flows, rows, pieces, red_send, red_recv, dp, mp, mp_count)
+        loads = [pltpu.make_async_copy(weights_hbm, weights, load_sem.at[0]),
+                 pltpu.make_async_copy(normed_hbm, normed, load_sem.at[1])]
+        shared_refs = (key_ref, value_ref)
+
+        def rows_of(k):
+            return pl.ds(k * quarter, quarter)
+
+        def lane_span(kind, head):
+            return pl.ds(pl.multiple_of(kind * columns + head * HEAD_DIM, HEAD_DIM), HEAD_DIM)
+
+        def landing(kind, k, head):
+            return landed.at[:, rows_of(k), lane_span(kind, head)]
+
+        def own_copy(kind, o):
+            return pltpu.make_async_copy(shared_refs[kind].at[(group ^ o) * members + member], own.at[kind, o],
+                                         own_sem.at[kind, o])
+
+        def part_copy(kind, o, p, k):
+            return remote(shared_refs[kind].at[(group ^ o) * members + (member ^ p), :, rows_of(k)],
+                          parts.at[kind, o, p - 1, :, rows_of(k)], part_send.at[kind, o, p - 1, k],
+                          part_recv.at[kind, o, p - 1, k], (group * members + (member ^ p), mp))
+
+        def head_copy(kind, o, k):
+            source = query_ref.at[group ^ o, :, rows_of(k)] if kind == 2 else stage.at[kind, o, :, rows_of(k)]
+            return remote(source, landing(kind, k, group), head_send.at[kind, o, k], head_recv.at[kind, o, k],
+                          ((group ^ o) * members + member, mp))
+
+        def local_copy(k):
+            return pltpu.make_async_copy(query_ref.at[group, :, rows_of(k)], landing(2, k, group), local_sem.at[k])
+
+        for k in range(QUARTERS):
+            for kind in range(2):
+                for o in range(heads):
+                    for p in range(1, members):
+                        part_copy(kind, o, p, k).start()
+            if k == 0:
+                for kind in range(2):
+                    for o in range(heads):
+                        own_copy(kind, o).start()
+                for copy in loads:
+                    copy.start()
+            for o in range(1, heads):
+                head_copy(2, o, k).start()
+            local_copy(k).start()
+        for k in range(QUARTERS):
+            for kind in range(2):
+                for o in list(range(1, heads)) + [0]:
+                    if k == 0:
+                        own_copy(kind, o).wait()
+                    value = own[kind, o, :, k * quarter : (k + 1) * quarter].astype(jnp.float32)
+                    for p in range(1, members):
+                        part_copy(kind, o, p, k).wait_recv()
+                        value = value + parts[kind, o, p - 1, :, k * quarter : (k + 1) * quarter].astype(jnp.float32)
+                    if o:
+                        stage[kind, o, :, k * quarter : (k + 1) * quarter] = value.astype(stage.dtype)
+                        head_copy(kind, o, k).start()
+                    else:
+                        landed[:, k * quarter : (k + 1) * quarter, lane_span(kind, group)] = value.astype(landed.dtype)
+
+        def arrived(k):
+            for kind in range(kinds):
+                for o in range(1, heads):
+                    head_copy(kind, o, k).wait_recv()
+            local_copy(k).wait()
+
+        def project(k, first, count):
+            span = pl.ds(pl.multiple_of(k * quarter, quarter), quarter)
+            left = landed[:, span].reshape(mp_count * quarter, kinds * columns)
+            features = pl.ds(pl.multiple_of(first, count), count)
+            value = contract_last(left, weights[features]).astype(part.dtype)
+            for block in range(mp_count):
+                at = pl.ds(pl.multiple_of(block * rows + k * quarter, quarter), quarter)
+                part[at, features] = value[block * quarter : (block + 1) * quarter]
+
+        def slab(owner):
+            return pl.ds(pl.multiple_of(owner * depth, depth), depth)
+
+        def pair(o):
+            return remote(slices.at[o], from_partner.at[o], pair_send.at[0, o], pair_recv.at[0, o], partner)
+
+        def cross(o, peer):
+            return remote(chip_sum.at[o], from_chips.at[o], cross_send.at[0, o], cross_recv.at[0, o], (peer, mp))
+
+        def out_pair(o):
+            return remote(out_ref.at[slab(dp ^ (2 * o) ^ 1)], out_partner.at[o], pair_send.at[1, o], pair_recv.at[1, o],
+                          partner)
+
+        def out_cross(o):
+            return remote(out_sum.at[o], out_chips.at[o], cross_send.at[1, o], cross_recv.at[1, o], (dp ^ (2 * o), mp))
+
+        def weight_slice(index):
+            o = (index + 1) % chips
+            mine = index >= chips
+            owner = dp ^ (2 * o) ^ jnp.where(mine, 0, 1)
+            rows_all = landed[...].reshape(group_rows, kinds * columns)
+            value = contract_first(normed[:, slab(owner)], rows_all)
+
+            @pl.when(jnp.logical_not(mine))
+            def _():
+                slices[o] = value.astype(slices.dtype)
+                pair(o).start()
+
+            @pl.when(mine)
+            def _():
+                pair(o).wait_recv()
+                both = value + from_partner[o].astype(jnp.float32)
+
+                @pl.when(o == 0)
+                def _():
+                    weight_grad_ref[...] = both
+
+                @pl.when(o != 0)
+                def _():
+                    chip_sum[o] = both.astype(chip_sum.dtype)
+                    cross(o, owner).start()
+
+        for copy in loads:
+            copy.wait()
+        arrived(0)
+        for part_index in range(per_quarter):
+            project(0, part_index * slice_rows, slice_rows)
+        for o in range(chips):
+            out_pair(o).start()
         sums_ref[...] = jnp.zeros_like(sums_ref)
 
-        @pl.loop(0, pieces + SKEW * (mp_count - 1))
+        @pl.loop(0, turns)
         def _(turn):
-            reduce.begin(jnp.minimum(turn + AHEAD, pieces - 1), turn + AHEAD < pieces)
+            @pl.when(turn < pieces)
+            def _():
+                reduce.begin(jnp.minimum(turn, pieces - 1))
+
             reduce.advance(turn)
             done = turn - SKEW * (mp_count - 1)
 
@@ -1156,31 +1344,91 @@
                 sums_ref[1:2] += jnp.sum(upstream, axis=0, keepdims=True)
                 grad_ref[span] = residual_ref[span] + norm_back(upstream, unit, inverse, gain_ref[...])
 
+            for k in range(1, QUARTERS):
+
+                @pl.when(turn == (k - 1) * per_quarter)
+                def _():
+                    arrived(k)
+
+            @pl.when(turn < (QUARTERS - 1) * per_quarter)
+            def _():
+                k, portion = turn // per_quarter + 1, turn % per_quarter
+                project(k, portion * slice_rows, slice_rows)
+
+            @pl.when(turn == slice_turn)
+            def _():
+                for o in list(range(1, chips)) + [0]:
+                    out_pair(o).wait_recv()
+                    value = out_ref[slab(dp ^ (2 * o))].astype(jnp.float32) + out_partner[o].astype(jnp.float32)
+                    if o:
+                        out_sum[o] = value.astype(out_sum.dtype)
+                        out_cross(o).start()
+                    else:
+                        out_grad_ref[...] = value
+
+            @pl.when((turn >= late_turn) & (turn < late_turn + dp_count // slices_each))
+            def _():
+                for i in range(slices_each):
+                    weight_slice((turn - late_turn) * slices_each + i)
+
         reduce.finish()
-        for w in range(count):
-            for o in range(1, chips):
-                cross(w, o).wait()
-                outs[w][...] += from_chips[w, o - 1].astype(jnp.float32)
-            for o in range(chips):
-                pair(w, o).wait_send()
-
+        column_ref[...] = jnp.zeros_like(column_ref)
+        column_ref[0:1] = jnp.sum(
+            landed[...].reshape(group_rows, kinds * columns).astype(jnp.float32), axis=0, keepdims=True)
+        for o in range(chips):
+            pair(o).wait_send()
+            out_pair(o).wait_send()
+            if o:
+                cross(o, dp ^ (2 * o)).wait()
+                weight_grad_ref[...] += from_chips[o].astype(jnp.float32)
+                out_cross(o).wait()
+                out_grad_ref[...] += out_chips[o].astype(jnp.float32)
+        for k in range(QUARTERS):
+            for o in range(heads):
+                for kind in range(2):
+                    for p in range(1, members):
+                        part_copy(kind, o, p, k).wait_send()
+                if o:
+                    for kind in range(kinds):
+                        head_copy(kind, o, k).wait_send()
+
+    late_turn = max(slice_turn, (QUARTERS - 2) * per_quarter + 1)
+    assert late_turn + dp_count // slices_each <= turns
     dma = pltpu.SemaphoreType.DMA
-    kind = weight_parts[0].dtype
+    bf16, f32 = jnp.bfloat16, jnp.float32
+    own_columns = out_part.shape[1]
     return pl.pallas_call(
         kernel,
-        out_shape=[jax.ShapeDtypeStruct((rows, width), jnp.float32), jax.ShapeDtypeStruct((8, width), jnp.float32)]
-        + [jax.ShapeDtypeStruct((depth, columns), jnp.float32)] * count,
-        in_specs=[VMEM] * (4 + count),
-        out_specs=[VMEM] * (2 + count),
-        scratch_shapes=[pltpu.VMEM((size, width), jnp.float32)]
+        out_shape=[
+            jax.ShapeDtypeStruct((rows, width), f32),
+            jax.ShapeDtypeStruct((8, width), f32),
+            jax.ShapeDtypeStruct((depth, kinds * columns), f32),
+            jax.ShapeDtypeStruct((depth, own_columns), f32),
+            jax.ShapeDtypeStruct((8, kinds * columns), f32),
+        ],
+        in_specs=[ANY] * 5 + [VMEM] * 4,
+        out_specs=[VMEM] * 5,
+        scratch_shapes=[
+            pltpu.VMEM((width, kinds * columns), bf16),
+            pltpu.VMEM((group_rows, width), bf16),
+            pltpu.VMEM((mp_count, rows, kinds * columns), bf16),
+            pltpu.VMEM((2, heads, mp_count, rows, HEAD_DIM), bf16),
+            pltpu.VMEM((2, heads, members - 1, mp_count, rows, HEAD_DIM), bf16),
+            pltpu.VMEM((2, heads, mp_count, rows, HEAD_DIM), bf16),
+            pltpu.VMEM((group_rows, width), bf16),
+            pltpu.VMEM((size, width), f32),
+        ]
         + LineReduce.scratch(mp_count, rows, width, pieces)
-        + [pltpu.VMEM((count, chips, depth, columns), kind), pltpu.VMEM((count, chips, depth, columns), kind),
-           pltpu.VMEM((count, chips - 1, depth, columns), kind)]
-        + [dma((count, chips)) for _ in range(4)],
+        + [pltpu.VMEM((chips, depth, kinds * columns), bf16) for _ in range(4)]
+        + [pltpu.VMEM((chips, depth, own_columns), bf16) for _ in range(3)]
+        + [dma((2,)), dma((2, heads))]
+        + [dma((2, heads, members - 1, QUARTERS)) for _ in range(2)]
+        + [dma((QUARTERS,)), dma((kinds, heads, QUARTERS)), dma((kinds, heads, QUARTERS))]
+        + [dma((2, chips)) for _ in range(4)],
         compiler_params=pltpu.CompilerParams(
-            collective_id=collective_id, has_side_effects=True, vmem_limit_bytes=60 * MIB),
-        cost_estimate=pl.CostEstimate(flops=0, bytes_accessed=300 * MIB, transcendentals=0),
-    )(part, residual_grad, hidden, gain, *weight_parts)
+            collective_id=collective_id, has_side_effects=True, vmem_limit_bytes=63 * MIB),
+        cost_estimate=pl.CostEstimate(flops=20 << 30, bytes_accessed=300 * MIB, transcendentals=0),
+    )(query_grad, *shared, weights, normed, residual_grad, hidden, gain, out_part)
 
 
 def sum_vectors(packed, collective_id):
@@ -1268,7 +1516,6 @@
         (key_weight, value_weight, query_weight), out_weight, heads_local, members, 0,
     )
     own_valid = live[:, :1] > 0
-    key_all, value_all, query_all = projections
     vector_rows = vector_rows.reshape(dp_count, -1, 128)
     each = model_width // dp_count // 128
     gain_one, _, _, _, bias_out, gain_two, shift_two, bias_down = (
@@ -1291,9 +1538,12 @@
     hidden_grad = jnp.dot(branch_rows_two, down_all, preferred_element_type=jnp.float32)
     pre_grad = jax.vjp(gelu_exact, pre_act)[1](hidden_grad)[0].astype(jnp.bfloat16)
     up_part = contract_last(pre_grad, up_all).astype(jnp.bfloat16)
-    down_weight_grad = owner_share(contract_first(branch_rows_two, hidden_low))
-    up_weight_grad = owner_share(contract_first(rows_two, pre_grad))
-    residual_grad, sums_two, branch_rows_one = reduce_back_gather(up_part, residual, branch_two, gain_two, 4)
+    residual_grad, sums_two, branch_rows_one, down_terms, up_terms = reduce_back_gather(
+        up_part, residual, branch_two, gain_two, ((branch_rows_two, hidden_low), (rows_two, pre_grad)), 4
+    )
+    down_weight_grad, up_weight_grad = (
+        jnp.sum(terms.astype(jnp.float32), axis=0) for terms in (down_terms, up_terms)
+    )
 
     hidden_low, branch_rows_one = lax.optimization_barrier((hidden_low, branch_rows_one))
     feed = row_share(contract_last(hidden_low, down_all))
@@ -1305,20 +1555,13 @@
     head_query_grad, head_key_grad, head_value_grad = attend_back(
         head_queries, head_shared, head_grad, exact_mix, log_total, *plan, members, blocks_each
     )
-    query_low, key_low, value_low = to_rows(
-        [head_query_grad], [head_key_grad, head_value_grad], heads_local, members, 6
+    out_weight_part = contract_first(branch_rows_one, attended_low).astype(jnp.bfloat16)
+    input_grad, sums_one, weight_grads, out_weight_grad, columns = finish_back(
+        head_query_grad, head_key_grad, head_value_grad, projections, rows_one, residual_grad, hidden_in, gain_one,
+        out_weight_part, heads_local, members, 7,
     )
-    last_part = contract_last(query_low, query_all)
-    last_part = last_part + contract_last(key_low, key_all)
-    last_part = (last_part + contract_last(value_low, value_all)).astype(jnp.bfloat16)
-    weight_parts = [
-        contract_first(left, right).astype(jnp.bfloat16)
-        for left, right in (
-            (rows_one, query_low), (rows_one, key_low), (rows_one, value_low), (branch_rows_one, attended_low)
-        )
-    ]
-    input_grad, sums_one, query_weight_grad, key_weight_grad, value_weight_grad, out_weight_grad = reduce_last(
-        last_part, residual_grad, hidden_in, gain_one, weight_parts, 7
+    key_weight_grad, value_weight_grad, query_weight_grad = (
+        weight_grads[:, k * head_width : (k + 1) * head_width] for k in range(3)
     )
 
     def column_sums(values):
@@ -1329,7 +1572,7 @@
         return lax.dynamic_update_slice_in_dim(whole, values, mp_index * values.shape[0], 0)
 
     sums = (
-        sums_one[0], sums_one[1], placed(column_sums(query_low)), placed(column_sums(value_low)), sums_two[2],
+        sums_one[0], sums_one[1], placed(columns[0, 2 * head_width :]), placed(columns[0, head_width : 2 * head_width]), sums_two[2],
         sums_two[0], sums_two[1], column_sums(branch_two), placed(column_sums(pre_grad)),
     )
     packed = jnp.concatenate([v.reshape(dp_count, -1, 128) for v in sums], axis=1)

time: 858 us -> 790 us (0.921)
  matrix products: 151 us -> 102 us
  Pallas kernels: 630 us -> 611 us
    pallas_call x2 -> x1, Pallas kernels: 75.9 us -> 16.7 us  [to_rows(): pl.pallas_call(kernel, out_shape=[jax.ShapeDtypeStruct((rows, heads * HEA...]
    pallas_call x2, Pallas kernels: 205 us -> 245 us  [the longest x1 123 us: reduce_back_gather(): pl.pallas_call(kernel, out_shape=[jax.ShapeDtypeStruct((rows, width), f32...]
    dot_general x6 -> x1, matrix products: 43.6 us -> 5.92 us  [contract_first(): lax.dot_general(left, right, (((0,), (0,)), ((), ())), preferred_element_...]
    dot_general x6 -> x3, matrix products: 52.8 us -> 42.7 us  [contract_last(): lax.dot_general(left, right, (((1,), (1,)), ((), ())), preferred_element_...]
    unnamed x57 -> x46, local copies, waits for them, and re-layouts: 23.2 us -> 15 us
  transfers between devices with their start and end apart: 4 -> 2, of which waited for: 0 -> 0; matrix products, arithmetic and copies ran while one was open for 13% -> 7% of each run, Pallas kernels for 48% -> 49%
where the time goes in v5:
time: 790 us; the launch traced here: 783 us
  Pallas kernels  611 us (77%)
  matrix products  102 us (13%)
  local copies, waits for them, and re-layouts  32.4 us (4%)
  other arithmetic  21.8 us (3%)
  between operations  14.7 us (2%)
    pallas_call x1, Pallas kernels, reduce_norm_gather(): pl.pallas_call(kernel, out_shape=[jax.ShapeDtypeStruct((rows, width), jnp...  135 us
    pallas_call x1, Pallas kernels, reduce_back_gather(): pl.pallas_call(kernel, out_shape=[jax.ShapeDtypeStruct((rows, width), f32...  123 us
    pallas_call x1, Pallas kernels, finish_back(): pl.pallas_call(kernel, out_shape=[jax.ShapeDtypeStruct((rows, width), f32...  122 us
    pallas_call x1, Pallas kernels, project_first(): pl.pallas_call(kernel, out_shape=[jax.ShapeDtypeStruct((group_rows, width...  102 us
    pallas_call x1, Pallas kernels, attend_back(): pl.pallas_call(kernel, out_shape=[jax.ShapeDtypeStruct(queries.shape, jnp...  43.5 us
    dot_general x3, matrix products, contract_last(): lax.dot_general(left, right, (((1,), (1,)), ((), ())), preferred_element_...  42.7 us
    pallas_call x1, Pallas kernels, attend(): pl.pallas_call(kernel, out_shape=[jax.ShapeDtypeStruct(queries.shape, jnp...  37.4 us
    dot_general x1, matrix products, per_device(): jnp.dot(branch_rows_two, down_all, preferred_element_type=jnp.float32)  32.9 us
  transfers between devices with their start and end apart: 2, of which 0 were waited for; matrix products, arithmetic and copies ran while one was open for 7% of the time, Pallas kernels for 49%

profile of v5, /device:TPU:0, one launch (start us, length us, event | category | flops | bytes accessed | tf_op | source)
XLA Modules:
  0.0 782.9 jit_solution(12985972024851714513)
XLA Ops:
  7.2 0.7 reshape.129.refs_0_
  7.9 0.7 reshape.130.refs_1_
  8.6 0.7 reshape.131.refs_2_
  9.2 0.7 reshape.132.refs_3_
  9.9 0.7 reshape.133.refs_4_
  10.5 0.7 reshape.134.refs_5_
  11.2 0.7 reshape.135.refs_6_
  11.8 0.7 reshape.136.refs_7_
  12.5 0.7 reshape.137.refs_8_
  13.2 1.2 copy-done.7
  14.4 1.2 copy-done.10
  15.6 0.9 copy-done.11
  16.6 0.9 copy-done.12
  17.5 0.9 copy-done.13
  18.5 0.9 copy-done.14
  20.1 0.7 copy-done.16
  20.8 102.2 %shard_map.323 = (bf16[1024,2048]{1,0:T(8,128)(2,1)}, f32[192,128]{1,0:T(8,128)S(1)}, bf16[2048,1536]{1,0:T(8,128)(2,1)}, bf16[2048,512]{1,0:T(8,128)(2,1)}, bf1...) custom-call(s32[8]{0:T(128)S(1)} %copy-done.16, ...), custom_call_target="tpu_custom_call" | custom-call | flops 8589934592 | bytes 262144000 | tf_op jit(solution)/shard_map/pallas_call | solution.py:916
  123.0 1.0 copy-done.17
  124.1 37.4 %shard_map.324 = (bf16[4096,128]{1,0:T(8,128)(2,1)}, f32[16,128,256]{2,1,0:T(8,128)}, f32[16,1,256]{2,1,0:T(1,128)}) custom-call(s32[8]{0:T(128)} %lengths_ref.5, s32[64]{0:T(128)} %slot_ref.3, bf16[4096,128]{1,0:T(8,128)(2,1)} %copy-done.17, bf16[2,8192,128]{2,1,0:T(8,128)(2,1)} %get-tuple-element.49.shared_ref), custom_call_target="tpu_custom_call" | custom-call | flops 8589934592 | bytes 52428800 | tf_op jit(solution)/shard_map/pallas_call | solution.py:356
  161.5 1.2 copy-done.4
  162.7 16.7 %shard_map.325 = bf16[1024,512]{1,0:T(8,128)(2,1)S(1)} custom-call(bf16[4096,128]{1,0:T(8,128)(2,1)S(1)} %copy-done.4), custom_call_target="tpu_custom_call" | custom-call | bytes 104857600 | tf_op jit(solution)/shard_map/pallas_call | solution.py:225
  180.1 6.0 convolution_convert_fusion.2.part_ref
  186.1 134.8 %shard_map.326 = (f32[256,2048]{1,0:T(8,128)S(1)}, bf16[1024,2048]{1,0:T(8,128)(2,1)}, bf16[2048,2048]{1,0:T(8,128)(2,1)}, bf16[2048,2048]{1,0:T(8,128)(2,1)}) custom-call(bf16[1024,2048]{1,0:T(8,128)(2,1)} %convolution_convert_fusion.2.part_ref, bf16[256,2048]{1,0:T(8,128)(2,1)S(1)} %copy-done.8, f32[1,2048]{1,0:T(1,128)S(1)} %bitcast.59, ...), custom_call_target="tpu_custom_call" | custom-call | bytes 314572800 | tf_op jit(solution)/shard_map/pallas_call | solution.py:1003
  321.0 1.3 copy-done
  322.3 14.5 %fusion.13 = f32[1024,2048]{1,0:T(8,128)} fusion(bf16[1024,2048]{1,0:T(8,128)(2,1)} %get-tuple-element.54.refs_2_, bf16[2048,2048]{1,0:T(8,128)(2,1)} %get-tuple-element.55), kind=kOutput, calls=%fused_computation.44 | convolution fusion | flops 8589934592 | bytes 20971520 | tf_op jit(solution)/shard_map/dot_general | solution.py:1536
  336.8 32.9 %convert_reduce_fusion.2 = (f32[2048]{0:T(1024)S(1)}, bf16[1024,2048]{1,0:T(8,128)(2,1)S(1)}, f32[1024,2048]{1,0:T(8,128)}) fusion(f32[1024,2048]{1,0:T(8,128)} %fusion.13, f32[2048]{0:T(1024)S(1)} %bitcast.64, bf16[1024,2048]{1,0:T(8,128)(2,1)} %all-gather.2.cloned.1.call-done.refs_0_, bf16[2048,2048]{1,0:T(8,128)(2,1)} %get-tuple-element.57), kind=kOutput, calls=%fused_computation.4 | convolution fusion | flops 8747218944 | bytes 33570816 | tf_op jit(solution)/shard_map/dot_general | solution.py:1538
  369.8 22.6 %convolution_convert_fusion.1.part_ref = bf16[1024,2048]{1,0:T(8,128)(2,1)} fusion(bf16[1024,2048]{1,0:T(8,128)(2,1)S(1)} %get-tuple-element.78.refs_3_, bf16[2048,2048]{1,0:T(8,128)(2,1)S(1)} %copy-done.20), kind=kOutput, calls=%fused_computation.21 | convolution fusion | flops 8592031744 | bytes 16777216 | tf_op jit(solution)/shard_map/dot_general | solution.py:36
  392.4 10.0 %multiply_convert_fusion.refs_1_ = bf16[1024,2048]{1,0:T(8,128)(2,1)} fusion(f32[1024,2048]{1,0:T(8,128)} %get-tuple-element.79, f32[1024,2048]{1,0:T(8,128)} %fusion.13, f32[2048]{0:T(1024)S(1)} %bitcast.65), kind=kLoop, calls=%fused_computation.6 | loop fusion | flops 8388608 | bytes 20979712 | tf_op jit(solution)/shard_map/convert_element_type | solution.py:1537
  402.4 123.1 %shard_map.327 = (f32[256,2048]{1,0:T(8,128)}, f32[8,2048]{1,0:T(8,128)}, bf16[1024,2048]{1,0:T(8,128)(2,1)}, bf16[4,256,2048]{2,1,0:T(8,128)(2,1)}, bf16[4,256,2048]{2,1,0:T(8,128)(2,1)}) custom-call(bf16[1024,2048]{1,0:T(8,128)(2,1)} %convolution_convert_fusion.1.part_ref, f32[256,2048]{1,0:T(8,128)} %copy-done, ...), custom_call_target="tpu_custom_call" | custom-call | flops 42949672960 | bytes 314572800 | tf_op jit(solution)/shard_map/pallas_call | solution.py:1142
  525.5 14.1 %convolution_convert_fusion = bf16[1024,2048]{1,0:T(8,128)(2,1)} fusion(bf16[1024,2048]{1,0:T(8,128)(2,1)} %multiply_convert_fusion.refs_1_, bf16[2048,2048]{1,0:T(8,128)(2,1)} %get-tuple-element.57), kind=kOutput, calls=%fused_computation.20 | convolution fusion | flops 8592031744 | bytes 16777216 | tf_op jit(solution)/shard_map/dot_general | solution.py:36
  539.8 1.4 convert_reduce_fusion.3
  541.2 6.2 convolution_convert_fusion.4.refs_0_
  547.4 14.1 %shard_map.328.g_ref = bf16[4096,128]{1,0:T(8,128)(2,1)} custom-call(bf16[1024,512]{1,0:T(8,128)(2,1)} %convolution_convert_fusion.4.refs_0_), custom_call_target="tpu_custom_call" | custom-call | bytes 104857600 | tf_op jit(solution)/shard_map/pallas_call | solution.py:132
  561.5 5.9 convolution_convert_fusion.3.out_ref
  567.4 43.5 %shard_map.329 = (bf16[4096,128]{1,0:T(8,128)(2,1)}, bf16[8192,128]{1,0:T(8,128)(2,1)}, bf16[8192,128]{1,0:T(8,128)(2,1)}) custom-call(s32[8]{0:T(128)} %lengths_ref.5, s32[64]{0:T(128)} %slot_ref.3, bf16[4096,128]{1,0:T(8,128)(2,1)} %copy-done.17, bf16[2,8192,128]{2,1,0:T(8,128)(2,1)} %get-tuple-element.49.shared_ref, bf16[4096,128]{1,0:T(8,128)(2,1)} %shard_map.328.g_ref, ...), custom_call_target="tpu_custom_call" | custom-call | flops 21474836480 | bytes 104857600 | tf_op jit(solution)/shard_map/pallas_call | solution.py:434
  610.9 122.3 %shard_map.330 = (f32[256,2048]{1,0:T(8,128)}, f32[8,2048]{1,0:T(8,128)}, f32[256,1536]{1,0:T(8,128)}, f32[256,512]{1,0:T(8,128)}, f32[8,1536]{1,0:T(8,128)}) custom-call(bf16[4,4,256,128]{3,2,1,0:T(8,128)(2,1)} %bitcast.78, bf16[8,4,256,128]{3,2,1,0:T(8,128)(2,1)} %bitcast.76, bf16[8,4,256,128]{3,2,1,0:T(8,128)(2,1)} %bitcast.77, ...), custom_call_target="tpu_custom_call" | custom-call | flops 21474836480 | bytes 314572800 | tf_op jit(solution)/shard_map/pallas_call | solution.py:1400
  733.6 0.9 fusion.12
  735.0 0.9 fusion.11
  735.9 1.0 fusion.10
  736.9 1.9 concatenate.3.in_ref
  738.8 17.3 %shard_map.331 = f32[24,128]{1,0:T(8,128)} custom-call(f32[8,24,128]{2,1,0:T(8,128)} %concatenate.3.in_ref), custom_call_target="tpu_custom_call" | custom-call | bytes 20971520 | tf_op jit(solution)/shard_map/pallas_call | solution.py:1465
  756.1 1.3 slice_bitcast_fusion
  757.4 1.4 slice_bitcast_fusion.1
  758.8 2.5 fusion.8
  761.3 7.8 convert_reduce_fusion
  769.1 2.5 select_convert_fusion
  771.6 3.1 copy.42
  774.8 0.8 copy.43
  (50 shorter events, 2.4 us)
Async XLA Ops:
  7.2 329.7 %all-gather.2.cloned.1.call-start = ((), (), s32[]{:S(2)}) async-start(), calls=%async_computation.1 | async-start | bytes 5242880 | tf_op jit(solution)/shard_map/all_gather | solution.py:48
  13.2 1.2 copy-start.7
  14.4 1.2 copy-start.10
  15.6 0.9 copy-start.11
  16.6 0.9 copy-start.12
  17.5 0.9 copy-start.13
  18.5 0.9 copy-start.14
  19.4 0.7 copy-start.15
  20.1 0.7 copy-start.16
  123.0 1.0 copy-start.17
  124.0 645.1 %reduce-scatter.2.cloned.1.call-start = ((), (), s32[]{:S(2)}) async-start(), calls=%async_computation.2 | async-start | bytes 5242880 | tf_op jit(solution)/shard_map/reduce_scatter | solution.py:53
  161.5 1.2 copy-start.4
  162.7 23.4 %copy-start.5 = (bf16[256,2048]{1,0:T(8,128)(2,1)S(1)}, bf16[256,2048]{1,0:T(8,128)(2,1)}, u32[]{:S(2)}) copy-start(bf16[256,2048]{1,0:T(8,128)(2,1)} %refs_0_.1) | copy-start | bytes 3145732
  162.7 23.4 %copy-start.6 = (bf16[256,2048]{1,0:T(8,128)(2,1)S(1)}, bf16[256,2048]{1,0:T(8,128)(2,1)}, u32[]{:S(2)}) copy-start(bf16[256,2048]{1,0:T(8,128)(2,1)} %refs_1_.1) | copy-start | bytes 3145732
  179.5 141.5 %copy-start.2 = (bf16[1024,512]{1,0:T(8,128)(2,1)}, bf16[1024,512]{1,0:T(8,128)(2,1)S(1)}, u32[]{:S(2)}) copy-start(bf16[1024,512]{1,0:T(8,128)(2,1)S(1)} %shard_map.325) | copy-start | bytes 3145732
  179.5 6.7 copy-start.8
  180.1 140.9 %copy-start.9 = (f32[8,2,128]{2,1,0:T(2,128)}, f32[8,2,128]{2,1,0:T(2,128)S(1)}, u32[]{:S(2)}) copy-start(f32[8,2,128]{2,1,0:T(2,128)S(1)} %get-tuple-element.86) | copy-start | bytes 24580
  321.0 1.3 copy-start
  336.8 33.0 %copy-start.20 = (bf16[2048,2048]{1,0:T(8,128)(2,1)S(1)}, bf16[2048,2048]{1,0:T(8,128)(2,1)}, u32[]{:S(2)}) copy-start(bf16[2048,2048]{1,0:T(8,128)(2,1)} %get-tuple-element.55) | copy-start | bytes 25165828
  369.8 22.6 %copy-start.21 = (bf16[1024,2048]{1,0:T(8,128)(2,1)}, bf16[1024,2048]{1,0:T(8,128)(2,1)S(1)}, u32[]{:S(2)}) copy-start(bf16[1024,2048]{1,0:T(8,128)(2,1)S(1)} %get-tuple-element.78.refs_3_) | copy-start | bytes 12582916
  541.2 20.3 %copy-start.3 = (bf16[1024,512]{1,0:T(8,128)(2,1)S(1)}, bf16[1024,512]{1,0:T(8,128)(2,1)}, u32[]{:S(2)}) copy-start(bf16[1024,512]{1,0:T(8,128)(2,1)} %copy-done.2) | copy-start | bytes 3145732
  733.2 35.9 %copy-start.1 = (f32[256,2048]{1,0:T(8,128)S(1)}, f32[256,2048]{1,0:T(8,128)}, u32[]{:S(2)}) copy-start(f32[256,2048]{1,0:T(8,128)} %copy-done) | copy-start | bytes 6291460
  733.3 35.9 %copy-start.19 = (f32[8,2,128]{2,1,0:T(2,128)S(1)}, f32[8,2,128]{2,1,0:T(2,128)}, u32[]{:S(2)}) copy-start(f32[8,2,128]{2,1,0:T(2,128)} %get-tuple-element.84) | copy-start | bytes 24580
  761.3 13.5 %copy-start.18 = (f32[256,512]{1,0:T(8,128)S(1)}, f32[256,512]{1,0:T(8,128)}, u32[]{:S(2)}) copy-start(f32[256,512]{1,0:T(8,128)} %get-tuple-element.131) | copy-start | bytes 1572868
Sparse Core Ops, SparseCore 0:
  124.1 90.4 all-gather.1
  539.8 76.3 reduce-scatter.1

commit v6 on v5

--- a/solution.py
+++ b/solution.py
@@ -1,3 +1,4 @@
+import functools
 import math
 
 import jax
@@ -26,10 +27,6 @@
     mean_grad = jnp.mean(scaled, axis=-1, keepdims=True)
     second = jnp.mean(scaled * normed, axis=-1, keepdims=True)
     return inverse * (scaled - mean_grad - normed * second)
-
-
-def gelu_exact(values):
-    return jax.nn.gelu(values, approximate=False)
 
 
 def contract_last(left, right):
@@ -687,24 +684,31 @@
     chips, pieces = dp_count // 2, pieces_of(rows)
     group_rows, depth, columns = mp_count * rows, projections[0].shape[0], projections[0].shape[1]
     each = width // dp_count // 128
-    tall = [v.shape[1] // 128 for v in vectors]
+    tall = [v.shape[0] // 128 for v in vectors]
     slab = sum(tall) + -sum(tall) % 8
     halves, kinds = heads // 2, 3
     arrays = kinds + 2
     offsets = sorted({2 * o for o in range(1, chips)} | {o for o in range(1, members)} | {o * members for o in range(1, heads)})
 
     def kernel(lengths_ref, order_ref, hidden_ref, upstream_ref, *refs):
-        parts, refs = refs[: len(vectors)], refs[len(vectors) :]
+        given, refs = refs[: len(vectors)], refs[len(vectors) :]
         weight_refs, out_weight_ref = refs[:kinds], refs[kinds]
         normed, all_vectors, weights, all_out, shared, queries, branch, live = refs[kinds + 1 : kinds + 9]
-        (vector_ref, raw, stage, gains, biases, line_send, line_recv, row_sem, own_sem, cross_send, cross_recv, core_send, core_recv,
+        parts, refs = refs[-len(vectors) :], refs[: -len(vectors)]
+        (vector_ref, upstream, load_sem, raw, stage, gains, biases, line_send, line_recv, row_sem, own_sem, cross_send, cross_recv, core_send, core_recv,
          head_local, head_send, head_recv, pair_send, pair_recv) = refs[kinds + 9 :]
         dp, mp = lax.axis_index("dp"), lax.axis_index("mp")
+        loads = [pltpu.make_async_copy(given[k], parts[k], load_sem.at[k]) for k in range(len(vectors))]
+        loads.append(pltpu.make_async_copy(upstream_ref, upstream, load_sem.at[len(vectors)]))
+        for copy in loads:
+            copy.start()
         vector_ref[...] = jnp.zeros_like(vector_ref)
+        for copy in loads:
+            copy.wait()
         first = 0
         for part, count in zip(parts, tall):
             for r in range(count):
-                vector_ref[first + r : first + r + 1] = part[:, r * 128 : (r + 1) * 128].astype(jnp.float32)
+                vector_ref[first + r] = part[r * 128 : (r + 1) * 128].astype(jnp.float32)
             first += count
         group, member = dp // members, dp % members
         partner = (dp ^ 1, mp)
@@ -752,7 +756,7 @@
             span = slice(block * BLOCK, (block + 1) * BLOCK)
             live[span] = (lax.broadcasted_iota(jnp.int32, (BLOCK, 128), 0) < valid).astype(jnp.float32)
             keep = lax.broadcasted_iota(jnp.int32, (BLOCK, width), 0) < valid
-            branch[span] = jnp.where(keep, upstream_ref[span].astype(jnp.float32), 0.0).astype(branch.dtype)
+            branch[span] = jnp.where(keep, upstream[span].astype(jnp.float32), 0.0).astype(branch.dtype)
         own_rows = pltpu.make_async_copy(hidden_ref, raw.at[block_span(mp)], row_sem)
         own_rows.start()
         for array in first_to_last:
@@ -925,10 +929,12 @@
             jax.ShapeDtypeStruct((rows, width), bf16),
             jax.ShapeDtypeStruct((rows, 128), f32),
         ],
-        in_specs=[SMEM, SMEM, VMEM, VMEM] + [VMEM] * len(vectors) + [ANY] * (kinds + 1),
+        in_specs=[SMEM, SMEM] + [ANY] * (len(vectors) + kinds + 3),
         out_specs=[VMEM, VMEM, VMEM, ANY, ANY, ANY, VMEM, VMEM],
         scratch_shapes=[
             pltpu.VMEM((slab, 128), f32),
+            pltpu.VMEM((rows, width), bf16),
+            dma((len(vectors) + 1,)),
             pltpu.VMEM((group_rows, width), bf16),
             pltpu.VMEM((kinds, mp_count, heads, rows, HEAD_DIM), bf16),
             pltpu.VMEM((8, width), f32),
@@ -938,9 +944,10 @@
         + [dma(()), dma((arrays,))]
         + [dma((arrays, chips)) for _ in range(4)]
         + [dma((kinds, mp_count)), dma((kinds, heads, mp_count)), dma((kinds, heads, mp_count))]
-        + [dma((2, heads, mp_count, members)) for _ in range(2)],
+        + [dma((2, heads, mp_count, members)) for _ in range(2)]
+        + [pltpu.VMEM(v.shape, v.dtype) for v in vectors],
         compiler_params=pltpu.CompilerParams(
-            collective_id=collective_id, has_side_effects=True, vmem_limit_bytes=48 * MIB),
+            collective_id=collective_id, has_side_effects=True, vmem_limit_bytes=63 * MIB),
         cost_estimate=pl.CostEstimate(flops=8 << 30, bytes_accessed=250 * MIB, transcendentals=0),
     )(lengths, order, hidden, output_grad, *vectors, *projections, out_weight)
 
@@ -1013,7 +1020,7 @@
         + LineReduce.scratch(mp_count, rows, width, pieces) + LineGather.semaphores(mp_count, pieces)
         + [pltpu.SemaphoreType.DMA(())] + ShardGather.semaphores(count, chips),
         compiler_params=pltpu.CompilerParams(
-            collective_id=collective_id, has_side_effects=True, vmem_limit_bytes=48 * MIB),
+            collective_id=collective_id, has_side_effects=True, vmem_limit_bytes=63 * MIB),
         cost_estimate=pl.CostEstimate(flops=0, bytes_accessed=300 * MIB, transcendentals=0),
     )(part, hidden, out_bias, gain, shift, *shards)
 
@@ -1171,7 +1178,7 @@
 QUARTERS = 4
 
 
-def finish_back(query_grad, key_part, value_part, weights, normed, residual_grad, hidden, gain, out_part, heads, members,
+def finish_back(query_grad, key_part, value_part, weights, normed, residual_grad, hidden, gain, out_part, vectors, heads, members,
                 collective_id):
     rows, width = hidden.shape
     dp_count, mp_count = lax.axis_size("dp"), lax.axis_size("mp")
@@ -1184,20 +1191,21 @@
     slices_each = max(dp_count // 8, 1)
     slice_turn = turns // 3
     group_rows = mp_count * rows
-    offsets = sorted({2 * o for o in range(1, chips)} | {o for o in range(1, members)} | {o * members for o in range(1, heads)})
+    slab, each = vectors.shape[1], width // dp_count // 128
     query_grad = query_grad.reshape(heads, mp_count, rows, HEAD_DIM)
     shared = [v.reshape(dp_count, mp_count, rows, HEAD_DIM) for v in (key_part, value_part)]
 
-    def kernel(query_ref, key_ref, value_ref, weights_hbm, normed_hbm, residual_ref, hidden_ref, gain_ref, out_ref,
-               grad_ref, sums_ref, weight_grad_ref, out_grad_ref, column_ref,
+    def kernel(query_ref, key_ref, value_ref, weights_hbm, normed_hbm, residual_ref, hidden_ref, gain_ref, out_ref, vector_ref,
+               grad_ref, weight_grad_ref, out_grad_ref, summed_ref,
                weights, normed, landed, own, parts, stage, part, total, flows, red_send, red_recv,
                slices, from_partner, chip_sum, from_chips, out_partner, out_sum, out_chips,
                load_sem, own_sem, part_send, part_recv, local_sem, head_send, head_recv,
-               pair_send, pair_recv, cross_send, cross_recv):
+               pair_send, pair_recv, cross_send, cross_recv,
+               sums_ref, column_ref, packed, vector_parts, line_parts, vec_send, vec_recv, line_send, line_recv):
         dp, mp = lax.axis_index("dp"), lax.axis_index("mp")
         group, member = dp // members, dp % members
         partner = (dp ^ 1, mp)
-        greet_all([(dp ^ o, mp) for o in offsets], dp, mp, mp_count)
+        greet_all([(dp ^ o, mp) for o in range(1, dp_count)] + [(dp, mp ^ o) for o in range(1, mp_count)], dp, mp, mp_count)
         reduce = LineReduce(part, flows, rows, pieces, red_send, red_recv, dp, mp, mp_count)
         loads = [pltpu.make_async_copy(weights_hbm, weights, load_sem.at[0]),
                  pltpu.make_async_copy(normed_hbm, normed, load_sem.at[1])]
@@ -1366,15 +1374,44 @@
                     else:
                         out_grad_ref[...] = value
 
+            @pl.when(turn == late_turn - 1)
+            def _():
+                column_ref[0:1] = jnp.sum(
+                    landed[...].reshape(group_rows, kinds * columns).astype(jnp.float32), axis=0, keepdims=True)
+
             @pl.when((turn >= late_turn) & (turn < late_turn + dp_count // slices_each))
             def _():
                 for i in range(slices_each):
                     weight_slice((turn - late_turn) * slices_each + i)
 
         reduce.finish()
-        column_ref[...] = jnp.zeros_like(column_ref)
-        column_ref[0:1] = jnp.sum(
-            landed[...].reshape(group_rows, kinds * columns).astype(jnp.float32), axis=0, keepdims=True)
+        packed[...] = vector_ref[...]
+        for owner in range(dp_count):
+            for r in range(each):
+                at = slice((owner * each + r) * 128, (owner * each + r + 1) * 128)
+                for k in range(2):
+                    packed[owner, k * each + r : k * each + r + 1] = sums_ref[k : k + 1, at]
+        for head in range(heads):
+            feature = mp * heads + head
+            for k, kind in ((2, 2), (3, 1)):
+                at = slice(kind * columns + head * HEAD_DIM, kind * columns + (head + 1) * HEAD_DIM)
+                packed[feature // each, pl.ds(k * each + feature % each, 1)] = column_ref[0:1, at]
+
+        def vector_copy(o):
+            return remote(packed.at[dp ^ o], vector_parts.at[o], vec_send.at[o], vec_recv.at[o], (dp ^ o, mp))
+
+        def line_copy(o):
+            return remote(line_parts.at[mp], line_parts.at[mp], line_send.at[o], line_recv.at[o], (dp, mp ^ o))
+
+        for o in range(1, dp_count):
+            vector_copy(o).start()
+        value = packed[dp]
+        for o in range(1, dp_count):
+            vector_copy(o).wait_recv()
+            value = value + vector_parts[o]
+        line_parts[mp] = value
+        for o in range(1, mp_count):
+            line_copy(o).start()
         for o in range(chips):
             pair(o).wait_send()
             out_pair(o).wait_send()
@@ -1391,6 +1428,14 @@
                 if o:
                     for kind in range(kinds):
                         head_copy(kind, o, k).wait_send()
+        for o in range(1, mp_count):
+            line_copy(o).wait()
+        value = line_parts[0]
+        for index in range(1, mp_count):
+            value = value + line_parts[index]
+        summed_ref[...] = value
+        for o in range(1, dp_count):
+            vector_copy(o).wait_send()
 
     late_turn = max(slice_turn, (QUARTERS - 2) * per_quarter + 1)
     assert late_turn + dp_count // slices_each <= turns
@@ -1401,13 +1446,12 @@
         kernel,
         out_shape=[
             jax.ShapeDtypeStruct((rows, width), f32),
-            jax.ShapeDtypeStruct((8, width), f32),
             jax.ShapeDtypeStruct((depth, kinds * columns), f32),
             jax.ShapeDtypeStruct((depth, own_columns), f32),
-            jax.ShapeDtypeStruct((8, kinds * columns), f32),
+            jax.ShapeDtypeStruct((slab, 128), f32),
         ],
-        in_specs=[ANY] * 5 + [VMEM] * 4,
-        out_specs=[VMEM] * 5,
+        in_specs=[ANY] * 5 + [VMEM] * 5,
+        out_specs=[VMEM] * 4,
         scratch_shapes=[
             pltpu.VMEM((width, kinds * columns), bf16),
             pltpu.VMEM((group_rows, width), bf16),
@@ -1424,57 +1468,89 @@
         + [dma((2,)), dma((2, heads))]
         + [dma((2, heads, members - 1, QUARTERS)) for _ in range(2)]
         + [dma((QUARTERS,)), dma((kinds, heads, QUARTERS)), dma((kinds, heads, QUARTERS))]
-        + [dma((2, chips)) for _ in range(4)],
+        + [dma((2, chips)) for _ in range(4)]
+        + [pltpu.VMEM((8, width), f32), pltpu.VMEM((8, kinds * columns), f32)]
+        + [pltpu.VMEM((count, slab, 128), f32) for count in (dp_count, dp_count, mp_count)]
+        + [dma((dp_count,)), dma((dp_count,)), dma((mp_count,)), dma((mp_count,))],
         compiler_params=pltpu.CompilerParams(
             collective_id=collective_id, has_side_effects=True, vmem_limit_bytes=63 * MIB),
         cost_estimate=pl.CostEstimate(flops=20 << 30, bytes_accessed=300 * MIB, transcendentals=0),
-    )(query_grad, *shared, weights, normed, residual_grad, hidden, gain, out_part)
-
-
-def sum_vectors(packed, collective_id):
-    dp_count, mp_count = lax.axis_size("dp"), lax.axis_size("mp")
-    depth, width = packed.shape[1:]
-
-    def kernel(in_ref, out_ref, landed, mine, others, send_sem, recv_sem, line_send, line_recv):
-        dp, mp = lax.axis_index("dp"), lax.axis_index("mp")
-        peers = [(dp ^ o, mp) for o in range(1, dp_count)]
-        along = [(dp, mp ^ o) for o in range(1, mp_count)]
-        greet(peers + along)
-        copies = []
-        for o in range(1, dp_count):
-            copies.append(remote(in_ref.at[dp ^ o], landed.at[o - 1], send_sem.at[o], recv_sem.at[o], peers[o - 1]))
-            copies[-1].start()
-        value = in_ref[dp]
-        for o in range(1, dp_count):
-            copies[o - 1].wait()
-            value = value + landed[o - 1]
-        mine[...] = value
-        others[mp] = value
-        copies = []
-        for o in range(1, mp_count):
-            copies.append(remote(mine, others.at[mp], line_send.at[o], line_recv.at[o], along[o - 1]))
-            copies[-1].start()
-        for copy in copies:
-            copy.wait()
-        value = others[0]
-        for index in range(1, mp_count):
-            value = value + others[index]
-        out_ref[...] = value
-
-    dma = pltpu.SemaphoreType.DMA
+    )(query_grad, *shared, weights, normed, residual_grad, hidden, gain, out_part, vectors)
+
+
+UNITS = 512
+CHUNK = 256
+
+
+def feed_both_ways(rows_two, branch_rows, up_all, down_all, up_bias):
+    rows, width = rows_two.shape
+    units = up_all.shape[1]
+    tile = min(UNITS, units)
+    half_root = 1.0 / math.sqrt(2.0)
+    density_scale = 1.0 / math.sqrt(2.0 * math.pi)
+
+    def kernel(rows_ref, branch_ref, up_ref, down_ref, bias_ref, hidden_ref, grad_ref, column_ref, part_ref, total):
+        step = pl.program_id(0)
+        columns = jnp.zeros((1, tile), jnp.float32)
+        up, down = up_ref[...], down_ref[...]
+        for first in range(0, rows, CHUNK):
+            span = slice(first, first + CHUNK)
+            pre = jnp.dot(rows_ref[span], up, preferred_element_type=jnp.float32) + bias_ref[...]
+            upstream = jnp.dot(branch_ref[span], down, preferred_element_type=jnp.float32)
+            share = 0.5 + 0.5 * lax.erf(pre * half_root)
+            hidden_ref[span] = (pre * share).astype(hidden_ref.dtype)
+            slope = share + pre * (density_scale * jnp.exp(-0.5 * pre * pre))
+            grad = (upstream * slope).astype(grad_ref.dtype)
+            grad_ref[span] = grad
+            columns = columns + jnp.sum(grad.astype(jnp.float32), axis=0, keepdims=True)
+            back = contract_last(grad, up)
+
+            @pl.when(step == 0)
+            def _():
+                total[span] = back
+
+            @pl.when(step != 0)
+            def _():
+                total[span] += back
+
+        column_ref[...] = columns
+
+        @pl.when(step == units // tile - 1)
+        def _():
+            part_ref[...] = total[...].astype(part_ref.dtype)
+
+    bf16 = jnp.bfloat16
     return pl.pallas_call(
         kernel,
-        out_shape=jax.ShapeDtypeStruct((depth, width), jnp.float32),
-        in_specs=[VMEM],
-        out_specs=VMEM,
-        scratch_shapes=[
-            pltpu.VMEM((dp_count - 1, depth, width), jnp.float32), pltpu.VMEM((depth, width), jnp.float32),
-            pltpu.VMEM((mp_count, depth, width), jnp.float32),
-            dma((dp_count,)), dma((dp_count,)), dma((mp_count,)), dma((mp_count,)),
+        grid=(units // tile,),
+        out_shape=[
+            jax.ShapeDtypeStruct((rows, units), bf16),
+            jax.ShapeDtypeStruct((rows, units), bf16),
+            jax.ShapeDtypeStruct((1, units), jnp.float32),
+            jax.ShapeDtypeStruct((rows, width), bf16),
         ],
-        compiler_params=pltpu.CompilerParams(collective_id=collective_id, has_side_effects=True),
-        cost_estimate=pl.CostEstimate(flops=0, bytes_accessed=20 * MIB, transcendentals=0),
-    )(packed)
+        in_specs=[
+            pl.BlockSpec((rows, width), lambda i: (0, 0)),
+            pl.BlockSpec((rows, width), lambda i: (0, 0)),
+            pl.BlockSpec((width, tile), lambda i: (0, i)),
+            pl.BlockSpec((width, tile), lambda i: (0, i)),
+            pl.BlockSpec((1, tile), lambda i: (0, i)),
+        ],
+        out_specs=[
+            pl.BlockSpec((rows, tile), lambda i: (0, i)),
+            pl.BlockSpec((rows, tile), lambda i: (0, i)),
+            pl.BlockSpec((1, tile), lambda i: (0, i)),
+            pl.BlockSpec((rows, width), lambda i: (0, 0)),
+        ],
+        scratch_shapes=[pltpu.VMEM((rows, width), jnp.float32)],
+        compiler_params=pltpu.CompilerParams(vmem_limit_bytes=60 * MIB),
+        cost_estimate=pl.CostEstimate(
+            flops=6 * rows * width * units, bytes_accessed=40 * MIB, transcendentals=2 * rows * units),
+    )(rows_two, branch_rows, up_all, down_all, up_bias)
+
+
+def sum_terms(terms):
+    return functools.reduce(jnp.add, [terms[k].astype(jnp.float32) for k in range(terms.shape[0])])
 
 
 def per_device(
@@ -1512,7 +1588,7 @@
 
     vectors = (first_gain, first_shift, query_bias, value_bias, out_bias, second_gain, second_shift, down_bias, up_bias)
     rows_one, vector_rows, projections, out_all, head_shared, head_queries, branch_two, live = project_first(
-        hidden_in, output_grad, seq_lengths, block_order, [v.reshape(1, -1) for v in vectors],
+        hidden_in, output_grad, seq_lengths, block_order, vectors,
         (key_weight, value_weight, query_weight), out_weight, heads_local, members, 0,
     )
     own_valid = live[:, :1] > 0
@@ -1533,16 +1609,12 @@
     )
 
     bias_hidden = lax.dynamic_slice_in_dim(bias_up, mp_index * hidden_width, hidden_width, 1)
-    pre_act = jnp.dot(rows_two, up_all, preferred_element_type=jnp.float32) + bias_hidden
-    hidden_low = gelu_exact(pre_act).astype(jnp.bfloat16)
-    hidden_grad = jnp.dot(branch_rows_two, down_all, preferred_element_type=jnp.float32)
-    pre_grad = jax.vjp(gelu_exact, pre_act)[1](hidden_grad)[0].astype(jnp.bfloat16)
-    up_part = contract_last(pre_grad, up_all).astype(jnp.bfloat16)
+    hidden_low, pre_grad, pre_columns, up_part = feed_both_ways(rows_two, branch_rows_two, up_all, down_all, bias_hidden)
     residual_grad, sums_two, branch_rows_one, down_terms, up_terms = reduce_back_gather(
         up_part, residual, branch_two, gain_two, ((branch_rows_two, hidden_low), (rows_two, pre_grad)), 4
     )
     down_weight_grad, up_weight_grad = (
-        jnp.sum(terms.astype(jnp.float32), axis=0) for terms in (down_terms, up_terms)
+        sum_terms(terms) for terms in (down_terms, up_terms)
     )
 
     hidden_low, branch_rows_one = lax.optimization_barrier((hidden_low, branch_rows_one))
@@ -1555,29 +1627,28 @@
     head_query_grad, head_key_grad, head_value_grad = attend_back(
         head_queries, head_shared, head_grad, exact_mix, log_total, *plan, members, blocks_each
     )
+
+    def column_sums(values):
+        return jnp.sum(values.astype(jnp.float32), axis=0)
+
+    def placed(values):
+        whole = jnp.zeros((values.shape[0] * mp_count,), jnp.float32)
+        return lax.dynamic_update_slice_in_dim(whole, values, mp_index * values.shape[0], 0)
+
+    none = jnp.zeros((model_width,), jnp.float32)
+    sums = (
+        none, none, none, none, sums_two[2], sums_two[0], sums_two[1], column_sums(branch_two), placed(pre_columns[0]),
+    )
+    packed = jnp.concatenate([v.reshape(dp_count, -1, 128) for v in sums], axis=1)
+    packed = jnp.pad(packed, ((0, 0), (0, -packed.shape[1] % 8), (0, 0)))
     out_weight_part = contract_first(branch_rows_one, attended_low).astype(jnp.bfloat16)
-    input_grad, sums_one, weight_grads, out_weight_grad, columns = finish_back(
+    input_grad, weight_grads, out_weight_grad, summed = finish_back(
         head_query_grad, head_key_grad, head_value_grad, projections, rows_one, residual_grad, hidden_in, gain_one,
-        out_weight_part, heads_local, members, 7,
+        out_weight_part, packed, heads_local, members, 7,
     )
     key_weight_grad, value_weight_grad, query_weight_grad = (
         weight_grads[:, k * head_width : (k + 1) * head_width] for k in range(3)
     )
-
-    def column_sums(values):
-        return jnp.sum(values.astype(jnp.float32), axis=0)
-
-    def placed(values):
-        whole = jnp.zeros((values.shape[0] * mp_count,), jnp.float32)
-        return lax.dynamic_update_slice_in_dim(whole, values, mp_index * values.shape[0], 0)
-
-    sums = (
-        sums_one[0], sums_one[1], placed(columns[0, 2 * head_width :]), placed(columns[0, head_width : 2 * head_width]), sums_two[2],
-        sums_two[0], sums_two[1], column_sums(branch_two), placed(column_sums(pre_grad)),
-    )
-    packed = jnp.concatenate([v.reshape(dp_count, -1, 128) for v in sums], axis=1)
-    packed = jnp.pad(packed, ((0, 0), (0, -packed.shape[1] % 8), (0, 0)))
-    summed = sum_vectors(packed, 8)
     vector_grads = [summed[k * each : (k + 1) * each].reshape(-1) for k in range(8)]
     up_bias_grad = summed[8 * each : 8 * each + up_each].reshape(-1)
     return (

time: 790 us -> 732 us (0.927)
  matrix products: 102 us -> 32.4 us
  Pallas kernels: 611 us -> 651 us
  local copies, waits for them, and re-layouts: 32.4 us -> 16 us
  other arithmetic: 21.8 us -> 10.2 us
    dot_general x2 -> x0, matrix products: 47.5 us -> none  [the longest x1 32.9 us: per_device(): jnp.dot(branch_rows_two, down_all, preferred_element_type=jnp.float32)]
    pallas_call x1, Pallas kernels: 17.3 us -> 41.6 us  [feed_both_ways(): pl.pallas_call(kernel, grid=(units // tile,), out_shape=[jax.ShapeDtypeSt...]
    dot_general x3 -> x2, matrix products: 42.7 us -> 20.2 us  [contract_last(): lax.dot_general(left, right, (((1,), (1,)), ((), ())), preferred_element_...]
    pallas_call x1, Pallas kernels: 122 us -> 138 us  [finish_back(): pl.pallas_call(kernel, out_shape=[jax.ShapeDtypeStruct((rows, width), f32...]
    unnamed x46 -> x22, local copies, waits for them, and re-layouts: 15 us -> 4.6 us
    convert_element_type x1 -> x0, other arithmetic: 9.98 us -> none  [per_device(): hidden_low = gelu_exact(pre_act).astype(jnp.bfloat16)]
  transfers between devices with their start and end apart: 2 -> 2, of which waited for: 0 -> 0; matrix products, arithmetic and copies ran while one was open for 7% -> 5% of each run, Pallas kernels for 49% -> 53%
where the time goes in v6:
time: 732 us; the launch traced here: 724 us
  Pallas kernels  651 us (89%)
  matrix products  32.4 us (4%)
  local copies, waits for them, and re-layouts  16 us (2%)
  between operations  14.4 us (2%)
  other arithmetic  10.2 us (1%)
    pallas_call x1, Pallas kernels, finish_back(): pl.pallas_call(kernel, out_shape=[jax.ShapeDtypeStruct((rows, width), f32...  138 us
    pallas_call x1, Pallas kernels, reduce_norm_gather(): pl.pallas_call(kernel, out_shape=[jax.ShapeDtypeStruct((rows, width), jnp...  134 us
    pallas_call x1, Pallas kernels, reduce_back_gather(): pl.pallas_call(kernel, out_shape=[jax.ShapeDtypeStruct((rows, width), f32...  123 us
    pallas_call x1, Pallas kernels, project_first(): pl.pallas_call(kernel, out_shape=[jax.ShapeDtypeStruct((group_rows, width...  104 us
    pallas_call x1, Pallas kernels, attend_back(): pl.pallas_call(kernel, out_shape=[jax.ShapeDtypeStruct(queries.shape, jnp...  42.3 us
    pallas_call x1, Pallas kernels, feed_both_ways(): pl.pallas_call(kernel, grid=(units // tile,), out_shape=[jax.ShapeDtypeSt...  41.6 us
    pallas_call x1, Pallas kernels, attend(): pl.pallas_call(kernel, out_shape=[jax.ShapeDtypeStruct(queries.shape, jnp...  36.6 us
    dot_general x2, matrix products, contract_last(): lax.dot_general(left, right, (((1,), (1,)), ((), ())), preferred_element_...  20.2 us
  transfers between devices with their start and end apart: 2, of which 0 were waited for; matrix products, arithmetic and copies ran while one was open for 5% of the time, Pallas kernels for 53%

profile of v6, /device:TPU:0, one launch (start us, length us, event | category | flops | bytes accessed | tf_op | source)
XLA Modules:
  0.0 724.5 jit_solution(2139367314084643481)
XLA Ops:
  7.2 0.0 all-gather.2.cloned.1.call-start
  7.2 104.2 %shard_map.323 = (bf16[1024,2048]{1,0:T(8,128)(2,1)}, f32[192,128]{1,0:T(8,128)}, bf16[2048,1536]{1,0:T(8,128)(2,1)}, bf16[2048,512]{1,0:T(8,128)(2,1)}, bf16[2,...) custom-call(s32[8]{0:T(128)} %lengths_ref.5, ...), custom_call_target="tpu_custom_call" | custom-call | flops 8589934592 | bytes 262144000 | tf_op jit(solution)/shard_map/pallas_call | solution.py:920
  111.4 0.0 all-gather.2.cloned.1.call-update
  111.4 0.0 reduce-scatter.2.cloned.1.call-start
  111.5 0.8 slice.123
  112.2 36.6 %shard_map.324 = (bf16[4096,128]{1,0:T(8,128)(2,1)}, f32[16,128,256]{2,1,0:T(8,128)}, f32[16,1,256]{2,1,0:T(1,128)}) custom-call(s32[8]{0:T(128)} %lengths_ref.5, s32[64]{0:T(128)} %slot_ref.3, bf16[4096,128]{1,0:T(8,128)(2,1)} %get-tuple-element.51.q_ref, bf16[2,8192,128]{2,1,0:T(8,128)(2,1)} %get-tuple-element.52.shared_ref), custom_call_target="tpu_custom_call" | custom-call | flops 8589934592 | bytes 52428800 | tf_op jit(solution)/shard_map/pallas_call | solution.py:353
  148.8 0.0 copy-start.2
  148.9 1.2 copy-done.2
  150.1 18.2 %shard_map.325 = bf16[1024,512]{1,0:T(8,128)(2,1)S(1)} custom-call(bf16[4096,128]{1,0:T(8,128)(2,1)S(1)} %copy-done.2), custom_call_target="tpu_custom_call" | custom-call | bytes 104857600 | tf_op jit(solution)/shard_map/pallas_call | solution.py:222
  168.2 0.0 copy-start
  168.3 1.6 fusion.2
  169.9 5.9 convolution_convert_fusion.1.part_ref
  175.8 0.0 copy-done
  175.8 134.0 %shard_map.326 = (f32[256,2048]{1,0:T(8,128)}, bf16[1024,2048]{1,0:T(8,128)(2,1)}, bf16[2048,2048]{1,0:T(8,128)(2,1)}, bf16[2048,2048]{1,0:T(8,128)(2,1)}) custom-call(bf16[1024,2048]{1,0:T(8,128)(2,1)} %convolution_convert_fusion.1.part_ref, bf16[256,2048]{1,0:T(8,128)(2,1)} %hidden_ref.5, f32[1,2048]{1,0:T(1,128)} %bitcast.58, f32[1,2048]{1,0:T(1,128)} %bitcast.55, ...), custom_call_target="tpu_custom_call" | custom-call | bytes 314572800 | tf_op jit(solution)/shard_map/pallas_call | solution.py:1010
  309.9 0.6 constant_dynamic-slice_fusion.bias_ref
  310.5 0.0 all-gather.2.cloned.1.call-done.branch_ref.refs_0_
  310.5 41.6 %shard_map.327 = (bf16[1024,2048]{1,0:T(8,128)(2,1)}, bf16[1024,2048]{1,0:T(8,128)(2,1)}, f32[1,2048]{1,0:T(1,128)}, bf16[1024,2048]{1,0:T(8,128)(2,1)}) custom-call(bf16[1024,2048]{1,0:T(8,128)(2,1)} %get-tuple-element.57.rows_ref.refs_2_, bf16[1024,2048]{1,0:T(8,128)(2,1)} %all-gather.2.cloned.1.call-done.branch_ref.refs_0_, ...), custom_call_target="tpu_custom_call" | custom-call | flops 25769803776 | bytes 41943040 | tf_op jit(solution)/shard_map/pallas_call | solution.py:1523
  352.1 122.9 %shard_map.328 = (f32[256,2048]{1,0:T(8,128)}, f32[8,2048]{1,0:T(8,128)}, bf16[1024,2048]{1,0:T(8,128)(2,1)}, bf16[4,256,2048]{2,1,0:T(8,128)(2,1)}, bf16[4,256,2048]{2,1,0:T(8,128)(2,1)}) custom-call(bf16[1024,2048]{1,0:T(8,128)(2,1)} %get-tuple-element.62.part_ref, f32[256,2048]{1,0:T(8,128)} %get-tuple-element.56.residual_ref, ...), custom_call_target="tpu_custom_call" | custom-call | flops 42949672960 | bytes 314572800 | tf_op jit(solution)/shard_map/pallas_call | solution.py:1149
  474.9 14.3 %convolution_convert_fusion = bf16[1024,2048]{1,0:T(8,128)(2,1)} fusion(bf16[1024,2048]{1,0:T(8,128)(2,1)} %get-tuple-element.65.refs_1_, bf16[2048,2048]{1,0:T(8,128)(2,1)} %get-tuple-element.60.down_ref), kind=kOutput, calls=%fused_computation | convolution fusion | flops 8592031744 | bytes 16777216 | tf_op jit(solution)/shard_map/dot_general | solution.py:33
  489.3 0.0 copy-start.7
  489.3 0.0 copy-start.3
  489.3 0.0 reduce-scatter.2.cloned.1.call-update
  489.3 0.9 copy-done.7
  490.2 0.1 fusion
  490.3 0.3 copy-done.3
  490.6 0.2 convert_reduce_fusion
  490.7 6.2 convolution_convert_fusion.3.refs_0_
  496.9 14.0 %shard_map.329.g_ref = bf16[4096,128]{1,0:T(8,128)(2,1)} custom-call(bf16[1024,512]{1,0:T(8,128)(2,1)} %convolution_convert_fusion.3.refs_0_), custom_call_target="tpu_custom_call" | custom-call | bytes 104857600 | tf_op jit(solution)/shard_map/pallas_call | solution.py:129
  510.9 0.0 copy-done.9
  510.9 0.3 dynamic_update_slice.3
  511.3 1.0 fusion.3
  512.3 1.9 concatenate.7.vector_ref
  514.1 0.0 copy-done.1
  514.1 6.0 convolution_convert_fusion.2.out_ref
  520.1 42.3 %shard_map.330 = (bf16[4096,128]{1,0:T(8,128)(2,1)}, bf16[8192,128]{1,0:T(8,128)(2,1)}, bf16[8192,128]{1,0:T(8,128)(2,1)}) custom-call(s32[8]{0:T(128)} %lengths_ref.5, s32[64]{0:T(128)} %slot_ref.3, bf16[4096,128]{1,0:T(8,128)(2,1)} %get-tuple-element.51.q_ref, bf16[2,8192,128]{2,1,0:T(8,128)(2,1)} %get-tuple-element.52.shared_ref, ...), custom_call_target="tpu_custom_call" | custom-call | flops 21474836480 | bytes 104857600 | tf_op jit(solution)/shard_map/pallas_call | solution.py:431
  562.5 137.6 %shard_map.331 = (f32[256,2048]{1,0:T(8,128)}, f32[256,1536]{1,0:T(8,128)}, f32[256,512]{1,0:T(8,128)}, f32[24,128]{1,0:T(8,128)}) custom-call(bf16[4,4,256,128]{3,2,1,0:T(8,128)(2,1)} %bitcast.63, bf16[8,4,256,128]{3,2,1,0:T(8,128)(2,1)} %bitcast.61, bf16[8,4,256,128]{3,2,1,0:T(8,128)(2,1)} %bitcast.62, bf16[2048,1536]{1,0:T(8,128)(2,1)} %get-tuple-element.72.weights_hbm, ...), custom_call_target="tpu_custom_call" | custom-call | flops 21474836480 | bytes 314572800 | tf_op jit(solution)/shard_map/pallas_call | solution.py:1445
  700.0 1.3 slice_bitcast_fusion
  701.3 1.4 slice_bitcast_fusion.1
  702.7 2.5 fusion.1
  705.3 7.3 %add_bitcast_fusion = (f32[256,2048]{1,0:T(8,128)}, f32[256,2048]{1,0:T(8,128)}) fusion(bf16[4,256,2048]{2,1,0:T(8,128)(2,1)} %get-tuple-element.82, bf16[4,256,2048]{2,1,0:T(8,128)(2,1)} %get-tuple-element.81), kind=kLoop, calls=%fused_computation.3 | loop fusion | flops 7340032 | bytes 12582912 | tf_op jit(solution)/shard_map/add | solution.py:1553
  712.6 0.0 copy-done.4
  712.6 0.0 copy-done.8
  712.6 0.0 copy-start.5
  712.6 2.7 select_convert_fusion
  715.2 0.0 copy-done.5
  715.2 1.3 copy.40
  716.6 0.1 copy-done.6
  716.6 0.8 copy.41
  (8 shorter events, 0.0 us)
Async XLA Ops:
  7.2 303.3 %all-gather.2.cloned.1.call-start = ((), (), s32[]{:S(2)}) async-start(), calls=%async_computation.1 | async-start | bytes 5242880 | tf_op jit(solution)/shard_map/all_gather | solution.py:45
  111.4 601.1 %reduce-scatter.2.cloned.1.call-start = ((), (), s32[]{:S(2)}) async-start(), calls=%async_computation.2 | async-start | bytes 5242880 | tf_op jit(solution)/shard_map/reduce_scatter | solution.py:50
  148.8 1.2 copy-start.2
  168.2 7.6 %copy-start = (bf16[1024,512]{1,0:T(8,128)(2,1)}, bf16[1024,512]{1,0:T(8,128)(2,1)S(1)}, u32[]{:S(2)}) copy-start(bf16[1024,512]{1,0:T(8,128)(2,1)S(1)} %shard_map.325) | copy-start | bytes 3145732
  489.3 0.9 copy-start.7
  489.3 1.3 copy-start.3
  496.9 14.0 %copy-start.9 = (f32[1,2048]{1,0:T(1,128)S(1)}, f32[1,2048]{1,0:T(1,128)}, u32[]{:S(2)}) copy-start(f32[1,2048]{1,0:T(1,128)} %get-tuple-element.76) | copy-start | bytes 24580
  496.9 17.2 %copy-start.1 = (bf16[1024,512]{1,0:T(8,128)(2,1)S(1)}, bf16[1024,512]{1,0:T(8,128)(2,1)}, u32[]{:S(2)}) copy-start(bf16[1024,512]{1,0:T(8,128)(2,1)} %copy-done) | copy-start | bytes 3145732
  705.3 7.3 %copy-start.4 = (f32[256,2048]{1,0:T(8,128)S(1)}, f32[256,2048]{1,0:T(8,128)}, u32[]{:S(2)}) copy-start(f32[256,2048]{1,0:T(8,128)} %get-tuple-element.56.residual_ref) | copy-start | bytes 6291460
  705.3 7.3 %copy-start.8 = (f32[8,2,128]{2,1,0:T(2,128)S(1)}, f32[8,2,128]{2,1,0:T(2,128)}, u32[]{:S(2)}) copy-start(f32[8,2,128]{2,1,0:T(2,128)} %get-tuple-element.87) | copy-start | bytes 24580
  712.6 2.7 copy-start.5
  715.2 1.4 copy-start.6
Sparse Core Ops, SparseCore 0:
  111.5 87.6 all-gather.1
  489.4 76.3 reduce-scatter.1

commit v7 on v6

--- a/solution.py
+++ b/solution.py
@@ -71,165 +71,6 @@
 
 def lanes(head):
     return pl.ds(pl.multiple_of(head * HEAD_DIM, HEAD_DIM), HEAD_DIM)
-
-
-def to_heads(owned, shared, heads, members, collective_id):
-    rows = (owned + shared)[0].shape[0]
-    n_owned, n_shared = len(owned), len(shared)
-    count = n_owned + n_shared
-
-    def kernel(*refs):
-        ins, outs = refs[:count], refs[count : 2 * count]
-        local_sem, send_sem, recv_sem, fwd_send, fwd_recv = refs[2 * count :]
-        me, group, member, mp = head_place(heads, members)
-
-        def dest(array, source):
-            place = (source // members) if array < n_owned else source
-            return outs[array].at[pl.ds(pl.multiple_of(place * rows, rows), rows)]
-
-        head_peers = [((group ^ o) * members + member, mp) for o in range(1, heads)]
-        pair_peers = [(group * members + (member ^ o), mp) for o in range(1, members)]
-        greet(head_peers + pair_peers)
-        order = list(range(n_owned, count)) + list(range(n_owned))
-        sends, locals_, forwards = {}, [], []
-        for a in order:
-            for o in range(1, heads):
-                copy = remote(ins[a].at[:, lanes(group ^ o)], dest(a, me), send_sem.at[a, o],
-                              recv_sem.at[a, o], head_peers[o - 1])
-                copy.start()
-                sends[a, o] = copy
-        for a in range(count):
-            copy = pltpu.make_async_copy(ins[a].at[:, lanes(group)], dest(a, me), local_sem.at[a])
-            copy.start()
-            locals_.append(copy)
-        for a in range(n_owned, count):
-            for o in range(heads):
-                source = (group ^ o) * members + member
-                if o:
-                    sends[a, o].wait_recv()
-                for p in range(1, members):
-                    piece = ins[a].at[:, lanes(group)] if o == 0 else dest(a, source)
-                    copy = remote(piece, dest(a, source), fwd_send.at[a - n_owned, o, p],
-                                  fwd_recv.at[a - n_owned, o, p], pair_peers[p - 1])
-                    copy.start()
-                    forwards.append(copy)
-        for copy in locals_:
-            copy.wait()
-        for (a, o), copy in sends.items():
-            copy.wait_send()
-            if a < n_owned:
-                copy.wait_recv()
-        for copy in forwards:
-            copy.wait()
-
-    total = rows * lax.axis_size("dp")
-    shapes = [jax.ShapeDtypeStruct((heads * rows, HEAD_DIM), a.dtype) for a in owned]
-    shapes += [jax.ShapeDtypeStruct((total, HEAD_DIM), a.dtype) for a in shared]
-    dma = pltpu.SemaphoreType.DMA
-    return pl.pallas_call(
-        kernel,
-        out_shape=shapes,
-        in_specs=[ANY] * count,
-        out_specs=[ANY] * count,
-        scratch_shapes=[
-            dma((count,)), dma((count, heads)), dma((count, heads)),
-            dma((max(n_shared, 1), heads, members)), dma((max(n_shared, 1), heads, members)),
-        ],
-        compiler_params=pltpu.CompilerParams(collective_id=collective_id, has_side_effects=True),
-        cost_estimate=pl.CostEstimate(flops=0, bytes_accessed=100 * MIB, transcendentals=0),
-    )(*owned, *shared)
-
-
-def to_rows(owned, shared, heads, members, collective_id):
-    rows = owned[0].shape[0] // heads
-    n_owned, n_shared = len(owned), len(shared)
-    count = n_owned + n_shared
-
-    def kernel(*refs):
-        ins, outs = refs[:count], refs[count : 2 * count]
-        local_sem, send_sem, recv_sem, own_sem, part_send, part_recv = refs[2 * count : 2 * count + 6]
-        me, group, member, mp = head_place(heads, members)
-        head_peers = [((group ^ o) * members + member, mp) for o in range(1, heads)]
-        pair_peers = [(group * members + (member ^ o), mp) for o in range(1, members)]
-        greet(head_peers + pair_peers)
-        if n_shared:
-            own, parts, total = refs[2 * count + 6 :]
-        copies, pending = [], {}
-
-        def part(array, o, who):
-            first = pl.multiple_of(((group ^ o) * members + who) * rows, rows)
-            return ins[array].at[pl.ds(first, rows)]
-
-        for s in range(n_shared):
-            for o in range(heads):
-                copy = pltpu.make_async_copy(part(n_owned + s, o, member), own.at[s, o], own_sem.at[s, o])
-                copy.start()
-                pending[s, o, 0] = copy
-                for p in range(1, members):
-                    copy = remote(part(n_owned + s, o, member ^ p), parts.at[s, o, p - 1],
-                                  part_send.at[s, o, p], part_recv.at[s, o, p], pair_peers[p - 1])
-                    copy.start()
-                    pending[s, o, p] = copy
-        for a in range(n_owned):
-            for o in range(heads):
-                piece = ins[a].at[pl.ds(pl.multiple_of((group ^ o) * rows, rows), rows)]
-                place = outs[a].at[:, lanes(group)]
-                if o:
-                    copy = remote(piece, place, send_sem.at[a, o], recv_sem.at[a, o], head_peers[o - 1])
-                else:
-                    copy = pltpu.make_async_copy(piece, place, local_sem.at[a])
-                copy.start()
-                copies.append(copy)
-        for o in list(range(1, heads)) + [0]:
-            for s in range(n_shared):
-                for p in range(members):
-                    if p:
-                        pending[s, o, p].wait_recv()
-                    else:
-                        pending[s, o, p].wait()
-                value = own[s, o].astype(jnp.float32)
-                for p in range(1, members):
-                    value = value + parts[s, o, p - 1].astype(jnp.float32)
-                total[s, o] = value.astype(total.dtype)
-                a = n_owned + s
-                place = outs[a].at[:, lanes(group)]
-                if o:
-                    copy = remote(total.at[s, o], place, send_sem.at[a, o], recv_sem.at[a, o], head_peers[o - 1])
-                else:
-                    copy = pltpu.make_async_copy(total.at[s, o], place, local_sem.at[a])
-                copy.start()
-                copies.append(copy)
-        for s in range(n_shared):
-            for o in range(heads):
-                for p in range(1, members):
-                    pending[s, o, p].wait_send()
-        for copy in copies:
-            copy.wait()
-
-    dma = pltpu.SemaphoreType.DMA
-    slots = max(n_shared, 1)
-    scratch = [
-        dma((count,)), dma((count, heads)), dma((count, heads)),
-        dma((slots, heads)), dma((slots, heads, members)), dma((slots, heads, members)),
-    ]
-    if n_shared:
-        kind = shared[0].dtype
-        scratch += [
-            pltpu.VMEM((n_shared, heads, rows, HEAD_DIM), kind),
-            pltpu.VMEM((n_shared, heads, members - 1, rows, HEAD_DIM), kind),
-            pltpu.VMEM((n_shared, heads, rows, HEAD_DIM), kind),
-        ]
-    return pl.pallas_call(
-        kernel,
-        out_shape=[jax.ShapeDtypeStruct((rows, heads * HEAD_DIM), a.dtype) for a in owned + shared],
-        in_specs=[ANY] * count,
-        out_specs=[ANY] * count,
-        scratch_shapes=scratch,
-        compiler_params=pltpu.CompilerParams(
-            collective_id=collective_id, has_side_effects=True, vmem_limit_bytes=48 * MIB
-        ),
-        cost_estimate=pl.CostEstimate(flops=0, bytes_accessed=100 * MIB, transcendentals=0),
-    )(*owned, *shared)
 
 
 def sequence_of(place, lengths):
@@ -493,8 +334,8 @@
 
         return exists, exists & there, copy
 
-    def advance(self, step, piece, also=True):
-        for way in range(2):
+    def advance(self, step, piece, also=True, ways=(0, 1)):
+        for way in ways:
             if step:
                 exists, _, _ = self.hop(way, step, piece)
                 _, _, earlier = self.hop(way, step - 1, piece)
@@ -661,6 +502,7 @@
 
 
 AHEAD = 1
+QUARTERS = 4
 MAX_PIECES = 16
 SKEW = 1
 
@@ -681,7 +523,8 @@
 ):
     rows, width = hidden.shape
     dp_count, mp_count = lax.axis_size("dp"), lax.axis_size("mp")
-    chips, pieces = dp_count // 2, pieces_of(rows)
+    chips, pieces, half = dp_count // 2, pieces_of(rows), rows // 2
+    half_pieces = pieces_of(half)
     group_rows, depth, columns = mp_count * rows, projections[0].shape[0], projections[0].shape[1]
     each = width // dp_count // 128
     tall = [v.shape[0] // 128 for v in vectors]
@@ -693,10 +536,10 @@
     def kernel(lengths_ref, order_ref, hidden_ref, upstream_ref, *refs):
         given, refs = refs[: len(vectors)], refs[len(vectors) :]
         weight_refs, out_weight_ref = refs[:kinds], refs[kinds]
-        normed, all_vectors, weights, all_out, shared, queries, branch, live = refs[kinds + 1 : kinds + 9]
+        normed, all_vectors, weights, all_out, shared, queries, branch, live, half_rows = refs[kinds + 1 : kinds + 10]
         parts, refs = refs[-len(vectors) :], refs[: -len(vectors)]
         (vector_ref, upstream, load_sem, raw, stage, gains, biases, line_send, line_recv, row_sem, own_sem, cross_send, cross_recv, core_send, core_recv,
-         head_local, head_send, head_recv, pair_send, pair_recv) = refs[kinds + 9 :]
+         head_local, head_send, head_recv, pair_send, pair_recv, half_send, half_recv, half_sem) = refs[kinds + 10 :]
         dp, mp = lax.axis_index("dp"), lax.axis_index("mp")
         loads = [pltpu.make_async_copy(given[k], parts[k], load_sem.at[k]) for k in range(len(vectors))]
         loads.append(pltpu.make_async_copy(upstream_ref, upstream, load_sem.at[len(vectors)]))
@@ -715,6 +558,22 @@
         greet_all([(dp ^ o, mp) for o in offsets], dp, mp, mp_count)
         line = LineGather(hidden_ref, raw, rows, pieces, line_send, line_recv, dp, mp, mp_count)
 
+        behind = LineGather(branch, half_rows, half, half_pieces, half_send, half_recv, dp, mp, mp_count)
+
+        def follow(step):
+            for way, steps in ((0, mp), (1, mp_count - 1 - mp)):
+
+                @pl.loop(0, half_pieces)
+                def _(piece):
+                    behind.advance(0, piece, steps == step, (way,))
+
+        between = (mp > 0) & (mp < mp_count - 1)
+
+        def hand_half(step, also=True):
+            @pl.loop(0, half_pieces)
+            def _(piece):
+                behind.advance(step, piece, also)
+
         def source(array):
             return (list(weight_refs) + [out_weight_ref, vector_ref])[array]
 
@@ -757,6 +616,10 @@
             live[span] = (lax.broadcasted_iota(jnp.int32, (BLOCK, 128), 0) < valid).astype(jnp.float32)
             keep = lax.broadcasted_iota(jnp.int32, (BLOCK, width), 0) < valid
             branch[span] = jnp.where(keep, upstream[span].astype(jnp.float32), 0.0).astype(branch.dtype)
+        own_half = pltpu.make_async_copy(
+            branch.at[pl.ds(0, half)], half_rows.at[pl.ds(pl.multiple_of(mp * half, half), half)], half_sem)
+        own_half.start()
+        follow(0)
         own_rows = pltpu.make_async_copy(hidden_ref, raw.at[block_span(mp)], row_sem)
         own_rows.start()
         for array in first_to_last:
@@ -852,6 +715,7 @@
             def _(piece):
                 line.advance(step, piece)
 
+            follow(step)
             if step == 1:
                 spread(kinds + 1)
                 settle(kinds + 1)
@@ -880,10 +744,16 @@
         def _(piece):
             line.advance(last - 1 if last == 1 else last, piece)
 
+            @pl.when(piece >= pieces - half_pieces)
+            def _():
+                behind.advance(1, piece - (pieces - half_pieces), between)
+
             @pl.when(piece < tiles)
             def _():
                 each_block(0, last - 1, lambda block: project(piece, block))
 
+        for step in range(2, last):
+            hand_half(step, between)
         each_block(last, last, norm)
 
         @pl.loop(0, tiles)
@@ -892,7 +762,12 @@
 
         each_block(0, last - 1, hand_on)
         each_block(last, last, hand_on)
+        for step in range(1, last):
+            hand_half(step, jnp.logical_not(between))
+        hand_half(last)
         line.finish()
+        behind.finish()
+        own_half.wait()
         settle(kinds)
         for array in first_to_last:
             for o in range(chips):
@@ -928,9 +803,10 @@
             jax.ShapeDtypeStruct((heads * group_rows, HEAD_DIM), bf16),
             jax.ShapeDtypeStruct((rows, width), bf16),
             jax.ShapeDtypeStruct((rows, 128), f32),
+            jax.ShapeDtypeStruct((mp_count * half, width), bf16),
         ],
         in_specs=[SMEM, SMEM] + [ANY] * (len(vectors) + kinds + 3),
-        out_specs=[VMEM, VMEM, VMEM, ANY, ANY, ANY, VMEM, VMEM],
+        out_specs=[VMEM, VMEM, VMEM, ANY, ANY, ANY, VMEM, VMEM, ANY],
         scratch_shapes=[
             pltpu.VMEM((slab, 128), f32),
             pltpu.VMEM((rows, width), bf16),
@@ -945,6 +821,7 @@
         + [dma((arrays, chips)) for _ in range(4)]
         + [dma((kinds, mp_count)), dma((kinds, heads, mp_count)), dma((kinds, heads, mp_count))]
         + [dma((2, heads, mp_count, members)) for _ in range(2)]
+        + LineGather.semaphores(mp_count, half_pieces) + [dma(())]
         + [pltpu.VMEM(v.shape, v.dtype) for v in vectors],
         compiler_params=pltpu.CompilerParams(
             collective_id=collective_id, has_side_effects=True, vmem_limit_bytes=63 * MIB),
@@ -952,24 +829,66 @@
     )(lengths, order, hidden, output_grad, *vectors, *projections, out_weight)
 
 
-def reduce_norm_gather(part, hidden, out_bias, gain, shift, shards, collective_id):
+def mix_norm_gather(mixed, out_weight, hidden, out_bias, gain, shift, shards, heads, members, collective_id):
     dp_count, mp_count = lax.axis_size("dp"), lax.axis_size("mp")
     chips, count = dp_count // 2, len(shards)
     rows, width = hidden.shape
     pieces = pieces_of(rows)
-    size = rows // pieces
-
+    size, columns, group_rows = rows // pieces, heads * HEAD_DIM, mp_count * rows
+    quarter, per_quarter = rows // QUARTERS, pieces // QUARTERS
+    slice_rows = width // per_quarter
+    offsets = sorted({2 * o for o in range(1, chips)} | {1} | {o * members for o in range(1, heads)})
+    mixed = mixed.reshape(heads, mp_count, rows, HEAD_DIM)
     turns = pieces + 2 * SKEW * (mp_count - 1)
 
-    def kernel(part_ref, hidden_ref, bias_ref, gain_ref, shift_ref, *refs):
-        shard_refs, (residual_ref, full_ref), whole_refs = refs[:count], refs[count : count + 2], refs[count + 2 : 2 * count + 2]
-        total, normed, flows, red_send, red_recv, line_send, line_recv, own_sem, *weight_sems = refs[2 * count + 2 :]
+    def kernel(mixed_ref, out_hbm, hidden_ref, bias_ref, gain_ref, shift_ref, *refs):
+        shard_refs, (residual_ref, landed, full_ref), refs = refs[:count], refs[count : count + 3], refs[count + 3 :]
+        whole_refs, refs = refs[:count], refs[count:]
+        (part, out_rows, load_sem, local_sem, head_send, head_recv,
+         total, normed, flows, red_send, red_recv, line_send, line_recv, own_sem, *weight_sems) = refs
         dp, mp = lax.axis_index("dp"), lax.axis_index("mp")
-        greet_all([(dp ^ (2 * o), mp) for o in range(1, chips)] + [(dp ^ 1, mp)], dp, mp, mp_count)
+        group, member = dp // members, dp % members
+        greet_all([(dp ^ o, mp) for o in offsets], dp, mp, mp_count)
+
+        def landing(k, head):
+            return landed.at[:, pl.ds(k * quarter, quarter), lanes(head)]
+
+        def head_copy(o, k):
+            return remote(mixed_ref.at[group ^ o, :, pl.ds(k * quarter, quarter)], landing(k, group),
+                          head_send.at[o, k], head_recv.at[o, k], ((group ^ o) * members + member, mp))
+
+        def local_copy(k):
+            return pltpu.make_async_copy(mixed_ref.at[group, :, pl.ds(k * quarter, quarter)], landing(k, group),
+                                         local_sem.at[k])
+
+        def arrived(k):
+            for o in range(1, heads):
+                head_copy(o, k).wait_recv()
+            local_copy(k).wait()
+
+        def project(k, first, count):
+            span = pl.ds(pl.multiple_of(k * quarter, quarter), quarter)
+            left = landed[:, span].reshape(mp_count * quarter, columns)
+            features = pl.ds(pl.multiple_of(first, count), count)
+            value = contract_last(left, out_rows[features]).astype(part.dtype)
+            for block in range(mp_count):
+                at = pl.ds(pl.multiple_of(block * rows + k * quarter, quarter), quarter)
+                part[at, features] = value[block * quarter : (block + 1) * quarter]
+
+        load = pltpu.make_async_copy(out_hbm, out_rows, load_sem)
+        load.start()
+        for k in range(QUARTERS):
+            for o in range(1, heads):
+                head_copy(o, k).start()
+            local_copy(k).start()
         weights = ShardGather(shard_refs, whole_refs, shards[0].shape[0], *weight_sems, dp, mp, chips)
         weights.begin()
-        reduce = LineReduce(part_ref, flows, rows, pieces, red_send, red_recv, dp, mp, mp_count)
+        reduce = LineReduce(part, flows, rows, pieces, red_send, red_recv, dp, mp, mp_count)
         gather = LineGather(normed, full_ref, rows, pieces, line_send, line_recv, dp, mp, mp_count)
+        load.wait()
+        arrived(0)
+        for portion in range(per_quarter):
+            project(0, portion * slice_rows, slice_rows)
         for piece in range(AHEAD):
             reduce.begin(piece)
 
@@ -980,6 +899,16 @@
                 @pl.when(turn == turns - 1 - 6 * (count - 1 - array))
                 def _():
                     weights.spread(array)
+
+            for k in range(1, QUARTERS):
+
+                @pl.when(turn == (k - 1) * per_quarter)
+                def _():
+                    arrived(k)
+
+            @pl.when(turn < (QUARTERS - 1) * per_quarter)
+            def _():
+                project(turn // per_quarter + 1, (turn % per_quarter) * slice_rows, slice_rows)
 
             reduce.begin(jnp.minimum(turn + AHEAD, pieces - 1), turn + AHEAD < pieces)
             reduce.advance(turn)
@@ -1006,57 +935,83 @@
         gather.finish()
         own.wait()
         weights.finish()
-
+        for k in range(QUARTERS):
+            for o in range(1, heads):
+                head_copy(o, k).wait_send()
+
+    dma = pltpu.SemaphoreType.DMA
     return pl.pallas_call(
         kernel,
         out_shape=[
             jax.ShapeDtypeStruct((rows, width), jnp.float32),
-            jax.ShapeDtypeStruct((mp_count * rows, width), jnp.bfloat16),
+            jax.ShapeDtypeStruct((mp_count, rows, columns), jnp.bfloat16),
+            jax.ShapeDtypeStruct((group_rows, width), jnp.bfloat16),
         ]
         + [jax.ShapeDtypeStruct((dp_count * a.shape[0], a.shape[1]), a.dtype) for a in shards],
-        in_specs=[VMEM] * 5 + [ANY] * count,
-        out_specs=[VMEM, ANY] + [ANY] * count,
-        scratch_shapes=[pltpu.VMEM((size, width), jnp.float32), pltpu.VMEM((rows, width), jnp.bfloat16)]
+        in_specs=[ANY] * 2 + [VMEM] * 4 + [ANY] * count,
+        out_specs=[VMEM, VMEM, ANY] + [ANY] * count,
+        scratch_shapes=[
+            pltpu.VMEM((group_rows, width), jnp.bfloat16), pltpu.VMEM((width, columns), jnp.bfloat16),
+            dma(()), dma((QUARTERS,)), dma((heads, QUARTERS)), dma((heads, QUARTERS)),
+        ]
+        + [pltpu.VMEM((size, width), jnp.float32), pltpu.VMEM((rows, width), jnp.bfloat16)]
         + LineReduce.scratch(mp_count, rows, width, pieces) + LineGather.semaphores(mp_count, pieces)
         + [pltpu.SemaphoreType.DMA(())] + ShardGather.semaphores(count, chips),
         compiler_params=pltpu.CompilerParams(
             collective_id=collective_id, has_side_effects=True, vmem_limit_bytes=63 * MIB),
         cost_estimate=pl.CostEstimate(flops=0, bytes_accessed=300 * MIB, transcendentals=0),
-    )(part, hidden, out_bias, gain, shift, *shards)
-
-
-def reduce_back_gather(part, residual, branch_two, gain, pairs, collective_id):
+    )(mixed, out_weight, hidden, out_bias, gain, shift, *shards)
+
+
+def reduce_back_gather(
+    part, residual, branch_two, gain, halves, pairs, down_weight, out_weight, heads, members, collective_id
+):
     dp_count, mp_count = lax.axis_size("dp"), lax.axis_size("mp")
     chips, count = dp_count // 2, len(pairs)
     rows, width = residual.shape
+    half = rows // 2
     pieces = pieces_of(rows)
     size, depth = rows // pieces, width // dp_count
     units = pairs[0][1].shape[1]
     turns = pieces + 2 * SKEW * (mp_count - 1)
     each = dp_count // 4
     busy = count * dp_count // each
-    assert 1 + busy <= turns
+    feed_slices = 8
+    feed_rows = width // feed_slices
+    assert 1 + busy + feed_slices <= turns
+    quarter, per_quarter, columns = rows // QUARTERS, pieces // QUARTERS, heads * HEAD_DIM
+    group_rows = mp_count * rows
+    offsets = sorted({2 * o for o in range(1, chips)} | {1} | {o * members for o in range(1, heads)})
 
     def kernel(part_ref, residual_ref, branch_ref, gain_ref, *refs):
-        operands, refs = refs[: 2 * count], refs[2 * count :]
-        (grad_ref, sums_ref, full_ref), terms, refs = refs[:3], refs[3 : 3 + count], refs[3 + count :]
+        operands, down_ref, out_hbm, refs = refs[: 2 * count + 1], refs[2 * count + 1], refs[2 * count + 2], refs[2 * count + 3 :]
+        (grad_ref, sums_ref, full_ref, feed_ref, heads_ref), terms, refs = refs[:5], refs[5 : 5 + count], refs[5 + count :]
         loaded, refs = refs[: 2 * count], refs[2 * count :]
-        (total, low, kept, slices, from_partner, chip_sum, load_sem, keep_sem, pair_send, pair_recv, cross_send, cross_recv,
+        (credit, down_rows, down_sem, fed, fed_sem, out_rows, out_sem, gathered, gathered_sem, stage,
+         stage_sem, head_send, head_recv, half_sem, total, low, kept, slices, from_partner, chip_sum, load_sem, keep_sem, pair_send, pair_recv, cross_send, cross_recv,
          flows, red_send, red_recv, line_send, line_recv, own_sem) = refs
         dp, mp = lax.axis_index("dp"), lax.axis_index("mp")
         partner = (dp ^ 1, mp)
-        greet_all([(dp ^ (2 * o), mp) for o in range(1, chips)] + [partner], dp, mp, mp_count)
+        group, member = dp // members, dp % members
+        greet_all([(dp ^ o, mp) for o in offsets], dp, mp, mp_count)
         reduce = LineReduce(part_ref, flows, rows, pieces, red_send, red_recv, dp, mp, mp_count)
         gather = LineGather(low, full_ref, rows, pieces, line_send, line_recv, dp, mp, mp_count)
         for piece in range(AHEAD):
             reduce.begin(piece)
-        loads = [pltpu.make_async_copy(operands[k], loaded[k], load_sem.at[k]) for k in range(2 * count)]
-        for copy in loads:
+        loads = [[] for _ in range(count)]
+        for h in range(2):
+            for b in range(mp_count):
+                to = pl.ds(b * rows + h * half, half)
+                loads[0].append(pltpu.make_async_copy(
+                    operands[h].at[pl.ds(b * half, half)], loaded[0].at[to], half_sem.at[h, b]))
+        for index in range(1, 2 * count):
+            loads[index // 2].append(pltpu.make_async_copy(operands[index + 1], loaded[index], load_sem.at[index]))
+        for copy in loads[0] + loads[1]:
             copy.start()
         sums_ref[...] = jnp.zeros_like(sums_ref)
 
         def pair(mat, o):
-            return remote(slices.at[o], from_partner.at[mat, o], pair_send.at[mat, o], pair_recv.at[mat, o], partner)
+            return remote(slices.at[o], from_partner.at[o], pair_send.at[mat, o], pair_recv.at[mat, o], partner)
 
         def cross(mat, o, peer):
             return remote(chip_sum.at[mat, o - 1], terms[mat].at[o], cross_send.at[mat, o], cross_recv.at[mat, o],
@@ -1073,13 +1028,16 @@
             def _():
                 if mat:
                     pair(mat - 1, o).wait_send()
+                    pl.semaphore_wait(credit, 1)
                 slices[o] = value.astype(slices.dtype)
                 pair(mat, o).start()
 
             @pl.when(mine)
             def _():
                 pair(mat, o).wait_recv()
-                both = (value + from_partner[mat, o].astype(jnp.float32)).astype(slices.dtype)
+                both = (value + from_partner[o].astype(jnp.float32)).astype(slices.dtype)
+                if mat < count - 1:
+                    pl.semaphore_signal(credit, inc=1, device_id=partner, device_id_type=MESH)
 
                 @pl.when(o == 0)
                 def _():
@@ -1090,6 +1048,68 @@
                 def _():
                     chip_sum[mat, o - 1] = both
                     cross(mat, o, owner).start()
+
+        def down_load(index):
+            at = pl.ds(pl.multiple_of(index * feed_rows, feed_rows), feed_rows)
+            return pltpu.make_async_copy(down_ref.at[at], down_rows.at[index % 2], down_sem.at[index % 2])
+
+        def feed_store(index):
+            at = pl.ds(pl.multiple_of(index * feed_rows, feed_rows), feed_rows)
+            return pltpu.make_async_copy(fed.at[index % 2], feed_ref.at[:, at], fed_sem.at[index % 2])
+
+        def feed_slice(index):
+            down_load(index).wait()
+
+            @pl.when(index + 1 < feed_slices)
+            def _():
+                down_load(index + 1).start()
+
+            @pl.when(index >= 2)
+            def _():
+                feed_store(index - 2).wait()
+
+            fed[index % 2] = contract_last(loaded[1][...], down_rows[index % 2]).astype(fed.dtype)
+            feed_store(index).start()
+
+        def rows_load(k, block, own):
+            source = low.at[pl.ds(k * quarter, quarter)] if own else full_ref.at[
+                pl.ds(pl.multiple_of(block * rows + k * quarter, quarter), quarter)]
+            return pltpu.make_async_copy(source, gathered.at[block], gathered_sem.at[block])
+
+        def head_copy(o, k):
+            span = pl.ds(k * quarter, quarter)
+            return remote(stage.at[:, span, lanes(group ^ o)], heads_ref.at[group, :, span], head_send.at[o, k],
+                          head_recv.at[o, k], ((group ^ o) * members + member, mp))
+
+        def local_copy(k):
+            span = pl.ds(k * quarter, quarter)
+            return pltpu.make_async_copy(stage.at[:, span, lanes(group)], heads_ref.at[group, :, span], stage_sem.at[k])
+
+        def to_heads(k):
+            for block in range(mp_count):
+                for own in (True, False):
+
+                    @pl.when((mp == block) if own else (mp != block))
+                    def _():
+                        rows_load(k, block, own).start()
+
+            for block in range(mp_count):
+                for own in (True, False):
+
+                    @pl.when((mp == block) if own else (mp != block))
+                    def _():
+                        rows_load(k, block, own).wait()
+
+            value = jnp.dot(gathered[...].reshape(mp_count * quarter, width), out_rows[...],
+                            preferred_element_type=jnp.float32)
+            stage[:, k * quarter : (k + 1) * quarter] = value.reshape(mp_count, quarter, columns).astype(stage.dtype)
+            for o in range(1, heads):
+                head_copy(o, k).start()
+            local_copy(k).start()
+
+        out_load = pltpu.make_async_copy(out_hbm, out_rows, out_sem)
+        out_load.start()
+        down_load(0).start()
 
         @pl.loop(0, turns)
         def _(turn):
@@ -1120,7 +1140,7 @@
 
                 @pl.when(turn == 1 + mat * busy // count)
                 def _():
-                    for copy in loads[2 * mat : 2 * mat + 2]:
+                    for copy in loads[mat]:
                         copy.wait()
 
                 first = turn - 1 - mat * busy // count
@@ -1129,12 +1149,30 @@
                 def _():
                     for i in range(each):
                         weight_slice(mat, first * each + i)
+
+            @pl.when((turn >= 1 + busy) & (turn < 1 + busy + feed_slices))
+            def _():
+                feed_slice(turn - 1 - busy)
+
+            for k in range(QUARTERS):
+
+                @pl.when(turn == (k + 1) * per_quarter - 1 + 2 * SKEW * (mp_count - 1))
+                def _():
+                    if k == 0:
+                        out_load.wait()
+                    to_heads(k)
 
         own = pltpu.make_async_copy(low, full_ref.at[pl.ds(pl.multiple_of(mp * rows, rows), rows)], own_sem)
         own.start()
         reduce.finish()
         gather.finish()
         own.wait()
+        for index in range(feed_slices - 2, feed_slices):
+            feed_store(index).wait()
+        for k in range(QUARTERS):
+            local_copy(k).wait()
+            for o in range(1, heads):
+                head_copy(o, k).wait()
         for mat in range(count):
             pltpu.make_async_copy(kept.at[mat], terms[mat].at[0], keep_sem.at[mat]).wait()
             for o in range(chips):
@@ -1145,24 +1183,34 @@
 
     bf16, f32 = jnp.bfloat16, jnp.float32
     dma = pltpu.SemaphoreType.DMA
-    flat = [array for two in pairs for array in two]
+    flat = [array for two in pairs for array in two][1:]
     return pl.pallas_call(
         kernel,
         out_shape=[
             jax.ShapeDtypeStruct((rows, width), f32),
             jax.ShapeDtypeStruct((8, width), f32),
-            jax.ShapeDtypeStruct((mp_count * rows, width), bf16),
+            jax.ShapeDtypeStruct((group_rows, width), bf16),
+            jax.ShapeDtypeStruct((group_rows, width), bf16),
+            jax.ShapeDtypeStruct((heads, mp_count, rows, HEAD_DIM), bf16),
         ]
         + [jax.ShapeDtypeStruct((chips, depth, units), bf16)] * count,
-        in_specs=[VMEM] * 4 + [ANY] * (2 * count),
-        out_specs=[VMEM, VMEM] + [ANY] * (1 + count),
-        scratch_shapes=[pltpu.VMEM(a.shape, a.dtype) for a in flat]
+        in_specs=[VMEM] * 4 + [ANY] * (2 * count + 3),
+        out_specs=[VMEM, VMEM] + [ANY] * (3 + count),
+        scratch_shapes=[pltpu.VMEM((mp_count * rows, width), bf16)] + [pltpu.VMEM(a.shape, a.dtype) for a in flat]
         + [
+            pltpu.SemaphoreType.REGULAR,
+            pltpu.VMEM((2, feed_rows, units), bf16), dma((2,)),
+            pltpu.VMEM((2, group_rows, feed_rows), bf16), dma((2,)),
+            pltpu.VMEM((width, columns), bf16), dma(()),
+            pltpu.VMEM((mp_count, quarter, width), bf16), dma((mp_count,)),
+            pltpu.VMEM((mp_count, rows, columns), bf16), dma((QUARTERS,)),
+            dma((heads, QUARTERS)), dma((heads, QUARTERS)),
+            dma((2, mp_count)),
             pltpu.VMEM((size, width), f32),
             pltpu.VMEM((rows, width), bf16),
             pltpu.VMEM((count, depth, units), bf16),
             pltpu.VMEM((chips, depth, units), bf16),
-            pltpu.VMEM((count, chips, depth, units), bf16),
+            pltpu.VMEM((chips, depth, units), bf16),
             pltpu.VMEM((count, chips - 1, depth, units), bf16),
             dma((2 * count,)), dma((count,)),
         ]
@@ -1172,10 +1220,7 @@
         compiler_params=pltpu.CompilerParams(
             collective_id=collective_id, has_side_effects=True, vmem_limit_bytes=63 * MIB),
         cost_estimate=pl.CostEstimate(flops=40 << 30, bytes_accessed=300 * MIB, transcendentals=0),
-    )(part, residual, branch_two, gain, *flat)
-
-
-QUARTERS = 4
+    )(part, residual, branch_two, gain, *halves, *flat, down_weight, out_weight)
 
 
 def finish_back(query_grad, key_part, value_part, weights, normed, residual_grad, hidden, gain, out_part, vectors, heads, members,
@@ -1482,21 +1527,25 @@
 CHUNK = 256
 
 
-def feed_both_ways(rows_two, branch_rows, up_all, down_all, up_bias):
+def feed_both_ways(rows_two, branch_halves, block, up_all, down_all, up_bias):
     rows, width = rows_two.shape
     units = up_all.shape[1]
     tile = min(UNITS, units)
+    half = block // 2
     half_root = 1.0 / math.sqrt(2.0)
     density_scale = 1.0 / math.sqrt(2.0 * math.pi)
 
-    def kernel(rows_ref, branch_ref, up_ref, down_ref, bias_ref, hidden_ref, grad_ref, column_ref, part_ref, total):
+    def kernel(rows_ref, first_ref, second_ref, up_ref, down_ref, bias_ref, hidden_ref, grad_ref, column_ref, part_ref, total):
         step = pl.program_id(0)
         columns = jnp.zeros((1, tile), jnp.float32)
         up, down = up_ref[...], down_ref[...]
         for first in range(0, rows, CHUNK):
             span = slice(first, first + CHUNK)
             pre = jnp.dot(rows_ref[span], up, preferred_element_type=jnp.float32) + bias_ref[...]
-            upstream = jnp.dot(branch_ref[span], down, preferred_element_type=jnp.float32)
+            upstream = jnp.concatenate([
+                jnp.dot(ref[b * half : (b + 1) * half], down, preferred_element_type=jnp.float32)
+                for b in range(first // block, (first + CHUNK) // block) for ref in (first_ref, second_ref)
+            ], axis=0)
             share = 0.5 + 0.5 * lax.erf(pre * half_root)
             hidden_ref[span] = (pre * share).astype(hidden_ref.dtype)
             slope = share + pre * (density_scale * jnp.exp(-0.5 * pre * pre))
@@ -1531,7 +1580,8 @@
         ],
         in_specs=[
             pl.BlockSpec((rows, width), lambda i: (0, 0)),
-            pl.BlockSpec((rows, width), lambda i: (0, 0)),
+            pl.BlockSpec((rows // 2, width), lambda i: (0, 0)),
+            pl.BlockSpec((rows // 2, width), lambda i: (0, 0)),
             pl.BlockSpec((width, tile), lambda i: (0, i)),
             pl.BlockSpec((width, tile), lambda i: (0, i)),
             pl.BlockSpec((1, tile), lambda i: (0, i)),
@@ -1546,7 +1596,7 @@
         compiler_params=pltpu.CompilerParams(vmem_limit_bytes=60 * MIB),
         cost_estimate=pl.CostEstimate(
             flops=6 * rows * width * units, bytes_accessed=40 * MIB, transcendentals=2 * rows * units),
-    )(rows_two, branch_rows, up_all, down_all, up_bias)
+    )(rows_two, *branch_halves, up_all, down_all, up_bias)
 
 
 def sum_terms(terms):
@@ -1587,7 +1637,7 @@
     plan = (seq_lengths, block_order, block_slot)
 
     vectors = (first_gain, first_shift, query_bias, value_bias, out_bias, second_gain, second_shift, down_bias, up_bias)
-    rows_one, vector_rows, projections, out_all, head_shared, head_queries, branch_two, live = project_first(
+    rows_one, vector_rows, projections, out_all, head_shared, head_queries, branch_two, live, branch_first = project_first(
         hidden_in, output_grad, seq_lengths, block_order, vectors,
         (key_weight, value_weight, query_weight), out_weight, heads_local, members, 0,
     )
@@ -1600,30 +1650,31 @@
     up_each = up_bias.shape[0] // 128
     bias_up = vector_rows[:, 8 * each : 8 * each + up_each].reshape(1, up_bias.shape[0] * dp_count)
 
-    branch_rows_two = whole_rows(branch_two)
+    half = local_rows // 2
+    branch_second = whole_rows(branch_two[half:])
     head_mix, exact_mix, log_total = attend(head_queries, head_shared, *plan, members, blocks_each)
-    (attended_low,) = to_rows([head_mix], [], heads_local, members, 2)
-    out_part = contract_last(attended_low, out_all).astype(jnp.bfloat16)
-    residual, rows_two, up_all, down_all = reduce_norm_gather(
-        out_part, hidden_in, bias_out, gain_two, shift_two, (up_weight, down_weight), 3
+    residual, attended_low, rows_two, up_all, down_all = mix_norm_gather(
+        head_mix, out_all, hidden_in, bias_out, gain_two, shift_two, (up_weight, down_weight), heads_local, members, 3
     )
+    attended_low = attended_low.reshape(group_rows, head_width)
 
     bias_hidden = lax.dynamic_slice_in_dim(bias_up, mp_index * hidden_width, hidden_width, 1)
-    hidden_low, pre_grad, pre_columns, up_part = feed_both_ways(rows_two, branch_rows_two, up_all, down_all, bias_hidden)
-    residual_grad, sums_two, branch_rows_one, down_terms, up_terms = reduce_back_gather(
-        up_part, residual, branch_two, gain_two, ((branch_rows_two, hidden_low), (rows_two, pre_grad)), 4
+    hidden_low, pre_grad, pre_columns, up_part = feed_both_ways(
+        rows_two, (branch_first, branch_second), local_rows, up_all, down_all, bias_hidden
+    )
+    residual_grad, sums_two, branch_rows_one, feed_part, head_grad, down_terms, up_terms = reduce_back_gather(
+        up_part, residual, branch_two, gain_two, (branch_first, branch_second),
+        ((None, hidden_low), (rows_two, pre_grad)), down_all, out_all, heads_local, members, 4,
     )
     down_weight_grad, up_weight_grad = (
         sum_terms(terms) for terms in (down_terms, up_terms)
     )
 
-    hidden_low, branch_rows_one = lax.optimization_barrier((hidden_low, branch_rows_one))
-    feed = row_share(contract_last(hidden_low, down_all))
+    feed = row_share(feed_part)
     result = residual + feed + bias_down
     output = jnp.where(own_valid, result, 0.0).astype(jnp.bfloat16)
 
-    attended_grad = jnp.dot(branch_rows_one, out_all, preferred_element_type=jnp.float32).astype(jnp.bfloat16)
-    (head_grad,) = to_heads([attended_grad], [], heads_local, members, 5)
+    head_grad = head_grad.reshape(heads_local * group_rows, HEAD_DIM)
     head_query_grad, head_key_grad, head_value_grad = attend_back(
         head_queries, head_shared, head_grad, exact_mix, log_total, *plan, members, blocks_each
     )

time: 732 us -> 700 us (0.956)
  matrix products: 32.4 us -> 5.9 us
    pallas_call x3 -> x1, Pallas kernels: 166 us -> 128 us  [mix_norm_gather(): pl.pallas_call(kernel, out_shape=[jax.ShapeDtypeStruct((rows, width), jnp...]
    dot_general x3 -> x0, matrix products: 26.4 us -> none  [the longest x2 20.2 us: contract_last(): lax.dot_general(left, right, (((1,), (1,)), ((), ())), preferred_element_...]
    pallas_call x1, Pallas kernels: 104 us -> 121 us  [project_first(): pl.pallas_call(kernel, out_shape=[jax.ShapeDtypeStruct((group_rows, width...]
  transfers between devices with their start and end apart: 2 -> 2, of which waited for: 0 -> 0; matrix products, arithmetic and copies ran while one was open for 5% -> 4% of each run, Pallas kernels for 53% -> 51%
where the time goes in v7:
time: 700 us; the launch traced here: 693 us
  Pallas kernels  645 us (92%)
  local copies, waits for them, and re-layouts  16.8 us (2%)
  between operations  14.5 us (2%)
  other arithmetic  10.3 us (1%)
    pallas_call x1, Pallas kernels, finish_back(): pl.pallas_call(kernel, out_shape=[jax.ShapeDtypeStruct((rows, width), f32...  138 us
    pallas_call x1, Pallas kernels, reduce_back_gather(): pl.pallas_call(kernel, out_shape=[jax.ShapeDtypeStruct((rows, width), f32...  130 us
    pallas_call x1, Pallas kernels, mix_norm_gather(): pl.pallas_call(kernel, out_shape=[jax.ShapeDtypeStruct((rows, width), jnp...  128 us
    pallas_call x1, Pallas kernels, project_first(): pl.pallas_call(kernel, out_shape=[jax.ShapeDtypeStruct((group_rows, width...  121 us
    pallas_call x1, Pallas kernels, attend_back(): pl.pallas_call(kernel, out_shape=[jax.ShapeDtypeStruct(queries.shape, jnp...  46.4 us
    pallas_call x1, Pallas kernels, feed_both_ways(): pl.pallas_call(kernel, grid=(units // tile,), out_shape=[jax.ShapeDtypeSt...  41.9 us
    pallas_call x1, Pallas kernels, attend(): pl.pallas_call(kernel, out_shape=[jax.ShapeDtypeStruct(queries.shape, jnp...  39.7 us
  transfers between devices with their start and end apart: 2, of which 0 were waited for; matrix products, arithmetic and copies ran while one was open for 4% of the time, Pallas kernels for 51%

profile of v7, /device:TPU:0, one launch (start us, length us, event | category | flops | bytes accessed | tf_op | source)
XLA Modules:
  0.0 692.8 jit_solution(8039292675985113842)
XLA Ops:
  7.2 0.0 all-gather.2.cloned.1.call-start
  7.2 120.8 %shard_map.323 = (bf16[1024,2048]{1,0:T(8,128)(2,1)}, f32[192,128]{1,0:T(8,128)}, bf16[2048,1536]{1,0:T(8,128)(2,1)}, bf16[2048,512]{1,0:T(8,128)(2,1)}, bf16[2,...) custom-call(s32[8]{0:T(128)} %lengths_ref.5, ...), custom_call_target="tpu_custom_call" | custom-call | flops 8589934592 | bytes 262144000 | tf_op jit(solution)/shard_map/pallas_call | solution.py:795
  128.1 1.9 slice.97
  129.9 0.0 all-gather.2.cloned.1.call-update
  130.0 0.0 reduce-scatter.2.cloned.1.call-start
  130.0 0.8 slice.127
  130.8 1.6 fusion.2
  132.4 39.7 %shard_map.324 = (bf16[4096,128]{1,0:T(8,128)(2,1)}, f32[16,128,256]{2,1,0:T(8,128)}, f32[16,1,256]{2,1,0:T(1,128)}) custom-call(s32[8]{0:T(128)} %lengths_ref.5, s32[64]{0:T(128)} %slot_ref.3, bf16[4096,128]{1,0:T(8,128)(2,1)} %get-tuple-element.53.q_ref, bf16[2,8192,128]{2,1,0:T(8,128)(2,1)} %get-tuple-element.54.shared_ref), custom_call_target="tpu_custom_call" | custom-call | flops 8589934592 | bytes 52428800 | tf_op jit(solution)/shard_map/pallas_call | solution.py:194
  172.1 128.3 %shard_map.325 = (f32[256,2048]{1,0:T(8,128)}, bf16[4,256,512]{2,1,0:T(8,128)(2,1)}, bf16[1024,2048]{1,0:T(8,128)(2,1)}, bf16[2048,2048]{1,0:T(8,128)(2,1)}, bf16[2048,2048]{1,0:T(8,128)(2,1)}) custom-call(bf16[4,4,256,128]{3,2,1,0:T(8,128)(2,1)} %bitcast.43, bf16[2048,512]{1,0:T(8,128)(2,1)} %get-tuple-element.56.out_hbm.refs_6_, ...), custom_call_target="tpu_custom_call" | custom-call | bytes 314572800 | tf_op jit(solution)/shard_map/pallas_call | solution.py:943
  300.4 0.6 constant_dynamic-slice_fusion.bias_ref
  301.0 0.0 all-gather.2.cloned.1.call-done.second_ref.refs_1_
  301.0 41.9 %shard_map.326 = (bf16[1024,2048]{1,0:T(8,128)(2,1)}, bf16[1024,2048]{1,0:T(8,128)(2,1)}, f32[1,2048]{1,0:T(1,128)}, bf16[1024,2048]{1,0:T(8,128)(2,1)}) custom-call(bf16[1024,2048]{1,0:T(8,128)(2,1)} %get-tuple-element.59.rows_ref.refs_3_, bf16[512,2048]{1,0:T(8,128)(2,1)} %get-tuple-element.60.first_ref.refs_0_, ...), custom_call_target="tpu_custom_call" | custom-call | flops 25769803776 | bytes 41943040 | tf_op jit(solution)/shard_map/pallas_call | solution.py:1572
  342.8 130.1 %shard_map.327 = (f32[256,2048]{1,0:T(8,128)}, f32[8,2048]{1,0:T(8,128)}, bf16[1024,2048]{1,0:T(8,128)(2,1)}, bf16[1024,2048]{1,0:T(8,128)(2,1)}, bf16[4,4,256,1...) custom-call(bf16[1024,2048]{1,0:T(8,128)(2,1)} %get-tuple-element.64.part_ref, ...), custom_call_target="tpu_custom_call" | custom-call | flops 42949672960 | bytes 314572800 | tf_op jit(solution)/shard_map/pallas_call | solution.py:1187
  472.9 0.0 copy-start.4
  472.9 0.0 copy-start
  472.9 0.0 copy-start.5
  473.0 0.0 copy-start.6
  473.0 0.0 reduce-scatter.2.cloned.1.call-update
  473.0 0.8 copy-done.4
  473.8 0.1 fusion
  473.9 0.3 copy-done
  474.2 0.2 convert_reduce_fusion
  474.4 0.0 copy-done.5
  474.4 0.5 dynamic_update_slice.3
  474.9 1.0 fusion.3
  475.9 1.9 concatenate.7.vector_ref
  477.8 0.0 copy-done.6
  477.8 5.9 convolution_convert_fusion.out_ref
  483.7 46.4 %shard_map.328 = (bf16[4096,128]{1,0:T(8,128)(2,1)}, bf16[8192,128]{1,0:T(8,128)(2,1)}, bf16[8192,128]{1,0:T(8,128)(2,1)}) custom-call(s32[8]{0:T(128)} %lengths_ref.5, s32[64]{0:T(128)} %slot_ref.3, bf16[4096,128]{1,0:T(8,128)(2,1)} %get-tuple-element.53.q_ref, bf16[2,8192,128]{2,1,0:T(8,128)(2,1)} %get-tuple-element.54.shared_ref, ...), custom_call_target="tpu_custom_call" | custom-call | flops 21474836480 | bytes 104857600 | tf_op jit(solution)/shard_map/pallas_call | solution.py:272
  530.1 138.2 %shard_map.329 = (f32[256,2048]{1,0:T(8,128)}, f32[256,1536]{1,0:T(8,128)}, f32[256,512]{1,0:T(8,128)}, f32[24,128]{1,0:T(8,128)}) custom-call(bf16[4,4,256,128]{3,2,1,0:T(8,128)(2,1)} %bitcast.63, bf16[8,4,256,128]{3,2,1,0:T(8,128)(2,1)} %bitcast.60, bf16[8,4,256,128]{3,2,1,0:T(8,128)(2,1)} %bitcast.61, bf16[2048,1536]{1,0:T(8,128)(2,1)} %get-tuple-element.74.weights_hbm, ...), custom_call_target="tpu_custom_call" | custom-call | flops 21474836480 | bytes 314572800 | tf_op jit(solution)/shard_map/pallas_call | solution.py:1490
  668.3 1.3 slice_bitcast_fusion
  669.6 1.4 slice_bitcast_fusion.1
  671.0 2.5 fusion.1
  673.5 0.0 copy-start.1
  673.5 7.3 %add_bitcast_fusion = (f32[256,2048]{1,0:T(8,128)}, f32[256,2048]{1,0:T(8,128)}) fusion(bf16[4,256,2048]{2,1,0:T(8,128)(2,1)} %get-tuple-element.86, bf16[4,256,2048]{2,1,0:T(8,128)(2,1)} %get-tuple-element.85), kind=kLoop, calls=%fused_computation.1 | loop fusion | flops 7340032 | bytes 12582912 | tf_op jit(solution)/shard_map/add | solution.py:1603
  680.8 0.0 reduce-scatter.2.cloned.1.call-done
  680.8 0.0 copy-done.1
  680.8 0.0 copy-start.2
  680.8 2.7 select_convert_fusion
  683.5 0.0 copy-done.2
  683.5 0.0 copy-start.3
  683.5 1.3 copy.40
  684.9 0.1 copy-done.3
  684.9 0.8 copy.41
  (2 shorter events, 0.0 us)
Async XLA Ops:
  7.2 293.8 %all-gather.2.cloned.1.call-start = ((), (), s32[]{:S(2)}) async-start(), calls=%async_computation.1 | async-start | bytes 2621440 | tf_op jit(solution)/shard_map/all_gather | solution.py:45
  130.0 550.8 %reduce-scatter.2.cloned.1.call-start = ((), (), s32[]{:S(2)}) async-start(), calls=%async_computation.2 | async-start | bytes 5242880 | tf_op jit(solution)/shard_map/reduce_scatter | solution.py:50
  472.9 0.9 copy-start.4
  472.9 1.3 copy-start
  472.9 1.5 copy-start.5
  473.0 4.9 copy-start.6
  673.5 7.3 %copy-start.1 = (f32[256,2048]{1,0:T(8,128)S(1)}, f32[256,2048]{1,0:T(8,128)}, u32[]{:S(2)}) copy-start(f32[256,2048]{1,0:T(8,128)} %get-tuple-element.58.residual_ref) | copy-start | bytes 6291460
  680.8 2.7 copy-start.2
  683.5 1.4 copy-start.3
Sparse Core Ops, SparseCore 0:
  130.1 45.1 all-gather.1
  473.1 79.6 reduce-scatter.1

commit v8 on v7

--- a/solution.py
+++ b/solution.py
@@ -536,10 +536,12 @@
     def kernel(lengths_ref, order_ref, hidden_ref, upstream_ref, *refs):
         given, refs = refs[: len(vectors)], refs[len(vectors) :]
         weight_refs, out_weight_ref = refs[:kinds], refs[kinds]
-        normed, all_vectors, weights, all_out, shared, queries, branch, live, half_rows = refs[kinds + 1 : kinds + 10]
+        (normed_out, all_vectors, weights_out, all_out, shared, queries, branch, rest, live,
+         half_rows) = refs[kinds + 1 : kinds + 11]
         parts, refs = refs[-len(vectors) :], refs[: -len(vectors)]
         (vector_ref, upstream, load_sem, raw, stage, gains, biases, line_send, line_recv, row_sem, own_sem, cross_send, cross_recv, core_send, core_recv,
-         head_local, head_send, head_recv, pair_send, pair_recv, half_send, half_recv, half_sem) = refs[kinds + 10 :]
+         head_local, head_send, head_recv, pair_send, pair_recv, half_send, half_recv, half_sem,
+         normed, weights, out_sem) = refs[kinds + 11 :]
         dp, mp = lax.axis_index("dp"), lax.axis_index("mp")
         loads = [pltpu.make_async_copy(given[k], parts[k], load_sem.at[k]) for k in range(len(vectors))]
         loads.append(pltpu.make_async_copy(upstream_ref, upstream, load_sem.at[len(vectors)]))
@@ -616,6 +618,7 @@
             live[span] = (lax.broadcasted_iota(jnp.int32, (BLOCK, 128), 0) < valid).astype(jnp.float32)
             keep = lax.broadcasted_iota(jnp.int32, (BLOCK, width), 0) < valid
             branch[span] = jnp.where(keep, upstream[span].astype(jnp.float32), 0.0).astype(branch.dtype)
+        rest[...] = branch[half:]
         own_half = pltpu.make_async_copy(
             branch.at[pl.ds(0, half)], half_rows.at[pl.ds(pl.multiple_of(mp * half, half), half)], half_sem)
         own_half.start()
@@ -644,6 +647,14 @@
                 span = pl.ds(pl.multiple_of(block * rows + part * chunk, chunk), chunk)
                 unit, _ = unit_rows(raw[span].astype(jnp.float32))
                 normed[span] = (unit * gains[0:1] + gains[1:2]).astype(normed.dtype)
+
+            normed_copy(block).start()
+
+        def normed_copy(block):
+            return pltpu.make_async_copy(
+                normed.at[block_span(block)], normed_out.at[block_span(block)], out_sem.at[block])
+
+        weights_copy = pltpu.make_async_copy(weights, weights_out, out_sem.at[mp_count])
 
         def each_block(low, high, visit):
             @pl.loop(0, mp_count)
@@ -738,6 +749,7 @@
             spread(array)
         for array in range(kinds):
             settle(array)
+        weights_copy.start()
         tiles = kinds * halves
 
         @pl.loop(0, pieces)
@@ -766,6 +778,9 @@
             hand_half(step, jnp.logical_not(between))
         hand_half(last)
         line.finish()
+        weights_copy.wait()
+        for block in range(mp_count):
+            normed_copy(block).wait()
         behind.finish()
         own_half.wait()
         settle(kinds)
@@ -802,11 +817,12 @@
             jax.ShapeDtypeStruct((2, dp_count * group_rows, HEAD_DIM), bf16),
             jax.ShapeDtypeStruct((heads * group_rows, HEAD_DIM), bf16),
             jax.ShapeDtypeStruct((rows, width), bf16),
+            jax.ShapeDtypeStruct((rows - half, width), bf16),
             jax.ShapeDtypeStruct((rows, 128), f32),
             jax.ShapeDtypeStruct((mp_count * half, width), bf16),
         ],
         in_specs=[SMEM, SMEM] + [ANY] * (len(vectors) + kinds + 3),
-        out_specs=[VMEM, VMEM, VMEM, ANY, ANY, ANY, VMEM, VMEM, ANY],
+        out_specs=[ANY, VMEM, ANY, ANY, ANY, ANY, VMEM, VMEM, VMEM, ANY],
         scratch_shapes=[
             pltpu.VMEM((slab, 128), f32),
             pltpu.VMEM((rows, width), bf16),
@@ -822,6 +838,7 @@
         + [dma((kinds, mp_count)), dma((kinds, heads, mp_count)), dma((kinds, heads, mp_count))]
         + [dma((2, heads, mp_count, members)) for _ in range(2)]
         + LineGather.semaphores(mp_count, half_pieces) + [dma(())]
+        + [pltpu.VMEM((group_rows, width), bf16), pltpu.VMEM((width, kinds * columns), bf16), dma((mp_count + 1,))]
         + [pltpu.VMEM(v.shape, v.dtype) for v in vectors],
         compiler_params=pltpu.CompilerParams(
             collective_id=collective_id, has_side_effects=True, vmem_limit_bytes=63 * MIB),
@@ -1233,8 +1250,7 @@
     per_quarter = pieces // QUARTERS
     slice_rows = width // per_quarter
     turns = pieces + SKEW * (mp_count - 1)
-    slices_each = max(dp_count // 8, 1)
-    slice_turn = turns // 3
+    slices_each = max(dp_count // 4, 1)
     group_rows = mp_count * rows
     slab, each = vectors.shape[1], width // dp_count // 128
     query_grad = query_grad.reshape(heads, mp_count, rows, HEAD_DIM)
@@ -1373,16 +1389,26 @@
         arrived(0)
         for part_index in range(per_quarter):
             project(0, part_index * slice_rows, slice_rows)
+        for piece in range(AHEAD):
+            reduce.begin(piece)
         for o in range(chips):
             out_pair(o).start()
         sums_ref[...] = jnp.zeros_like(sums_ref)
 
         @pl.loop(0, turns)
         def _(turn):
-            @pl.when(turn < pieces)
-            def _():
-                reduce.begin(jnp.minimum(turn, pieces - 1))
-
+            for k in range(1, QUARTERS):
+
+                @pl.when(turn == min(2, per_quarter) * (k - 1))
+                def _():
+                    arrived(k)
+
+            @pl.when(turn < (QUARTERS - 1) * per_quarter)
+            def _():
+                k, portion = turn // per_quarter + 1, turn % per_quarter
+                project(k, portion * slice_rows, slice_rows)
+
+            reduce.begin(jnp.minimum(turn + AHEAD, pieces - 1), turn + AHEAD < pieces)
             reduce.advance(turn)
             done = turn - SKEW * (mp_count - 1)
 
@@ -1397,18 +1423,7 @@
                 sums_ref[1:2] += jnp.sum(upstream, axis=0, keepdims=True)
                 grad_ref[span] = residual_ref[span] + norm_back(upstream, unit, inverse, gain_ref[...])
 
-            for k in range(1, QUARTERS):
-
-                @pl.when(turn == (k - 1) * per_quarter)
-                def _():
-                    arrived(k)
-
-            @pl.when(turn < (QUARTERS - 1) * per_quarter)
-            def _():
-                k, portion = turn // per_quarter + 1, turn % per_quarter
-                project(k, portion * slice_rows, slice_rows)
-
-            @pl.when(turn == slice_turn)
+            @pl.when(turn == late_turn - 1)
             def _():
                 for o in list(range(1, chips)) + [0]:
                     out_pair(o).wait_recv()
@@ -1482,7 +1497,7 @@
         for o in range(1, dp_count):
             vector_copy(o).wait_send()
 
-    late_turn = max(slice_turn, (QUARTERS - 2) * per_quarter + 1)
+    late_turn = min(2, per_quarter) * (QUARTERS - 2) + 1
     assert late_turn + dp_count // slices_each <= turns
     dma = pltpu.SemaphoreType.DMA
     bf16, f32 = jnp.bfloat16, jnp.float32
@@ -1637,7 +1652,7 @@
     plan = (seq_lengths, block_order, block_slot)
 
     vectors = (first_gain, first_shift, query_bias, value_bias, out_bias, second_gain, second_shift, down_bias, up_bias)
-    rows_one, vector_rows, projections, out_all, head_shared, head_queries, branch_two, live, branch_first = project_first(
+    rows_one, vector_rows, projections, out_all, head_shared, head_queries, branch_two, branch_rest, live, branch_first = project_first(
         hidden_in, output_grad, seq_lengths, block_order, vectors,
         (key_weight, value_weight, query_weight), out_weight, heads_local, members, 0,
     )
@@ -1650,8 +1665,7 @@
     up_each = up_bias.shape[0] // 128
     bias_up = vector_rows[:, 8 * each : 8 * each + up_each].reshape(1, up_bias.shape[0] * dp_count)
 
-    half = local_rows // 2
-    branch_second = whole_rows(branch_two[half:])
+    branch_second = whole_rows(branch_rest)
     head_mix, exact_mix, log_total = attend(head_queries, head_shared, *plan, members, blocks_each)
     residual, attended_low, rows_two, up_all, down_all = mix_norm_gather(
         head_mix, out_all, hidden_in, bias_out, gain_two, shift_two, (up_weight, down_weight), heads_local, members, 3
@@ -1668,6 +1682,9 @@
     )
     down_weight_grad, up_weight_grad = (
         sum_terms(terms) for terms in (down_terms, up_terms)
+    )
+    residual_grad, down_weight_grad, up_weight_grad = lax.optimization_barrier(
+        (residual_grad, down_weight_grad, up_weight_grad)
     )
 
     feed = row_share(feed_part)

time: 700 us -> 673 us (0.961)
  Pallas kernels: 645 us -> 625 us
    pallas_call x1, Pallas kernels: 138 us -> 113 us  [finish_back(): pl.pallas_call(kernel, out_shape=[jax.ShapeDtypeStruct((rows, width), f32...]
  transfers between devices with their start and end apart: 2 -> 2, of which waited for: 0 -> 0; matrix products, arithmetic and copies ran while one was open for 4% -> 4% of each run, Pallas kernels for 51% -> 50%
where the time goes in v8:
time: 673 us; the launch traced here: 671 us
  Pallas kernels  625 us (93%)
  local copies, waits for them, and re-layouts  15 us (2%)
  between operations  14.4 us (2%)
  other arithmetic  10.2 us (2%)
    pallas_call x1, Pallas kernels, reduce_back_gather(): pl.pallas_call(kernel, out_shape=[jax.ShapeDtypeStruct((rows, width), f32...  130 us
    pallas_call x1, Pallas kernels, mix_norm_gather(): pl.pallas_call(kernel, out_shape=[jax.ShapeDtypeStruct((rows, width), jnp...  128 us
    pallas_call x1, Pallas kernels, project_first(): pl.pallas_call(kernel, out_shape=[jax.ShapeDtypeStruct((group_rows, width...  118 us
    pallas_call x1, Pallas kernels, finish_back(): pl.pallas_call(kernel, out_shape=[jax.ShapeDtypeStruct((rows, width), f32...  113 us
    pallas_call x1, Pallas kernels, attend_back(): pl.pallas_call(kernel, out_shape=[jax.ShapeDtypeStruct(queries.shape, jnp...  50.7 us
    pallas_call x1, Pallas kernels, attend(): pl.pallas_call(kernel, out_shape=[jax.ShapeDtypeStruct(queries.shape, jnp...  43.5 us
    pallas_call x1, Pallas kernels, feed_both_ways(): pl.pallas_call(kernel, grid=(units // tile,), out_shape=[jax.ShapeDtypeSt...  41.8 us
  transfers between devices with their start and end apart: 2, of which 0 were waited for; matrix products, arithmetic and copies ran while one was open for 4% of the time, Pallas kernels for 50%

profile of v8, /device:TPU:0, one launch (start us, length us, event | category | flops | bytes accessed | tf_op | source)
XLA Modules:
  0.0 670.8 jit_solution(3995258839746398213)
XLA Ops:
  7.2 0.0 all-gather.2.cloned.1.call-start
  7.2 117.8 %shard_map.323 = (bf16[1024,2048]{1,0:T(8,128)(2,1)}, f32[192,128]{1,0:T(8,128)}, bf16[2048,1536]{1,0:T(8,128)(2,1)}, bf16[2048,512]{1,0:T(8,128)(2,1)}, bf16[2,...) custom-call(s32[8]{0:T(128)} %lengths_ref.5, ...), custom_call_target="tpu_custom_call" | custom-call | flops 8589934592 | bytes 262144000 | tf_op jit(solution)/shard_map/pallas_call | solution.py:810
  125.1 0.0 all-gather.2.cloned.1.call-update
  125.1 0.0 reduce-scatter.2.cloned.1.call-start
  125.1 0.8 slice.123
  125.9 1.7 fusion.2
  127.6 43.5 %shard_map.324 = (bf16[4096,128]{1,0:T(8,128)(2,1)}, f32[16,128,256]{2,1,0:T(8,128)}, f32[16,1,256]{2,1,0:T(1,128)}) custom-call(s32[8]{0:T(128)} %lengths_ref.5, s32[64]{0:T(128)} %slot_ref.3, bf16[4096,128]{1,0:T(8,128)(2,1)} %get-tuple-element.57.q_ref, bf16[2,8192,128]{2,1,0:T(8,128)(2,1)} %get-tuple-element.58.shared_ref), custom_call_target="tpu_custom_call" | custom-call | flops 8589934592 | bytes 52428800 | tf_op jit(solution)/shard_map/pallas_call | solution.py:194
  171.0 128.3 %shard_map.325 = (f32[256,2048]{1,0:T(8,128)}, bf16[4,256,512]{2,1,0:T(8,128)(2,1)}, bf16[1024,2048]{1,0:T(8,128)(2,1)}, bf16[2048,2048]{1,0:T(8,128)(2,1)}, bf16[2048,2048]{1,0:T(8,128)(2,1)}) custom-call(bf16[4,4,256,128]{3,2,1,0:T(8,128)(2,1)} %bitcast.43, bf16[2048,512]{1,0:T(8,128)(2,1)} %get-tuple-element.60.out_hbm.refs_6_, ...), custom_call_target="tpu_custom_call" | custom-call | bytes 314572800 | tf_op jit(solution)/shard_map/pallas_call | solution.py:960
  299.4 0.6 constant_dynamic-slice_fusion.bias_ref
  300.0 0.0 all-gather.2.cloned.1.call-done.second_ref.refs_1_
  300.0 41.8 %shard_map.326 = (bf16[1024,2048]{1,0:T(8,128)(2,1)}, bf16[1024,2048]{1,0:T(8,128)(2,1)}, f32[1,2048]{1,0:T(1,128)}, bf16[1024,2048]{1,0:T(8,128)(2,1)}) custom-call(bf16[1024,2048]{1,0:T(8,128)(2,1)} %get-tuple-element.63.rows_ref.refs_3_, bf16[512,2048]{1,0:T(8,128)(2,1)} %get-tuple-element.64.first_ref.refs_0_, ...), custom_call_target="tpu_custom_call" | custom-call | flops 25769803776 | bytes 41943040 | tf_op jit(solution)/shard_map/pallas_call | solution.py:1587
  341.8 130.0 %shard_map.327 = (f32[256,2048]{1,0:T(8,128)}, f32[8,2048]{1,0:T(8,128)}, bf16[1024,2048]{1,0:T(8,128)(2,1)}, bf16[1024,2048]{1,0:T(8,128)(2,1)}, bf16[4,4,256,1...) custom-call(bf16[1024,2048]{1,0:T(8,128)(2,1)} %get-tuple-element.68.part_ref, ...), custom_call_target="tpu_custom_call" | custom-call | flops 42949672960 | bytes 314572800 | tf_op jit(solution)/shard_map/pallas_call | solution.py:1204
  471.9 0.0 copy-start.4
  471.9 0.0 copy-start.2
  471.9 0.0 reduce-scatter.2.cloned.1.call-update
  471.9 0.9 copy-done.4
  472.8 0.1 fusion
  472.9 0.3 copy-done.2
  473.2 0.2 convert_reduce_fusion
  473.3 0.0 copy-start.5
  473.3 0.0 copy-start.6
  473.4 7.2 %add_bitcast_fusion = (f32[256,2048]{1,0:T(8,128)}, f32[256,2048]{1,0:T(8,128)}) fusion(bf16[4,256,2048]{2,1,0:T(8,128)(2,1)} %get-tuple-element.83, bf16[4,256,2048]{2,1,0:T(8,128)(2,1)} %get-tuple-element.82), kind=kLoop, calls=%fused_computation.2 | loop fusion | flops 7340032 | bytes 12582912 | tf_op jit(solution)/shard_map/add | solution.py:1618
  480.6 0.0 copy-done.5
  480.6 0.3 dynamic_update_slice.3
  480.9 1.0 fusion.3
  481.9 1.9 concatenate.7.vector_ref
  483.8 0.0 copy-done.6
  483.8 5.9 convolution_convert_fusion.out_ref
  489.7 50.7 %shard_map.328 = (bf16[4096,128]{1,0:T(8,128)(2,1)}, bf16[8192,128]{1,0:T(8,128)(2,1)}, bf16[8192,128]{1,0:T(8,128)(2,1)}) custom-call(s32[8]{0:T(128)} %lengths_ref.5, s32[64]{0:T(128)} %slot_ref.3, bf16[4096,128]{1,0:T(8,128)(2,1)} %get-tuple-element.57.q_ref, bf16[2,8192,128]{2,1,0:T(8,128)(2,1)} %get-tuple-element.58.shared_ref, ...), custom_call_target="tpu_custom_call" | custom-call | flops 21474836480 | bytes 104857600 | tf_op jit(solution)/shard_map/pallas_call | solution.py:272
  540.4 113.1 %shard_map.329 = (f32[256,2048]{1,0:T(8,128)}, f32[256,1536]{1,0:T(8,128)}, f32[256,512]{1,0:T(8,128)}, f32[24,128]{1,0:T(8,128)}) custom-call(bf16[4,4,256,128]{3,2,1,0:T(8,128)(2,1)} %bitcast.63, bf16[8,4,256,128]{3,2,1,0:T(8,128)(2,1)} %bitcast.60, bf16[8,4,256,128]{3,2,1,0:T(8,128)(2,1)} %bitcast.61, bf16[2048,1536]{1,0:T(8,128)(2,1)} %get-tuple-element.79.weights_hbm, ...), custom_call_target="tpu_custom_call" | custom-call | flops 21474836480 | bytes 314572800 | tf_op jit(solution)/shard_map/pallas_call | solution.py:1505
  653.4 0.0 copy-start
  653.5 1.4 slice_bitcast_fusion
  654.9 1.4 slice_bitcast_fusion.1
  656.3 2.5 fusion.1
  658.8 0.0 reduce-scatter.2.cloned.1.call-done
  658.8 0.0 copy-done
  658.8 0.0 copy-start.1
  658.8 2.7 select_convert_fusion
  661.6 0.0 copy-done.1
  661.6 0.0 copy-start.3
  661.6 1.3 copy.40
  662.9 0.1 copy-done.3
  663.0 0.8 copy.41
  (2 shorter events, 0.0 us)
Async XLA Ops:
  7.2 292.8 %all-gather.2.cloned.1.call-start = ((), (), s32[]{:S(2)}) async-start(), calls=%async_computation.1 | async-start | bytes 2621440 | tf_op jit(solution)/shard_map/all_gather | solution.py:45
  125.1 533.7 %reduce-scatter.2.cloned.1.call-start = ((), (), s32[]{:S(2)}) async-start(), calls=%async_computation.2 | async-start | bytes 5242880 | tf_op jit(solution)/shard_map/reduce_scatter | solution.py:50
  471.9 0.9 copy-start.4
  471.9 1.3 copy-start.2
  473.3 7.3 %copy-start.5 = (f32[1,2048]{1,0:T(1,128)S(1)}, f32[1,2048]{1,0:T(1,128)}, u32[]{:S(2)}) copy-start(f32[1,2048]{1,0:T(1,128)} %get-tuple-element.88) | copy-start | bytes 24580
  473.3 10.5 %copy-start.6 = (bf16[4,256,512]{2,1,0:T(8,128)(2,1)S(1)}, bf16[4,256,512]{2,1,0:T(8,128)(2,1)}, u32[]{:S(2)}) copy-start(bf16[4,256,512]{2,1,0:T(8,128)(2,1)} %get-tuple-element.86) | copy-start | bytes 3145732
  653.4 5.4 copy-start
  658.8 2.7 copy-start.1
  661.6 1.4 copy-start.3
Sparse Core Ops, SparseCore 0:
  125.2 45.1 all-gather.1
  472.0 79.6 reduce-scatter.1

commit v9 on v8

--- a/solution.py
+++ b/solution.py
@@ -1539,7 +1539,7 @@
 
 
 UNITS = 512
-CHUNK = 256
+CHUNK = 1024
 
 
 def feed_both_ways(rows_two, branch_halves, block, up_all, down_all, up_bias):

time: 673 us -> 667 us (level)
  Pallas kernels: 625 us -> 616 us
    pallas_call x1, Pallas kernels: 50.7 us -> 42.8 us  [attend_back(): pl.pallas_call(kernel, out_shape=[jax.ShapeDtypeStruct(queries.shape, jnp...]
    pallas_call x1, Pallas kernels: 43.5 us -> 36.7 us  [attend(): pl.pallas_call(kernel, out_shape=[jax.ShapeDtypeStruct(queries.shape, jnp...]
where the time goes in v9:
time: 667 us; the launch traced here: 661 us
  Pallas kernels  616 us (92%)
  local copies, waits for them, and re-layouts  15 us (2%)
  between operations  14.4 us (2%)
  other arithmetic  10.2 us (2%)
    pallas_call x1, Pallas kernels, reduce_back_gather(): pl.pallas_call(kernel, out_shape=[jax.ShapeDtypeStruct((rows, width), f32...  130 us
    pallas_call x1, Pallas kernels, mix_norm_gather(): pl.pallas_call(kernel, out_shape=[jax.ShapeDtypeStruct((rows, width), jnp...  130 us
    pallas_call x1, Pallas kernels, finish_back(): pl.pallas_call(kernel, out_shape=[jax.ShapeDtypeStruct((rows, width), f32...  119 us
    pallas_call x1, Pallas kernels, project_first(): pl.pallas_call(kernel, out_shape=[jax.ShapeDtypeStruct((group_rows, width...  118 us
    pallas_call x1, Pallas kernels, attend_back(): pl.pallas_call(kernel, out_shape=[jax.ShapeDtypeStruct(queries.shape, jnp...  42.8 us
    pallas_call x1, Pallas kernels, feed_both_ways(): pl.pallas_call(kernel, grid=(units // tile,), out_shape=[jax.ShapeDtypeSt...  38.7 us
    pallas_call x1, Pallas kernels, attend(): pl.pallas_call(kernel, out_shape=[jax.ShapeDtypeStruct(queries.shape, jnp...  36.7 us
  transfers between devices with their start and end apart: 2, of which 0 were waited for; matrix products, arithmetic and copies ran while one was open for 4% of the time, Pallas kernels for 50%

profile of v9, /device:TPU:0, one launch (start us, length us, event | category | flops | bytes accessed | tf_op | source)
XLA Modules:
  0.0 661.3 jit_solution(6968260582730406106)
XLA Ops:
  7.2 0.0 all-gather.2.cloned.1.call-start
  7.2 117.8 %shard_map.323 = (bf16[1024,2048]{1,0:T(8,128)(2,1)}, f32[192,128]{1,0:T(8,128)}, bf16[2048,1536]{1,0:T(8,128)(2,1)}, bf16[2048,512]{1,0:T(8,128)(2,1)}, bf16[2,...) custom-call(s32[8]{0:T(128)} %lengths_ref.5, ...), custom_call_target="tpu_custom_call" | custom-call | flops 8589934592 | bytes 262144000 | tf_op jit(solution)/shard_map/pallas_call | solution.py:810
  125.1 0.0 all-gather.2.cloned.1.call-update
  125.1 0.0 reduce-scatter.2.cloned.1.call-start
  125.1 0.8 slice.123
  125.9 1.7 fusion.2
  127.6 36.7 %shard_map.324 = (bf16[4096,128]{1,0:T(8,128)(2,1)}, f32[16,128,256]{2,1,0:T(8,128)}, f32[16,1,256]{2,1,0:T(1,128)}) custom-call(s32[8]{0:T(128)} %lengths_ref.5, s32[64]{0:T(128)} %slot_ref.3, bf16[4096,128]{1,0:T(8,128)(2,1)} %get-tuple-element.57.q_ref, bf16[2,8192,128]{2,1,0:T(8,128)(2,1)} %get-tuple-element.58.shared_ref), custom_call_target="tpu_custom_call" | custom-call | flops 8589934592 | bytes 52428800 | tf_op jit(solution)/shard_map/pallas_call | solution.py:194
  164.2 130.0 %shard_map.325 = (f32[256,2048]{1,0:T(8,128)}, bf16[4,256,512]{2,1,0:T(8,128)(2,1)}, bf16[1024,2048]{1,0:T(8,128)(2,1)}, bf16[2048,2048]{1,0:T(8,128)(2,1)}, bf16[2048,2048]{1,0:T(8,128)(2,1)}) custom-call(bf16[4,4,256,128]{3,2,1,0:T(8,128)(2,1)} %bitcast.43, bf16[2048,512]{1,0:T(8,128)(2,1)} %get-tuple-element.60.out_hbm.refs_6_, ...), custom_call_target="tpu_custom_call" | custom-call | bytes 314572800 | tf_op jit(solution)/shard_map/pallas_call | solution.py:960
  294.2 0.6 constant_dynamic-slice_fusion.bias_ref
  294.8 0.0 all-gather.2.cloned.1.call-done.second_ref.refs_1_
  294.8 38.7 %shard_map.326 = (bf16[1024,2048]{1,0:T(8,128)(2,1)}, bf16[1024,2048]{1,0:T(8,128)(2,1)}, f32[1,2048]{1,0:T(1,128)}, bf16[1024,2048]{1,0:T(8,128)(2,1)}) custom-call(bf16[1024,2048]{1,0:T(8,128)(2,1)} %get-tuple-element.63.rows_ref.refs_3_, bf16[512,2048]{1,0:T(8,128)(2,1)} %get-tuple-element.64.first_ref.refs_0_, ...), custom_call_target="tpu_custom_call" | custom-call | flops 25769803776 | bytes 41943040 | tf_op jit(solution)/shard_map/pallas_call | solution.py:1587
  333.6 130.3 %shard_map.327 = (f32[256,2048]{1,0:T(8,128)}, f32[8,2048]{1,0:T(8,128)}, bf16[1024,2048]{1,0:T(8,128)(2,1)}, bf16[1024,2048]{1,0:T(8,128)(2,1)}, bf16[4,4,256,1...) custom-call(bf16[1024,2048]{1,0:T(8,128)(2,1)} %get-tuple-element.68.part_ref, ...), custom_call_target="tpu_custom_call" | custom-call | flops 42949672960 | bytes 314572800 | tf_op jit(solution)/shard_map/pallas_call | solution.py:1204
  463.9 0.0 copy-start.4
  463.9 0.0 copy-start.2
  463.9 0.0 reduce-scatter.2.cloned.1.call-update
  464.0 0.9 copy-done.4
  464.8 0.1 fusion
  464.9 0.3 copy-done.2
  465.2 0.2 convert_reduce_fusion
  465.4 0.0 copy-start.5
  465.4 0.0 copy-start.6
  465.4 7.2 %add_bitcast_fusion = (f32[256,2048]{1,0:T(8,128)}, f32[256,2048]{1,0:T(8,128)}) fusion(bf16[4,256,2048]{2,1,0:T(8,128)(2,1)} %get-tuple-element.83, bf16[4,256,2048]{2,1,0:T(8,128)(2,1)} %get-tuple-element.82), kind=kLoop, calls=%fused_computation.2 | loop fusion | flops 7340032 | bytes 12582912 | tf_op jit(solution)/shard_map/add | solution.py:1618
  472.6 0.0 copy-done.5
  472.6 0.3 dynamic_update_slice.3
  473.0 1.0 fusion.3
  474.0 1.9 concatenate.7.vector_ref
  475.9 0.0 copy-done.6
  475.9 5.9 convolution_convert_fusion.out_ref
  481.8 42.8 %shard_map.328 = (bf16[4096,128]{1,0:T(8,128)(2,1)}, bf16[8192,128]{1,0:T(8,128)(2,1)}, bf16[8192,128]{1,0:T(8,128)(2,1)}) custom-call(s32[8]{0:T(128)} %lengths_ref.5, s32[64]{0:T(128)} %slot_ref.3, bf16[4096,128]{1,0:T(8,128)(2,1)} %get-tuple-element.57.q_ref, bf16[2,8192,128]{2,1,0:T(8,128)(2,1)} %get-tuple-element.58.shared_ref, ...), custom_call_target="tpu_custom_call" | custom-call | flops 21474836480 | bytes 104857600 | tf_op jit(solution)/shard_map/pallas_call | solution.py:272
  524.6 119.4 %shard_map.329 = (f32[256,2048]{1,0:T(8,128)}, f32[256,1536]{1,0:T(8,128)}, f32[256,512]{1,0:T(8,128)}, f32[24,128]{1,0:T(8,128)}) custom-call(bf16[4,4,256,128]{3,2,1,0:T(8,128)(2,1)} %bitcast.63, bf16[8,4,256,128]{3,2,1,0:T(8,128)(2,1)} %bitcast.60, bf16[8,4,256,128]{3,2,1,0:T(8,128)(2,1)} %bitcast.61, bf16[2048,1536]{1,0:T(8,128)(2,1)} %get-tuple-element.79.weights_hbm, ...), custom_call_target="tpu_custom_call" | custom-call | flops 21474836480 | bytes 314572800 | tf_op jit(solution)/shard_map/pallas_call | solution.py:1505
  644.0 0.0 copy-start
  644.0 1.4 slice_bitcast_fusion
  645.4 1.4 slice_bitcast_fusion.1
  646.8 2.5 fusion.1
  649.3 0.0 reduce-scatter.2.cloned.1.call-done
  649.3 0.0 copy-done
  649.3 0.0 copy-start.1
  649.3 2.7 select_convert_fusion
  652.1 0.0 copy-done.1
  652.1 0.0 copy-start.3
  652.1 1.3 copy.40
  653.4 0.1 copy-done.3
  653.5 0.8 copy.41
  (2 shorter events, 0.0 us)
Async XLA Ops:
  7.2 287.6 %all-gather.2.cloned.1.call-start = ((), (), s32[]{:S(2)}) async-start(), calls=%async_computation.1 | async-start | bytes 2621440 | tf_op jit(solution)/shard_map/all_gather | solution.py:45
  125.1 524.2 %reduce-scatter.2.cloned.1.call-start = ((), (), s32[]{:S(2)}) async-start(), calls=%async_computation.2 | async-start | bytes 5242880 | tf_op jit(solution)/shard_map/reduce_scatter | solution.py:50
  463.9 0.9 copy-start.4
  463.9 1.3 copy-start.2
  465.4 7.3 %copy-start.5 = (f32[1,2048]{1,0:T(1,128)S(1)}, f32[1,2048]{1,0:T(1,128)}, u32[]{:S(2)}) copy-start(f32[1,2048]{1,0:T(1,128)} %get-tuple-element.88) | copy-start | bytes 24580
  465.4 10.5 %copy-start.6 = (bf16[4,256,512]{2,1,0:T(8,128)(2,1)S(1)}, bf16[4,256,512]{2,1,0:T(8,128)(2,1)}, u32[]{:S(2)}) copy-start(bf16[4,256,512]{2,1,0:T(8,128)(2,1)} %get-tuple-element.86) | copy-start | bytes 3145732
  644.0 5.4 copy-start
  649.3 2.7 copy-start.1
  652.1 1.4 copy-start.3
Sparse Core Ops, SparseCore 0:
  125.2 45.1 all-gather.1
  464.1 79.5 reduce-scatter.1

commit v10 on v9

--- a/solution.py
+++ b/solution.py
@@ -913,7 +913,7 @@
         def _(turn):
             for array in range(count):
 
-                @pl.when(turn == turns - 1 - 6 * (count - 1 - array))
+                @pl.when(turn == turns - 3 - 6 * (count - 1 - array))
                 def _():
                     weights.spread(array)
 

time: 667 us -> 664 us (level)
  no operation moved by 1% of the time
where the time goes in v10:
time: 664 us; the launch traced here: 660 us
  Pallas kernels  615 us (93%)
  local copies, waits for them, and re-layouts  14.9 us (2%)
  between operations  14.4 us (2%)
  other arithmetic  10.4 us (2%)
    pallas_call x1, Pallas kernels, reduce_back_gather(): pl.pallas_call(kernel, out_shape=[jax.ShapeDtypeStruct((rows, width), f32...  130 us
    pallas_call x1, Pallas kernels, mix_norm_gather(): pl.pallas_call(kernel, out_shape=[jax.ShapeDtypeStruct((rows, width), jnp...  126 us
    pallas_call x1, Pallas kernels, project_first(): pl.pallas_call(kernel, out_shape=[jax.ShapeDtypeStruct((group_rows, width...  118 us
    pallas_call x1, Pallas kernels, finish_back(): pl.pallas_call(kernel, out_shape=[jax.ShapeDtypeStruct((rows, width), f32...  114 us
    pallas_call x1, Pallas kernels, attend_back(): pl.pallas_call(kernel, out_shape=[jax.ShapeDtypeStruct(queries.shape, jnp...  47.4 us
    pallas_call x1, Pallas kernels, attend(): pl.pallas_call(kernel, out_shape=[jax.ShapeDtypeStruct(queries.shape, jnp...  40.6 us
    pallas_call x1, Pallas kernels, feed_both_ways(): pl.pallas_call(kernel, grid=(units // tile,), out_shape=[jax.ShapeDtypeSt...  38.7 us
  transfers between devices with their start and end apart: 2, of which 0 were waited for; matrix products, arithmetic and copies ran while one was open for 4% of the time, Pallas kernels for 50%

profile of v10, /device:TPU:0, one launch (start us, length us, event | category | flops | bytes accessed | tf_op | source)
XLA Modules:
  0.0 660.3 jit_solution(5346510947332711891)
XLA Ops:
  7.2 0.0 all-gather.2.cloned.1.call-start
  7.2 117.8 %shard_map.323 = (bf16[1024,2048]{1,0:T(8,128)(2,1)}, f32[192,128]{1,0:T(8,128)}, bf16[2048,1536]{1,0:T(8,128)(2,1)}, bf16[2048,512]{1,0:T(8,128)(2,1)}, bf16[2,...) custom-call(s32[8]{0:T(128)} %lengths_ref.5, ...), custom_call_target="tpu_custom_call" | custom-call | flops 8589934592 | bytes 262144000 | tf_op jit(solution)/shard_map/pallas_call | solution.py:810
  125.1 0.0 all-gather.2.cloned.1.call-update
  125.1 0.0 reduce-scatter.2.cloned.1.call-start
  125.1 0.8 slice.123
  125.9 1.7 fusion.2
  127.6 40.6 %shard_map.324 = (bf16[4096,128]{1,0:T(8,128)(2,1)}, f32[16,128,256]{2,1,0:T(8,128)}, f32[16,1,256]{2,1,0:T(1,128)}) custom-call(s32[8]{0:T(128)} %lengths_ref.5, s32[64]{0:T(128)} %slot_ref.3, bf16[4096,128]{1,0:T(8,128)(2,1)} %get-tuple-element.57.q_ref, bf16[2,8192,128]{2,1,0:T(8,128)(2,1)} %get-tuple-element.58.shared_ref), custom_call_target="tpu_custom_call" | custom-call | flops 8589934592 | bytes 52428800 | tf_op jit(solution)/shard_map/pallas_call | solution.py:194
  168.1 125.7 %shard_map.325 = (f32[256,2048]{1,0:T(8,128)}, bf16[4,256,512]{2,1,0:T(8,128)(2,1)}, bf16[1024,2048]{1,0:T(8,128)(2,1)}, bf16[2048,2048]{1,0:T(8,128)(2,1)}, bf16[2048,2048]{1,0:T(8,128)(2,1)}) custom-call(bf16[4,4,256,128]{3,2,1,0:T(8,128)(2,1)} %bitcast.43, bf16[2048,512]{1,0:T(8,128)(2,1)} %get-tuple-element.60.out_hbm.refs_6_, ...), custom_call_target="tpu_custom_call" | custom-call | bytes 314572800 | tf_op jit(solution)/shard_map/pallas_call | solution.py:960
  293.8 0.6 constant_dynamic-slice_fusion.bias_ref
  294.4 0.0 all-gather.2.cloned.1.call-done.second_ref.refs_1_
  294.5 38.7 %shard_map.326 = (bf16[1024,2048]{1,0:T(8,128)(2,1)}, bf16[1024,2048]{1,0:T(8,128)(2,1)}, f32[1,2048]{1,0:T(1,128)}, bf16[1024,2048]{1,0:T(8,128)(2,1)}) custom-call(bf16[1024,2048]{1,0:T(8,128)(2,1)} %get-tuple-element.63.rows_ref.refs_3_, bf16[512,2048]{1,0:T(8,128)(2,1)} %get-tuple-element.64.first_ref.refs_0_, ...), custom_call_target="tpu_custom_call" | custom-call | flops 25769803776 | bytes 41943040 | tf_op jit(solution)/shard_map/pallas_call | solution.py:1587
  333.2 130.3 %shard_map.327 = (f32[256,2048]{1,0:T(8,128)}, f32[8,2048]{1,0:T(8,128)}, bf16[1024,2048]{1,0:T(8,128)(2,1)}, bf16[1024,2048]{1,0:T(8,128)(2,1)}, bf16[4,4,256,1...) custom-call(bf16[1024,2048]{1,0:T(8,128)(2,1)} %get-tuple-element.68.part_ref, ...), custom_call_target="tpu_custom_call" | custom-call | flops 42949672960 | bytes 314572800 | tf_op jit(solution)/shard_map/pallas_call | solution.py:1204
  463.5 0.0 copy-start.4
  463.5 0.0 copy-start.2
  463.5 0.0 reduce-scatter.2.cloned.1.call-update
  463.5 0.9 copy-done.4
  464.4 0.1 fusion
  464.5 0.3 copy-done.2
  464.8 0.2 convert_reduce_fusion
  464.9 0.0 copy-start.5
  465.0 0.0 copy-start.6
  465.0 7.4 %add_bitcast_fusion = (f32[256,2048]{1,0:T(8,128)}, f32[256,2048]{1,0:T(8,128)}) fusion(bf16[4,256,2048]{2,1,0:T(8,128)(2,1)} %get-tuple-element.83, bf16[4,256,2048]{2,1,0:T(8,128)(2,1)} %get-tuple-element.82), kind=kLoop, calls=%fused_computation.2 | loop fusion | flops 7340032 | bytes 12582912 | tf_op jit(solution)/shard_map/add | solution.py:1618
  472.4 0.0 copy-done.5
  472.4 0.3 dynamic_update_slice.3
  472.7 1.0 fusion.3
  473.7 1.9 concatenate.7.vector_ref
  475.6 0.0 copy-done.6
  475.6 5.9 convolution_convert_fusion.out_ref
  481.5 47.4 %shard_map.328 = (bf16[4096,128]{1,0:T(8,128)(2,1)}, bf16[8192,128]{1,0:T(8,128)(2,1)}, bf16[8192,128]{1,0:T(8,128)(2,1)}) custom-call(s32[8]{0:T(128)} %lengths_ref.5, s32[64]{0:T(128)} %slot_ref.3, bf16[4096,128]{1,0:T(8,128)(2,1)} %get-tuple-element.57.q_ref, bf16[2,8192,128]{2,1,0:T(8,128)(2,1)} %get-tuple-element.58.shared_ref, ...), custom_call_target="tpu_custom_call" | custom-call | flops 21474836480 | bytes 104857600 | tf_op jit(solution)/shard_map/pallas_call | solution.py:272
  528.9 114.1 %shard_map.329 = (f32[256,2048]{1,0:T(8,128)}, f32[256,1536]{1,0:T(8,128)}, f32[256,512]{1,0:T(8,128)}, f32[24,128]{1,0:T(8,128)}) custom-call(bf16[4,4,256,128]{3,2,1,0:T(8,128)(2,1)} %bitcast.63, bf16[8,4,256,128]{3,2,1,0:T(8,128)(2,1)} %bitcast.60, bf16[8,4,256,128]{3,2,1,0:T(8,128)(2,1)} %bitcast.61, bf16[2048,1536]{1,0:T(8,128)(2,1)} %get-tuple-element.79.weights_hbm, ...), custom_call_target="tpu_custom_call" | custom-call | flops 21474836480 | bytes 314572800 | tf_op jit(solution)/shard_map/pallas_call | solution.py:1505
  643.0 0.0 copy-start
  643.0 1.4 slice_bitcast_fusion
  644.4 1.4 slice_bitcast_fusion.1
  645.9 2.5 fusion.1
  648.4 0.0 reduce-scatter.2.cloned.1.call-done
  648.4 0.0 copy-done
  648.4 0.0 copy-start.1
  648.4 2.7 select_convert_fusion
  651.1 0.0 copy-done.1
  651.1 0.0 copy-start.3
  651.1 1.3 copy.40
  652.4 0.1 copy-done.3
  652.5 0.8 copy.41
  (2 shorter events, 0.0 us)
Async XLA Ops:
  7.2 287.3 %all-gather.2.cloned.1.call-start = ((), (), s32[]{:S(2)}) async-start(), calls=%async_computation.1 | async-start | bytes 2621440 | tf_op jit(solution)/shard_map/all_gather | solution.py:45
  125.1 523.3 %reduce-scatter.2.cloned.1.call-start = ((), (), s32[]{:S(2)}) async-start(), calls=%async_computation.2 | async-start | bytes 5242880 | tf_op jit(solution)/shard_map/reduce_scatter | solution.py:50
  463.5 0.9 copy-start.4
  463.5 1.3 copy-start.2
  464.9 7.4 %copy-start.5 = (f32[1,2048]{1,0:T(1,128)S(1)}, f32[1,2048]{1,0:T(1,128)}, u32[]{:S(2)}) copy-start(f32[1,2048]{1,0:T(1,128)} %get-tuple-element.88) | copy-start | bytes 24580
  465.0 10.6 %copy-start.6 = (bf16[4,256,512]{2,1,0:T(8,128)(2,1)S(1)}, bf16[4,256,512]{2,1,0:T(8,128)(2,1)}, u32[]{:S(2)}) copy-start(bf16[4,256,512]{2,1,0:T(8,128)(2,1)} %get-tuple-element.86) | copy-start | bytes 3145732
  643.0 5.4 copy-start
  648.4 2.7 copy-start.1
  651.1 1.4 copy-start.3
Sparse Core Ops, SparseCore 0:
  125.2 45.1 all-gather.1
  463.6 78.6 reduce-scatter.1
